TPU v7x, 32 devices: a whole 2x2x4 slice. The times are simulated.
32 devices in a mesh: sector: 4 (over z), tm: 2 (over x), space: 4 (over y, core).
Axes of the slice: x: 2, y: 2, z: 4, core: 2. Of those that a mesh axis runs over, the one named last changes fastest.
Arguments:
- records: bfloat16 [16, 592, 3, 8192], P('sector', 'tm', None, 'space'), may hold values from -6 to 6
- block_start: int32 [16], replicated, may hold values from 0 to 231, as said below
- slab_index: int32 [8192], P('space'), may hold values from 0 to 15
- weight_table: float32 [16], replicated, may hold values from 0.25 to 4
Outputs:
- mode_fields: bfloat16 [8, 32, 2, 8, 3, 8192], P(None, ('sector', 'tm'), None, None, None, 'space')
- energy: float32 [8, 32, 8], P(None, ('sector', 'tm'))
Inputs may be any that keep to these rules, and one draw needn't show every extreme that they name: `block_start`: block j of each record (j < 8) starts at j * 32 plus 0 to 7 snapshots.
All inputs are finite; a program needn't handle non-finite values.
Results may differ from a plain program's by a relative error of at most 0.02.
Values may be sent and summed in bfloat16 or wider, within the bound.
No kernel may reach another device: no remote copies, remote signals or barrier semaphores. Data moves between devices by JAX's collectives and lax.ppermute only.
A program may use at most 128 MiB of HBM per device.

v0:
```python
import math

import jax
import jax.numpy as jnp
from jax import lax
from jax.sharding import PartitionSpec as P

NFFT = 64
NFREQ = 32
MODES = 8
SUBIT = 4


EPSILON = 1e-06


def time_table(length, freq_count):
    steps_t = jnp.arange(length, dtype=jnp.float32)
    freq_f = jnp.arange(freq_count, dtype=jnp.float32)
    window = 0.5 - 0.5 * jnp.cos(2.0 * math.pi * steps_t / length)
    angles = 2.0 * math.pi * freq_f[:, None] * steps_t[None, :] / length
    both = jnp.stack([window * jnp.cos(angles), -window * jnp.sin(angles)])
    return (both / math.sqrt(length)).astype(jnp.bfloat16)


def order_table(orders, sectors):
    order_m = jnp.arange(orders, dtype=jnp.float32)[:, None]
    sector_s = jnp.arange(sectors, dtype=jnp.float32)[None, :]
    angles = 2.0 * math.pi * order_m * sector_s / sectors
    cosine = jnp.cos(angles)
    sine_part = jnp.sin(angles)
    upper_row = jnp.stack([cosine, sine_part], -1)
    lower_row = jnp.stack([-sine_part, cosine], -1)
    return (jnp.stack([upper_row, lower_row], 1) / math.sqrt(sectors)).astype(jnp.bfloat16)


def matmul_high(left_side, right_side):
    return jnp.matmul(left_side, right_side, precision=lax.Precision.HIGHEST)


def subspace(gram_re, gram_im):
    order_size = gram_re.shape[-1]
    basis_re = jnp.broadcast_to(
        jnp.eye(order_size, MODES, dtype=jnp.float32), gram_re.shape[:-1] + (MODES,)
    )
    basis_im = jnp.zeros_like(basis_re)
    for sweep in range(SUBIT):
        image_re = matmul_high(gram_re, basis_re) - matmul_high(gram_im, basis_im)
        image_im = matmul_high(gram_re, basis_im) + matmul_high(gram_im, basis_re)
        done_re = []
        done_im = []
        for column in range(MODES):
            vec_re = image_re[..., column]
            vec_im = image_im[..., column]
            for earlier in range(column):
                old_re = done_re[earlier]
                old_im = done_im[earlier]
                proj_re = jnp.sum(old_re * vec_re + old_im * vec_im, -1, keepdims=True)
                proj_im = jnp.sum(old_re * vec_im - old_im * vec_re, -1, keepdims=True)
                vec_re = vec_re - (proj_re * old_re - proj_im * old_im)
                vec_im = vec_im - (proj_re * old_im + proj_im * old_re)
            length_v = jnp.sqrt(
                jnp.sum(vec_re * vec_re + vec_im * vec_im, -1, keepdims=True) + EPSILON
            )
            done_re.append(vec_re / length_v)
            done_im.append(vec_im / length_v)
        basis_re = jnp.stack(done_re, -1)
        basis_im = jnp.stack(done_im, -1)
    return (basis_re, basis_im)


def cell_weight(slab_rows, weight_table):
    choose = (
        slab_rows[:, None] == jnp.arange(weight_table.shape[0], dtype=jnp.int32)[None, :]
    ).astype(jnp.float32)
    return jnp.dot(choose, weight_table, precision=lax.Precision.HIGHEST)


def gram(coeffs, weight):
    weighted = (coeffs.astype(jnp.float32) * weight).astype(jnp.bfloat16)
    products = jnp.einsum(
        "mcbfkx,mdefkx->mfcbde", weighted, coeffs, preferred_element_type=jnp.float32
    )
    gram_re = products[:, :, 0, :, 0, :] + products[:, :, 1, :, 1, :]
    gram_im = products[:, :, 0, :, 1, :] - products[:, :, 1, :, 0, :]
    return (gram_re, gram_im)


def finish(coeffs, gram_re, gram_im, weight, cell_total):
    basis_re, basis_im = subspace(gram_re, gram_im)
    image_re = matmul_high(gram_re, basis_re) - matmul_high(gram_im, basis_im)
    image_im = matmul_high(gram_re, basis_im) + matmul_high(gram_im, basis_re)
    energy = jnp.sum(basis_re * image_re + basis_im * image_im, -2) / cell_total
    short_re = basis_re.astype(jnp.bfloat16)
    short_im = basis_im.astype(jnp.bfloat16)
    first_row = jnp.stack([short_re, short_im], -2)
    second_row = jnp.stack([-short_im, short_re], -2)
    mixing = jnp.stack([first_row, second_row], 2)
    fields_out = jnp.einsum(
        "mcbfkx,mfcbdj->mfdjkx", coeffs, mixing, preferred_element_type=jnp.float32
    )
    factor = lax.rsqrt(energy)[:, :, None, :, None, None] * jnp.sqrt(weight)
    return ((fields_out * factor).astype(jnp.bfloat16), energy)


def local(records, block_start, slab_index, weight_table):
    sec_local, rec_len, fields, cell_local = records.shape
    sec_count = lax.axis_size("sector")
    tm_count = lax.axis_size("tm")
    block_count = block_start.shape[0] // tm_count
    order_total = sec_local * sec_count // 2
    time_basis = time_table(NFFT, NFREQ)
    azimuth = order_table(order_total, sec_local * sec_count)
    own_starts = lax.dynamic_slice_in_dim(
        block_start, lax.axis_index("tm") * block_count, block_count
    )

    def spectra_of(start_at):
        segment = lax.dynamic_slice_in_dim(records, start_at, NFFT, 1)
        return jnp.einsum(
            "cft,stkx->scfkx", time_basis, segment, preferred_element_type=jnp.float32
        ).astype(jnp.bfloat16)

    spectra = lax.map(spectra_of, own_starts)
    arrived = lax.all_to_all(
        spectra[None], ("sector", "tm"), split_axis=4, concat_axis=0, tiled=True
    )
    arrived = arrived.reshape((sec_count, tm_count) + arrived.shape[1:])
    coeffs = jnp.einsum(
        "mcase,ajbsefkx->mcjbfkx",
        azimuth.reshape(order_total, 2, sec_count, sec_local, 2),
        arrived,
        preferred_element_type=jnp.float32,
    ).astype(jnp.bfloat16)
    coeffs = coeffs.reshape((order_total, 2, tm_count * block_count) + coeffs.shape[4:])
    weight = cell_weight(slab_index, weight_table)
    gram_re, gram_im = gram(coeffs, weight)
    gram_re, gram_im = lax.psum((gram_re, gram_im), "space")
    cell_total = fields * cell_local * lax.axis_size("space")
    mode_fields, energy = finish(coeffs, gram_re, gram_im, weight, cell_total)
    return (mode_fields, energy)


def solution(mesh):
    placed = (P("sector", "tm", None, "space"), P(), P("space"), P())
    return jax.shard_map(
        local,
        mesh=mesh,
        in_specs=placed,
        out_specs=(
            P(None, ("sector", "tm"), None, None, None, "space"),
            P(None, ("sector", "tm"), None),
        ),
        check_vma=False,
    )
```

profile of v0, /device:TPU:16, one launch (start us, length us, event | category | flops | bytes accessed | tf_op | source)
XLA Modules:
  0.0 861.9 jit_solution(12346992819027908676)
XLA Ops:
  7.4 0.7 dynamic_slice.10
  8.2 58.6 %while.10 = (s32[]{:T(128)}, bf16[8,4,2,32,3,2048]{5,3,2,4,1,0:T(8,128)(2,1)}, s32[8]{0:T(128)S(1)}, bf16[4,296,3,2048]{3,1,2,0:T(8,128)(2,1)}, bf16[2,32,64]{2,...) while((s32[]{:T(128)}, bf16[8,4,2,32,3,2048]{5,3,2,4,1,0:T(8,128)(2,1)}, s32[8]{0:T(128)S(1)}, ...), condition=%wide.region_1.2_spmd, body=%wide.region_0.1_spmd.sunk | while | flops 202899456 | bytes 6300295 | solution.py:124
  8.2 0.6 dynamic_slice.20
  10.7 4.8 bitcast_dynamic-update-slice_fusion.2
  15.5 0.6 dynamic_slice.20
  18.0 4.8 bitcast_dynamic-update-slice_fusion.2
  22.8 0.6 dynamic_slice.20
  25.4 4.8 bitcast_dynamic-update-slice_fusion.2
  30.2 0.6 dynamic_slice.20
  32.7 4.8 bitcast_dynamic-update-slice_fusion.2
  37.5 0.6 dynamic_slice.20
  40.0 4.8 bitcast_dynamic-update-slice_fusion.2
  44.8 0.6 dynamic_slice.20
  47.3 4.8 bitcast_dynamic-update-slice_fusion.2
  52.1 0.6 dynamic_slice.20
  54.6 4.8 bitcast_dynamic-update-slice_fusion.2
  59.5 0.6 dynamic_slice.20
  62.0 4.8 bitcast_dynamic-update-slice_fusion.2
  66.8 26.9 %copy.2352 = bf16[8,4,2,32,3,2048]{5,0,4,2,1,3:T(8,128)(2,1)} copy(bf16[8,4,2,32,3,2048]{5,3,2,4,1,0:T(8,128)(2,1)} %get-tuple-element.29) | data formatting | bytes 50331648 | tf_op jit(solution)/shard_map/while | solution.py:124
  93.6 6.5 all-to-all-start
  100.6 0.7 fusion.23
  101.3 539.4 %all-to-all-done = bf16[1,8,4,2,32,3,2048]{6,1,5,3,2,0,4:T(8,128)(2,1)} async-done(((bf16[1,8,4,2,32,3,2048]{6,1,5,3,2,0,4:T(8,128)(2,1)}), bf16[1,8,4,2,32,3,2048]{6,1,5,3,2,0,4:T(8,128)(2,1)}, u32[]{:S(2)}, u32[]{:S(2)}) %all-to-all-start) | async-done | bytes 25165856 | tf_op jit(solution)/shard_map/all_to_all | solution.py:125
  640.7 69.6 %bitcast_convert_fusion = bf16[8,2,2,8,4,3,2048]{6,0,5,4,3,2,1:T(8,128)(2,1)} fusion(bf16[4,2,8,4,2,4,3,2048]{7,2,6,4,3,5,1,0:T(8,128)(2,1)} %bitcast.419, bf16[8,2,4,4,2,1,1,1,1]{0,3,4,2,8,7,6,5,1:T(4,128)(2,1)S(1)} %fusion.630), kind=kOutput, calls=%fused_computation.6 | convolution fusion | flops 408944640 | bytes 37749760 | tf_op jit(solution)/shard_map/mcase,ajbsefkx->mcjbfkx/dot_general | solution.py:129
  710.3 41.6 %fusion.18 = f32[8,4,2,16,2,16]{5,3,4,2,1,0:T(8,128)S(1)} fusion(bf16[8,2,16,4,3,2048,1]{5,0,4,3,2,1,6:T(8,128)(2,1)} %bitcast.5398, bf16[8,2,16,4,3,2048]{5,0,4,3,2,1:T(8,128)(2,1)} %bitcast.5399, f32[2048]{0:T(1024)S(1)} %bitcast.5401), kind=kOutput, calls=%fused_computation.20 | convolution fusion | flops 421527552 | bytes 25305088 | tf_op jit(solution)/shard_map/mcbfkx,mdefkx->mfcbde/dot_general | solution.py:81
  751.9 0.9 fusion.26
  752.8 34.6 %all-reduce.3.cloned.1.call-done = (f32[8,4,16,16]{3,2,1,0:T(8,128)}, f32[8,4,16,16]{3,2,1,0:T(8,128)}) async-done(((f32[8,4,16,16]{3,2,1,0:T(8,128)}, f32[8,4,16,16]{3,2,1,0:T(8,128)}), (f32[8,4,16,16]{3,2,1,0:T(8,128)}, f32[8,4,16,16]{3,2,1,0:T(8,128)})) %all-reduce.3.cloned.1.call-update) | async-done | bytes 65552 | tf_op jit(solution)/shard_map/psum | solution.py:138
  787.4 1.5 fusion.64
  789.0 1.5 fusion.70
  790.4 1.5 fusion.68
  791.9 1.5 fusion.66
  798.4 1.5 fusion.58
  799.9 1.5 fusion.56
  802.4 1.5 fusion.62
  803.9 1.5 fusion.60
  810.3 0.5 fusion.50
  810.9 0.5 fusion.48
  812.5 0.7 fusion.54
  813.2 0.5 fusion.52
  818.7 0.5 fusion.42
  819.3 0.5 fusion.40
  820.8 0.5 fusion.46
  821.4 0.5 fusion.44
  827.8 0.5 fusion.34
  828.3 0.5 fusion.32
  830.2 0.9 fusion.38
  831.1 0.5 fusion.36
  832.2 0.7 copy.2245
  833.2 21.7 %fusion.10 = bf16[8,4,2,8,3,2048]{5,3,4,2,1,0:T(8,128)(2,1)} fusion(f32[8,4,8,2048]{3,2,1,0:T(8,128)S(1)} %broadcast_multiply_fusion, bf16[8,2,16,4,3,2048,1]{5,0,4,3,2,1,6:T(8,128)(2,1)} %bitcast.5400, bf16[8,4,2,16,2,8,1]{3,0,1,5,4,2,6:T(8,128)(2,1)S(1)} %maximum_bitcast_fusion), kind=kOutput, calls=%fused_computation.14 | convolution fusion | flops 207618048 | bytes 21004288 | tf_op jit(solution)/shard_map/mcbfkx,mfcbdj->mfdjkx/dot_general | solution.py:99
  (209 shorter events, 26.2 us)
Async XLA Ops:
  7.2 93.4 %copy-start = (f32[16]{0:T(128)S(1)}, f32[16]{0:T(128)}, u32[]{:S(2)}) copy-start(f32[16]{0:T(128)} %param.9) | copy-start | bytes 196
  93.6 7.0 copy-start.4
  93.6 547.0 %all-to-all-start = ((bf16[1,8,4,2,32,3,2048]{6,1,5,3,2,0,4:T(8,128)(2,1)}), bf16[1,8,4,2,32,3,2048]{6,1,5,3,2,0,4:T(8,128)(2,1)}, u32[]{:S(2)}, u32[]{:S(2)}) async-start(bf16[1,8,4,2,32,3,2048]{6,1,5,3,2,0,4:T(8,128)(2,1)} %bitcast.5397), calls=%async_computation | async-start | bytes 50331648 | tf_op jit(solution)/shard_map/all_to_all | solution.py:125
  100.2 687.3 %all-reduce.3.cloned.1.call-start = ((), (), s32[]{:S(2)}) async-start(), calls=%async_computation.1 | async-start | bytes 1048576 | tf_op jit(solution)/shard_map/psum | solution.py:138
  787.4 22.9 %copy-start.2 = (f32[8,4,16,16]{3,2,1,0:T(8,128)S(1)}, f32[8,4,16,16]{3,2,1,0:T(8,128)}, u32[]{:S(2)}) copy-start(f32[8,4,16,16]{3,2,1,0:T(8,128)} %get-tuple-element.386) | copy-start | bytes 98308
  787.4 23.5 %copy-start.3 = (f32[8,4,16,16]{3,2,1,0:T(8,128)S(1)}, f32[8,4,16,16]{3,2,1,0:T(8,128)}, u32[]{:S(2)}) copy-start(f32[8,4,16,16]{3,2,1,0:T(8,128)} %get-tuple-element.387) | copy-start | bytes 98308
  831.7 23.2 %copy-start.1 = (f32[16]{0:T(128)S(1)}, f32[16]{0:T(128)}, u32[]{:S(2)}) copy-start(f32[16]{0:T(128)} %param.9) | copy-start | bytes 196
Sparse Core Ops, SparseCore 0:
  752.9 34.4 all-reduce.2
where the time goes:
time: 874 us; the launch traced here: 862 us
  waiting for transfers between devices  574 us (66%)
  matrix products  191 us (22%)
  local copies, waits for them, and re-layouts  33.1 us (4%)
  other arithmetic  26.6 us (3%)
  loops' own time  15.6 us (2%)
  between operations  15 us (2%)
    all_to_all x1, waiting for transfers between devices, local(): lax.all_to_all(spectra[None], ('sector', 'tm'), split_axis=4, concat_axis...  539 us
    dot_general x1, matrix products, local(): jnp.einsum('mcase,ajbsefkx->mcjbfkx', azimuth.reshape(order_total, 2, sec...  69.6 us
    dot_general x1, matrix products, gram(): jnp.einsum('mcbfkx,mdefkx->mfcbde', weighted, coeffs, preferred_element_t...  41.6 us
    dot_general x8, matrix products, spectra_of(): jnp.einsum('cft,stkx->scfkx', time_basis, segment, preferred_element_type...  38.4 us
    psum x1, waiting for transfers between devices, local(): gram_re, gram_im = lax.psum((gram_re, gram_im), 'space')  34.6 us
    while x1, local copies, waits for them, and re-layouts, local(): spectra = lax.map(spectra_of, own_starts)  26.9 us
    dot_general x1, matrix products, finish(): jnp.einsum('mcbfkx,mfcbdj->mfdjkx', coeffs, mixing, preferred_element_typ...  21.7 us
    dot_general x20, matrix products, matmul_high(): return jnp.matmul(left_side, right_side, precision=lax.Precision.HIGHEST)  18.9 us
  transfers between devices with their start and end apart: 2, of which 2 were waited for; matrix products, arithmetic and copies ran while one was open for 0% of the time, Pallas kernels for 0%

commit v1 on v0

v1 whole, which is shorter than its diff:
```python
import functools
import math

import jax
import jax.numpy as jnp
from jax import lax
from jax.experimental import pallas as pl
from jax.experimental.pallas import tpu as pltpu
from jax.sharding import PartitionSpec as P

NFFT = 64
NFREQ = 32
MODES = 8
SUBIT = 4
LANES = 128
EPSILON = 1e-06
VMEM_LIMIT = 48 * 1024 * 1024


def time_table(length, freq_count):
    steps_t = jnp.arange(length, dtype=jnp.float32)
    freq_f = jnp.arange(freq_count, dtype=jnp.float32)
    window = 0.5 - 0.5 * jnp.cos(2.0 * math.pi * steps_t / length)
    angles = 2.0 * math.pi * freq_f[:, None] * steps_t[None, :] / length
    both = jnp.stack([window * jnp.cos(angles), -window * jnp.sin(angles)])
    return (both / math.sqrt(length)).astype(jnp.bfloat16)


def order_table(orders, sectors):
    order_m = jnp.arange(orders, dtype=jnp.float32)[:, None]
    sector_s = jnp.arange(sectors, dtype=jnp.float32)[None, :]
    angles = 2.0 * math.pi * order_m * sector_s / sectors
    cosine = jnp.cos(angles)
    sine_part = jnp.sin(angles)
    upper_row = jnp.stack([cosine, sine_part], -1)
    lower_row = jnp.stack([-sine_part, cosine], -1)
    return (jnp.stack([upper_row, lower_row], 1) / math.sqrt(sectors)).astype(jnp.bfloat16)


def placed_time_basis(block_start, tm_count, rec_len):
    blocks = block_start.shape[0] // tm_count
    basis = time_table(NFFT, NFREQ)
    place = (
        block_start[:, None, None] + jnp.arange(NFFT, dtype=jnp.int32)[None, :, None]
        == jnp.arange(rec_len, dtype=jnp.int32)[None, None, :]
    ).astype(jnp.bfloat16)
    table = jnp.einsum(
        "eft,jbtu->jfebu",
        basis,
        place.reshape(tm_count, blocks, NFFT, rec_len),
        preferred_element_type=jnp.float32,
    ).astype(jnp.bfloat16)
    return table.reshape(tm_count, NFREQ * 2 * blocks, rec_len)


def coeff_kernel(sectors, freqs, time_ref, azimuth_ref, weight_ref, before_ref, record_ref,
                 coeff_ref, gram_ref, spectra):
    step = pl.program_id(0)
    tm_count = time_ref.shape[0]
    rows = azimuth_ref.shape[0]
    depth = azimuth_ref.shape[1] // sectors
    columns = record_ref.shape[-1]

    @pl.when(step < sectors)
    def _():
        parts = [
            jnp.dot(time_ref[j], record_ref[0, j, 0], preferred_element_type=jnp.float32)
            for j in range(tm_count)
        ]
        block_rows = depth // (2 * tm_count)
        joined = jnp.stack([x.reshape(-1, block_rows, columns) for x in parts], 1)
        spectra[step] = joined.reshape(spectra.shape[1:]).astype(jnp.bfloat16)

    @pl.when(step >= sectors)
    def _():
        first = (step - sectors) * freqs
        blocks = depth // 2
        packed = LANES // depth
        lane = lax.broadcasted_iota(jnp.int32, (blocks, LANES), 1)
        owner = lax.broadcasted_iota(jnp.int32, (depth, LANES), 1) // depth
        for n in range(freqs):
            at = pl.multiple_of((first + n) * depth, depth)
            own = spectra[:, pl.ds(at, depth), :].reshape(sectors * depth, columns)
            coeffs = jnp.dot(
                azimuth_ref[...], own, preferred_element_type=jnp.float32
            ).astype(jnp.bfloat16)
            coeff_ref[n] = coeffs
            weighted = (coeffs.astype(jnp.float32) * weight_ref[...]).astype(jnp.bfloat16)
            products = lax.dot_general(
                weighted, coeffs, (((1,), (1,)), ((), ())), preferred_element_type=jnp.float32
            )
            for g in range(rows // LANES):
                part = products[g * LANES:(g + 1) * LANES, g * LANES:(g + 1) * LANES]
                own_order = jnp.zeros((depth, LANES), jnp.float32)
                for q in range(packed):
                    own_order = jnp.where(owner == q, part[q * depth:(q + 1) * depth], own_order)
                upper, lower = own_order[:blocks], own_order[blocks:]
                crossed = jnp.where(
                    lane % depth < blocks,
                    pltpu.roll(lower, LANES - blocks, 1),
                    -pltpu.roll(lower, blocks, 1),
                )
                gram_ref[n, g] = before_ref[n, g] + upper + crossed


def coeffs_and_gram(arrived, time_basis, azimuth, weight, before):
    sec_count, tm_count, sec_local, rec_len, columns = arrived.shape
    sectors = sec_count * sec_local
    rows = azimuth.shape[0]
    depth = azimuth.shape[1] // sectors
    freqs = 4
    steps = NFREQ // freqs
    later = lambda i: jnp.maximum(i - sectors, 0)
    early = lambda i: jnp.minimum(i, sectors - 1)
    gram_block = (freqs,) + before.shape[1:]
    flops = 2 * columns * (
        sectors * tm_count * time_basis.shape[1] * rec_len
        + NFREQ * rows * sectors * depth
        + NFREQ * rows * rows
    )
    return pl.pallas_call(
        functools.partial(coeff_kernel, sectors, freqs),
        grid=(sectors + steps,),
        in_specs=[
            pl.BlockSpec(time_basis.shape, lambda i: (0, 0, 0)),
            pl.BlockSpec(azimuth.shape, lambda i: (0, 0)),
            pl.BlockSpec(weight.shape, lambda i: (0, 0)),
            pl.BlockSpec(gram_block, lambda i: (later(i), 0, 0, 0)),
            pl.BlockSpec(
                (1, tm_count, 1, rec_len, columns),
                lambda i: (early(i) // sec_local, 0, early(i) % sec_local, 0, 0),
            ),
        ],
        out_specs=[
            pl.BlockSpec((freqs, rows, columns), lambda i: (later(i), 0, 0)),
            pl.BlockSpec(gram_block, lambda i: (later(i), 0, 0, 0)),
        ],
        out_shape=[
            jax.ShapeDtypeStruct((NFREQ, rows, columns), jnp.bfloat16),
            jax.ShapeDtypeStruct(before.shape, jnp.float32),
        ],
        scratch_shapes=[pltpu.VMEM((sectors, NFREQ * depth, columns), jnp.bfloat16)],
        compiler_params=pltpu.CompilerParams(vmem_limit_bytes=VMEM_LIMIT),
        cost_estimate=pl.CostEstimate(
            flops=flops, bytes_accessed=2 * (arrived.size + NFREQ * rows * columns), transcendentals=0
        ),
        name="coeffs_and_gram",
    )(time_basis, azimuth, weight, before, arrived)


def subspace_kernel(cell_total, re_ref, im_ref, basis_ref, energy_ref):
    size = re_ref.shape[0]
    column_re = [re_ref[q] for q in range(size)]
    column_im = [im_ref[q] for q in range(size)]

    def image_of(vec_re, vec_im):
        out_re, out_im = [], []
        for j in range(MODES):
            sum_re = jnp.zeros_like(column_re[0])
            sum_im = jnp.zeros_like(column_re[0])
            for q in range(size):
                at_re, at_im = vec_re[j][q:q + 1], vec_im[j][q:q + 1]
                sum_re += column_re[q] * at_re - column_im[q] * at_im
                sum_im += column_re[q] * at_im + column_im[q] * at_re
            out_re.append(sum_re)
            out_im.append(sum_im)
        return out_re, out_im

    total = lambda x: jnp.sum(x, 0, keepdims=True)
    vec_re, vec_im = column_re[:MODES], column_im[:MODES]
    for sweep in range(SUBIT):
        if sweep > 0:
            vec_re, vec_im = image_of(vec_re, vec_im)
        vec_re, vec_im = list(vec_re), list(vec_im)
        for i in range(MODES):
            scale = 1.0 / jnp.sqrt(total(vec_re[i] * vec_re[i] + vec_im[i] * vec_im[i]) + EPSILON)
            own_re, own_im = vec_re[i] * scale, vec_im[i] * scale
            vec_re[i], vec_im[i] = own_re, own_im
            for j in range(i + 1, MODES):
                proj_re = total(own_re * vec_re[j] + own_im * vec_im[j])
                proj_im = total(own_re * vec_im[j] - own_im * vec_re[j])
                vec_re[j] = vec_re[j] - (proj_re * own_re - proj_im * own_im)
                vec_im[j] = vec_im[j] - (proj_re * own_im + proj_im * own_re)
    image_re, image_im = image_of(vec_re, vec_im)
    for j in range(MODES):
        basis_ref[0, j] = vec_re[j]
        basis_ref[1, j] = vec_im[j]
        energy_ref[j:j + 1] = total(vec_re[j] * image_re[j] + vec_im[j] * image_im[j]) / cell_total


def subspace(gram_re, gram_im, cell_total):
    size, _, pairs = gram_re.shape
    return pl.pallas_call(
        functools.partial(subspace_kernel, float(cell_total)),
        out_shape=[
            jax.ShapeDtypeStruct((2, MODES, size, pairs), jnp.float32),
            jax.ShapeDtypeStruct((MODES, pairs), jnp.float32),
        ],
        name="subspace",
    )(gram_re, gram_im)


def mix_kernel(orders, coeff_ref, mixing_ref, factor_ref, root_ref, out_ref):
    freqs, rows, depth = mixing_ref.shape
    total = orders * depth
    row = lax.broadcasted_iota(jnp.int32, (rows, total), 0) // (rows // orders)
    column = lax.broadcasted_iota(jnp.int32, (rows, total), 1) // depth
    for n in range(freqs):
        wide = jnp.concatenate([mixing_ref[n]] * orders, axis=1)
        wide = jnp.where(row == column, wide, jnp.zeros_like(wide))
        fields = jnp.dot(wide, coeff_ref[n], preferred_element_type=jnp.float32)
        out_ref[0, n] = (fields * (factor_ref[n] * root_ref[...])).astype(jnp.bfloat16)


def mix(coeffs, mixing, factor, root_weight, owners, orders):
    _, rows, columns = coeffs.shape
    out_rows, depth = mixing.shape[1:]
    freqs = NFREQ // owners
    return pl.pallas_call(
        functools.partial(mix_kernel, orders),
        grid=(owners,),
        in_specs=[
            pl.BlockSpec((freqs, rows, columns), lambda i: (i, 0, 0)),
            pl.BlockSpec((freqs, out_rows, depth), lambda i: (i, 0, 0)),
            pl.BlockSpec((freqs, out_rows, 1), lambda i: (i, 0, 0)),
            pl.BlockSpec(root_weight.shape, lambda i: (0, 0)),
        ],
        out_specs=pl.BlockSpec((1, freqs, out_rows, columns), lambda i: (i, 0, 0, 0)),
        out_shape=jax.ShapeDtypeStruct((owners, freqs, out_rows, columns), jnp.bfloat16),
        compiler_params=pltpu.CompilerParams(vmem_limit_bytes=VMEM_LIMIT),
        cost_estimate=pl.CostEstimate(
            flops=2 * NFREQ * out_rows * rows * columns,
            bytes_accessed=2 * NFREQ * (rows + out_rows) * columns,
            transcendentals=0,
        ),
        name="mix",
    )(coeffs, mixing, factor, root_weight)


def pack_kernel(record_ref, out_ref):
    owners, _, _, part = out_ref.shape
    for d in range(owners):
        out_ref[d, 0] = record_ref[0, 0, :, d * part:(d + 1) * part]


def pack(by_field, k, owners):
    sec_local, _, rec_len, cells = by_field.shape
    part = cells // owners
    return pl.pallas_call(
        pack_kernel,
        grid=(sec_local,),
        in_specs=[pl.BlockSpec((1, 1, rec_len, cells), lambda i: (i, k, 0, 0))],
        out_specs=pl.BlockSpec((owners, 1, rec_len, part), lambda i: (0, i, 0, 0)),
        out_shape=jax.ShapeDtypeStruct((owners, sec_local, rec_len, part), by_field.dtype),
        compiler_params=pltpu.CompilerParams(vmem_limit_bytes=VMEM_LIMIT),
        cost_estimate=pl.CostEstimate(
            flops=0, bytes_accessed=4 * sec_local * rec_len * cells, transcendentals=0
        ),
        name="pack",
    )(by_field)


def unpack_kernel(piece_ref, *refs):
    out_ref = refs[-1]
    owners, part = piece_ref.shape[0], piece_ref.shape[-1]
    for d in range(owners):
        out_ref[:, 0, :, 0, :, d * part:(d + 1) * part] = piece_ref[d, 0]


def unpack(pieces, k, fields, whole):
    owners, freqs, orders, two, modes, part = pieces.shape
    shape = (orders, freqs, two, fields, modes, owners * part)
    inputs = [pieces] if whole is None else [pieces, whole]
    in_specs = [
        pl.BlockSpec((owners, 1, orders, two, modes, part), lambda i: (0, i, 0, 0, 0, 0)),
        pl.BlockSpec(memory_space=pl.ANY),
    ]
    return pl.pallas_call(
        unpack_kernel,
        grid=(freqs,),
        in_specs=in_specs[:len(inputs)],
        out_specs=pl.BlockSpec(
            (orders, 1, two, 1, modes, owners * part), lambda i: (0, i, 0, k, 0, 0)
        ),
        out_shape=jax.ShapeDtypeStruct(shape, pieces.dtype),
        input_output_aliases={} if whole is None else {1: 0},
        compiler_params=pltpu.CompilerParams(vmem_limit_bytes=VMEM_LIMIT),
        cost_estimate=pl.CostEstimate(flops=0, bytes_accessed=4 * pieces.size, transcendentals=0),
        name="unpack",
    )(*inputs)


def local(records, block_start, slab_index, weight_table):
    sec_local, rec_len, fields, cell_local = records.shape
    sec_count = lax.axis_size("sector")
    tm_count = lax.axis_size("tm")
    space_count = lax.axis_size("space")
    owners = sec_count * tm_count
    owner_axes = ("sector", "tm")
    sectors = sec_local * sec_count
    orders = sectors // 2
    blocks = block_start.shape[0]
    depth = 2 * blocks
    part = cell_local // owners
    own_freqs = NFREQ // owners
    me = lax.axis_index("sector") * tm_count + lax.axis_index("tm")

    by_field = jnp.transpose(records, (0, 2, 1, 3))
    arrived = []
    for k in range(fields):
        send = pack(by_field, k, owners)
        got = lax.all_to_all(send, owner_axes, split_axis=0, concat_axis=0, tiled=True)
        arrived.append(got.reshape(sec_count, tm_count, sec_local, rec_len, part))

    time_basis = placed_time_basis(block_start, tm_count, rec_len)
    azimuth = jnp.einsum(
        "mcse,bd->mcbsed",
        order_table(orders, sectors),
        jnp.eye(blocks, dtype=jnp.bfloat16),
    ).reshape(orders * depth, sectors * depth)
    own_slab = lax.dynamic_slice_in_dim(slab_index, me * part, part)
    weight = jnp.sum(
        jnp.where(
            own_slab[None, :] == jnp.arange(weight_table.shape[0], dtype=jnp.int32)[:, None],
            weight_table[:, None],
            0.0,
        ),
        0,
        keepdims=True,
    )

    groups = orders * depth // LANES
    gram = jnp.zeros((NFREQ, groups, blocks, LANES), jnp.float32)
    coeffs = []
    for k in range(fields):
        own, gram = coeffs_and_gram(arrived[k], time_basis, azimuth, weight, gram)
        coeffs.append(own)

    if own_freqs % space_count == 0:
        axes = owner_axes + ("space",)
    else:
        gram = lax.psum(gram, "space")
        axes = owner_axes
    solvers = math.prod(lax.axis_size(a) for a in axes)
    solved = NFREQ // solvers
    gram = gram.reshape((solvers, solved) + gram.shape[1:])
    gram = lax.all_to_all(gram, axes, split_axis=0, concat_axis=0, tiled=True)
    gram = jnp.sum(gram, 0).reshape(solved, groups, blocks, LANES // depth, 2, blocks)
    gram = jnp.transpose(gram, (4, 5, 2, 0, 1, 3)).reshape(2, blocks, blocks, solved * orders)
    basis, energy = subspace(gram[0], gram[1], fields * cell_local * space_count)

    short = basis.astype(jnp.bfloat16).reshape(2, MODES, blocks, solved, orders)
    short = jnp.transpose(short, (3, 4, 0, 1, 2))
    short_re, short_im = short[:, :, 0], short[:, :, 1]
    mixing = jnp.stack(
        [jnp.concatenate([short_re, -short_im], -1), jnp.concatenate([short_im, short_re], -1)], 2
    ).reshape(solved, orders * 2 * MODES * depth)
    energy = jnp.transpose(energy.reshape(MODES, solved, orders), (1, 2, 0)).reshape(solved, -1)
    high = energy.astype(jnp.bfloat16)
    rest = energy - high.astype(jnp.float32)
    middle = rest.astype(jnp.bfloat16)
    low = (rest - middle.astype(jnp.float32)).astype(jnp.bfloat16)
    packet = jnp.concatenate([mixing, high, middle, low], 1)
    width = -(-packet.shape[1] // LANES) * LANES
    packet = jnp.pad(packet, ((0, 0), (0, width - packet.shape[1])))
    packet = packet.reshape(1, solved, width // LANES, LANES)
    packet = jnp.broadcast_to(packet, (solvers,) + packet.shape[1:])
    packet = lax.all_to_all(packet, axes, split_axis=0, concat_axis=0, tiled=True)
    packet = packet.reshape(NFREQ, width)
    count = orders * MODES
    mixing = packet[:, :orders * 2 * MODES * depth].reshape(NFREQ, orders * 2 * MODES, depth)
    tail = packet[:, orders * 2 * MODES * depth:].astype(jnp.float32)
    energy = (tail[:, :count] + tail[:, count:2 * count]) + tail[:, 2 * count:3 * count]
    energy = energy.reshape(NFREQ, orders, MODES)
    factor = jnp.broadcast_to(
        lax.rsqrt(energy)[:, :, None, :], (NFREQ, orders, 2, MODES)
    ).reshape(NFREQ, orders * 2 * MODES, 1)
    root_weight = jnp.sqrt(weight)

    mode_fields = None
    for k in range(fields):
        send = mix(coeffs[k], mixing, factor, root_weight, owners, orders)
        got = lax.all_to_all(send, owner_axes, split_axis=0, concat_axis=0, tiled=True)
        got = got.reshape(owners, own_freqs, orders, 2, MODES, part)
        mode_fields = unpack(got, k, fields, mode_fields)
    mode_fields = jnp.transpose(mode_fields, (0, 1, 2, 4, 3, 5))
    own_energy = lax.dynamic_slice_in_dim(energy, me * own_freqs, own_freqs)
    return (mode_fields, jnp.transpose(own_energy, (1, 0, 2)))


def solution(mesh):
    placed = (P("sector", "tm", None, "space"), P(), P("space"), P())
    return jax.shard_map(
        local,
        mesh=mesh,
        in_specs=placed,
        out_specs=(
            P(None, ("sector", "tm"), None, None, None, "space"),
            P(None, ("sector", "tm"), None),
        ),
        check_vma=False,
    )
```

time: 874 us -> 583 us (0.67)
  waiting for transfers between devices: 574 us -> 362 us
  matrix products: 191 us -> 0.59 us
  Pallas kernels: 0 us -> 117 us
  starting transfers between devices: 6.74 us -> 49.2 us
  other arithmetic: 26.6 us -> 3.27 us
  blocking collectives: 0 us -> 19.8 us
  loops' own time: 15.6 us -> 0 us
  between operations: 15 us -> 0.94 us
  local copies, waits for them, and re-layouts: 33.1 us -> 23.6 us
    dot_general x32 -> x1, matrix products: 191 us -> 0.59 us  [placed_time_basis(): jnp.einsum('eft,jbtu->jfebu', basis, place.reshape(tm_count, blocks, NFFT...]
    all_to_all x1 -> x7, waiting for transfers between devices: 539 us -> 362 us  [the longest x6 353 us: local(): lax.all_to_all(send, owner_axes, split_axis=0, concat_axis=0, tiled=True)]
    pallas_call x0 -> x13, Pallas kernels: none -> 117 us  [the longest x3 75.8 us: coeffs_and_gram(): pl.pallas_call(functools.partial(coeff_kernel, sectors, freqs), grid=(sec...]
    all_to_all x1 -> x7, starting transfers between devices: 6.52 us -> 49.2 us  [the longest x6 43.8 us: local(): lax.all_to_all(send, owner_axes, split_axis=0, concat_axis=0, tiled=True)]
    psum x1 -> x0, waiting for transfers between devices: 34.6 us -> none  [local(): gram_re, gram_im = lax.psum((gram_re, gram_im), 'space')]
    while x1 -> x0, local copies, waits for them, and re-layouts: 26.9 us -> none  [local(): spectra = lax.map(spectra_of, own_starts)]
    all_to_all x0 -> x1, blocking collectives: none -> 19.8 us  [local(): gram = lax.all_to_all(gram, axes, split_axis=0, concat_axis=0, tiled=True)]
    another operation x1 -> x0, loops' own time: 15.6 us -> none  [local(): spectra = lax.map(spectra_of, own_starts)]
  transfers between devices with their start and end apart: 2 -> 7, of which waited for: 2 -> 7; matrix products, arithmetic and copies ran while one was open for 0% -> 1% of each run, Pallas kernels for 0% -> 13%
where the time goes in v1:
time: 583 us; the launch traced here: 576 us
  waiting for transfers between devices  362 us (62%)
  Pallas kernels  117 us (20%)
  starting transfers between devices  49.2 us (8%)
  local copies, waits for them, and re-layouts  23.6 us (4%)
  blocking collectives  19.8 us (3%)
    all_to_all x6, waiting for transfers between devices, local(): lax.all_to_all(send, owner_axes, split_axis=0, concat_axis=0, tiled=True)  353 us
    pallas_call x3, Pallas kernels, coeffs_and_gram(): pl.pallas_call(functools.partial(coeff_kernel, sectors, freqs), grid=(sec...  75.8 us
    all_to_all x6, starting transfers between devices, local(): lax.all_to_all(send, owner_axes, split_axis=0, concat_axis=0, tiled=True)  43.8 us
    all_to_all x1, blocking collectives, local(): gram = lax.all_to_all(gram, axes, split_axis=0, concat_axis=0, tiled=True)  19.8 us
    pallas_call x3, Pallas kernels, mix(): pl.pallas_call(functools.partial(mix_kernel, orders), grid=(owners,), in_...  17.6 us
  transfers between devices with their start and end apart: 7, of which 7 were waited for; matrix products, arithmetic and copies ran while one was open for 1% of the time, Pallas kernels for 13%

profile of v1, /device:TPU:16, one launch (start us, length us, event | category | flops | bytes accessed | tf_op | source)
XLA Modules:
  0.0 576.4 jit_solution(7098028951440152620)
XLA Ops:
  0.6 3.4 pack.3
  4.0 2.2 copy-done.2
  6.3 6.1 %all-to-all-start = ((bf16[8,4,296,256]{3,2,1,0:T(8,128)(2,1)}), bf16[8,4,296,256]{3,2,1,0:T(8,128)(2,1)}, u32[]{:S(2)}, u32[]{:S(2)}) async-start(bf16[8,4,296,256]{3,2,1,0:T(8,128)(2,1)} %copy-done.2), calls=%async_computation | async-start | bytes 9699328 | tf_op jit(solution)/shard_map/all_to_all | solution.py:312
  12.4 3.4 pack.4
  15.8 2.3 copy-done.1
  18.0 98.3 %all-to-all-done = bf16[8,4,296,256]{3,2,1,0:T(8,128)(2,1)} async-done(((bf16[8,4,296,256]{3,2,1,0:T(8,128)(2,1)}), bf16[8,4,296,256]{3,2,1,0:T(8,128)(2,1)}, u32[]{:S(2)}, u32[]{:S(2)}) %all-to-all-start) | async-done | bytes 4849696 | tf_op jit(solution)/shard_map/all_to_all | solution.py:312
  116.3 7.9 %all-to-all-start.1 = ((bf16[8,4,296,256]{3,2,1,0:T(8,128)(2,1)}), bf16[8,4,296,256]{3,2,1,0:T(8,128)(2,1)}, u32[]{:S(2)}, u32[]{:S(2)}) async-start(bf16[8,4,296,256]{3,2,1,0:T(8,128)(2,1)} %copy-done.1), calls=%async_computation.1 | async-start | bytes 9699328 | tf_op jit(solution)/shard_map/all_to_all | solution.py:312
  124.2 3.4 pack.5
  127.6 2.2 copy-done
  129.9 97.6 %all-to-all-done.1 = bf16[8,4,296,256]{3,2,1,0:T(8,128)(2,1)} async-done(((bf16[8,4,296,256]{3,2,1,0:T(8,128)(2,1)}), bf16[8,4,296,256]{3,2,1,0:T(8,128)(2,1)}, u32[]{:S(2)}, u32[]{:S(2)}) %all-to-all-start.1) | async-done | bytes 4849696 | tf_op jit(solution)/shard_map/all_to_all | solution.py:312
  227.5 7.9 %all-to-all-start.2 = ((bf16[8,4,296,256]{3,2,1,0:T(8,128)(2,1)}), bf16[8,4,296,256]{3,2,1,0:T(8,128)(2,1)}, u32[]{:S(2)}, u32[]{:S(2)}) async-start(bf16[8,4,296,256]{3,2,1,0:T(8,128)(2,1)} %copy-done), calls=%async_computation.2 | async-start | bytes 9699328 | tf_op jit(solution)/shard_map/all_to_all | solution.py:312
  235.8 0.6 fusion.6
  236.4 0.5 copy.44
  237.2 1.6 multiply_bitcast_fusion
  238.8 3.6 reshape.402.azimuth_ref
  242.4 0.8 dynamic_slice.6
  243.3 25.3 %coeffs_and_gram.3 = (bf16[32,256,256]{2,1,0:T(8,128)(2,1)}, f32[32,2,16,128]{3,2,1,0:T(8,128)S(1)}) custom-call(bf16[2,512,296]{2,1,0:T(8,128)(2,1)S(1)} %bitcast.73, bf16[256,512]{1,0:T(8,128)(2,1)S(1)} %reshape.402.azimuth_ref, f32[1,256]{1,0:T(1,128)S(1)} %bitcast.77, f32[32,2,16,128]{3,2,1,0:T(8,128)S(1)} %broadcast_in_dim.25.before_ref, ...), custom_call_target="tpu_custom_call" | custom-call | flops 5704253440 | bytes 9043968 | tf_op jit(solution)/shard_map/coeffs_and_gram/pallas_call | solution.py:121
  268.6 25.2 %coeffs_and_gram.4 = (bf16[32,256,256]{2,1,0:T(8,128)(2,1)}, f32[32,2,16,128]{3,2,1,0:T(8,128)S(1)}) custom-call(bf16[2,512,296]{2,1,0:T(8,128)(2,1)S(1)} %bitcast.74, bf16[256,512]{1,0:T(8,128)(2,1)S(1)} %reshape.402.azimuth_ref, f32[1,256]{1,0:T(1,128)S(1)} %bitcast.78, f32[32,2,16,128]{3,2,1,0:T(8,128)S(1)} %get-tuple-element.10.before_ref, ...), custom_call_target="tpu_custom_call" | custom-call | flops 5704253440 | bytes 9043968 | tf_op jit(solution)/shard_map/coeffs_and_gram/pallas_call | solution.py:121
  293.8 44.8 %all-to-all-done.2 = bf16[8,4,296,256]{3,2,1,0:T(8,128)(2,1)} async-done(((bf16[8,4,296,256]{3,2,1,0:T(8,128)(2,1)}), bf16[8,4,296,256]{3,2,1,0:T(8,128)(2,1)}, u32[]{:S(2)}, u32[]{:S(2)}) %all-to-all-start.2) | async-done | bytes 4849696 | tf_op jit(solution)/shard_map/all_to_all | solution.py:312
  338.7 25.3 %coeffs_and_gram.5 = (bf16[32,256,256]{2,1,0:T(8,128)(2,1)}, f32[32,2,16,128]{3,2,1,0:T(8,128)S(1)}) custom-call(bf16[2,512,296]{2,1,0:T(8,128)(2,1)S(1)} %bitcast.75, bf16[256,512]{1,0:T(8,128)(2,1)S(1)} %reshape.402.azimuth_ref, f32[1,256]{1,0:T(1,128)S(1)} %bitcast.79, f32[32,2,16,128]{3,2,1,0:T(8,128)S(1)} %get-tuple-element.11.before_ref, ...), custom_call_target="tpu_custom_call" | custom-call | flops 5704253440 | bytes 9043968 | tf_op jit(solution)/shard_map/coeffs_and_gram/pallas_call | solution.py:121
  363.9 19.8 %all_to_all.40 = f32[32,1,2,16,128]{4,3,2,1,0:T(8,128)S(1)} all-to-all(f32[32,1,2,16,128]{4,3,2,1,0:T(8,128)S(1)} %bitcast.76), channel_id=1, replica_groups=mesh['sector'=4,'tm'=2,'space'=4] {'sector','tm','space'}, dimensions={0} | all-to-all | bytes 1048576 | tf_op jit(solution)/shard_map/all_to_all | solution.py:347
  383.8 0.2 reshape.407
  384.2 0.8 copy.49.re_ref
  385.1 0.8 copy.50.im_ref
  385.9 4.0 subspace.1
  389.8 0.9 convert_bitcast_fusion
  391.3 0.8 copy.57
  392.3 0.8 broadcast_in_dim.27
  393.1 5.4 all-to-all-start.4
  398.5 9.2 %all-to-all-done.4 = bf16[32,1,34,128]{3,2,1,0:T(8,128)(2,1)S(1)} async-done(((bf16[32,1,34,128]{3,2,1,0:T(8,128)(2,1)}), bf16[32,1,34,128]{3,2,1,0:T(8,128)(2,1)S(1)}, u32[]{:S(2)}, u32[]{:S(2)}) %all-to-all-start.4) | async-done | bytes 278560 | tf_op jit(solution)/shard_map/all_to_all | solution.py:368
  407.8 0.8 reshape.413.mixing_ref
  408.8 1.9 copy.59.factor_ref
  410.7 5.9 %mix.4 = bf16[8,4,128,256]{3,2,1,0:T(8,128)(2,1)S(1)} custom-call(bf16[32,256,256]{2,1,0:T(8,128)(2,1)} %get-tuple-element.16.coeff_ref, bf16[32,128,32]{2,1,0:T(8,128)(2,1)S(1)} %reshape.413.mixing_ref, f32[32,128,1]{2,1,0:T(8,128)S(1)} %copy.59.factor_ref, f32[1,256]{1,0:T(1,128)S(1)} %sqrt.3.root_ref), custom_call_target="tpu_custom_call" | custom-call | flops 536870912 | bytes 6291456 | tf_op jit(solution)/shard_map/mix/pallas_call | solution.py:219
  416.6 1.3 copy-done.5
  417.9 7.3 %all-to-all-start.6 = ((bf16[8,4,128,256]{3,2,1,0:T(8,128)(2,1)}), bf16[8,4,128,256]{3,2,1,0:T(8,128)(2,1)}, u32[]{:S(2)}, u32[]{:S(2)}) async-start(bf16[8,4,128,256]{3,2,1,0:T(8,128)(2,1)} %copy-done.5), calls=%async_computation.6 | async-start | bytes 4194304 | tf_op jit(solution)/shard_map/all_to_all | solution.py:383
  425.1 5.9 %mix.5 = bf16[8,4,128,256]{3,2,1,0:T(8,128)(2,1)S(1)} custom-call(bf16[32,256,256]{2,1,0:T(8,128)(2,1)} %get-tuple-element.17.coeff_ref, bf16[32,128,32]{2,1,0:T(8,128)(2,1)S(1)} %reshape.413.mixing_ref, f32[32,128,1]{2,1,0:T(8,128)S(1)} %copy.59.factor_ref, f32[1,256]{1,0:T(1,128)S(1)} %sqrt.3.root_ref), custom_call_target="tpu_custom_call" | custom-call | flops 536870912 | bytes 6291456 | tf_op jit(solution)/shard_map/mix/pallas_call | solution.py:219
  431.0 1.3 copy-done.4
  432.3 37.7 %all-to-all-done.6 = bf16[8,4,128,256]{3,2,1,0:T(8,128)(2,1)} async-done(((bf16[8,4,128,256]{3,2,1,0:T(8,128)(2,1)}), bf16[8,4,128,256]{3,2,1,0:T(8,128)(2,1)}, u32[]{:S(2)}, u32[]{:S(2)}) %all-to-all-start.6) | async-done | bytes 2097184 | tf_op jit(solution)/shard_map/all_to_all | solution.py:383
  470.1 7.6 %all-to-all-start.7 = ((bf16[8,4,128,256]{3,2,1,0:T(8,128)(2,1)}), bf16[8,4,128,256]{3,2,1,0:T(8,128)(2,1)}, u32[]{:S(2)}, u32[]{:S(2)}) async-start(bf16[8,4,128,256]{3,2,1,0:T(8,128)(2,1)} %copy-done.4), calls=%async_computation.7 | async-start | bytes 4194304 | tf_op jit(solution)/shard_map/all_to_all | solution.py:383
  477.7 5.8 %mix.3 = bf16[8,4,128,256]{3,2,1,0:T(8,128)(2,1)S(1)} custom-call(bf16[32,256,256]{2,1,0:T(8,128)(2,1)} %get-tuple-element.12.coeff_ref, bf16[32,128,32]{2,1,0:T(8,128)(2,1)S(1)} %reshape.413.mixing_ref, f32[32,128,1]{2,1,0:T(8,128)S(1)} %copy.59.factor_ref, f32[1,256]{1,0:T(1,128)S(1)} %sqrt.3.root_ref), custom_call_target="tpu_custom_call" | custom-call | flops 536870912 | bytes 6291456 | tf_op jit(solution)/shard_map/mix/pallas_call | solution.py:219
  483.6 1.3 copy-done.3
  484.9 37.4 %all-to-all-done.7 = bf16[8,4,128,256]{3,2,1,0:T(8,128)(2,1)} async-done(((bf16[8,4,128,256]{3,2,1,0:T(8,128)(2,1)}), bf16[8,4,128,256]{3,2,1,0:T(8,128)(2,1)}, u32[]{:S(2)}, u32[]{:S(2)}) %all-to-all-start.7) | async-done | bytes 2097184 | tf_op jit(solution)/shard_map/all_to_all | solution.py:383
  522.2 7.0 %all-to-all-start.5 = ((bf16[8,4,128,256]{3,2,1,0:T(8,128)(2,1)}), bf16[8,4,128,256]{3,2,1,0:T(8,128)(2,1)S(1)}, u32[]{:S(2)}, u32[]{:S(2)}) async-start(bf16[8,4,128,256]{3,2,1,0:T(8,128)(2,1)} %copy-done.3), calls=%async_computation.5 | async-start | bytes 4194304 | tf_op jit(solution)/shard_map/all_to_all | solution.py:383
  529.3 0.7 copy.62
  530.0 3.8 unpack.3.refs_0_
  533.9 3.8 unpack.4.refs_0_
  537.7 36.7 %all-to-all-done.5 = bf16[8,4,128,256]{3,2,1,0:T(8,128)(2,1)S(1)} async-done(((bf16[8,4,128,256]{3,2,1,0:T(8,128)(2,1)}), bf16[8,4,128,256]{3,2,1,0:T(8,128)(2,1)S(1)}, u32[]{:S(2)}, u32[]{:S(2)}) %all-to-all-start.5) | async-done | bytes 2097184 | tf_op jit(solution)/shard_map/all_to_all | solution.py:383
  574.4 2.0 unpack.5
  (48 shorter events, 2.2 us)
Async XLA Ops:
  4.0 2.2 copy-start.2
  6.3 110.1 %all-to-all-start = ((bf16[8,4,296,256]{3,2,1,0:T(8,128)(2,1)}), bf16[8,4,296,256]{3,2,1,0:T(8,128)(2,1)}, u32[]{:S(2)}, u32[]{:S(2)}) async-start(bf16[8,4,296,256]{3,2,1,0:T(8,128)(2,1)} %copy-done.2), calls=%async_computation | async-start | bytes 9699328 | tf_op jit(solution)/shard_map/all_to_all | solution.py:312
  15.8 2.3 copy-start.1
  116.3 111.2 %all-to-all-start.1 = ((bf16[8,4,296,256]{3,2,1,0:T(8,128)(2,1)}), bf16[8,4,296,256]{3,2,1,0:T(8,128)(2,1)}, u32[]{:S(2)}, u32[]{:S(2)}) async-start(bf16[8,4,296,256]{3,2,1,0:T(8,128)(2,1)} %copy-done.1), calls=%async_computation.1 | async-start | bytes 9699328 | tf_op jit(solution)/shard_map/all_to_all | solution.py:312
  127.6 2.2 copy-start
  129.9 105.5 %copy-start.7 = (s32[16]{0:T(128)S(1)}, s32[16]{0:T(128)}, u32[]{:S(2)}) copy-start(s32[16]{0:T(128)} %param.5) | copy-start | bytes 196
  227.5 111.2 %all-to-all-start.2 = ((bf16[8,4,296,256]{3,2,1,0:T(8,128)(2,1)}), bf16[8,4,296,256]{3,2,1,0:T(8,128)(2,1)}, u32[]{:S(2)}, u32[]{:S(2)}) async-start(bf16[8,4,296,256]{3,2,1,0:T(8,128)(2,1)} %copy-done), calls=%async_computation.2 | async-start | bytes 9699328 | tf_op jit(solution)/shard_map/all_to_all | solution.py:312
  237.2 6.0 %copy-start.6 = (f32[16]{0:T(128)S(1)}, f32[16]{0:T(128)}, u32[]{:S(2)}) copy-start(f32[16]{0:T(128)} %param.7) | copy-start | bytes 196
  393.1 14.6 %all-to-all-start.4 = ((bf16[32,1,34,128]{3,2,1,0:T(8,128)(2,1)}), bf16[32,1,34,128]{3,2,1,0:T(8,128)(2,1)S(1)}, u32[]{:S(2)}, u32[]{:S(2)}) async-start(bf16[32,1,34,128]{3,2,1,0:T(8,128)(2,1)} %broadcast_in_dim.27), calls=%async_computation.4 | async-start | bytes 655360 | tf_op jit(solution)/shard_map/all_to_all | solution.py:368
  416.6 1.3 copy-start.5
  417.9 52.2 %all-to-all-start.6 = ((bf16[8,4,128,256]{3,2,1,0:T(8,128)(2,1)}), bf16[8,4,128,256]{3,2,1,0:T(8,128)(2,1)}, u32[]{:S(2)}, u32[]{:S(2)}) async-start(bf16[8,4,128,256]{3,2,1,0:T(8,128)(2,1)} %copy-done.5), calls=%async_computation.6 | async-start | bytes 4194304 | tf_op jit(solution)/shard_map/all_to_all | solution.py:383
  431.0 1.3 copy-start.4
  470.1 52.2 %all-to-all-start.7 = ((bf16[8,4,128,256]{3,2,1,0:T(8,128)(2,1)}), bf16[8,4,128,256]{3,2,1,0:T(8,128)(2,1)}, u32[]{:S(2)}, u32[]{:S(2)}) async-start(bf16[8,4,128,256]{3,2,1,0:T(8,128)(2,1)} %copy-done.4), calls=%async_computation.7 | async-start | bytes 4194304 | tf_op jit(solution)/shard_map/all_to_all | solution.py:383
  483.6 1.3 copy-start.3
  522.2 52.2 %all-to-all-start.5 = ((bf16[8,4,128,256]{3,2,1,0:T(8,128)(2,1)}), bf16[8,4,128,256]{3,2,1,0:T(8,128)(2,1)S(1)}, u32[]{:S(2)}, u32[]{:S(2)}) async-start(bf16[8,4,128,256]{3,2,1,0:T(8,128)(2,1)} %copy-done.3), calls=%async_computation.5 | async-start | bytes 4194304 | tf_op jit(solution)/shard_map/all_to_all | solution.py:383

commit v2 on v1

v2 whole, which is shorter than its diff:
```python
import functools
import math

import jax
import jax.numpy as jnp
from jax import lax
from jax.experimental import pallas as pl
from jax.experimental.pallas import tpu as pltpu
from jax.sharding import PartitionSpec as P

NFFT = 64
NFREQ = 32
MODES = 8
SUBIT = 4
LANES = 128
EPSILON = 1e-06
VMEM_LIMIT = 48 * 1024 * 1024


def time_table(length, freq_count):
    steps_t = jnp.arange(length, dtype=jnp.float32)
    freq_f = jnp.arange(freq_count, dtype=jnp.float32)
    window = 0.5 - 0.5 * jnp.cos(2.0 * math.pi * steps_t / length)
    angles = 2.0 * math.pi * freq_f[:, None] * steps_t[None, :] / length
    both = jnp.stack([window * jnp.cos(angles), -window * jnp.sin(angles)])
    return (both / math.sqrt(length)).astype(jnp.bfloat16)


def order_table(orders, sectors):
    order_m = jnp.arange(orders, dtype=jnp.float32)[:, None]
    sector_s = jnp.arange(sectors, dtype=jnp.float32)[None, :]
    angles = 2.0 * math.pi * order_m * sector_s / sectors
    cosine = jnp.cos(angles)
    sine_part = jnp.sin(angles)
    upper_row = jnp.stack([cosine, sine_part], -1)
    lower_row = jnp.stack([-sine_part, cosine], -1)
    return (jnp.stack([upper_row, lower_row], 1) / math.sqrt(sectors)).astype(jnp.bfloat16)


def half_span(blocks):
    half = blocks // 2
    return half, (half - 1) * (NFFT // 2) + NFFT // 8 + NFFT


def placed_time_basis(block_start, tm_count):
    blocks = block_start.shape[0] // tm_count
    half, span = half_span(blocks)
    basis = time_table(NFFT, NFREQ)
    first = jnp.arange(blocks, dtype=jnp.int32) // half * (half * (NFFT // 2))
    inside = block_start.reshape(tm_count, blocks) - first[None, :]
    place = (
        inside[:, :, None, None] + jnp.arange(NFFT, dtype=jnp.int32)[:, None]
        == jnp.arange(span, dtype=jnp.int32)[None, :]
    ).astype(jnp.bfloat16)
    table = jnp.einsum(
        "eft,jhbtu->jhfebu",
        basis,
        place.reshape(tm_count, 2, half, NFFT, span),
        preferred_element_type=jnp.float32,
    ).astype(jnp.bfloat16)
    return table.reshape(tm_count, 2, NFREQ * 2 * half, span)


def coeff_kernel(sec_count, freqs, orders, time_ref, azimuth_ref, weight_ref, before_ref, record_ref,
                 coeff_ref, gram_ref, spectra):
    step = pl.program_id(0)
    tm_count, halves, _, span = time_ref.shape
    sec_local, rec_len, columns = record_ref.shape[2:]
    sectors = spectra.shape[0]
    rows = spectra.shape[2] // NFREQ

    @pl.when(step < sec_count)
    def _():
        for s in range(sec_local):
            for h in range(halves):
                first = h * (rec_len - span) // (halves - 1)
                parts = [
                    jnp.dot(
                        time_ref[j, h],
                        record_ref[0, j, s, first:first + span],
                        preferred_element_type=jnp.float32,
                    ).reshape(NFREQ, rows // tm_count, columns)
                    for j in range(tm_count)
                ]
                joined = jnp.stack(parts, 1).reshape(NFREQ * rows, columns)
                spectra[step * sec_local + s, h] = joined.astype(jnp.bfloat16)

    @pl.when(step >= sec_count)
    def _():
        half_rows = azimuth_ref.shape[0]
        depth = half_rows // (2 * orders)
        blocks = depth * halves
        wide = orders * blocks
        row = lax.broadcasted_iota(jnp.int32, (wide, wide), 0) % blocks
        column = lax.broadcasted_iota(jnp.int32, (wide, wide), 1) % blocks
        owner = lax.broadcasted_iota(jnp.int32, (blocks, wide), 1) // blocks
        for n in range(freqs):
            at = pl.multiple_of(((step - sec_count) * freqs + n) * rows, rows)
            parts = [
                jnp.dot(
                    azimuth_ref[...],
                    spectra[:, h, pl.ds(at, rows), :].reshape(sectors * rows, columns),
                    preferred_element_type=jnp.float32,
                ).reshape(2 * orders, depth, columns)
                for h in range(halves)
            ]
            coeffs = jnp.stack(parts, 1).reshape(2 * wide, columns).astype(jnp.bfloat16)
            coeff_ref[n] = coeffs
            weighted = (coeffs.astype(jnp.float32) * weight_ref[...]).astype(jnp.bfloat16)
            swapped = jnp.concatenate([coeffs[wide:], coeffs[:wide]], 0)
            across = (((1,), (1,)), ((), ()))
            upper = lax.dot_general(
                weighted[:wide], coeffs, across, preferred_element_type=jnp.float32
            )
            lower = lax.dot_general(
                weighted[wide:], swapped, across, preferred_element_type=jnp.float32
            )
            real = upper[:, :wide] + lower[:, :wide]
            imag = upper[:, wide:] - lower[:, wide:]
            packed = jnp.where(row <= column, real, imag)
            own = packed[:blocks]
            for m in range(1, orders):
                own = jnp.where(owner == m, packed[m * blocks:(m + 1) * blocks], own)
            gram_ref[n] = before_ref[n] + own


def coeffs_and_gram(arrived, time_basis, azimuth, weight, before):
    sec_count, tm_count, sec_local, rec_len, columns = arrived.shape
    sectors = sec_count * sec_local
    halves = time_basis.shape[1]
    blocks, wide = before.shape[1:]
    rows = azimuth.shape[1] // sectors
    steps = 4
    freqs = NFREQ // steps
    later = lambda i: jnp.maximum(i - sec_count, 0)
    early = lambda i: jnp.minimum(i, sec_count - 1)
    flops = 2 * columns * (
        sectors * time_basis.size + NFREQ * halves * azimuth.size + NFREQ * 4 * wide * wide
    )
    return pl.pallas_call(
        functools.partial(coeff_kernel, sec_count, freqs, wide // blocks),
        grid=(sec_count + steps,),
        in_specs=[
            pl.BlockSpec(time_basis.shape, lambda i: (0, 0, 0, 0)),
            pl.BlockSpec(azimuth.shape, lambda i: (0, 0)),
            pl.BlockSpec(weight.shape, lambda i: (0, 0)),
            pl.BlockSpec((freqs, blocks, wide), lambda i: (later(i), 0, 0)),
            pl.BlockSpec(
                (1, tm_count, sec_local, rec_len, columns), lambda i: (early(i), 0, 0, 0, 0)
            ),
        ],
        out_specs=[
            pl.BlockSpec((freqs, 2 * wide, columns), lambda i: (later(i), 0, 0)),
            pl.BlockSpec((freqs, blocks, wide), lambda i: (later(i), 0, 0)),
        ],
        out_shape=[
            jax.ShapeDtypeStruct((NFREQ, 2 * wide, columns), jnp.bfloat16),
            jax.ShapeDtypeStruct(before.shape, jnp.float32),
        ],
        scratch_shapes=[pltpu.VMEM((sectors, halves, NFREQ * rows, columns), jnp.bfloat16)],
        compiler_params=pltpu.CompilerParams(vmem_limit_bytes=VMEM_LIMIT),
        cost_estimate=pl.CostEstimate(
            flops=flops,
            bytes_accessed=2 * (arrived.size + NFREQ * 2 * wide * columns),
            transcendentals=0,
        ),
        name="coeffs_and_gram",
    )(time_basis, azimuth, weight, before, arrived)


def subspace_kernel(cell_total, first, packed_ref, basis_ref, energy_ref):
    size, _, pairs = packed_ref.shape
    row = lax.broadcasted_iota(jnp.int32, (size, pairs), 0)
    column_re, column_im = [], []
    for q in range(size):
        down, along = packed_ref[q], packed_ref[:, q, :]
        column_re.append(jnp.where(row <= q, down, along))
        column_im.append(jnp.where(row > q, down, jnp.where(row == q, 0.0, -along)))

    def image_of(vec_re, vec_im):
        out_re, out_im = [], []
        for j in range(MODES):
            sum_re = jnp.zeros_like(column_re[0])
            sum_im = jnp.zeros_like(column_re[0])
            for q in range(size):
                at_re, at_im = vec_re[j][q:q + 1], vec_im[j][q:q + 1]
                sum_re += column_re[q] * at_re - column_im[q] * at_im
                sum_im += column_re[q] * at_im + column_im[q] * at_re
            out_re.append(sum_re)
            out_im.append(sum_im)
        return out_re, out_im

    total = lambda x: jnp.sum(x, 0, keepdims=True)
    vec_re = [column_re[q] for q in first]
    vec_im = [column_im[q] for q in first]
    for sweep in range(SUBIT):
        if sweep > 0:
            vec_re, vec_im = image_of(vec_re, vec_im)
        vec_re, vec_im = list(vec_re), list(vec_im)
        for i in range(MODES):
            scale = 1.0 / jnp.sqrt(total(vec_re[i] * vec_re[i] + vec_im[i] * vec_im[i]) + EPSILON)
            own_re, own_im = vec_re[i] * scale, vec_im[i] * scale
            vec_re[i], vec_im[i] = own_re, own_im
            for j in range(i + 1, MODES):
                proj_re = total(own_re * vec_re[j] + own_im * vec_im[j])
                proj_im = total(own_re * vec_im[j] - own_im * vec_re[j])
                vec_re[j] = vec_re[j] - (proj_re * own_re - proj_im * own_im)
                vec_im[j] = vec_im[j] - (proj_re * own_im + proj_im * own_re)
    image_re, image_im = image_of(vec_re, vec_im)
    for j in range(MODES):
        basis_ref[0, j] = vec_re[j]
        basis_ref[1, j] = vec_im[j]
        energy_ref[j:j + 1] = total(vec_re[j] * image_re[j] + vec_im[j] * image_im[j]) / cell_total


def subspace(packed, first, cell_total):
    size, _, pairs = packed.shape
    return pl.pallas_call(
        functools.partial(subspace_kernel, float(cell_total), first),
        out_shape=[
            jax.ShapeDtypeStruct((2, MODES, size, pairs), jnp.float32),
            jax.ShapeDtypeStruct((MODES, pairs), jnp.float32),
        ],
        name="subspace",
    )(packed)


def mix_kernel(orders, own_freqs, coeff_ref, mixing_ref, spread_ref, factor_ref, root_ref, *refs):
    out_ref = refs[-1]
    freqs, rows, _ = mixing_ref.shape
    total = spread_ref.shape[1]
    blocks = total // (2 * orders)
    row = lax.broadcasted_iota(jnp.int32, (rows, total), 0) // (rows // orders)
    column = lax.broadcasted_iota(jnp.int32, (rows, total), 1) // blocks % orders
    factor = jnp.transpose(factor_ref[...])
    for n in range(freqs):
        wide = jnp.dot(mixing_ref[n], spread_ref[...], preferred_element_type=jnp.float32)
        wide = jnp.where(row == column, wide, 0.0).astype(jnp.bfloat16)
        fields = jnp.dot(wide, coeff_ref[n], preferred_element_type=jnp.float32)
        scaled = fields * (factor[:, n:n + 1] * root_ref[...])
        out_ref[n // own_freqs, 0, n % own_freqs] = scaled.astype(jnp.bfloat16)


def mix(coeffs, mixing, spread, factor, root_weight, owners, orders, at, count, whole):
    _, rows, columns = coeffs.shape
    out_rows, depth = mixing.shape[1:]
    own_freqs = NFREQ // owners
    steps = 4
    freqs = NFREQ // steps
    inputs = [coeffs, mixing, spread, factor, root_weight] + ([] if whole is None else [whole])
    in_specs = [
        pl.BlockSpec((freqs, rows, columns), lambda i: (i, 0, 0)),
        pl.BlockSpec((freqs, out_rows, depth), lambda i: (i, 0, 0)),
        pl.BlockSpec(spread.shape, lambda i: (0, 0)),
        pl.BlockSpec((freqs, out_rows), lambda i: (i, 0)),
        pl.BlockSpec(root_weight.shape, lambda i: (0, 0)),
        pl.BlockSpec(memory_space=pl.ANY),
    ]
    return pl.pallas_call(
        functools.partial(mix_kernel, orders, own_freqs),
        grid=(steps,),
        in_specs=in_specs[:len(inputs)],
        out_specs=pl.BlockSpec(
            (owners // steps, 1, own_freqs, out_rows, columns), lambda i: (i, at, 0, 0, 0)
        ),
        out_shape=jax.ShapeDtypeStruct((owners, count, own_freqs, out_rows, columns), jnp.bfloat16),
        input_output_aliases={} if whole is None else {5: 0},
        compiler_params=pltpu.CompilerParams(vmem_limit_bytes=VMEM_LIMIT),
        cost_estimate=pl.CostEstimate(
            flops=2 * NFREQ * out_rows * rows * columns,
            bytes_accessed=2 * NFREQ * (rows + out_rows) * columns,
            transcendentals=0,
        ),
        name="mix",
    )(*inputs)


def pack_kernel(record_ref, out_ref):
    owners, _, _, part = out_ref.shape
    for d in range(owners):
        out_ref[d, 0] = record_ref[0, 0, :, d * part:(d + 1) * part]


def pack(by_field, k, owners):
    sec_local, _, rec_len, cells = by_field.shape
    part = cells // owners
    return pl.pallas_call(
        pack_kernel,
        grid=(sec_local,),
        in_specs=[pl.BlockSpec((1, 1, rec_len, cells), lambda i: (i, k, 0, 0))],
        out_specs=pl.BlockSpec((owners, 1, rec_len, part), lambda i: (0, i, 0, 0)),
        out_shape=jax.ShapeDtypeStruct((owners, sec_local, rec_len, part), by_field.dtype),
        compiler_params=pltpu.CompilerParams(vmem_limit_bytes=VMEM_LIMIT),
        cost_estimate=pl.CostEstimate(
            flops=0, bytes_accessed=4 * sec_local * rec_len * cells, transcendentals=0
        ),
        name="pack",
    )(by_field)


def unpack_kernel(piece_ref, *refs):
    out_ref = refs[-1]
    owners, count, part = piece_ref.shape[0], piece_ref.shape[1], piece_ref.shape[-1]
    for k in range(count):
        for d in range(owners):
            out_ref[:, 0, :, k, :, d * part:(d + 1) * part] = piece_ref[d, k, 0]


def unpack(pieces, first, fields, whole):
    owners, count, freqs, orders, two, modes, part = pieces.shape
    shape = (orders, freqs, two, fields, modes, owners * part)
    inputs = [pieces] if whole is None else [pieces, whole]
    in_specs = [
        pl.BlockSpec((owners, count, 1, orders, two, modes, part), lambda i: (0, 0, i, 0, 0, 0, 0)),
        pl.BlockSpec(memory_space=pl.ANY),
    ]
    return pl.pallas_call(
        unpack_kernel,
        grid=(freqs,),
        in_specs=in_specs[:len(inputs)],
        out_specs=pl.BlockSpec(
            (orders, 1, two, count, modes, owners * part),
            lambda i: (0, i, 0, first // count, 0, 0),
        ),
        out_shape=jax.ShapeDtypeStruct(shape, pieces.dtype),
        input_output_aliases={} if whole is None else {1: 0},
        compiler_params=pltpu.CompilerParams(vmem_limit_bytes=VMEM_LIMIT),
        cost_estimate=pl.CostEstimate(flops=0, bytes_accessed=4 * pieces.size, transcendentals=0),
        name="unpack",
    )(*inputs)


def local(records, block_start, slab_index, weight_table):
    sec_local, rec_len, fields, cell_local = records.shape
    sec_count = lax.axis_size("sector")
    tm_count = lax.axis_size("tm")
    space_count = lax.axis_size("space")
    owners = sec_count * tm_count
    owner_axes = ("sector", "tm")
    sectors = sec_local * sec_count
    orders = sectors // 2
    blocks = block_start.shape[0]
    depth = 2 * blocks
    part = cell_local // owners
    own_freqs = NFREQ // owners
    me = lax.axis_index("sector") * tm_count + lax.axis_index("tm")

    by_field = jnp.transpose(records, (0, 2, 1, 3))
    arrived = []
    for k in range(fields):
        send = pack(by_field, k, owners)
        got = lax.all_to_all(send, owner_axes, split_axis=0, concat_axis=0, tiled=True)
        arrived.append(got.reshape(sec_count, tm_count, sec_local, rec_len, part))

    time_basis = placed_time_basis(block_start, tm_count)
    half, _ = half_span(blocks // tm_count)
    halves = blocks // tm_count // half
    azimuth = jnp.einsum(
        "mcse,ij,bd->cmibsjed",
        order_table(orders, sectors),
        jnp.eye(tm_count, dtype=jnp.bfloat16),
        jnp.eye(half, dtype=jnp.bfloat16),
    ).reshape(2 * orders * tm_count * half, sectors * tm_count * 2 * half)
    place = [
        (b // half % halves * tm_count + b // (half * halves)) * half + b % half
        for b in range(blocks)
    ]
    own_slab = lax.dynamic_slice_in_dim(slab_index, me * part, part)
    weight = jnp.sum(
        jnp.where(
            own_slab[None, :] == jnp.arange(weight_table.shape[0], dtype=jnp.int32)[:, None],
            weight_table[:, None],
            0.0,
        ),
        0,
        keepdims=True,
    )

    gram = jnp.zeros((NFREQ, blocks, orders * blocks), jnp.float32)
    coeffs = []
    for k in range(fields):
        own, gram = coeffs_and_gram(arrived[k], time_basis, azimuth, weight, gram)
        coeffs.append(own)

    if own_freqs % space_count == 0:
        axes = owner_axes + ("space",)
    else:
        gram = lax.psum(gram, "space")
        axes = owner_axes
    solvers = math.prod(lax.axis_size(a) for a in axes)
    solved = NFREQ // solvers
    gram = gram.reshape((solvers, solved) + gram.shape[1:])
    gram = lax.all_to_all(gram, axes, split_axis=0, concat_axis=0, tiled=True)
    gram = jnp.sum(gram, 0).reshape(solved, blocks, orders, blocks)
    gram = jnp.transpose(gram, (3, 1, 0, 2)).reshape(blocks, blocks, solved * orders)
    basis, energy = subspace(gram, tuple(place[:MODES]), fields * cell_local * space_count)

    short = basis.astype(jnp.bfloat16).reshape(2, MODES, blocks, solved, orders)
    short = jnp.transpose(short, (3, 4, 0, 1, 2))
    short_re, short_im = short[:, :, 0], short[:, :, 1]
    mixing = jnp.stack(
        [jnp.concatenate([short_re, -short_im], -1), jnp.concatenate([short_im, short_re], -1)], 2
    ).reshape(solved, orders * 2 * MODES * depth)
    energy = jnp.transpose(energy.reshape(MODES, solved, orders), (1, 2, 0)).reshape(solved, -1)
    high = energy.astype(jnp.bfloat16)
    rest = energy - high.astype(jnp.float32)
    middle = rest.astype(jnp.bfloat16)
    low = (rest - middle.astype(jnp.float32)).astype(jnp.bfloat16)
    packet = jnp.concatenate([mixing, high, middle, low], 1)
    width = -(-packet.shape[1] // LANES) * LANES
    packet = jnp.pad(packet, ((0, 0), (0, width - packet.shape[1])))
    packet = packet.reshape(1, solved, width // LANES, LANES)
    packet = jnp.broadcast_to(packet, (solvers,) + packet.shape[1:])
    packet = lax.all_to_all(packet, axes, split_axis=0, concat_axis=0, tiled=True)
    packet = packet.reshape(NFREQ, width)
    count = orders * MODES
    mixing = packet[:, :orders * 2 * MODES * depth].reshape(NFREQ, orders * 2 * MODES, depth)
    tail = packet[:, orders * 2 * MODES * depth:].astype(jnp.float32)
    energy = (tail[:, :count] + tail[:, count:2 * count]) + tail[:, 2 * count:3 * count]
    energy = energy.reshape(NFREQ, orders, MODES)
    factor = jnp.broadcast_to(
        lax.rsqrt(energy)[:, :, None, :], (NFREQ, orders, 2, MODES)
    ).reshape(NFREQ, orders * 2 * MODES)
    root_weight = jnp.sqrt(weight)
    spread = jnp.broadcast_to(
        jnp.eye(depth, dtype=jnp.bfloat16).reshape(depth, 2, 1, blocks), (depth, 2, orders, blocks)
    ).reshape(depth, depth * orders)

    mode_fields = None
    for first, count in ((fields - 1, 1), (0, fields - 1)):
        send = None
        for n in range(count):
            send = mix(
                coeffs[first + n], mixing, spread, factor, root_weight, owners, orders, n, count, send
            )
        got = lax.all_to_all(send, owner_axes, split_axis=0, concat_axis=0, tiled=True)
        got = got.reshape(owners, count, own_freqs, orders, 2, MODES, part)
        mode_fields = unpack(got, first, fields, mode_fields)
    mode_fields = jnp.transpose(mode_fields, (0, 1, 2, 4, 3, 5))
    own_energy = lax.dynamic_slice_in_dim(energy, me * own_freqs, own_freqs)
    return (mode_fields, jnp.transpose(own_energy, (1, 0, 2)))


def solution(mesh):
    placed = (P("sector", "tm", None, "space"), P(), P("space"), P())
    return jax.shard_map(
        local,
        mesh=mesh,
        in_specs=placed,
        out_specs=(
            P(None, ("sector", "tm"), None, None, None, "space"),
            P(None, ("sector", "tm"), None),
        ),
        check_vma=False,
    )
```

time: 583 us -> 557 us (0.955)
  Pallas kernels: 117 us -> 74.2 us
  waiting for transfers between devices: 362 us -> 390 us
  starting transfers between devices: 49.2 us -> 41.3 us
    pallas_call x7, Pallas kernels: 97.3 us -> 57.3 us  [the longest x3 40.5 us: coeffs_and_gram(): pl.pallas_call(functools.partial(coeff_kernel, sec_count, freqs, wide //...]
    all_to_all x6 -> x5, waiting for transfers between devices: 353 us -> 381 us  [local(): lax.all_to_all(send, owner_axes, split_axis=0, concat_axis=0, tiled=True)]
    all_to_all x6 -> x5, starting transfers between devices: 43.8 us -> 36.3 us  [local(): lax.all_to_all(send, owner_axes, split_axis=0, concat_axis=0, tiled=True)]
    unnamed x18 -> x22, local copies, waits for them, and re-layouts: 11.4 us -> 16.7 us
  transfers between devices with their start and end apart: 7 -> 6, of which waited for: 7 -> 6; matrix products, arithmetic and copies ran while one was open for 1% -> 2% of each run, Pallas kernels for 13% -> 8%
where the time goes in v2:
time: 557 us; the launch traced here: 551 us
  waiting for transfers between devices  390 us (70%)
  Pallas kernels  74.2 us (13%)
  starting transfers between devices  41.3 us (7%)
  local copies, waits for them, and re-layouts  26.6 us (5%)
  blocking collectives  14.8 us (3%)
    all_to_all x5, waiting for transfers between devices, local(): lax.all_to_all(send, owner_axes, split_axis=0, concat_axis=0, tiled=True)  381 us
    pallas_call x3, Pallas kernels, coeffs_and_gram(): pl.pallas_call(functools.partial(coeff_kernel, sec_count, freqs, wide //...  40.5 us
    all_to_all x5, starting transfers between devices, local(): lax.all_to_all(send, owner_axes, split_axis=0, concat_axis=0, tiled=True)  36.3 us
    unnamed x22, local copies, waits for them, and re-layouts  16.7 us
    all_to_all x1, blocking collectives, local(): gram = lax.all_to_all(gram, axes, split_axis=0, concat_axis=0, tiled=True)  14.8 us
    pallas_call x3, Pallas kernels, mix(): pl.pallas_call(functools.partial(mix_kernel, orders, own_freqs), grid=(st...  12.7 us
  transfers between devices with their start and end apart: 6, of which 6 were waited for; matrix products, arithmetic and copies ran while one was open for 2% of the time, Pallas kernels for 8%

profile of v2, /device:TPU:16, one launch (start us, length us, event | category | flops | bytes accessed | tf_op | source)
XLA Modules:
  0.0 551.4 jit_solution(331774083200277169)
XLA Ops:
  0.6 3.4 pack.3
  4.0 2.2 copy-done.3
  6.3 6.1 %all-to-all-start = ((bf16[8,4,296,256]{3,2,1,0:T(8,128)(2,1)}), bf16[8,4,296,256]{3,2,1,0:T(8,128)(2,1)}, u32[]{:S(2)}, u32[]{:S(2)}) async-start(bf16[8,4,296,256]{3,2,1,0:T(8,128)(2,1)} %copy-done.3), calls=%async_computation | async-start | bytes 9699328 | tf_op jit(solution)/shard_map/all_to_all | solution.py:352
  12.4 3.4 pack.4
  15.8 2.3 copy-done.2
  18.0 98.3 %all-to-all-done = bf16[8,4,296,256]{3,2,1,0:T(8,128)(2,1)} async-done(((bf16[8,4,296,256]{3,2,1,0:T(8,128)(2,1)}), bf16[8,4,296,256]{3,2,1,0:T(8,128)(2,1)}, u32[]{:S(2)}, u32[]{:S(2)}) %all-to-all-start) | async-done | bytes 4849696 | tf_op jit(solution)/shard_map/all_to_all | solution.py:352
  116.3 7.9 %all-to-all-start.1 = ((bf16[8,4,296,256]{3,2,1,0:T(8,128)(2,1)}), bf16[8,4,296,256]{3,2,1,0:T(8,128)(2,1)}, u32[]{:S(2)}, u32[]{:S(2)}) async-start(bf16[8,4,296,256]{3,2,1,0:T(8,128)(2,1)} %copy-done.2), calls=%async_computation.1 | async-start | bytes 9699328 | tf_op jit(solution)/shard_map/all_to_all | solution.py:352
  124.2 3.4 pack.5
  127.6 2.2 copy-done.1
  129.9 97.6 %all-to-all-done.1 = bf16[8,4,296,256]{3,2,1,0:T(8,128)(2,1)} async-done(((bf16[8,4,296,256]{3,2,1,0:T(8,128)(2,1)}), bf16[8,4,296,256]{3,2,1,0:T(8,128)(2,1)}, u32[]{:S(2)}, u32[]{:S(2)}) %all-to-all-start.1) | async-done | bytes 4849696 | tf_op jit(solution)/shard_map/all_to_all | solution.py:352
  227.5 7.9 %all-to-all-start.2 = ((bf16[8,4,296,256]{3,2,1,0:T(8,128)(2,1)}), bf16[8,4,296,256]{3,2,1,0:T(8,128)(2,1)}, u32[]{:S(2)}, u32[]{:S(2)}) async-start(bf16[8,4,296,256]{3,2,1,0:T(8,128)(2,1)} %copy-done.1), calls=%async_computation.2 | async-start | bytes 9699328 | tf_op jit(solution)/shard_map/all_to_all | solution.py:352
  235.6 0.1 cosine_multiply_fusion
  235.8 0.5 fusion
  236.3 0.5 copy.48
  236.9 0.1 fusion.10
  237.0 0.2 copy.49
  237.3 1.6 multiply_bitcast_fusion
  238.9 4.0 reshape.445.azimuth_ref
  242.9 0.8 dynamic_slice.6
  243.8 13.5 %coeffs_and_gram.3 = (bf16[32,256,256]{2,1,0:T(8,128)(2,1)S(1)}, f32[32,16,128]{2,1,0:T(8,128)S(1)}) custom-call(bf16[2,2,256,168]{3,2,1,0:T(8,128)(2,1)S(1)} %copy.51.time_ref, bf16[128,256]{1,0:T(8,128)(2,1)S(1)} %reshape.445.azimuth_ref, f32[1,256]{1,0:T(1,128)S(1)} %bitcast.70, f32[32,16,128]{2,1,0:T(8,128)S(1)} %broadcast_in_dim.54.before_ref, ...), custom_call_target="tpu_custom_call" | custom-call | flops 3556769792 | bytes 9043968 | tf_op jit(solution)/shard_map/coeffs_and_gram/pallas_call | solution.py:140
  257.3 1.9 copy-done.5
  259.3 13.5 %coeffs_and_gram.4 = (bf16[32,256,256]{2,1,0:T(8,128)(2,1)S(1)}, f32[32,16,128]{2,1,0:T(8,128)S(1)}) custom-call(bf16[2,2,256,168]{3,2,1,0:T(8,128)(2,1)S(1)} %copy.51.time_ref, bf16[128,256]{1,0:T(8,128)(2,1)S(1)} %reshape.445.azimuth_ref, f32[1,256]{1,0:T(1,128)S(1)} %bitcast.71, f32[32,16,128]{2,1,0:T(8,128)S(1)} %get-tuple-element.10.before_ref, ...), custom_call_target="tpu_custom_call" | custom-call | flops 3556769792 | bytes 9043968 | tf_op jit(solution)/shard_map/coeffs_and_gram/pallas_call | solution.py:140
  272.8 2.0 copy-done.6
  274.8 63.9 %all-to-all-done.2 = bf16[8,4,296,256]{3,2,1,0:T(8,128)(2,1)} async-done(((bf16[8,4,296,256]{3,2,1,0:T(8,128)(2,1)}), bf16[8,4,296,256]{3,2,1,0:T(8,128)(2,1)}, u32[]{:S(2)}, u32[]{:S(2)}) %all-to-all-start.2) | async-done | bytes 4849696 | tf_op jit(solution)/shard_map/all_to_all | solution.py:352
  338.7 13.5 %coeffs_and_gram.5 = (bf16[32,256,256]{2,1,0:T(8,128)(2,1)S(1)}, f32[32,16,128]{2,1,0:T(8,128)S(1)}) custom-call(bf16[2,2,256,168]{3,2,1,0:T(8,128)(2,1)S(1)} %copy.51.time_ref, bf16[128,256]{1,0:T(8,128)(2,1)S(1)} %reshape.445.azimuth_ref, f32[1,256]{1,0:T(1,128)S(1)} %bitcast.72, f32[32,16,128]{2,1,0:T(8,128)S(1)} %get-tuple-element.12.before_ref, ...), custom_call_target="tpu_custom_call" | custom-call | flops 3556769792 | bytes 9043968 | tf_op jit(solution)/shard_map/coeffs_and_gram/pallas_call | solution.py:140
  352.2 2.0 copy-done.7
  354.2 14.8 %all_to_all.35 = f32[32,1,16,128]{3,2,1,0:T(8,128)S(1)} all-to-all(f32[32,1,16,128]{3,2,1,0:T(8,128)S(1)} %bitcast.69), channel_id=1, replica_groups=mesh['sector'=4,'tm'=2,'space'=4] {'sector','tm','space'}, dimensions={0} | all-to-all | bytes 524288 | tf_op jit(solution)/shard_map/all_to_all | solution.py:393
  369.1 0.8 copy.54
  369.9 4.0 subspace.1
  373.9 0.9 convert_bitcast_fusion
  375.4 0.8 copy.61
  376.2 0.1 concatenate.11
  376.4 0.8 broadcast_in_dim.56
  377.2 4.9 all-to-all-start.4
  382.3 8.9 %all-to-all-done.4 = bf16[32,1,34,128]{3,2,1,0:T(8,128)(2,1)S(1)} async-done(((bf16[32,1,34,128]{3,2,1,0:T(8,128)(2,1)}), bf16[32,1,34,128]{3,2,1,0:T(8,128)(2,1)S(1)}, u32[]{:S(2)}, u32[]{:S(2)}) %all-to-all-start.4) | async-done | bytes 278560 | tf_op jit(solution)/shard_map/all_to_all | solution.py:414
  391.4 0.8 reshape.457.mixing_ref
  392.4 4.2 mix.5
  396.6 1.3 copy-done.4
  397.9 6.7 %all-to-all-start.6 = ((bf16[8,1,4,128,256]{4,3,2,1,0:T(8,128)(2,1)}), bf16[8,1,4,128,256]{4,3,2,1,0:T(8,128)(2,1)S(1)}, u32[]{:S(2)}, u32[]{:S(2)}) async-start(bf16[8,1,4,128,256]{4,3,2,1,0:T(8,128)(2,1)} %copy-done.4), calls=%async_computation.6 | async-start | bytes 4194304 | tf_op jit(solution)/shard_map/all_to_all | solution.py:436
  404.6 4.2 mix.3.refs_0_
  408.9 4.3 mix.4
  413.1 2.0 copy-done
  415.1 34.4 %all-to-all-done.6 = bf16[8,1,4,128,256]{4,3,2,1,0:T(8,128)(2,1)S(1)} async-done(((bf16[8,1,4,128,256]{4,3,2,1,0:T(8,128)(2,1)}), bf16[8,1,4,128,256]{4,3,2,1,0:T(8,128)(2,1)S(1)}, u32[]{:S(2)}, u32[]{:S(2)}) %all-to-all-start.6) | async-done | bytes 2097184 | tf_op jit(solution)/shard_map/all_to_all | solution.py:436
  449.6 7.7 %all-to-all-start.5 = ((bf16[8,2,4,128,256]{4,3,2,1,0:T(8,128)(2,1)}), bf16[8,2,4,128,256]{4,3,2,1,0:T(8,128)(2,1)}, u32[]{:S(2)}, u32[]{:S(2)}) async-start(bf16[8,2,4,128,256]{4,3,2,1,0:T(8,128)(2,1)} %copy-done), calls=%async_computation.5 | async-start | bytes 8388608 | tf_op jit(solution)/shard_map/all_to_all | solution.py:436
  457.4 0.7 copy.69
  458.1 2.0 unpack.2.refs_0_
  460.1 86.5 %all-to-all-done.5 = bf16[8,2,4,128,256]{4,3,2,1,0:T(8,128)(2,1)} async-done(((bf16[8,2,4,128,256]{4,3,2,1,0:T(8,128)(2,1)}), bf16[8,2,4,128,256]{4,3,2,1,0:T(8,128)(2,1)}, u32[]{:S(2)}, u32[]{:S(2)}) %all-to-all-start.5) | async-done | bytes 4194336 | tf_op jit(solution)/shard_map/all_to_all | solution.py:436
  546.6 4.8 unpack.3
  (54 shorter events, 1.8 us)
Async XLA Ops:
  4.0 2.2 copy-start.3
  6.3 110.1 %all-to-all-start = ((bf16[8,4,296,256]{3,2,1,0:T(8,128)(2,1)}), bf16[8,4,296,256]{3,2,1,0:T(8,128)(2,1)}, u32[]{:S(2)}, u32[]{:S(2)}) async-start(bf16[8,4,296,256]{3,2,1,0:T(8,128)(2,1)} %copy-done.3), calls=%async_computation | async-start | bytes 9699328 | tf_op jit(solution)/shard_map/all_to_all | solution.py:352
  15.8 2.3 copy-start.2
  116.3 111.2 %all-to-all-start.1 = ((bf16[8,4,296,256]{3,2,1,0:T(8,128)(2,1)}), bf16[8,4,296,256]{3,2,1,0:T(8,128)(2,1)}, u32[]{:S(2)}, u32[]{:S(2)}) async-start(bf16[8,4,296,256]{3,2,1,0:T(8,128)(2,1)} %copy-done.2), calls=%async_computation.1 | async-start | bytes 9699328 | tf_op jit(solution)/shard_map/all_to_all | solution.py:352
  127.6 2.2 copy-start.1
  129.9 105.5 %copy-start.8 = (s32[16]{0:T(128)S(1)}, s32[16]{0:T(128)}, u32[]{:S(2)}) copy-start(s32[16]{0:T(128)} %param.5) | copy-start | bytes 196
  227.5 111.1 %all-to-all-start.2 = ((bf16[8,4,296,256]{3,2,1,0:T(8,128)(2,1)}), bf16[8,4,296,256]{3,2,1,0:T(8,128)(2,1)}, u32[]{:S(2)}, u32[]{:S(2)}) async-start(bf16[8,4,296,256]{3,2,1,0:T(8,128)(2,1)} %copy-done.1), calls=%async_computation.2 | async-start | bytes 9699328 | tf_op jit(solution)/shard_map/all_to_all | solution.py:352
  235.4 8.3 %copy-start.9 = (f32[16]{0:T(128)S(1)}, f32[16]{0:T(128)}, u32[]{:S(2)}) copy-start(f32[16]{0:T(128)} %param.7) | copy-start | bytes 196
  257.3 1.9 copy-start.5
  272.8 2.0 copy-start.6
  352.2 2.0 copy-start.7
  377.2 14.1 %all-to-all-start.4 = ((bf16[32,1,34,128]{3,2,1,0:T(8,128)(2,1)}), bf16[32,1,34,128]{3,2,1,0:T(8,128)(2,1)S(1)}, u32[]{:S(2)}, u32[]{:S(2)}) async-start(bf16[32,1,34,128]{3,2,1,0:T(8,128)(2,1)} %broadcast_in_dim.56), calls=%async_computation.4 | async-start | bytes 655360 | tf_op jit(solution)/shard_map/all_to_all | solution.py:414
  396.6 1.3 copy-start.4
  397.9 51.6 %all-to-all-start.6 = ((bf16[8,1,4,128,256]{4,3,2,1,0:T(8,128)(2,1)}), bf16[8,1,4,128,256]{4,3,2,1,0:T(8,128)(2,1)S(1)}, u32[]{:S(2)}, u32[]{:S(2)}) async-start(bf16[8,1,4,128,256]{4,3,2,1,0:T(8,128)(2,1)} %copy-done.4), calls=%async_computation.6 | async-start | bytes 4194304 | tf_op jit(solution)/shard_map/all_to_all | solution.py:436
  413.1 2.0 copy-start
  449.6 97.0 %all-to-all-start.5 = ((bf16[8,2,4,128,256]{4,3,2,1,0:T(8,128)(2,1)}), bf16[8,2,4,128,256]{4,3,2,1,0:T(8,128)(2,1)}, u32[]{:S(2)}, u32[]{:S(2)}) async-start(bf16[8,2,4,128,256]{4,3,2,1,0:T(8,128)(2,1)} %copy-done), calls=%async_computation.5 | async-start | bytes 8388608 | tf_op jit(solution)/shard_map/all_to_all | solution.py:436

commit v3 on v2

--- a/solution.py
+++ b/solution.py
@@ -61,31 +61,35 @@
     return table.reshape(tm_count, 2, NFREQ * 2 * half, span)
 
 
-def coeff_kernel(sec_count, freqs, orders, time_ref, azimuth_ref, weight_ref, before_ref, record_ref,
-                 coeff_ref, gram_ref, spectra):
+def coeff_kernel(sec_count, sec_local, freqs, orders, place_ref, time_ref, azimuth_ref, weight_ref,
+                 before_ref, *refs):
+    record_refs, (coeff_ref, gram_ref, spectra) = refs[:-3], refs[-3:]
     step = pl.program_id(0)
     tm_count, halves, _, span = time_ref.shape
-    sec_local, rec_len, columns = record_ref.shape[2:]
+    rec_len, columns = record_refs[0].shape[1:]
     sectors = spectra.shape[0]
     rows = spectra.shape[2] // NFREQ
 
-    @pl.when(step < sec_count)
+    @pl.when(step < sec_local)
     def _():
-        for s in range(sec_local):
+        for shift in range(sec_count):
+            source = lax.rem(place_ref[0] + sec_count - shift, sec_count)
+            own = record_refs[shift * tm_count:(shift + 1) * tm_count]
             for h in range(halves):
                 first = h * (rec_len - span) // (halves - 1)
-                parts = [
-                    jnp.dot(
-                        time_ref[j, h],
-                        record_ref[0, j, s, first:first + span],
-                        preferred_element_type=jnp.float32,
-                    ).reshape(NFREQ, rows // tm_count, columns)
-                    for j in range(tm_count)
-                ]
+                pieces = [ref[0, first:first + span] for ref in own]
+                parts = []
+                for j in range(tm_count):
+                    piece = pieces[0]
+                    for n in range(1, tm_count):
+                        here = lax.rem(place_ref[1] + tm_count - n, tm_count) == j
+                        piece = jnp.where(here, pieces[n], piece)
+                    part = jnp.dot(time_ref[j, h], piece, preferred_element_type=jnp.float32)
+                    parts.append(part.reshape(NFREQ, rows // tm_count, columns))
                 joined = jnp.stack(parts, 1).reshape(NFREQ * rows, columns)
-                spectra[step * sec_local + s, h] = joined.astype(jnp.bfloat16)
-
-    @pl.when(step >= sec_count)
+                spectra[source * sec_local + step, h] = joined.astype(jnp.bfloat16)
+
+    @pl.when(step >= sec_local)
     def _():
         half_rows = azimuth_ref.shape[0]
         depth = half_rows // (2 * orders)
@@ -95,7 +99,7 @@
         column = lax.broadcasted_iota(jnp.int32, (wide, wide), 1) % blocks
         owner = lax.broadcasted_iota(jnp.int32, (blocks, wide), 1) // blocks
         for n in range(freqs):
-            at = pl.multiple_of(((step - sec_count) * freqs + n) * rows, rows)
+            at = pl.multiple_of(((step - sec_local) * freqs + n) * rows, rows)
             parts = [
                 jnp.dot(
                     azimuth_ref[...],
@@ -124,48 +128,49 @@
             gram_ref[n] = before_ref[n] + own
 
 
-def coeffs_and_gram(arrived, time_basis, azimuth, weight, before):
-    sec_count, tm_count, sec_local, rec_len, columns = arrived.shape
+def coeffs_and_gram(place, arrived, sec_count, time_basis, azimuth, weight, before):
+    sec_local, rec_len, columns = arrived[0].shape
     sectors = sec_count * sec_local
     halves = time_basis.shape[1]
     blocks, wide = before.shape[1:]
     rows = azimuth.shape[1] // sectors
     steps = 4
     freqs = NFREQ // steps
-    later = lambda i: jnp.maximum(i - sec_count, 0)
-    early = lambda i: jnp.minimum(i, sec_count - 1)
+    later = lambda i: jnp.maximum(i - sec_local, 0)
+    early = lambda i: jnp.minimum(i, sec_local - 1)
     flops = 2 * columns * (
         sectors * time_basis.size + NFREQ * halves * azimuth.size + NFREQ * 4 * wide * wide
     )
+    piece = pl.BlockSpec((1, rec_len, columns), lambda i, _: (early(i), 0, 0))
     return pl.pallas_call(
-        functools.partial(coeff_kernel, sec_count, freqs, wide // blocks),
-        grid=(sec_count + steps,),
-        in_specs=[
-            pl.BlockSpec(time_basis.shape, lambda i: (0, 0, 0, 0)),
-            pl.BlockSpec(azimuth.shape, lambda i: (0, 0)),
-            pl.BlockSpec(weight.shape, lambda i: (0, 0)),
-            pl.BlockSpec((freqs, blocks, wide), lambda i: (later(i), 0, 0)),
-            pl.BlockSpec(
-                (1, tm_count, sec_local, rec_len, columns), lambda i: (early(i), 0, 0, 0, 0)
-            ),
-        ],
-        out_specs=[
-            pl.BlockSpec((freqs, 2 * wide, columns), lambda i: (later(i), 0, 0)),
-            pl.BlockSpec((freqs, blocks, wide), lambda i: (later(i), 0, 0)),
-        ],
+        functools.partial(coeff_kernel, sec_count, sec_local, freqs, wide // blocks),
+        grid_spec=pltpu.PrefetchScalarGridSpec(
+            num_scalar_prefetch=1,
+            grid=(sec_local + steps,),
+            in_specs=[
+                pl.BlockSpec(time_basis.shape, lambda i, _: (0, 0, 0, 0)),
+                pl.BlockSpec(azimuth.shape, lambda i, _: (0, 0)),
+                pl.BlockSpec(weight.shape, lambda i, _: (0, 0)),
+                pl.BlockSpec((freqs, blocks, wide), lambda i, _: (later(i), 0, 0)),
+            ] + [piece] * len(arrived),
+            out_specs=[
+                pl.BlockSpec((freqs, 2 * wide, columns), lambda i, _: (later(i), 0, 0)),
+                pl.BlockSpec((freqs, blocks, wide), lambda i, _: (later(i), 0, 0)),
+            ],
+            scratch_shapes=[pltpu.VMEM((sectors, halves, NFREQ * rows, columns), jnp.bfloat16)],
+        ),
         out_shape=[
             jax.ShapeDtypeStruct((NFREQ, 2 * wide, columns), jnp.bfloat16),
             jax.ShapeDtypeStruct(before.shape, jnp.float32),
         ],
-        scratch_shapes=[pltpu.VMEM((sectors, halves, NFREQ * rows, columns), jnp.bfloat16)],
         compiler_params=pltpu.CompilerParams(vmem_limit_bytes=VMEM_LIMIT),
         cost_estimate=pl.CostEstimate(
             flops=flops,
-            bytes_accessed=2 * (arrived.size + NFREQ * 2 * wide * columns),
+            bytes_accessed=2 * (len(arrived) * arrived[0].size + NFREQ * 2 * wide * columns),
             transcendentals=0,
         ),
         name="coeffs_and_gram",
-    )(time_basis, azimuth, weight, before, arrived)
+    )(place, time_basis, azimuth, weight, before, *arrived)
 
 
 def subspace_kernel(cell_total, first, packed_ref, basis_ref, energy_ref):
@@ -275,27 +280,32 @@
     )(*inputs)
 
 
-def pack_kernel(record_ref, out_ref):
-    owners, _, _, part = out_ref.shape
-    for d in range(owners):
-        out_ref[d, 0] = record_ref[0, 0, :, d * part:(d + 1) * part]
-
-
-def pack(by_field, k, owners):
+def take_kernel(place_ref, record_ref, out_ref):
+    out_ref[...] = record_ref[:, 0]
+
+
+def take(by_field, k, owner, owners):
     sec_local, _, rec_len, cells = by_field.shape
     part = cells // owners
+    if part % LANES:
+        return lax.dynamic_slice_in_dim(by_field[:, k], owner * part, part, 2)
     return pl.pallas_call(
-        pack_kernel,
-        grid=(sec_local,),
-        in_specs=[pl.BlockSpec((1, 1, rec_len, cells), lambda i: (i, k, 0, 0))],
-        out_specs=pl.BlockSpec((owners, 1, rec_len, part), lambda i: (0, i, 0, 0)),
-        out_shape=jax.ShapeDtypeStruct((owners, sec_local, rec_len, part), by_field.dtype),
+        take_kernel,
+        grid_spec=pltpu.PrefetchScalarGridSpec(
+            num_scalar_prefetch=1,
+            grid=(1,),
+            in_specs=[
+                pl.BlockSpec((sec_local, 1, rec_len, part), lambda i, at: (0, k, 0, at[0]))
+            ],
+            out_specs=pl.BlockSpec((sec_local, rec_len, part), lambda i, at: (0, 0, 0)),
+        ),
+        out_shape=jax.ShapeDtypeStruct((sec_local, rec_len, part), by_field.dtype),
         compiler_params=pltpu.CompilerParams(vmem_limit_bytes=VMEM_LIMIT),
         cost_estimate=pl.CostEstimate(
-            flops=0, bytes_accessed=4 * sec_local * rec_len * cells, transcendentals=0
-        ),
-        name="pack",
-    )(by_field)
+            flops=0, bytes_accessed=4 * sec_local * rec_len * part, transcendentals=0
+        ),
+        name="take",
+    )(jnp.reshape(owner, (1,)), by_field)
 
 
 def unpack_kernel(piece_ref, *refs):
@@ -346,11 +356,24 @@
     me = lax.axis_index("sector") * tm_count + lax.axis_index("tm")
 
     by_field = jnp.transpose(records, (0, 2, 1, 3))
+    sec_at, tm_at = lax.axis_index("sector"), lax.axis_index("tm")
+    shifts = [(z, x) for z in range(sec_count) for x in range(tm_count)]
+    in_order = sorted(shifts, key=lambda r: (r[0] == 0, abs(2 * r[0] - sec_count), r))
     arrived = []
     for k in range(fields):
-        send = pack(by_field, k, owners)
-        got = lax.all_to_all(send, owner_axes, split_axis=0, concat_axis=0, tiled=True)
-        arrived.append(got.reshape(sec_count, tm_count, sec_local, rec_len, part))
+        got = {}
+        for z, x in in_order:
+            owner = (sec_at + z) % sec_count * tm_count + (tm_at + x) % tm_count
+            piece = take(by_field, k, owner, owners)
+            if (z, x) != (0, 0):
+                hops = [
+                    (a * tm_count + j, (a + z) % sec_count * tm_count + (j + x) % tm_count)
+                    for a in range(sec_count)
+                    for j in range(tm_count)
+                ]
+                piece = lax.ppermute(piece, owner_axes, hops)
+            got[z, x] = piece
+        arrived.append([got[r] for r in shifts])
 
     time_basis = placed_time_basis(block_start, tm_count)
     half, _ = half_span(blocks // tm_count)
@@ -379,7 +402,9 @@
     gram = jnp.zeros((NFREQ, blocks, orders * blocks), jnp.float32)
     coeffs = []
     for k in range(fields):
-        own, gram = coeffs_and_gram(arrived[k], time_basis, azimuth, weight, gram)
+        own, gram = coeffs_and_gram(
+            jnp.stack([sec_at, tm_at]), arrived[k], sec_count, time_basis, azimuth, weight, gram
+        )
         coeffs.append(own)
 
     if own_freqs % space_count == 0:

time: 557 us -> 536 us (0.962)
  waiting for transfers between devices: 390 us -> 278 us
  starting transfers between devices: 41.3 us -> 99.4 us
  Pallas kernels: 74.2 us -> 101 us
    all_to_all x5 -> x2, waiting for transfers between devices: 381 us -> 121 us  [local(): lax.all_to_all(send, owner_axes, split_axis=0, concat_axis=0, tiled=True)]
    ppermute x0 -> x21, waiting for transfers between devices: none -> 148 us  [local(): piece = lax.ppermute(piece, owner_axes, hops)]
    ppermute x0 -> x21, starting transfers between devices: none -> 80.1 us  [local(): piece = lax.ppermute(piece, owner_axes, hops)]
    pallas_call x6 -> x27, Pallas kernels: 50.7 us -> 77.3 us  [the longest x3 45 us: coeffs_and_gram(): pl.pallas_call(functools.partial(coeff_kernel, sec_count, sec_local, freq...]
    all_to_all x5 -> x2, starting transfers between devices: 36.3 us -> 14.4 us  [local(): lax.all_to_all(send, owner_axes, split_axis=0, concat_axis=0, tiled=True)]
    unnamed x22 -> x46, local copies, waits for them, and re-layouts: 16.7 us -> 13 us
  transfers between devices with their start and end apart: 6 -> 24, of which waited for: 6 -> 11; matrix products, arithmetic and copies ran while one was open for 2% -> 3% of each run, Pallas kernels for 8% -> 14%
where the time goes in v3:
time: 536 us; the launch traced here: 529 us
  waiting for transfers between devices  278 us (52%)
  Pallas kernels  101 us (19%)
  starting transfers between devices  99.4 us (19%)
  local copies, waits for them, and re-layouts  26.4 us (5%)
  blocking collectives  14.9 us (3%)
  other arithmetic  8.74 us (2%)
    ppermute x21, waiting for transfers between devices, local(): piece = lax.ppermute(piece, owner_axes, hops)  148 us
    all_to_all x2, waiting for transfers between devices, local(): lax.all_to_all(send, owner_axes, split_axis=0, concat_axis=0, tiled=True)  121 us
    ppermute x21, starting transfers between devices, local(): piece = lax.ppermute(piece, owner_axes, hops)  80.1 us
    pallas_call x3, Pallas kernels, coeffs_and_gram(): pl.pallas_call(functools.partial(coeff_kernel, sec_count, sec_local, freq...  45 us
    pallas_call x24, Pallas kernels, take(): pl.pallas_call(take_kernel, grid_spec=pltpu.PrefetchScalarGridSpec(num_sc...  32.4 us
    all_to_all x1, blocking collectives, local(): gram = lax.all_to_all(gram, axes, split_axis=0, concat_axis=0, tiled=True)  14.9 us
    all_to_all x2, starting transfers between devices, local(): lax.all_to_all(send, owner_axes, split_axis=0, concat_axis=0, tiled=True)  14.4 us
    unnamed x46, local copies, waits for them, and re-layouts  13 us
  transfers between devices with their start and end apart: 24, of which 11 were waited for; matrix products, arithmetic and copies ran while one was open for 3% of the time, Pallas kernels for 14%

profile of v3, /device:TPU:16, one launch (start us, length us, event | category | flops | bytes accessed | tf_op | source)
XLA Modules:
  0.0 529.4 jit_solution(9136875476672635969)
XLA Ops:
  1.8 1.6 collective-permute-start
  4.5 1.6 collective-permute-start.1
  8.5 1.9 collective-permute-start.3
  11.5 2.2 collective-permute-start.4
  13.9 1.9 take.30
  17.4 1.6 collective-permute-start.5
  19.0 2.0 take.33
  21.0 2.0 take.34
  22.9 2.0 take.35
  24.9 1.9 take.36
  26.8 2.0 take.31
  30.0 56.2 %collective-permute-done.2.refs_3_ = bf16[4,296,256]{2,1,0:T(8,128)(2,1)} collective-permute-done((bf16[4,296,256]{2,1,0:T(8,128)(2,1)S(1)}, bf16[4,296,256]{2,1,0:T(8,128)(2,1)}, u32[]{:S(2)}, u32[]{:S(2)}) %collective-permute-start.2) | collective-permute-done | bytes 606240 | tf_op jit(solution)/shard_map/ppermute | solution.py:374
  86.2 1.5 collective-permute-start.7
  87.7 13.0 %collective-permute-start.8 = (bf16[4,296,256]{2,1,0:T(8,128)(2,1)}, bf16[4,296,256]{2,1,0:T(8,128)(2,1)}, u32[]{:S(2)}, u32[]{:S(2)}) collective-permute-start(bf16[4,296,256]{2,1,0:T(8,128)(2,1)} %take.34), channel_id=1, source_target_pairs={{0,8},{4,12},{8,16},{12,20},{16,24},{20,28},{24,0},{28,4},{1,9},{5... | collective-permute-start | bytes 1818632 | tf_op jit(solution)/shard_map/ppermute | solution.py:374
  100.7 13.9 %collective-permute-start.9 = (bf16[4,296,256]{2,1,0:T(8,128)(2,1)}, bf16[4,296,256]{2,1,0:T(8,128)(2,1)}, u32[]{:S(2)}, u32[]{:S(2)}) collective-permute-start(bf16[4,296,256]{2,1,0:T(8,128)(2,1)} %take.35), channel_id=1, source_target_pairs={{0,12},{4,8},{8,20},{12,16},{16,28},{20,24},{24,4},{28,0},{1,13},{... | collective-permute-start | bytes 1818632 | tf_op jit(solution)/shard_map/ppermute | solution.py:374
  132.6 1.4 take.45
  137.5 1.5 copy.49
  139.1 9.5 %collective-permute-done.6.refs_7_ = bf16[4,296,256]{2,1,0:T(8,128)(2,1)} collective-permute-done((bf16[4,296,256]{2,1,0:T(8,128)(2,1)}, bf16[4,296,256]{2,1,0:T(8,128)(2,1)}, u32[]{:S(2)}, u32[]{:S(2)}) %collective-permute-start.6) | collective-permute-done | bytes 606240 | tf_op jit(solution)/shard_map/ppermute | solution.py:374
  148.7 2.5 collective-permute-start.12
  151.1 1.9 collective-permute-start.13
  153.6 21.1 %collective-permute-done.10.refs_4_ = bf16[4,296,256]{2,1,0:T(8,128)(2,1)} collective-permute-done((bf16[4,296,256]{2,1,0:T(8,128)(2,1)}, bf16[4,296,256]{2,1,0:T(8,128)(2,1)}, u32[]{:S(2)}, u32[]{:S(2)}) %collective-permute-start.10) | collective-permute-done | bytes 606240 | tf_op jit(solution)/shard_map/ppermute | solution.py:374
  174.7 29.9 %collective-permute-start.15 = (bf16[4,296,256]{2,1,0:T(8,128)(2,1)}, bf16[4,296,256]{2,1,0:T(8,128)(2,1)}, u32[]{:S(2)}, u32[]{:S(2)}) collective-permute-start(bf16[4,296,256]{2,1,0:T(8,128)(2,1)} %copy-done.6), channel_id=1, source_target_pairs={{0,8},{4,12},{8,16},{12,20},{16,24},{20,28},{24,0},{28,4},{1,9},{5... | collective-permute-start | bytes 1818632 | tf_op jit(solution)/shard_map/ppermute | solution.py:374
  204.6 3.7 multiply_bitcast_fusion
  208.3 5.7 %reshape.476.azimuth_ref = bf16[128,256]{1,0:T(8,128)(2,1)} reshape(bf16[2,8,2,4,16,2,2,4]{7,6,5,4,3,2,1,0:T(2,128)(2,1)} %multiply_bitcast_fusion) | data formatting | bytes 131072 | tf_op jit(solution)/shard_map/reshape | solution.py:386
  215.6 3.0 collective-permute-start.16
  218.6 34.1 %collective-permute-done.13.refs_7_ = bf16[4,296,256]{2,1,0:T(8,128)(2,1)} collective-permute-done((bf16[4,296,256]{2,1,0:T(8,128)(2,1)}, bf16[4,296,256]{2,1,0:T(8,128)(2,1)}, u32[]{:S(2)}, u32[]{:S(2)}) %collective-permute-start.13) | collective-permute-done | bytes 606240 | tf_op jit(solution)/shard_map/ppermute | solution.py:374
  252.7 2.4 collective-permute-start.19
  255.1 2.0 collective-permute-start.20
  260.1 15.1 %coeffs_and_gram.3 = (bf16[32,256,256]{2,1,0:T(8,128)(2,1)}, f32[32,16,128]{2,1,0:T(8,128)S(1)}) custom-call(s32[2]{0:T(128)S(1)} %pad_add_fusion.place_ref, bf16[2,2,256,168]{3,2,1,0:T(8,128)(2,1)S(1)} %copy.51.time_ref, bf16[128,256]{1,0:T(8,128)(2,1)S(1)} %copy-done.11, f32[1,256]{1,0:T(1,128)S(1)} %bitcast.77, ...), custom_call_target="tpu_custom_call" | custom-call | flops 3556769792 | bytes 9043968 | tf_op jit(solution)/shard_map/coeffs_and_gram/pallas_call | solution.py:145
  275.2 15.2 %coeffs_and_gram.4 = (bf16[32,256,256]{2,1,0:T(8,128)(2,1)}, f32[32,16,128]{2,1,0:T(8,128)S(1)}) custom-call(s32[2]{0:T(128)S(1)} %pad_add_fusion.place_ref, bf16[2,2,256,168]{3,2,1,0:T(8,128)(2,1)S(1)} %copy.51.time_ref, bf16[128,256]{1,0:T(8,128)(2,1)S(1)} %copy-done.11, f32[1,256]{1,0:T(1,128)S(1)} %bitcast.78, ...), custom_call_target="tpu_custom_call" | custom-call | flops 3556769792 | bytes 9043968 | tf_op jit(solution)/shard_map/coeffs_and_gram/pallas_call | solution.py:145
  291.6 13.0 %collective-permute-done.19.refs_6_ = bf16[4,296,256]{2,1,0:T(8,128)(2,1)S(1)} collective-permute-done((bf16[4,296,256]{2,1,0:T(8,128)(2,1)S(1)}, bf16[4,296,256]{2,1,0:T(8,128)(2,1)S(1)}, u32[]{:S(2)}, u32[]{:S(2)}) %collective-permute-start.19) | collective-permute-done | bytes 606240 | tf_op jit(solution)/shard_map/ppermute | solution.py:374
  304.6 12.9 %collective-permute-done.20.refs_7_ = bf16[4,296,256]{2,1,0:T(8,128)(2,1)S(1)} collective-permute-done((bf16[4,296,256]{2,1,0:T(8,128)(2,1)S(1)}, bf16[4,296,256]{2,1,0:T(8,128)(2,1)S(1)}, u32[]{:S(2)}, u32[]{:S(2)}) %collective-permute-start.20) | collective-permute-done | bytes 606240 | tf_op jit(solution)/shard_map/ppermute | solution.py:374
  317.5 14.6 %coeffs_and_gram.5 = (bf16[32,256,256]{2,1,0:T(8,128)(2,1)}, f32[32,16,128]{2,1,0:T(8,128)S(1)}) custom-call(s32[2]{0:T(128)S(1)} %pad_add_fusion.place_ref, bf16[2,2,256,168]{3,2,1,0:T(8,128)(2,1)S(1)} %copy.51.time_ref, bf16[128,256]{1,0:T(8,128)(2,1)S(1)} %copy-done.11, f32[1,256]{1,0:T(1,128)S(1)} %bitcast.79, ...), custom_call_target="tpu_custom_call" | custom-call | flops 3556769792 | bytes 9043968 | tf_op jit(solution)/shard_map/coeffs_and_gram/pallas_call | solution.py:145
  332.1 14.9 %all_to_all.20 = f32[32,1,16,128]{3,2,1,0:T(8,128)S(1)} all-to-all(f32[32,1,16,128]{3,2,1,0:T(8,128)S(1)} %bitcast.76), channel_id=1, replica_groups=mesh['sector'=4,'tm'=2,'space'=4] {'sector','tm','space'}, dimensions={0} | all-to-all | bytes 524288 | tf_op jit(solution)/shard_map/all_to_all | solution.py:418
  347.9 4.0 subspace.1
  355.2 4.9 all-to-all-start.1
  360.9 8.3 %all-to-all-done.1 = bf16[32,1,34,128]{3,2,1,0:T(8,128)(2,1)S(1)} async-done(((bf16[32,1,34,128]{3,2,1,0:T(8,128)(2,1)}), bf16[32,1,34,128]{3,2,1,0:T(8,128)(2,1)S(1)}, u32[]{:S(2)}, u32[]{:S(2)}) %all-to-all-start.1) | async-done | bytes 278560 | tf_op jit(solution)/shard_map/all_to_all | solution.py:439
  370.4 4.2 mix.5
  374.6 1.4 copy-done.1
  376.0 6.7 %all-to-all-start.3 = ((bf16[8,1,4,128,256]{4,3,2,1,0:T(8,128)(2,1)}), bf16[8,1,4,128,256]{4,3,2,1,0:T(8,128)(2,1)S(1)}, u32[]{:S(2)}, u32[]{:S(2)}) async-start(bf16[8,1,4,128,256]{4,3,2,1,0:T(8,128)(2,1)} %copy-done.1), calls=%async_computation.3 | async-start | bytes 4194304 | tf_op jit(solution)/shard_map/all_to_all | solution.py:461
  382.7 4.2 mix.3.refs_0_
  386.9 4.3 mix.4
  391.2 2.0 copy-done
  393.2 34.5 %all-to-all-done.3 = bf16[8,1,4,128,256]{4,3,2,1,0:T(8,128)(2,1)S(1)} async-done(((bf16[8,1,4,128,256]{4,3,2,1,0:T(8,128)(2,1)}), bf16[8,1,4,128,256]{4,3,2,1,0:T(8,128)(2,1)S(1)}, u32[]{:S(2)}, u32[]{:S(2)}) %all-to-all-start.3) | async-done | bytes 2097184 | tf_op jit(solution)/shard_map/all_to_all | solution.py:461
  427.6 7.7 %all-to-all-start.2 = ((bf16[8,2,4,128,256]{4,3,2,1,0:T(8,128)(2,1)}), bf16[8,2,4,128,256]{4,3,2,1,0:T(8,128)(2,1)}, u32[]{:S(2)}, u32[]{:S(2)}) async-start(bf16[8,2,4,128,256]{4,3,2,1,0:T(8,128)(2,1)} %copy-done), calls=%async_computation.2 | async-start | bytes 8388608 | tf_op jit(solution)/shard_map/all_to_all | solution.py:461
  436.2 2.0 unpack.2.refs_0_
  438.1 86.5 %all-to-all-done.2 = bf16[8,2,4,128,256]{4,3,2,1,0:T(8,128)(2,1)} async-done(((bf16[8,2,4,128,256]{4,3,2,1,0:T(8,128)(2,1)}), bf16[8,2,4,128,256]{4,3,2,1,0:T(8,128)(2,1)}, u32[]{:S(2)}, u32[]{:S(2)}) %all-to-all-start.2) | async-done | bytes 4194336 | tf_op jit(solution)/shard_map/all_to_all | solution.py:461
  524.6 4.8 unpack.3
  (136 shorter events, 43.2 us)
Async XLA Ops:
  1.8 15.6 %collective-permute-start = (bf16[4,296,256]{2,1,0:T(8,128)(2,1)S(1)}, bf16[4,296,256]{2,1,0:T(8,128)(2,1)}, u32[]{:S(2)}, u32[]{:S(2)}) collective-permute-start(bf16[4,296,256]{2,1,0:T(8,128)(2,1)S(1)} %take.25), channel_id=1, source_target_pairs={{0,4},{4,0},{8,12},{12,8},{16,20},{20,16},{24,28},{28,24},{1,5},{5... | collective-permute-start | bytes 1818632 | tf_op jit(solution)/shard_map/ppermute | solution.py:374
  4.5 25.0 %collective-permute-start.1 = (bf16[4,296,256]{2,1,0:T(8,128)(2,1)S(1)}, bf16[4,296,256]{2,1,0:T(8,128)(2,1)}, u32[]{:S(2)}, u32[]{:S(2)}) collective-permute-start(bf16[4,296,256]{2,1,0:T(8,128)(2,1)S(1)} %take.26), channel_id=1, source_target_pairs={{0,8},{4,12},{8,16},{12,20},{16,24},{20,28},{24,0},{28,4},{1,9},{5... | collective-permute-start | bytes 1818632 | tf_op jit(solution)/shard_map/ppermute | solution.py:374
  7.2 78.9 %collective-permute-start.2 = (bf16[4,296,256]{2,1,0:T(8,128)(2,1)S(1)}, bf16[4,296,256]{2,1,0:T(8,128)(2,1)}, u32[]{:S(2)}, u32[]{:S(2)}) collective-permute-start(bf16[4,296,256]{2,1,0:T(8,128)(2,1)S(1)} %take.27), channel_id=1, source_target_pairs={{0,12},{4,8},{8,20},{12,16},{16,28},{20,24},{24,4},{28,0},{1,13},{... | collective-permute-start | bytes 1818632 | tf_op jit(solution)/shard_map/ppermute | solution.py:374
  8.5 79.2 %collective-permute-start.3 = (bf16[4,296,256]{2,1,0:T(8,128)(2,1)S(1)}, bf16[4,296,256]{2,1,0:T(8,128)(2,1)}, u32[]{:S(2)}, u32[]{:S(2)}) collective-permute-start(bf16[4,296,256]{2,1,0:T(8,128)(2,1)S(1)} %take.28), channel_id=1, source_target_pairs={{0,16},{4,20},{8,24},{12,28},{16,0},{20,4},{24,8},{28,12},{1,17},{... | collective-permute-start | bytes 1818632 | tf_op jit(solution)/shard_map/ppermute | solution.py:374
  10.4 3.4 copy-start.21
  11.5 89.1 %collective-permute-start.4 = (bf16[4,296,256]{2,1,0:T(8,128)(2,1)S(1)}, bf16[4,296,256]{2,1,0:T(8,128)(2,1)}, u32[]{:S(2)}, u32[]{:S(2)}) collective-permute-start(bf16[4,296,256]{2,1,0:T(8,128)(2,1)S(1)} %take.29), channel_id=1, source_target_pairs={{0,20},{4,16},{8,28},{12,24},{16,4},{20,0},{24,12},{28,8},{1,21},{... | collective-permute-start | bytes 1818632 | tf_op jit(solution)/shard_map/ppermute | solution.py:374
  17.4 97.2 %collective-permute-start.5 = (bf16[4,296,256]{2,1,0:T(8,128)(2,1)}, bf16[4,296,256]{2,1,0:T(8,128)(2,1)S(1)}, u32[]{:S(2)}, u32[]{:S(2)}) collective-permute-start(bf16[4,296,256]{2,1,0:T(8,128)(2,1)} %take.30), channel_id=1, source_target_pairs={{0,24},{4,28},{8,0},{12,4},{16,8},{20,12},{24,16},{28,20},{1,25},{... | collective-permute-start | bytes 1818632 | tf_op jit(solution)/shard_map/ppermute | solution.py:374
  26.8 2.2 copy-start.15
  26.8 87.8 %copy-start.18 = (f32[8,16,1]{1,0,2:T(8,128)S(1)}, f32[8,16,1]{1,0,2:T(8,128)}, u32[]{:S(2)}) copy-start(f32[8,16,1]{1,0,2:T(8,128)} %get-tuple-element.33) | copy-start | bytes 1540
  26.8 87.8 %copy-start.19 = (f32[8,16,1]{1,0,2:T(8,128)S(1)}, f32[8,16,1]{1,0,2:T(8,128)}, u32[]{:S(2)}) copy-start(f32[8,16,1]{1,0,2:T(8,128)} %get-tuple-element.34) | copy-start | bytes 1540
  26.8 87.8 %copy-start.20 = (f32[8,16,1]{1,0,2:T(8,128)S(1)}, f32[8,16,1]{1,0,2:T(8,128)}, u32[]{:S(2)}) copy-start(f32[8,16,1]{1,0,2:T(8,128)} %get-tuple-element.35) | copy-start | bytes 1540
  29.5 119.1 %collective-permute-start.6 = (bf16[4,296,256]{2,1,0:T(8,128)(2,1)}, bf16[4,296,256]{2,1,0:T(8,128)(2,1)}, u32[]{:S(2)}, u32[]{:S(2)}) collective-permute-start(bf16[4,296,256]{2,1,0:T(8,128)(2,1)} %take.31), channel_id=1, source_target_pairs={{0,28},{4,24},{8,4},{12,0},{16,12},{20,8},{24,20},{28,16},{1,29},{... | collective-permute-start | bytes 1818632 | tf_op jit(solution)/shard_map/ppermute | solution.py:374
  86.2 62.5 %collective-permute-start.7 = (bf16[4,296,256]{2,1,0:T(8,128)(2,1)}, bf16[4,296,256]{2,1,0:T(8,128)(2,1)}, u32[]{:S(2)}, u32[]{:S(2)}) collective-permute-start(bf16[4,296,256]{2,1,0:T(8,128)(2,1)} %take.33), channel_id=1, source_target_pairs={{0,4},{4,0},{8,12},{12,8},{16,20},{20,16},{24,28},{28,24},{1,5},{5... | collective-permute-start | bytes 1818632 | tf_op jit(solution)/shard_map/ppermute | solution.py:374
  87.7 63.4 %collective-permute-start.8 = (bf16[4,296,256]{2,1,0:T(8,128)(2,1)}, bf16[4,296,256]{2,1,0:T(8,128)(2,1)}, u32[]{:S(2)}, u32[]{:S(2)}) collective-permute-start(bf16[4,296,256]{2,1,0:T(8,128)(2,1)} %take.34), channel_id=1, source_target_pairs={{0,8},{4,12},{8,16},{12,20},{16,24},{20,28},{24,0},{28,4},{1,9},{5... | collective-permute-start | bytes 1818632 | tf_op jit(solution)/shard_map/ppermute | solution.py:374
  100.7 52.4 %collective-permute-start.9 = (bf16[4,296,256]{2,1,0:T(8,128)(2,1)}, bf16[4,296,256]{2,1,0:T(8,128)(2,1)}, u32[]{:S(2)}, u32[]{:S(2)}) collective-permute-start(bf16[4,296,256]{2,1,0:T(8,128)(2,1)} %take.35), channel_id=1, source_target_pairs={{0,12},{4,8},{8,20},{12,16},{16,28},{20,24},{24,4},{28,0},{1,13},{... | collective-permute-start | bytes 1818632 | tf_op jit(solution)/shard_map/ppermute | solution.py:374
  114.6 1.8 copy-start.13
  114.6 60.1 %collective-permute-start.10 = (bf16[4,296,256]{2,1,0:T(8,128)(2,1)}, bf16[4,296,256]{2,1,0:T(8,128)(2,1)}, u32[]{:S(2)}, u32[]{:S(2)}) collective-permute-start(bf16[4,296,256]{2,1,0:T(8,128)(2,1)} %take.36), channel_id=1, source_target_pairs={{0,16},{4,20},{8,24},{12,28},{16,0},{20,4},{24,8},{28,12},{1,17},{... | collective-permute-start | bytes 1818632 | tf_op jit(solution)/shard_map/ppermute | solution.py:374
  116.4 0.8 copy-start.4
  119.6 0.9 copy-start.10
  121.6 0.8 copy-start.9
  123.5 0.8 copy-start.8
  126.6 0.8 copy-start.7
  128.6 0.8 copy-start.6
  130.6 0.9 copy-start.3
  132.6 1.4 copy-start.2
  135.1 1.8 copy-start.16
  135.1 1.8 copy-start.17
  148.6 66.9 %collective-permute-start.11 = (bf16[4,296,256]{2,1,0:T(8,128)(2,1)}, bf16[4,296,256]{2,1,0:T(8,128)(2,1)}, u32[]{:S(2)}, u32[]{:S(2)}) collective-permute-start(bf16[4,296,256]{2,1,0:T(8,128)(2,1)} %copy-done.10), channel_id=1, source_target_pairs={{0,20},{4,16},{8,28},{12,24},{16,4},{20,0},{24,12},{28,8},{1,21},{... | collective-permute-start | bytes 1818632 | tf_op jit(solution)/shard_map/ppermute | solution.py:374
  148.7 69.9 %collective-permute-start.12 = (bf16[4,296,256]{2,1,0:T(8,128)(2,1)}, bf16[4,296,256]{2,1,0:T(8,128)(2,1)}, u32[]{:S(2)}, u32[]{:S(2)}) collective-permute-start(bf16[4,296,256]{2,1,0:T(8,128)(2,1)} %copy-done.9), channel_id=1, source_target_pairs={{0,24},{4,28},{8,0},{12,4},{16,8},{20,12},{24,16},{28,20},{1,25},{... | collective-permute-start | bytes 1818632 | tf_op jit(solution)/shard_map/ppermute | solution.py:374
  151.1 101.5 %collective-permute-start.13 = (bf16[4,296,256]{2,1,0:T(8,128)(2,1)}, bf16[4,296,256]{2,1,0:T(8,128)(2,1)}, u32[]{:S(2)}, u32[]{:S(2)}) collective-permute-start(bf16[4,296,256]{2,1,0:T(8,128)(2,1)} %copy-done.8), channel_id=1, source_target_pairs={{0,28},{4,24},{8,4},{12,0},{16,12},{20,8},{24,20},{28,16},{1,29},{... | collective-permute-start | bytes 1818632 | tf_op jit(solution)/shard_map/ppermute | solution.py:374
  153.0 99.6 %collective-permute-start.14 = (bf16[4,296,256]{2,1,0:T(8,128)(2,1)}, bf16[4,296,256]{2,1,0:T(8,128)(2,1)}, u32[]{:S(2)}, u32[]{:S(2)}) collective-permute-start(bf16[4,296,256]{2,1,0:T(8,128)(2,1)} %copy-done.7), channel_id=1, source_target_pairs={{0,4},{4,0},{8,12},{12,8},{16,20},{20,16},{24,28},{28,24},{1,5},{5... | collective-permute-start | bytes 1818632 | tf_op jit(solution)/shard_map/ppermute | solution.py:374
  174.7 80.4 %collective-permute-start.15 = (bf16[4,296,256]{2,1,0:T(8,128)(2,1)}, bf16[4,296,256]{2,1,0:T(8,128)(2,1)}, u32[]{:S(2)}, u32[]{:S(2)}) collective-permute-start(bf16[4,296,256]{2,1,0:T(8,128)(2,1)} %copy-done.6), channel_id=1, source_target_pairs={{0,8},{4,12},{8,16},{12,20},{16,24},{20,28},{24,0},{28,4},{1,9},{5... | collective-permute-start | bytes 1818632 | tf_op jit(solution)/shard_map/ppermute | solution.py:374
  215.6 101.9 %copy-start.12 = (f32[256]{0:T(256)}, f32[256]{0:T(256)S(1)}, u32[]{:S(2)}) copy-start(f32[256]{0:T(256)S(1)} %select_reduce_fusion) | copy-start | bytes 3076
  215.6 74.8 %collective-permute-start.16 = (bf16[4,296,256]{2,1,0:T(8,128)(2,1)}, bf16[4,296,256]{2,1,0:T(8,128)(2,1)S(1)}, u32[]{:S(2)}, u32[]{:S(2)}) collective-permute-start(bf16[4,296,256]{2,1,0:T(8,128)(2,1)} %copy-done.3), channel_id=1, source_target_pairs={{0,12},{4,8},{8,20},{12,16},{16,28},{20,24},{24,4},{28,0},{1,13},{... | collective-permute-start | bytes 1818632 | tf_op jit(solution)/shard_map/ppermute | solution.py:374
  218.6 71.8 %collective-permute-start.17 = (bf16[4,296,256]{2,1,0:T(8,128)(2,1)}, bf16[4,296,256]{2,1,0:T(8,128)(2,1)S(1)}, u32[]{:S(2)}, u32[]{:S(2)}) collective-permute-start(bf16[4,296,256]{2,1,0:T(8,128)(2,1)} %copy-done.2), channel_id=1, source_target_pairs={{0,16},{4,20},{8,24},{12,28},{16,0},{20,4},{24,8},{28,12},{1,17},{... | collective-permute-start | bytes 1818632 | tf_op jit(solution)/shard_map/ppermute | solution.py:374
  252.7 39.0 %collective-permute-start.18 = (bf16[4,296,256]{2,1,0:T(8,128)(2,1)S(1)}, bf16[4,296,256]{2,1,0:T(8,128)(2,1)S(1)}, u32[]{:S(2)}, u32[]{:S(2)}) collective-permute-start(bf16[4,296,256]{2,1,0:T(8,128)(2,1)S(1)} %take.45), channel_id=1, source_target_pairs={{0,20},{4,16},{8,28},{12,24},{16,4},{20,0},{24,12},{28,8},{1,21},{... | collective-permute-start | bytes 1818632 | tf_op jit(solution)/shard_map/ppermute | solution.py:374
  252.7 51.9 %collective-permute-start.19 = (bf16[4,296,256]{2,1,0:T(8,128)(2,1)S(1)}, bf16[4,296,256]{2,1,0:T(8,128)(2,1)S(1)}, u32[]{:S(2)}, u32[]{:S(2)}) collective-permute-start(bf16[4,296,256]{2,1,0:T(8,128)(2,1)S(1)} %take.46), channel_id=1, source_target_pairs={{0,24},{4,28},{8,0},{12,4},{16,8},{20,12},{24,16},{28,20},{1,25},{... | collective-permute-start | bytes 1818632 | tf_op jit(solution)/shard_map/ppermute | solution.py:374
  255.1 62.4 %collective-permute-start.20 = (bf16[4,296,256]{2,1,0:T(8,128)(2,1)S(1)}, bf16[4,296,256]{2,1,0:T(8,128)(2,1)S(1)}, u32[]{:S(2)}, u32[]{:S(2)}) collective-permute-start(bf16[4,296,256]{2,1,0:T(8,128)(2,1)S(1)} %take.47), channel_id=1, source_target_pairs={{0,28},{4,24},{8,4},{12,0},{16,12},{20,8},{24,20},{28,16},{1,29},{... | collective-permute-start | bytes 1818632 | tf_op jit(solution)/shard_map/ppermute | solution.py:374
  257.1 1.1 copy-start.5
  258.1 0.8 copy-start.11
  259.0 1.1 copy-start.14
  355.2 14.1 %all-to-all-start.1 = ((bf16[32,1,34,128]{3,2,1,0:T(8,128)(2,1)}), bf16[32,1,34,128]{3,2,1,0:T(8,128)(2,1)S(1)}, u32[]{:S(2)}, u32[]{:S(2)}) async-start(bf16[32,1,34,128]{3,2,1,0:T(8,128)(2,1)} %broadcast_in_dim.56), calls=%async_computation.1 | async-start | bytes 655360 | tf_op jit(solution)/shard_map/all_to_all | solution.py:439
  374.6 1.4 copy-start.1
  376.0 51.6 %all-to-all-start.3 = ((bf16[8,1,4,128,256]{4,3,2,1,0:T(8,128)(2,1)}), bf16[8,1,4,128,256]{4,3,2,1,0:T(8,128)(2,1)S(1)}, u32[]{:S(2)}, u32[]{:S(2)}) async-start(bf16[8,1,4,128,256]{4,3,2,1,0:T(8,128)(2,1)} %copy-done.1), calls=%async_computation.3 | async-start | bytes 4194304 | tf_op jit(solution)/shard_map/all_to_all | solution.py:461
  391.2 2.0 copy-start
  427.6 97.0 %all-to-all-start.2 = ((bf16[8,2,4,128,256]{4,3,2,1,0:T(8,128)(2,1)}), bf16[8,2,4,128,256]{4,3,2,1,0:T(8,128)(2,1)}, u32[]{:S(2)}, u32[]{:S(2)}) async-start(bf16[8,2,4,128,256]{4,3,2,1,0:T(8,128)(2,1)} %copy-done), calls=%async_computation.2 | async-start | bytes 8388608 | tf_op jit(solution)/shard_map/all_to_all | solution.py:461

commit v4 on v3

--- a/solution.py
+++ b/solution.py
@@ -230,114 +230,117 @@
     )(packed)
 
 
-def mix_kernel(orders, own_freqs, coeff_ref, mixing_ref, spread_ref, factor_ref, root_ref, *refs):
-    out_ref = refs[-1]
+def mix_kernel(orders, parts, owner_ref, mixing_ref, spread_ref, factor_ref, root_ref, *refs):
+    coeff_refs, out_ref = refs[:-1], refs[-1]
     freqs, rows, _ = mixing_ref.shape
     total = spread_ref.shape[1]
     blocks = total // (2 * orders)
     row = lax.broadcasted_iota(jnp.int32, (rows, total), 0) // (rows // orders)
     column = lax.broadcasted_iota(jnp.int32, (rows, total), 1) // blocks % orders
-    factor = jnp.transpose(factor_ref[...])
+    factor = jnp.transpose(factor_ref[0])
     for n in range(freqs):
         wide = jnp.dot(mixing_ref[n], spread_ref[...], preferred_element_type=jnp.float32)
         wide = jnp.where(row == column, wide, 0.0).astype(jnp.bfloat16)
-        fields = jnp.dot(wide, coeff_ref[n], preferred_element_type=jnp.float32)
-        scaled = fields * (factor[:, n:n + 1] * root_ref[...])
-        out_ref[n // own_freqs, 0, n % own_freqs] = scaled.astype(jnp.bfloat16)
-
-
-def mix(coeffs, mixing, spread, factor, root_weight, owners, orders, at, count, whole):
-    _, rows, columns = coeffs.shape
+        for (k, low, high), coeff_ref in zip(parts, coeff_refs):
+            fields = jnp.dot(wide, coeff_ref[n], preferred_element_type=jnp.float32)
+            scaled = fields * (factor[:, n:n + 1] * root_ref[:, low:high])
+            out_ref[k, n, :, low:high] = scaled.astype(jnp.bfloat16)
+
+
+def mix(owner, coeffs, parts, mixing, spread, factor, root_weight, owners, orders, fields):
+    rows = coeffs[0].shape[1]
     out_rows, depth = mixing.shape[1:]
-    own_freqs = NFREQ // owners
-    steps = 4
-    freqs = NFREQ // steps
-    inputs = [coeffs, mixing, spread, factor, root_weight] + ([] if whole is None else [whole])
-    in_specs = [
-        pl.BlockSpec((freqs, rows, columns), lambda i: (i, 0, 0)),
-        pl.BlockSpec((freqs, out_rows, depth), lambda i: (i, 0, 0)),
-        pl.BlockSpec(spread.shape, lambda i: (0, 0)),
-        pl.BlockSpec((freqs, out_rows), lambda i: (i, 0)),
-        pl.BlockSpec(root_weight.shape, lambda i: (0, 0)),
-        pl.BlockSpec(memory_space=pl.ANY),
-    ]
+    columns = root_weight.shape[1]
+    freqs = NFREQ // owners
     return pl.pallas_call(
-        functools.partial(mix_kernel, orders, own_freqs),
-        grid=(steps,),
-        in_specs=in_specs[:len(inputs)],
-        out_specs=pl.BlockSpec(
-            (owners // steps, 1, own_freqs, out_rows, columns), lambda i: (i, at, 0, 0, 0)
-        ),
-        out_shape=jax.ShapeDtypeStruct((owners, count, own_freqs, out_rows, columns), jnp.bfloat16),
-        input_output_aliases={} if whole is None else {5: 0},
+        functools.partial(mix_kernel, orders, parts),
+        grid_spec=pltpu.PrefetchScalarGridSpec(
+            num_scalar_prefetch=1,
+            grid=(1,),
+            in_specs=[
+                pl.BlockSpec((freqs, out_rows, depth), lambda i, at: (at[0], 0, 0)),
+                pl.BlockSpec(spread.shape, lambda i, at: (0, 0)),
+                pl.BlockSpec((1, freqs, out_rows), lambda i, at: (at[0], 0, 0)),
+                pl.BlockSpec(root_weight.shape, lambda i, at: (0, 0)),
+            ] + [
+                pl.BlockSpec((freqs, rows, x.shape[2]), lambda i, at: (at[0], 0, 0)) for x in coeffs
+            ],
+            out_specs=pl.BlockSpec((fields, freqs, out_rows, columns), lambda i, at: (0, 0, 0, 0)),
+        ),
+        out_shape=jax.ShapeDtypeStruct((fields, freqs, out_rows, columns), jnp.bfloat16),
         compiler_params=pltpu.CompilerParams(vmem_limit_bytes=VMEM_LIMIT),
         cost_estimate=pl.CostEstimate(
-            flops=2 * NFREQ * out_rows * rows * columns,
-            bytes_accessed=2 * NFREQ * (rows + out_rows) * columns,
+            flops=2 * freqs * out_rows * rows * fields * columns,
+            bytes_accessed=2 * freqs * (rows + out_rows) * fields * columns,
             transcendentals=0,
         ),
         name="mix",
-    )(*inputs)
+    )(jnp.reshape(owner, (1,)), mixing, spread, factor, root_weight, *coeffs)
 
 
 def take_kernel(place_ref, record_ref, out_ref):
     out_ref[...] = record_ref[:, 0]
 
 
-def take(by_field, k, owner, owners):
+def take(by_field, owner, owners, part):
     sec_local, _, rec_len, cells = by_field.shape
-    part = cells // owners
-    if part % LANES:
-        return lax.dynamic_slice_in_dim(by_field[:, k], owner * part, part, 2)
+    k, low, high = part
+    count = high - low
+    own = cells // owners
+    if count % LANES:
+        return lax.dynamic_slice_in_dim(by_field[:, k], owner * own + low, count, 2)
     return pl.pallas_call(
         take_kernel,
         grid_spec=pltpu.PrefetchScalarGridSpec(
             num_scalar_prefetch=1,
             grid=(1,),
             in_specs=[
-                pl.BlockSpec((sec_local, 1, rec_len, part), lambda i, at: (0, k, 0, at[0]))
+                pl.BlockSpec((sec_local, 1, rec_len, count), lambda i, at: (0, k, 0, at[0]))
             ],
-            out_specs=pl.BlockSpec((sec_local, rec_len, part), lambda i, at: (0, 0, 0)),
-        ),
-        out_shape=jax.ShapeDtypeStruct((sec_local, rec_len, part), by_field.dtype),
+            out_specs=pl.BlockSpec((sec_local, rec_len, count), lambda i, at: (0, 0, 0)),
+        ),
+        out_shape=jax.ShapeDtypeStruct((sec_local, rec_len, count), by_field.dtype),
         compiler_params=pltpu.CompilerParams(vmem_limit_bytes=VMEM_LIMIT),
         cost_estimate=pl.CostEstimate(
-            flops=0, bytes_accessed=4 * sec_local * rec_len * part, transcendentals=0
+            flops=0, bytes_accessed=4 * sec_local * rec_len * count, transcendentals=0
         ),
         name="take",
-    )(jnp.reshape(owner, (1,)), by_field)
-
-
-def unpack_kernel(piece_ref, *refs):
+    )(jnp.reshape(owner * (own // count) + low // count, (1,)), by_field)
+
+
+def unpack_kernel(owner_ref, piece_ref, *refs):
     out_ref = refs[-1]
-    owners, count, part = piece_ref.shape[0], piece_ref.shape[1], piece_ref.shape[-1]
-    for k in range(count):
-        for d in range(owners):
-            out_ref[:, 0, :, k, :, d * part:(d + 1) * part] = piece_ref[d, k, 0]
-
-
-def unpack(pieces, first, fields, whole):
-    owners, count, freqs, orders, two, modes, part = pieces.shape
+    for k in range(piece_ref.shape[0]):
+        for f in range(piece_ref.shape[1]):
+            out_ref[:, f, :, k] = piece_ref[k, f]
+
+
+def unpack(owner, piece, owners, whole):
+    fields, freqs, orders, two, modes, part = piece.shape
     shape = (orders, freqs, two, fields, modes, owners * part)
-    inputs = [pieces] if whole is None else [pieces, whole]
+    if part % LANES:
+        whole = jnp.zeros(shape, piece.dtype) if whole is None else whole
+        piece = jnp.transpose(piece, (2, 1, 3, 0, 4, 5))
+        return lax.dynamic_update_slice_in_dim(whole, piece, owner * part, 5)
+    inputs = [piece] if whole is None else [piece, whole]
     in_specs = [
-        pl.BlockSpec((owners, count, 1, orders, two, modes, part), lambda i: (0, 0, i, 0, 0, 0, 0)),
+        pl.BlockSpec(piece.shape, lambda i, at: (0, 0, 0, 0, 0, 0)),
         pl.BlockSpec(memory_space=pl.ANY),
     ]
     return pl.pallas_call(
         unpack_kernel,
-        grid=(freqs,),
-        in_specs=in_specs[:len(inputs)],
-        out_specs=pl.BlockSpec(
-            (orders, 1, two, count, modes, owners * part),
-            lambda i: (0, i, 0, first // count, 0, 0),
-        ),
-        out_shape=jax.ShapeDtypeStruct(shape, pieces.dtype),
-        input_output_aliases={} if whole is None else {1: 0},
+        grid_spec=pltpu.PrefetchScalarGridSpec(
+            num_scalar_prefetch=1,
+            grid=(1,),
+            in_specs=in_specs[:len(inputs)],
+            out_specs=pl.BlockSpec(shape[:5] + (part,), lambda i, at: (0, 0, 0, 0, 0, at[0])),
+        ),
+        out_shape=jax.ShapeDtypeStruct(shape, piece.dtype),
+        input_output_aliases={} if whole is None else {2: 0},
         compiler_params=pltpu.CompilerParams(vmem_limit_bytes=VMEM_LIMIT),
-        cost_estimate=pl.CostEstimate(flops=0, bytes_accessed=4 * pieces.size, transcendentals=0),
+        cost_estimate=pl.CostEstimate(flops=0, bytes_accessed=4 * piece.size, transcendentals=0),
         name="unpack",
-    )(*inputs)
+    )(jnp.reshape(owner, (1,)), *inputs)
 
 
 def local(records, block_start, slab_index, weight_table):
@@ -359,20 +362,26 @@
     sec_at, tm_at = lax.axis_index("sector"), lax.axis_index("tm")
     shifts = [(z, x) for z in range(sec_count) for x in range(tm_count)]
     in_order = sorted(shifts, key=lambda r: (r[0] == 0, abs(2 * r[0] - sec_count), r))
+
+    def owner_after(z, x):
+        return (sec_at + z) % sec_count * tm_count + (tm_at + x) % tm_count
+
+    def send(piece, z, x):
+        if (z, x) == (0, 0):
+            return piece
+        hops = [
+            (a * tm_count + j, (a + z) % sec_count * tm_count + (j + x) % tm_count)
+            for a in range(sec_count)
+            for j in range(tm_count)
+        ]
+        return lax.ppermute(piece, owner_axes, hops)
+
+    parts = [(k, 0, part) for k in range(fields)]
+    if part % (2 * LANES) == 0:
+        parts[-1:] = [(fields - 1, 0, part // 2), (fields - 1, part // 2, part)]
     arrived = []
-    for k in range(fields):
-        got = {}
-        for z, x in in_order:
-            owner = (sec_at + z) % sec_count * tm_count + (tm_at + x) % tm_count
-            piece = take(by_field, k, owner, owners)
-            if (z, x) != (0, 0):
-                hops = [
-                    (a * tm_count + j, (a + z) % sec_count * tm_count + (j + x) % tm_count)
-                    for a in range(sec_count)
-                    for j in range(tm_count)
-                ]
-                piece = lax.ppermute(piece, owner_axes, hops)
-            got[z, x] = piece
+    for own_part in parts:
+        got = {r: send(take(by_field, owner_after(*r), owners, own_part), *r) for r in in_order}
         arrived.append([got[r] for r in shifts])
 
     time_basis = placed_time_basis(block_start, tm_count)
@@ -401,9 +410,9 @@
 
     gram = jnp.zeros((NFREQ, blocks, orders * blocks), jnp.float32)
     coeffs = []
-    for k in range(fields):
+    for pieces, (_, low, high) in zip(arrived, parts):
         own, gram = coeffs_and_gram(
-            jnp.stack([sec_at, tm_at]), arrived[k], sec_count, time_basis, azimuth, weight, gram
+            jnp.stack([sec_at, tm_at]), pieces, sec_count, time_basis, azimuth, weight[:, low:high], gram
         )
         coeffs.append(own)
 
@@ -445,22 +454,22 @@
     energy = energy.reshape(NFREQ, orders, MODES)
     factor = jnp.broadcast_to(
         lax.rsqrt(energy)[:, :, None, :], (NFREQ, orders, 2, MODES)
-    ).reshape(NFREQ, orders * 2 * MODES)
+    ).reshape(owners, own_freqs, orders * 2 * MODES)
     root_weight = jnp.sqrt(weight)
     spread = jnp.broadcast_to(
         jnp.eye(depth, dtype=jnp.bfloat16).reshape(depth, 2, 1, blocks), (depth, 2, orders, blocks)
     ).reshape(depth, depth * orders)
 
     mode_fields = None
-    for first, count in ((fields - 1, 1), (0, fields - 1)):
-        send = None
-        for n in range(count):
-            send = mix(
-                coeffs[first + n], mixing, spread, factor, root_weight, owners, orders, n, count, send
-            )
-        got = lax.all_to_all(send, owner_axes, split_axis=0, concat_axis=0, tiled=True)
-        got = got.reshape(owners, count, own_freqs, orders, 2, MODES, part)
-        mode_fields = unpack(got, first, fields, mode_fields)
+    arrived = []
+    for z, x in in_order:
+        piece = mix(
+            owner_after(z, x), coeffs, parts, mixing, spread, factor, root_weight, owners, orders, fields
+        )
+        arrived.append((owner_after(-z, -x), send(piece, z, x)))
+    for owner, piece in arrived:
+        piece = piece.reshape(fields, own_freqs, orders, 2, MODES, part)
+        mode_fields = unpack(owner, piece, owners, mode_fields)
     mode_fields = jnp.transpose(mode_fields, (0, 1, 2, 4, 3, 5))
     own_energy = lax.dynamic_slice_in_dim(energy, me * own_freqs, own_freqs)
     return (mode_fields, jnp.transpose(own_energy, (1, 0, 2)))

time: 536 us -> 534 us (level)
  waiting for transfers between devices: 278 us -> 179 us
  starting transfers between devices: 99.4 us -> 156 us
  Pallas kernels: 101 us -> 132 us
  local copies, waits for them, and re-layouts: 26.4 us -> 41.9 us
    all_to_all x2 -> x0, waiting for transfers between devices: 121 us -> none  [local(): lax.all_to_all(send, owner_axes, split_axis=0, concat_axis=0, tiled=True)]
    ppermute x21 -> x35, starting transfers between devices: 80.1 us -> 152 us  [send(): return lax.ppermute(piece, owner_axes, hops)]
    ppermute x21 -> x35, waiting for transfers between devices: 148 us -> 170 us  [send(): return lax.ppermute(piece, owner_axes, hops)]
    unnamed x46 -> x120, local copies, waits for them, and re-layouts: 13 us -> 29.2 us
    pallas_call x5 -> x16, Pallas kernels: 19.5 us -> 35.1 us  [the longest x8 22 us: mix(): pl.pallas_call(functools.partial(mix_kernel, orders, parts), grid_spec=pl...]
    all_to_all x2 -> x0, starting transfers between devices: 14.4 us -> none  [local(): lax.all_to_all(send, owner_axes, split_axis=0, concat_axis=0, tiled=True)]
    pallas_call x3 -> x4, Pallas kernels: 45 us -> 54.8 us  [coeffs_and_gram(): pl.pallas_call(functools.partial(coeff_kernel, sec_count, sec_local, freq...]
    pallas_call x24 -> x32, Pallas kernels: 32.4 us -> 38.3 us  [take(): pl.pallas_call(take_kernel, grid_spec=pltpu.PrefetchScalarGridSpec(num_sc...]
  transfers between devices with their start and end apart: 24 -> 36, of which waited for: 11 -> 9; matrix products, arithmetic and copies ran while one was open for 3% -> 3% of each run, Pallas kernels for 14% -> 21%
where the time goes in v4:
time: 534 us; the launch traced here: 531 us
  waiting for transfers between devices  179 us (34%)
  starting transfers between devices  156 us (29%)
  Pallas kernels  132 us (25%)
  local copies, waits for them, and re-layouts  41.9 us (8%)
  blocking collectives  13.4 us (3%)
  other arithmetic  5.87 us (1%)
    ppermute x35, waiting for transfers between devices, send(): return lax.ppermute(piece, owner_axes, hops)  170 us
    ppermute x35, starting transfers between devices, send(): return lax.ppermute(piece, owner_axes, hops)  152 us
    pallas_call x4, Pallas kernels, coeffs_and_gram(): pl.pallas_call(functools.partial(coeff_kernel, sec_count, sec_local, freq...  54.8 us
    pallas_call x32, Pallas kernels, take(): pl.pallas_call(take_kernel, grid_spec=pltpu.PrefetchScalarGridSpec(num_sc...  38.3 us
    unnamed x120, local copies, waits for them, and re-layouts  29.2 us
    pallas_call x8, Pallas kernels, mix(): pl.pallas_call(functools.partial(mix_kernel, orders, parts), grid_spec=pl...  22 us
    all_to_all x1, blocking collectives, local(): gram = lax.all_to_all(gram, axes, split_axis=0, concat_axis=0, tiled=True)  13.4 us
    pallas_call x8, Pallas kernels, unpack(): pl.pallas_call(unpack_kernel, grid_spec=pltpu.PrefetchScalarGridSpec(num_...  13.1 us
  transfers between devices with their start and end apart: 36, of which 9 were waited for; matrix products, arithmetic and copies ran while one was open for 3% of the time, Pallas kernels for 21%

profile of v4, /device:TPU:16, one launch (start us, length us, event | category | flops | bytes accessed | tf_op | source)
XLA Modules:
  0.0 531.3 jit_solution(12442678975160143691)
XLA Ops:
  8.0 1.9 collective-permute-start.17
  10.9 2.2 collective-permute-start.18
  16.4 2.0 take.36
  18.4 2.0 take.35
  20.3 2.0 take.34
  22.3 1.9 take.33
  26.8 20.1 %collective-permute-done.16.refs_3_ = bf16[4,296,128]{2,1,0:T(8,128)(2,1)S(1)} collective-permute-done((bf16[4,296,128]{2,1,0:T(8,128)(2,1)S(1)}, bf16[4,296,128]{2,1,0:T(8,128)(2,1)S(1)}, u32[]{:S(2)}, u32[]{:S(2)}) %collective-permute-start.16) | collective-permute-done | bytes 303136 | tf_op jit(solution)/shard_map/ppermute | solution.py:377
  48.9 11.7 %collective-permute-start.1 = (bf16[4,296,256]{2,1,0:T(8,128)(2,1)}, bf16[4,296,256]{2,1,0:T(8,128)(2,1)}, u32[]{:S(2)}, u32[]{:S(2)}) collective-permute-start(bf16[4,296,256]{2,1,0:T(8,128)(2,1)} %take.34), channel_id=1, source_target_pairs={{0,8},{4,12},{8,16},{12,20},{16,24},{20,28},{24,0},{28,4},{1,9},{5... | collective-permute-start | bytes 1818632 | tf_op jit(solution)/shard_map/ppermute | solution.py:377
  80.6 3.5 collective-permute-start.22
  86.4 31.7 %collective-permute-done.22.refs_2_ = bf16[4,296,128]{2,1,0:T(8,128)(2,1)S(1)} collective-permute-done((bf16[4,296,128]{2,1,0:T(8,128)(2,1)}, bf16[4,296,128]{2,1,0:T(8,128)(2,1)S(1)}, u32[]{:S(2)}, u32[]{:S(2)}) %collective-permute-start.22) | collective-permute-done | bytes 303136 | tf_op jit(solution)/shard_map/ppermute | solution.py:377
  118.1 4.3 collective-permute-start.6
  123.0 4.2 collective-permute-done.3.refs_4_
  127.9 2.9 multiply_bitcast_fusion
  130.8 12.6 %collective-permute-done.4.refs_5_ = bf16[4,296,256]{2,1,0:T(8,128)(2,1)S(1)} collective-permute-done((bf16[4,296,256]{2,1,0:T(8,128)(2,1)}, bf16[4,296,256]{2,1,0:T(8,128)(2,1)S(1)}, u32[]{:S(2)}, u32[]{:S(2)}) %collective-permute-start.4) | collective-permute-done | bytes 606240 | tf_op jit(solution)/shard_map/ppermute | solution.py:377
  144.3 29.8 %collective-permute-start.9 = (bf16[4,296,256]{2,1,0:T(8,128)(2,1)S(1)}, bf16[4,296,256]{2,1,0:T(8,128)(2,1)}, u32[]{:S(2)}, u32[]{:S(2)}) collective-permute-start(bf16[4,296,256]{2,1,0:T(8,128)(2,1)S(1)} %take.43), channel_id=1, source_target_pairs={{0,12},{4,8},{8,20},{12,16},{16,28},{20,24},{24,4},{28,0},{1,13},{... | collective-permute-start | bytes 1818632 | tf_op jit(solution)/shard_map/ppermute | solution.py:377
  174.1 8.2 %collective-permute-done.5.refs_6_ = bf16[4,296,256]{2,1,0:T(8,128)(2,1)S(1)} collective-permute-done((bf16[4,296,256]{2,1,0:T(8,128)(2,1)}, bf16[4,296,256]{2,1,0:T(8,128)(2,1)S(1)}, u32[]{:S(2)}, u32[]{:S(2)}) %collective-permute-start.5) | collective-permute-done | bytes 606240 | tf_op jit(solution)/shard_map/ppermute | solution.py:377
  183.1 25.2 %collective-permute-done.6.refs_7_ = bf16[4,296,256]{2,1,0:T(8,128)(2,1)S(1)} collective-permute-done((bf16[4,296,256]{2,1,0:T(8,128)(2,1)}, bf16[4,296,256]{2,1,0:T(8,128)(2,1)S(1)}, u32[]{:S(2)}, u32[]{:S(2)}) %collective-permute-start.6) | collective-permute-done | bytes 606240 | tf_op jit(solution)/shard_map/ppermute | solution.py:377
  210.0 3.3 collective-permute-start.12
  232.1 5.7 %reshape.576.azimuth_ref = bf16[128,256]{1,0:T(8,128)(2,1)} reshape(bf16[2,8,2,4,16,2,2,4]{7,6,5,4,3,2,1,0:T(2,128)(2,1)} %multiply_bitcast_fusion) | data formatting | bytes 131072 | tf_op jit(solution)/shard_map/reshape | solution.py:395
  244.9 15.2 %coeffs_and_gram.4 = (bf16[32,256,256]{2,1,0:T(8,128)(2,1)}, f32[32,16,128]{2,1,0:T(8,128)S(1)}) custom-call(s32[2]{0:T(128)S(1)} %copy-done.55, bf16[2,2,256,168]{3,2,1,0:T(8,128)(2,1)S(1)} %copy.66.time_ref, bf16[128,256]{1,0:T(8,128)(2,1)S(1)} %copy-done.30, f32[1,256]{1,0:T(1,128)S(1)} %bitcast.108, f32[32,16,128]{2,1,0:T(8,128)S(1)} %broadcast_in_dim.64.before_ref, ...), custom_call_target="tpu_custom_call" | custom-call | flops 3556769792 | bytes 9043968 | tf_op jit(solution)/shard_map/coeffs_and_gram/pallas_call | solution.py:145
  260.1 1.9 collective-permute-start.23
  262.0 3.8 collective-permute-start.24
  266.8 31.4 %collective-permute-start.26 = (bf16[4,296,128]{2,1,0:T(8,128)(2,1)S(1)}, bf16[4,296,128]{2,1,0:T(8,128)(2,1)S(1)}, u32[]{:S(2)}, u32[]{:S(2)}) collective-permute-start(bf16[4,296,128]{2,1,0:T(8,128)(2,1)S(1)} %copy-done.21), channel_id=1, source_target_pairs={{0,24},{4,28},{8,0},{12,4},{16,8},{20,12},{24,16},{28,20},{1,25},{... | collective-permute-start | bytes 909320 | tf_op jit(solution)/shard_map/ppermute | solution.py:377
  299.2 15.1 %coeffs_and_gram.5 = (bf16[32,256,256]{2,1,0:T(8,128)(2,1)}, f32[32,16,128]{2,1,0:T(8,128)S(1)}) custom-call(s32[2]{0:T(128)S(1)} %copy-done.55, bf16[2,2,256,168]{3,2,1,0:T(8,128)(2,1)S(1)} %copy.66.time_ref, bf16[128,256]{1,0:T(8,128)(2,1)S(1)} %copy-done.30, f32[1,256]{1,0:T(1,128)S(1)} %bitcast.109, f32[32,16,128]{2,1,0:T(8,128)S(1)} %get-tuple-element.12.before_ref, ...), custom_call_target="tpu_custom_call" | custom-call | flops 3556769792 | bytes 9043968 | tf_op jit(solution)/shard_map/coeffs_and_gram/pallas_call | solution.py:145
  314.4 12.3 %coeffs_and_gram.6 = (bf16[32,256,128]{2,1,0:T(8,128)(2,1)S(1)}, f32[32,16,128]{2,1,0:T(8,128)S(1)}) custom-call(s32[2]{0:T(128)S(1)} %copy-done.55, bf16[2,2,256,168]{3,2,1,0:T(8,128)(2,1)S(1)} %copy.66.time_ref, bf16[128,256]{1,0:T(8,128)(2,1)S(1)} %copy-done.30, f32[1,128]{1,0:T(1,128)S(1)} %get-tuple-element.34.weight_ref, ...), custom_call_target="tpu_custom_call" | custom-call | flops 1778384896 | bytes 4521984 | tf_op jit(solution)/shard_map/coeffs_and_gram/pallas_call | solution.py:145
  326.8 12.2 %coeffs_and_gram.7 = (bf16[32,256,128]{2,1,0:T(8,128)(2,1)S(1)}, f32[32,16,128]{2,1,0:T(8,128)S(1)}) custom-call(s32[2]{0:T(128)S(1)} %copy-done.55, bf16[2,2,256,168]{3,2,1,0:T(8,128)(2,1)S(1)} %copy.66.time_ref, bf16[128,256]{1,0:T(8,128)(2,1)S(1)} %copy-done.30, f32[1,128]{1,0:T(1,128)S(1)} %get-tuple-element.35.weight_ref, ...), custom_call_target="tpu_custom_call" | custom-call | flops 1778384896 | bytes 4521984 | tf_op jit(solution)/shard_map/coeffs_and_gram/pallas_call | solution.py:145
  340.3 13.4 %all_to_all.10 = f32[32,1,16,128]{3,2,1,0:T(8,128)S(1)} all-to-all(f32[32,1,16,128]{3,2,1,0:T(8,128)S(1)} %bitcast.106), channel_id=1, replica_groups=mesh['sector'=4,'tm'=2,'space'=4] {'sector','tm','space'}, dimensions={0} | all-to-all | bytes 524288 | tf_op jit(solution)/shard_map/all_to_all | solution.py:427
  354.6 4.0 subspace.1
  361.9 4.9 all-to-all-start.1
  367.1 8.9 %all-to-all-done.1 = bf16[32,1,34,128]{3,2,1,0:T(8,128)(2,1)S(1)} async-done(((bf16[32,1,34,128]{3,2,1,0:T(8,128)(2,1)}), bf16[32,1,34,128]{3,2,1,0:T(8,128)(2,1)S(1)}, u32[]{:S(2)}, u32[]{:S(2)}) %all-to-all-start.1) | async-done | bytes 278560 | tf_op jit(solution)/shard_map/all_to_all | solution.py:448
  379.2 2.2 mix.14
  381.4 3.5 collective-permute-start.33
  384.9 2.2 mix.15
  387.2 3.1 mix.10
  390.3 2.9 collective-permute-start.29
  393.2 3.0 mix.11
  397.5 3.1 mix.12
  401.5 3.1 mix.13
  404.6 31.2 %collective-permute-done.33 = bf16[3,4,128,256]{3,2,1,0:T(8,128)(2,1)S(1)} collective-permute-done((bf16[3,4,128,256]{3,2,1,0:T(8,128)(2,1)S(1)}, bf16[3,4,128,256]{3,2,1,0:T(8,128)(2,1)S(1)}, u32[]{:S(2)}, u32[]{:S(2)}) %collective-permute-start.33) | collective-permute-done | bytes 786464 | tf_op jit(solution)/shard_map/ppermute | solution.py:377
  435.8 36.9 %collective-permute-start.32 = (bf16[3,4,128,256]{3,2,1,0:T(8,128)(2,1)}, bf16[3,4,128,256]{3,2,1,0:T(8,128)(2,1)}, u32[]{:S(2)}, u32[]{:S(2)}) collective-permute-start(bf16[3,4,128,256]{3,2,1,0:T(8,128)(2,1)} %mix.13), channel_id=1, source_target_pairs={{0,8},{4,12},{8,16},{12,20},{16,24},{20,28},{24,0},{28,4},{1,9},{5... | collective-permute-start | bytes 2359304 | tf_op jit(solution)/shard_map/ppermute | solution.py:377
  472.7 3.1 mix.8
  479.1 2.2 mix.9
  483.6 36.4 %collective-permute-done.32 = bf16[3,4,128,256]{3,2,1,0:T(8,128)(2,1)} collective-permute-done((bf16[3,4,128,256]{3,2,1,0:T(8,128)(2,1)}, bf16[3,4,128,256]{3,2,1,0:T(8,128)(2,1)}, u32[]{:S(2)}, u32[]{:S(2)}) %collective-permute-start.32) | collective-permute-done | bytes 786464 | tf_op jit(solution)/shard_map/ppermute | solution.py:377
  520.0 2.1 unpack.10.refs_0_
  522.1 2.1 unpack.11.refs_0_
  524.2 2.1 unpack.12.refs_0_
  526.2 2.1 unpack.13.refs_0_
  529.2 2.1 unpack.15
  (256 shorter events, 88.2 us)
Async XLA Ops:
  1.7 22.7 %collective-permute-start.14 = (bf16[4,296,128]{2,1,0:T(8,128)(2,1)S(1)}, bf16[4,296,128]{2,1,0:T(8,128)(2,1)S(1)}, u32[]{:S(2)}, u32[]{:S(2)}) collective-permute-start(bf16[4,296,128]{2,1,0:T(8,128)(2,1)S(1)} %take.49), channel_id=1, source_target_pairs={{0,4},{4,0},{8,12},{12,8},{16,20},{20,16},{24,28},{28,24},{1,5},{5... | collective-permute-start | bytes 909320 | tf_op jit(solution)/shard_map/ppermute | solution.py:377
  4.2 22.0 %collective-permute-start.15 = (bf16[4,296,128]{2,1,0:T(8,128)(2,1)S(1)}, bf16[4,296,128]{2,1,0:T(8,128)(2,1)S(1)}, u32[]{:S(2)}, u32[]{:S(2)}) collective-permute-start(bf16[4,296,128]{2,1,0:T(8,128)(2,1)S(1)} %take.50), channel_id=1, source_target_pairs={{0,8},{4,12},{8,16},{12,20},{16,24},{20,28},{24,0},{28,4},{1,9},{5... | collective-permute-start | bytes 909320 | tf_op jit(solution)/shard_map/ppermute | solution.py:377
  6.9 40.0 %collective-permute-start.16 = (bf16[4,296,128]{2,1,0:T(8,128)(2,1)S(1)}, bf16[4,296,128]{2,1,0:T(8,128)(2,1)S(1)}, u32[]{:S(2)}, u32[]{:S(2)}) collective-permute-start(bf16[4,296,128]{2,1,0:T(8,128)(2,1)S(1)} %take.51), channel_id=1, source_target_pairs={{0,12},{4,8},{8,20},{12,16},{16,28},{20,24},{24,4},{28,0},{1,13},{... | collective-permute-start | bytes 909320 | tf_op jit(solution)/shard_map/ppermute | solution.py:377
  8.0 40.4 %collective-permute-start.17 = (bf16[4,296,128]{2,1,0:T(8,128)(2,1)S(1)}, bf16[4,296,128]{2,1,0:T(8,128)(2,1)}, u32[]{:S(2)}, u32[]{:S(2)}) collective-permute-start(bf16[4,296,128]{2,1,0:T(8,128)(2,1)S(1)} %take.52), channel_id=1, source_target_pairs={{0,16},{4,20},{8,24},{12,28},{16,0},{20,4},{24,8},{28,12},{1,17},{... | collective-permute-start | bytes 909320 | tf_op jit(solution)/shard_map/ppermute | solution.py:377
  10.9 38.0 %collective-permute-start.18 = (bf16[4,296,128]{2,1,0:T(8,128)(2,1)S(1)}, bf16[4,296,128]{2,1,0:T(8,128)(2,1)}, u32[]{:S(2)}, u32[]{:S(2)}) collective-permute-start(bf16[4,296,128]{2,1,0:T(8,128)(2,1)S(1)} %take.53), channel_id=1, source_target_pairs={{0,20},{4,16},{8,28},{12,24},{16,4},{20,0},{24,12},{28,8},{1,21},{... | collective-permute-start | bytes 909320 | tf_op jit(solution)/shard_map/ppermute | solution.py:377
  24.4 39.8 %copy-start.43 = (bf16[4,296,128]{2,1,0:T(8,128)(2,1)}, bf16[4,296,128]{2,1,0:T(8,128)(2,1)S(1)}, u32[]{:S(2)}) copy-start(bf16[4,296,128]{2,1,0:T(8,128)(2,1)S(1)} %collective-permute-done.14.refs_1_) | copy-start | bytes 909316
  24.4 36.3 %collective-permute-start.19 = (bf16[4,296,128]{2,1,0:T(8,128)(2,1)S(1)}, bf16[4,296,128]{2,1,0:T(8,128)(2,1)S(1)}, u32[]{:S(2)}, u32[]{:S(2)}) collective-permute-start(bf16[4,296,128]{2,1,0:T(8,128)(2,1)S(1)} %take.54), channel_id=1, source_target_pairs={{0,24},{4,28},{8,0},{12,4},{16,8},{20,12},{24,16},{28,20},{1,25},{... | collective-permute-start | bytes 909320 | tf_op jit(solution)/shard_map/ppermute | solution.py:377
  26.2 38.0 %copy-start.45 = (bf16[4,296,128]{2,1,0:T(8,128)(2,1)}, bf16[4,296,128]{2,1,0:T(8,128)(2,1)S(1)}, u32[]{:S(2)}) copy-start(bf16[4,296,128]{2,1,0:T(8,128)(2,1)S(1)} %collective-permute-done.15.refs_2_) | copy-start | bytes 909316
  26.2 36.1 %collective-permute-start.20 = (bf16[4,296,128]{2,1,0:T(8,128)(2,1)S(1)}, bf16[4,296,128]{2,1,0:T(8,128)(2,1)S(1)}, u32[]{:S(2)}, u32[]{:S(2)}) collective-permute-start(bf16[4,296,128]{2,1,0:T(8,128)(2,1)S(1)} %take.55), channel_id=1, source_target_pairs={{0,28},{4,24},{8,4},{12,0},{16,12},{20,8},{24,20},{28,16},{1,29},{... | collective-permute-start | bytes 909320 | tf_op jit(solution)/shard_map/ppermute | solution.py:377
  46.9 33.7 %collective-permute-start.21 = (bf16[4,296,128]{2,1,0:T(8,128)(2,1)S(1)}, bf16[4,296,128]{2,1,0:T(8,128)(2,1)}, u32[]{:S(2)}, u32[]{:S(2)}) collective-permute-start(bf16[4,296,128]{2,1,0:T(8,128)(2,1)S(1)} %take.57), channel_id=1, source_target_pairs={{0,4},{4,0},{8,12},{12,8},{16,20},{20,16},{24,28},{28,24},{1,5},{5... | collective-permute-start | bytes 909320 | tf_op jit(solution)/shard_map/ppermute | solution.py:377
  48.4 69.7 %collective-permute-start = (bf16[4,296,256]{2,1,0:T(8,128)(2,1)}, bf16[4,296,256]{2,1,0:T(8,128)(2,1)}, u32[]{:S(2)}, u32[]{:S(2)}) collective-permute-start(bf16[4,296,256]{2,1,0:T(8,128)(2,1)} %take.33), channel_id=1, source_target_pairs={{0,4},{4,0},{8,12},{12,8},{16,20},{20,16},{24,28},{28,24},{1,5},{5... | collective-permute-start | bytes 1818632 | tf_op jit(solution)/shard_map/ppermute | solution.py:377
  48.9 69.2 %collective-permute-start.1 = (bf16[4,296,256]{2,1,0:T(8,128)(2,1)}, bf16[4,296,256]{2,1,0:T(8,128)(2,1)}, u32[]{:S(2)}, u32[]{:S(2)}) collective-permute-start(bf16[4,296,256]{2,1,0:T(8,128)(2,1)} %take.34), channel_id=1, source_target_pairs={{0,8},{4,12},{8,16},{12,20},{16,24},{20,28},{24,0},{28,4},{1,9},{5... | collective-permute-start | bytes 1818632 | tf_op jit(solution)/shard_map/ppermute | solution.py:377
  61.4 61.1 %collective-permute-start.2 = (bf16[4,296,256]{2,1,0:T(8,128)(2,1)}, bf16[4,296,256]{2,1,0:T(8,128)(2,1)}, u32[]{:S(2)}, u32[]{:S(2)}) collective-permute-start(bf16[4,296,256]{2,1,0:T(8,128)(2,1)} %take.35), channel_id=1, source_target_pairs={{0,12},{4,8},{8,20},{12,16},{16,28},{20,24},{24,4},{28,0},{1,13},{... | collective-permute-start | bytes 1818632 | tf_op jit(solution)/shard_map/ppermute | solution.py:377
  63.0 64.2 %collective-permute-start.3 = (bf16[4,296,256]{2,1,0:T(8,128)(2,1)}, bf16[4,296,256]{2,1,0:T(8,128)(2,1)}, u32[]{:S(2)}, u32[]{:S(2)}) collective-permute-start(bf16[4,296,256]{2,1,0:T(8,128)(2,1)} %take.36), channel_id=1, source_target_pairs={{0,16},{4,20},{8,24},{12,28},{16,0},{20,4},{24,8},{28,12},{1,17},{... | collective-permute-start | bytes 1818632 | tf_op jit(solution)/shard_map/ppermute | solution.py:377
  78.7 48.5 %copy-start.58 = (f32[16]{0:T(128)S(1)}, f32[16]{0:T(128)}, u32[]{:S(2)}) copy-start(f32[16]{0:T(128)} %param.7) | copy-start | bytes 196
  80.6 37.4 %collective-permute-start.22 = (bf16[4,296,128]{2,1,0:T(8,128)(2,1)}, bf16[4,296,128]{2,1,0:T(8,128)(2,1)S(1)}, u32[]{:S(2)}, u32[]{:S(2)}) collective-permute-start(bf16[4,296,128]{2,1,0:T(8,128)(2,1)} %take.58), channel_id=1, source_target_pairs={{0,8},{4,12},{8,16},{12,20},{16,24},{20,28},{24,0},{28,4},{1,9},{5... | collective-permute-start | bytes 909320 | tf_op jit(solution)/shard_map/ppermute | solution.py:377
  118.0 98.9 %copy-start.53 = (bf16[4,296,128]{2,1,0:T(8,128)(2,1)}, bf16[4,296,128]{2,1,0:T(8,128)(2,1)S(1)}, u32[]{:S(2)}) copy-start(bf16[4,296,128]{2,1,0:T(8,128)(2,1)S(1)} %collective-permute-done.22.refs_2_) | copy-start | bytes 909316
  118.0 25.3 %collective-permute-start.4 = (bf16[4,296,256]{2,1,0:T(8,128)(2,1)}, bf16[4,296,256]{2,1,0:T(8,128)(2,1)S(1)}, u32[]{:S(2)}, u32[]{:S(2)}) collective-permute-start(bf16[4,296,256]{2,1,0:T(8,128)(2,1)} %copy-done.13), channel_id=1, source_target_pairs={{0,20},{4,16},{8,28},{12,24},{16,4},{20,0},{24,12},{28,8},{1,21},{... | collective-permute-start | bytes 1818632 | tf_op jit(solution)/shard_map/ppermute | solution.py:377
  118.1 64.2 %collective-permute-start.5 = (bf16[4,296,256]{2,1,0:T(8,128)(2,1)}, bf16[4,296,256]{2,1,0:T(8,128)(2,1)S(1)}, u32[]{:S(2)}, u32[]{:S(2)}) collective-permute-start(bf16[4,296,256]{2,1,0:T(8,128)(2,1)} %copy-done.10), channel_id=1, source_target_pairs={{0,24},{4,28},{8,0},{12,4},{16,8},{20,12},{24,16},{28,20},{1,25},{... | collective-permute-start | bytes 1818632 | tf_op jit(solution)/shard_map/ppermute | solution.py:377
  118.1 90.2 %collective-permute-start.6 = (bf16[4,296,256]{2,1,0:T(8,128)(2,1)}, bf16[4,296,256]{2,1,0:T(8,128)(2,1)S(1)}, u32[]{:S(2)}, u32[]{:S(2)}) collective-permute-start(bf16[4,296,256]{2,1,0:T(8,128)(2,1)} %copy-done.9), channel_id=1, source_target_pairs={{0,28},{4,24},{8,4},{12,0},{16,12},{20,8},{24,20},{28,16},{1,29},{... | collective-permute-start | bytes 1818632 | tf_op jit(solution)/shard_map/ppermute | solution.py:377
  122.4 86.7 %collective-permute-start.7 = (bf16[4,296,256]{2,1,0:T(8,128)(2,1)}, bf16[4,296,256]{2,1,0:T(8,128)(2,1)S(1)}, u32[]{:S(2)}, u32[]{:S(2)}) collective-permute-start(bf16[4,296,256]{2,1,0:T(8,128)(2,1)} %copy-done.8), channel_id=1, source_target_pairs={{0,4},{4,0},{8,12},{12,8},{16,20},{20,16},{24,28},{28,24},{1,5},{5... | collective-permute-start | bytes 1818632 | tf_op jit(solution)/shard_map/ppermute | solution.py:377
  127.2 86.0 %collective-permute-start.8 = (bf16[4,296,256]{2,1,0:T(8,128)(2,1)}, bf16[4,296,256]{2,1,0:T(8,128)(2,1)S(1)}, u32[]{:S(2)}, u32[]{:S(2)}) collective-permute-start(bf16[4,296,256]{2,1,0:T(8,128)(2,1)} %copy-done.7), channel_id=1, source_target_pairs={{0,8},{4,12},{8,16},{12,20},{16,24},{20,28},{24,0},{28,4},{1,9},{5... | collective-permute-start | bytes 1818632 | tf_op jit(solution)/shard_map/ppermute | solution.py:377
  144.3 115.8 %collective-permute-start.9 = (bf16[4,296,256]{2,1,0:T(8,128)(2,1)S(1)}, bf16[4,296,256]{2,1,0:T(8,128)(2,1)}, u32[]{:S(2)}, u32[]{:S(2)}) collective-permute-start(bf16[4,296,256]{2,1,0:T(8,128)(2,1)S(1)} %take.43), channel_id=1, source_target_pairs={{0,12},{4,8},{8,20},{12,16},{16,28},{20,24},{24,4},{28,0},{1,13},{... | collective-permute-start | bytes 1818632 | tf_op jit(solution)/shard_map/ppermute | solution.py:377
  183.1 78.9 %collective-permute-start.10 = (bf16[4,296,256]{2,1,0:T(8,128)(2,1)S(1)}, bf16[4,296,256]{2,1,0:T(8,128)(2,1)}, u32[]{:S(2)}, u32[]{:S(2)}) collective-permute-start(bf16[4,296,256]{2,1,0:T(8,128)(2,1)S(1)} %take.44), channel_id=1, source_target_pairs={{0,16},{4,20},{8,24},{12,28},{16,0},{20,4},{24,8},{28,12},{1,17},{... | collective-permute-start | bytes 1818632 | tf_op jit(solution)/shard_map/ppermute | solution.py:377
  209.1 56.7 %collective-permute-start.11 = (bf16[4,296,256]{2,1,0:T(8,128)(2,1)S(1)}, bf16[4,296,256]{2,1,0:T(8,128)(2,1)}, u32[]{:S(2)}, u32[]{:S(2)}) collective-permute-start(bf16[4,296,256]{2,1,0:T(8,128)(2,1)S(1)} %take.45), channel_id=1, source_target_pairs={{0,20},{4,16},{8,28},{12,24},{16,4},{20,0},{24,12},{28,8},{1,21},{... | collective-permute-start | bytes 1818632 | tf_op jit(solution)/shard_map/ppermute | solution.py:377
  210.0 56.9 %collective-permute-start.12 = (bf16[4,296,256]{2,1,0:T(8,128)(2,1)S(1)}, bf16[4,296,256]{2,1,0:T(8,128)(2,1)}, u32[]{:S(2)}, u32[]{:S(2)}) collective-permute-start(bf16[4,296,256]{2,1,0:T(8,128)(2,1)S(1)} %take.46), channel_id=1, source_target_pairs={{0,24},{4,28},{8,0},{12,4},{16,8},{20,12},{24,16},{28,20},{1,25},{... | collective-permute-start | bytes 1818632 | tf_op jit(solution)/shard_map/ppermute | solution.py:377
  214.1 84.1 %collective-permute-start.13 = (bf16[4,296,256]{2,1,0:T(8,128)(2,1)S(1)}, bf16[4,296,256]{2,1,0:T(8,128)(2,1)}, u32[]{:S(2)}, u32[]{:S(2)}) collective-permute-start(bf16[4,296,256]{2,1,0:T(8,128)(2,1)S(1)} %take.47), channel_id=1, source_target_pairs={{0,28},{4,24},{8,4},{12,0},{16,12},{20,8},{24,20},{28,16},{1,29},{... | collective-permute-start | bytes 1818632 | tf_op jit(solution)/shard_map/ppermute | solution.py:377
  244.9 20.9 %copy-start.23 = (bf16[4,296,128]{2,1,0:T(8,128)(2,1)S(1)}, bf16[4,296,128]{2,1,0:T(8,128)(2,1)}, u32[]{:S(2)}) copy-start(bf16[4,296,128]{2,1,0:T(8,128)(2,1)} %copy-done.22) | copy-start | bytes 909316
  244.9 21.9 %copy-start.21 = (bf16[4,296,128]{2,1,0:T(8,128)(2,1)S(1)}, bf16[4,296,128]{2,1,0:T(8,128)(2,1)}, u32[]{:S(2)}) copy-start(bf16[4,296,128]{2,1,0:T(8,128)(2,1)} %copy-done.20) | copy-start | bytes 909316
  244.9 53.3 %copy-start.19 = (bf16[4,296,128]{2,1,0:T(8,128)(2,1)S(1)}, bf16[4,296,128]{2,1,0:T(8,128)(2,1)}, u32[]{:S(2)}) copy-start(bf16[4,296,128]{2,1,0:T(8,128)(2,1)} %copy-done.18) | copy-start | bytes 909316
  244.9 54.2 %copy-start.12 = (bf16[4,296,256]{2,1,0:T(8,128)(2,1)S(1)}, bf16[4,296,256]{2,1,0:T(8,128)(2,1)}, u32[]{:S(2)}) copy-start(bf16[4,296,256]{2,1,0:T(8,128)(2,1)} %copy-done.11) | copy-start | bytes 1818628
  244.9 54.2 %copy-start.34 = (bf16[4,296,256]{2,1,0:T(8,128)(2,1)S(1)}, bf16[4,296,256]{2,1,0:T(8,128)(2,1)}, u32[]{:S(2)}) copy-start(bf16[4,296,256]{2,1,0:T(8,128)(2,1)} %copy-done.33) | copy-start | bytes 1818628
  244.9 54.2 %copy-start.36 = (bf16[4,296,256]{2,1,0:T(8,128)(2,1)S(1)}, bf16[4,296,256]{2,1,0:T(8,128)(2,1)}, u32[]{:S(2)}) copy-start(bf16[4,296,256]{2,1,0:T(8,128)(2,1)} %copy-done.35) | copy-start | bytes 1818628
  260.1 66.6 %collective-permute-start.23 = (bf16[4,296,128]{2,1,0:T(8,128)(2,1)S(1)}, bf16[4,296,128]{2,1,0:T(8,128)(2,1)S(1)}, u32[]{:S(2)}, u32[]{:S(2)}) collective-permute-start(bf16[4,296,128]{2,1,0:T(8,128)(2,1)S(1)} %copy-done.27), channel_id=1, source_target_pairs={{0,12},{4,8},{8,20},{12,16},{16,28},{20,24},{24,4},{28,0},{1,13},{... | collective-permute-start | bytes 909320 | tf_op jit(solution)/shard_map/ppermute | solution.py:377
  262.0 64.7 %collective-permute-start.24 = (bf16[4,296,128]{2,1,0:T(8,128)(2,1)S(1)}, bf16[4,296,128]{2,1,0:T(8,128)(2,1)S(1)}, u32[]{:S(2)}, u32[]{:S(2)}) collective-permute-start(bf16[4,296,128]{2,1,0:T(8,128)(2,1)S(1)} %copy-done.25), channel_id=1, source_target_pairs={{0,16},{4,20},{8,24},{12,28},{16,0},{20,4},{24,8},{28,12},{1,17},{... | collective-permute-start | bytes 909320 | tf_op jit(solution)/shard_map/ppermute | solution.py:377
  265.8 60.9 %collective-permute-start.25 = (bf16[4,296,128]{2,1,0:T(8,128)(2,1)S(1)}, bf16[4,296,128]{2,1,0:T(8,128)(2,1)S(1)}, u32[]{:S(2)}, u32[]{:S(2)}) collective-permute-start(bf16[4,296,128]{2,1,0:T(8,128)(2,1)S(1)} %copy-done.23), channel_id=1, source_target_pairs={{0,20},{4,16},{8,28},{12,24},{16,4},{20,0},{24,12},{28,8},{1,21},{... | collective-permute-start | bytes 909320 | tf_op jit(solution)/shard_map/ppermute | solution.py:377
  266.8 59.9 %collective-permute-start.26 = (bf16[4,296,128]{2,1,0:T(8,128)(2,1)S(1)}, bf16[4,296,128]{2,1,0:T(8,128)(2,1)S(1)}, u32[]{:S(2)}, u32[]{:S(2)}) collective-permute-start(bf16[4,296,128]{2,1,0:T(8,128)(2,1)S(1)} %copy-done.21), channel_id=1, source_target_pairs={{0,24},{4,28},{8,0},{12,4},{16,8},{20,12},{24,16},{28,20},{1,25},{... | collective-permute-start | bytes 909320 | tf_op jit(solution)/shard_map/ppermute | solution.py:377
  298.2 28.5 %collective-permute-start.27 = (bf16[4,296,128]{2,1,0:T(8,128)(2,1)S(1)}, bf16[4,296,128]{2,1,0:T(8,128)(2,1)S(1)}, u32[]{:S(2)}, u32[]{:S(2)}) collective-permute-start(bf16[4,296,128]{2,1,0:T(8,128)(2,1)S(1)} %copy-done.19), channel_id=1, source_target_pairs={{0,28},{4,24},{8,4},{12,0},{16,12},{20,8},{24,20},{28,16},{1,29},{... | collective-permute-start | bytes 909320 | tf_op jit(solution)/shard_map/ppermute | solution.py:377
  326.7 40.2 %copy-start.32 = (f32[256]{0:T(256)S(1)}, f32[256]{0:T(256)}, u32[]{:S(2)}) copy-start(f32[256]{0:T(256)} %select_reduce_fusion) | copy-start | bytes 3076
  361.9 14.1 %all-to-all-start.1 = ((bf16[32,1,34,128]{3,2,1,0:T(8,128)(2,1)}), bf16[32,1,34,128]{3,2,1,0:T(8,128)(2,1)S(1)}, u32[]{:S(2)}, u32[]{:S(2)}) async-start(bf16[32,1,34,128]{3,2,1,0:T(8,128)(2,1)} %broadcast_in_dim.66), calls=%async_computation.1 | async-start | bytes 655360 | tf_op jit(solution)/shard_map/all_to_all | solution.py:448
  381.4 54.4 %collective-permute-start.33 = (bf16[3,4,128,256]{3,2,1,0:T(8,128)(2,1)S(1)}, bf16[3,4,128,256]{3,2,1,0:T(8,128)(2,1)S(1)}, u32[]{:S(2)}, u32[]{:S(2)}) collective-permute-start(bf16[3,4,128,256]{3,2,1,0:T(8,128)(2,1)S(1)} %mix.14), channel_id=1, source_target_pairs={{0,20},{4,16},{8,28},{12,24},{16,4},{20,0},{24,12},{28,8},{1,21},{... | collective-permute-start | bytes 2359304 | tf_op jit(solution)/shard_map/ppermute | solution.py:377
  387.1 88.7 %collective-permute-start.34 = (bf16[3,4,128,256]{3,2,1,0:T(8,128)(2,1)S(1)}, bf16[3,4,128,256]{3,2,1,0:T(8,128)(2,1)S(1)}, u32[]{:S(2)}, u32[]{:S(2)}) collective-permute-start(bf16[3,4,128,256]{3,2,1,0:T(8,128)(2,1)S(1)} %mix.15), channel_id=1, source_target_pairs={{0,16},{4,20},{8,24},{12,28},{16,0},{20,4},{24,8},{28,12},{1,17},{... | collective-permute-start | bytes 2359304 | tf_op jit(solution)/shard_map/ppermute | solution.py:377
  390.3 136.0 %collective-permute-start.29 = (bf16[3,4,128,256]{3,2,1,0:T(8,128)(2,1)}, bf16[3,4,128,256]{3,2,1,0:T(8,128)(2,1)}, u32[]{:S(2)}, u32[]{:S(2)}) collective-permute-start(bf16[3,4,128,256]{3,2,1,0:T(8,128)(2,1)} %mix.10), channel_id=1, source_target_pairs={{0,28},{4,24},{8,4},{12,0},{16,12},{20,8},{24,20},{28,16},{1,29},{... | collective-permute-start | bytes 2359304 | tf_op jit(solution)/shard_map/ppermute | solution.py:377
  396.3 127.9 %collective-permute-start.30 = (bf16[3,4,128,256]{3,2,1,0:T(8,128)(2,1)}, bf16[3,4,128,256]{3,2,1,0:T(8,128)(2,1)}, u32[]{:S(2)}, u32[]{:S(2)}) collective-permute-start(bf16[3,4,128,256]{3,2,1,0:T(8,128)(2,1)} %mix.11), channel_id=1, source_target_pairs={{0,24},{4,28},{8,0},{12,4},{16,8},{20,12},{24,16},{28,20},{1,25},{... | collective-permute-start | bytes 2359304 | tf_op jit(solution)/shard_map/ppermute | solution.py:377
  400.5 121.6 %collective-permute-start.31 = (bf16[3,4,128,256]{3,2,1,0:T(8,128)(2,1)}, bf16[3,4,128,256]{3,2,1,0:T(8,128)(2,1)}, u32[]{:S(2)}, u32[]{:S(2)}) collective-permute-start(bf16[3,4,128,256]{3,2,1,0:T(8,128)(2,1)} %mix.12), channel_id=1, source_target_pairs={{0,12},{4,8},{8,20},{12,16},{16,28},{20,24},{24,4},{28,0},{1,13},{... | collective-permute-start | bytes 2359304 | tf_op jit(solution)/shard_map/ppermute | solution.py:377
  435.8 39.9 %copy-start.5 = (bf16[3,4,128,256]{3,2,1,0:T(8,128)(2,1)}, bf16[3,4,128,256]{3,2,1,0:T(8,128)(2,1)S(1)}, u32[]{:S(2)}) copy-start(bf16[3,4,128,256]{3,2,1,0:T(8,128)(2,1)S(1)} %collective-permute-done.33) | copy-start | bytes 2359300
  435.8 84.2 %collective-permute-start.32 = (bf16[3,4,128,256]{3,2,1,0:T(8,128)(2,1)}, bf16[3,4,128,256]{3,2,1,0:T(8,128)(2,1)}, u32[]{:S(2)}, u32[]{:S(2)}) collective-permute-start(bf16[3,4,128,256]{3,2,1,0:T(8,128)(2,1)} %mix.13), channel_id=1, source_target_pairs={{0,8},{4,12},{8,16},{12,20},{16,24},{20,28},{24,0},{28,4},{1,9},{5... | collective-permute-start | bytes 2359304 | tf_op jit(solution)/shard_map/ppermute | solution.py:377
  476.7 52.6 %collective-permute-start.28 = (bf16[3,4,128,256]{3,2,1,0:T(8,128)(2,1)}, bf16[3,4,128,256]{3,2,1,0:T(8,128)(2,1)}, u32[]{:S(2)}, u32[]{:S(2)}) collective-permute-start(bf16[3,4,128,256]{3,2,1,0:T(8,128)(2,1)} %mix.8), channel_id=1, source_target_pairs={{0,4},{4,0},{8,12},{12,8},{16,20},{20,16},{24,28},{28,24},{1,5},{5... | collective-permute-start | bytes 2359304 | tf_op jit(solution)/shard_map/ppermute | solution.py:377
  (47 other events, 202.0 us)

commit v5 on v4

--- a/solution.py
+++ b/solution.py
@@ -70,24 +70,31 @@
     sectors = spectra.shape[0]
     rows = spectra.shape[2] // NFREQ
 
+    beside = 2 if columns == LANES and sec_count % 2 == 0 else 1
+
     @pl.when(step < sec_local)
     def _():
-        for shift in range(sec_count):
-            source = lax.rem(place_ref[0] + sec_count - shift, sec_count)
-            own = record_refs[shift * tm_count:(shift + 1) * tm_count]
+        for shift in range(0, sec_count, beside):
             for h in range(halves):
                 first = h * (rec_len - span) // (halves - 1)
-                pieces = [ref[0, first:first + span] for ref in own]
                 parts = []
                 for j in range(tm_count):
-                    piece = pieces[0]
-                    for n in range(1, tm_count):
-                        here = lax.rem(place_ref[1] + tm_count - n, tm_count) == j
-                        piece = jnp.where(here, pieces[n], piece)
-                    part = jnp.dot(time_ref[j, h], piece, preferred_element_type=jnp.float32)
-                    parts.append(part.reshape(NFREQ, rows // tm_count, columns))
-                joined = jnp.stack(parts, 1).reshape(NFREQ * rows, columns)
-                spectra[source * sec_local + step, h] = joined.astype(jnp.bfloat16)
+                    row = []
+                    for n in range(beside):
+                        own = record_refs[(shift + n) * tm_count:(shift + n + 1) * tm_count]
+                        piece = own[0][0, first:first + span]
+                        for x in range(1, tm_count):
+                            here = lax.rem(place_ref[1] + tm_count - x, tm_count) == j
+                            piece = jnp.where(here, own[x][0, first:first + span], piece)
+                        row.append(piece)
+                    wide_piece = row[0] if beside == 1 else jnp.concatenate(row, 1)
+                    part = jnp.dot(time_ref[j, h], wide_piece, preferred_element_type=jnp.float32)
+                    parts.append(part.reshape(NFREQ, rows // tm_count, beside * columns))
+                joined = jnp.stack(parts, 1).reshape(NFREQ * rows, beside * columns)
+                joined = joined.astype(jnp.bfloat16)
+                for n in range(beside):
+                    source = lax.rem(place_ref[0] + sec_count - shift - n, sec_count)
+                    spectra[source * sec_local + step, h] = joined[:, n * columns:(n + 1) * columns]
 
     @pl.when(step >= sec_local)
     def _():
@@ -100,27 +107,28 @@
         owner = lax.broadcasted_iota(jnp.int32, (blocks, wide), 1) // blocks
         for n in range(freqs):
             at = pl.multiple_of(((step - sec_local) * freqs + n) * rows, rows)
-            parts = [
-                jnp.dot(
-                    azimuth_ref[...],
-                    spectra[:, h, pl.ds(at, rows), :].reshape(sectors * rows, columns),
-                    preferred_element_type=jnp.float32,
-                ).reshape(2 * orders, depth, columns)
+            own = [
+                spectra[:, h, pl.ds(at, rows), :].reshape(sectors * rows, columns)
                 for h in range(halves)
             ]
+            if beside == halves:
+                both = jnp.dot(
+                    azimuth_ref[...], jnp.concatenate(own, 1), preferred_element_type=jnp.float32
+                )
+                parts = [both[:, h * columns:(h + 1) * columns] for h in range(halves)]
+            else:
+                parts = [
+                    jnp.dot(azimuth_ref[...], x, preferred_element_type=jnp.float32) for x in own
+                ]
+            parts = [x.reshape(2 * orders, depth, columns) for x in parts]
             coeffs = jnp.stack(parts, 1).reshape(2 * wide, columns).astype(jnp.bfloat16)
             coeff_ref[n] = coeffs
             weighted = (coeffs.astype(jnp.float32) * weight_ref[...]).astype(jnp.bfloat16)
-            swapped = jnp.concatenate([coeffs[wide:], coeffs[:wide]], 0)
-            across = (((1,), (1,)), ((), ()))
-            upper = lax.dot_general(
-                weighted[:wide], coeffs, across, preferred_element_type=jnp.float32
+            products = lax.dot_general(
+                weighted, coeffs, (((1,), (1,)), ((), ())), preferred_element_type=jnp.float32
             )
-            lower = lax.dot_general(
-                weighted[wide:], swapped, across, preferred_element_type=jnp.float32
-            )
-            real = upper[:, :wide] + lower[:, :wide]
-            imag = upper[:, wide:] - lower[:, wide:]
+            real = products[:wide, :wide] + products[wide:, wide:]
+            imag = products[:wide, wide:] - products[wide:, :wide]
             packed = jnp.where(row <= column, real, imag)
             own = packed[:blocks]
             for m in range(1, orders):
@@ -231,15 +239,22 @@
 
 
 def mix_kernel(orders, parts, owner_ref, mixing_ref, spread_ref, factor_ref, root_ref, *refs):
-    coeff_refs, out_ref = refs[:-1], refs[-1]
-    freqs, rows, _ = mixing_ref.shape
-    total = spread_ref.shape[1]
+    coeff_refs, out_ref = refs[:len(parts)], refs[-1]
+    freqs, own_rows, _ = mixing_ref.shape
+    rows = 2 * own_rows
+    total = spread_ref.shape[2]
     blocks = total // (2 * orders)
-    row = lax.broadcasted_iota(jnp.int32, (rows, total), 0) // (rows // orders)
+    row = lax.broadcasted_iota(jnp.int32, (rows, total), 0) % own_rows // (own_rows // orders)
     column = lax.broadcasted_iota(jnp.int32, (rows, total), 1) // blocks % orders
     factor = jnp.transpose(factor_ref[0])
     for n in range(freqs):
-        wide = jnp.dot(mixing_ref[n], spread_ref[...], preferred_element_type=jnp.float32)
+        wide = jnp.concatenate(
+            [
+                jnp.dot(mixing_ref[n], spread_ref[d], preferred_element_type=jnp.float32)
+                for d in range(2)
+            ],
+            0,
+        )
         wide = jnp.where(row == column, wide, 0.0).astype(jnp.bfloat16)
         for (k, low, high), coeff_ref in zip(parts, coeff_refs):
             fields = jnp.dot(wide, coeff_ref[n], preferred_element_type=jnp.float32)
@@ -247,9 +262,10 @@
             out_ref[k, n, :, low:high] = scaled.astype(jnp.bfloat16)
 
 
-def mix(owner, coeffs, parts, mixing, spread, factor, root_weight, owners, orders, fields):
+def mix(owner, coeffs, parts, mixing, spread, factor, root_weight, owners, orders, fields, after):
     rows = coeffs[0].shape[1]
-    out_rows, depth = mixing.shape[1:]
+    own_rows, depth = mixing.shape[1:]
+    out_rows = 2 * own_rows
     columns = root_weight.shape[1]
     freqs = NFREQ // owners
     return pl.pallas_call(
@@ -258,13 +274,13 @@
             num_scalar_prefetch=1,
             grid=(1,),
             in_specs=[
-                pl.BlockSpec((freqs, out_rows, depth), lambda i, at: (at[0], 0, 0)),
-                pl.BlockSpec(spread.shape, lambda i, at: (0, 0)),
+                pl.BlockSpec((freqs, own_rows, depth), lambda i, at: (at[0], 0, 0)),
+                pl.BlockSpec(spread.shape, lambda i, at: (0, 0, 0)),
                 pl.BlockSpec((1, freqs, out_rows), lambda i, at: (at[0], 0, 0)),
                 pl.BlockSpec(root_weight.shape, lambda i, at: (0, 0)),
             ] + [
                 pl.BlockSpec((freqs, rows, x.shape[2]), lambda i, at: (at[0], 0, 0)) for x in coeffs
-            ],
+            ] + [pl.BlockSpec(memory_space=pl.ANY)] * len(after),
             out_specs=pl.BlockSpec((fields, freqs, out_rows, columns), lambda i, at: (0, 0, 0, 0)),
         ),
         out_shape=jax.ShapeDtypeStruct((fields, freqs, out_rows, columns), jnp.bfloat16),
@@ -275,14 +291,15 @@
             transcendentals=0,
         ),
         name="mix",
-    )(jnp.reshape(owner, (1,)), mixing, spread, factor, root_weight, *coeffs)
-
-
-def take_kernel(place_ref, record_ref, out_ref):
+    )(jnp.reshape(owner, (1,)), mixing, spread, factor, root_weight, *coeffs, *after)
+
+
+def take_kernel(place_ref, record_ref, *refs):
+    out_ref = refs[-1]
     out_ref[...] = record_ref[:, 0]
 
 
-def take(by_field, owner, owners, part):
+def take(by_field, owner, owners, part, after):
     sec_local, _, rec_len, cells = by_field.shape
     k, low, high = part
     count = high - low
@@ -296,7 +313,7 @@
             grid=(1,),
             in_specs=[
                 pl.BlockSpec((sec_local, 1, rec_len, count), lambda i, at: (0, k, 0, at[0]))
-            ],
+            ] + [pl.BlockSpec(memory_space=pl.ANY)] * len(after),
             out_specs=pl.BlockSpec((sec_local, rec_len, count), lambda i, at: (0, 0, 0)),
         ),
         out_shape=jax.ShapeDtypeStruct((sec_local, rec_len, count), by_field.dtype),
@@ -305,22 +322,23 @@
             flops=0, bytes_accessed=4 * sec_local * rec_len * count, transcendentals=0
         ),
         name="take",
-    )(jnp.reshape(owner * (own // count) + low // count, (1,)), by_field)
+    )(jnp.reshape(owner * (own // count) + low // count, (1,)), by_field, *after)
 
 
 def unpack_kernel(owner_ref, piece_ref, *refs):
     out_ref = refs[-1]
     for k in range(piece_ref.shape[0]):
         for f in range(piece_ref.shape[1]):
-            out_ref[:, f, :, k] = piece_ref[k, f]
+            for d in range(piece_ref.shape[2]):
+                out_ref[:, f, d, k] = piece_ref[k, f, d]
 
 
 def unpack(owner, piece, owners, whole):
-    fields, freqs, orders, two, modes, part = piece.shape
+    fields, freqs, two, orders, modes, part = piece.shape
     shape = (orders, freqs, two, fields, modes, owners * part)
     if part % LANES:
         whole = jnp.zeros(shape, piece.dtype) if whole is None else whole
-        piece = jnp.transpose(piece, (2, 1, 3, 0, 4, 5))
+        piece = jnp.transpose(piece, (3, 1, 2, 0, 4, 5))
         return lax.dynamic_update_slice_in_dim(whole, piece, owner * part, 5)
     inputs = [piece] if whole is None else [piece, whole]
     in_specs = [
@@ -361,7 +379,10 @@
     by_field = jnp.transpose(records, (0, 2, 1, 3))
     sec_at, tm_at = lax.axis_index("sector"), lax.axis_index("tm")
     shifts = [(z, x) for z in range(sec_count) for x in range(tm_count)]
-    in_order = sorted(shifts, key=lambda r: (r[0] == 0, abs(2 * r[0] - sec_count), r))
+    in_order = sorted(
+        [r for r in shifts if r[0] > 0], key=lambda r: (abs(2 * r[0] - sec_count), r)
+    )
+    in_order[2:2] = [r for r in shifts if r[0] == 0 and r[1] > 0] + [(0, 0)]
 
     def owner_after(z, x):
         return (sec_at + z) % sec_count * tm_count + (tm_at + x) % tm_count
@@ -379,11 +400,6 @@
     parts = [(k, 0, part) for k in range(fields)]
     if part % (2 * LANES) == 0:
         parts[-1:] = [(fields - 1, 0, part // 2), (fields - 1, part // 2, part)]
-    arrived = []
-    for own_part in parts:
-        got = {r: send(take(by_field, owner_after(*r), owners, own_part), *r) for r in in_order}
-        arrived.append([got[r] for r in shifts])
-
     time_basis = placed_time_basis(block_start, tm_count)
     half, _ = half_span(blocks // tm_count)
     halves = blocks // tm_count // half
@@ -409,11 +425,26 @@
     )
 
     gram = jnp.zeros((NFREQ, blocks, orders * blocks), jnp.float32)
-    coeffs = []
-    for pieces, (_, low, high) in zip(arrived, parts):
-        own, gram = coeffs_and_gram(
+
+    def coeffs_of(n, pieces, gram):
+        _, low, high = parts[n]
+        return coeffs_and_gram(
             jnp.stack([sec_at, tm_at]), pieces, sec_count, time_basis, azimuth, weight[:, low:high], gram
         )
+
+    coeffs = []
+    arrived = []
+    for own_part in parts:
+        if len(arrived) > 1:
+            own, gram = coeffs_of(len(coeffs), arrived[len(coeffs)], gram)
+            coeffs.append(own)
+            after = (gram,)
+        else:
+            after = ()
+        got = {r: send(take(by_field, owner_after(*r), owners, own_part, after), *r) for r in in_order}
+        arrived.append([got[r] for r in shifts])
+    while len(coeffs) < len(parts):
+        own, gram = coeffs_of(len(coeffs), arrived[len(coeffs)], gram)
         coeffs.append(own)
 
     if own_freqs % space_count == 0:
@@ -430,11 +461,7 @@
     basis, energy = subspace(gram, tuple(place[:MODES]), fields * cell_local * space_count)
 
     short = basis.astype(jnp.bfloat16).reshape(2, MODES, blocks, solved, orders)
-    short = jnp.transpose(short, (3, 4, 0, 1, 2))
-    short_re, short_im = short[:, :, 0], short[:, :, 1]
-    mixing = jnp.stack(
-        [jnp.concatenate([short_re, -short_im], -1), jnp.concatenate([short_im, short_re], -1)], 2
-    ).reshape(solved, orders * 2 * MODES * depth)
+    mixing = jnp.transpose(short, (3, 4, 1, 0, 2)).reshape(solved, orders * MODES * depth)
     energy = jnp.transpose(energy.reshape(MODES, solved, orders), (1, 2, 0)).reshape(solved, -1)
     high = energy.astype(jnp.bfloat16)
     rest = energy - high.astype(jnp.float32)
@@ -448,28 +475,45 @@
     packet = lax.all_to_all(packet, axes, split_axis=0, concat_axis=0, tiled=True)
     packet = packet.reshape(NFREQ, width)
     count = orders * MODES
-    mixing = packet[:, :orders * 2 * MODES * depth].reshape(NFREQ, orders * 2 * MODES, depth)
-    tail = packet[:, orders * 2 * MODES * depth:].astype(jnp.float32)
+    mixing = packet[:, :orders * MODES * depth].reshape(NFREQ, orders * MODES, depth)
+    tail = packet[:, orders * MODES * depth:].astype(jnp.float32)
     energy = (tail[:, :count] + tail[:, count:2 * count]) + tail[:, 2 * count:3 * count]
+    factor = lax.rsqrt(energy)
+    factor = jnp.concatenate([factor, factor], 1).reshape(owners, own_freqs, orders * 2 * MODES)
     energy = energy.reshape(NFREQ, orders, MODES)
-    factor = jnp.broadcast_to(
-        lax.rsqrt(energy)[:, :, None, :], (NFREQ, orders, 2, MODES)
-    ).reshape(owners, own_freqs, orders * 2 * MODES)
     root_weight = jnp.sqrt(weight)
+    signs = jnp.array([[[1, 0], [0, -1]], [[0, 1], [1, 0]]], jnp.bfloat16)
     spread = jnp.broadcast_to(
-        jnp.eye(depth, dtype=jnp.bfloat16).reshape(depth, 2, 1, blocks), (depth, 2, orders, blocks)
-    ).reshape(depth, depth * orders)
+        signs[:, :, None, :, None, None]
+        * jnp.eye(blocks, dtype=jnp.bfloat16)[None, None, :, None, None, :],
+        (2, 2, blocks, 2, orders, blocks),
+    ).reshape(2, depth, depth * orders)
 
     mode_fields = None
-    arrived = []
+    sent = []
+    unpacked = 0
+    in_flight = 5
+
+    def unpack_next(mode_fields):
+        owner, piece = sent[unpacked]
+        piece = piece.reshape(fields, own_freqs, 2, orders, MODES, part)
+        return unpack(owner, piece, owners, mode_fields)
+
+    before = ()
     for z, x in in_order:
+        if len(sent) > in_flight and part % LANES == 0:
+            mode_fields = unpack_next(mode_fields)
+            unpacked += 1
+            before = before + (mode_fields,)
         piece = mix(
-            owner_after(z, x), coeffs, parts, mixing, spread, factor, root_weight, owners, orders, fields
+            owner_after(z, x), coeffs, parts, mixing, spread, factor, root_weight, owners, orders,
+            fields, before,
         )
-        arrived.append((owner_after(-z, -x), send(piece, z, x)))
-    for owner, piece in arrived:
-        piece = piece.reshape(fields, own_freqs, orders, 2, MODES, part)
-        mode_fields = unpack(owner, piece, owners, mode_fields)
+        before = (piece,)
+        sent.append((owner_after(-z, -x), send(piece, z, x)))
+    while unpacked < len(sent):
+        mode_fields = unpack_next(mode_fields)
+        unpacked += 1
     mode_fields = jnp.transpose(mode_fields, (0, 1, 2, 4, 3, 5))
     own_energy = lax.dynamic_slice_in_dim(energy, me * own_freqs, own_freqs)
     return (mode_fields, jnp.transpose(own_energy, (1, 0, 2)))

time: 534 us -> 526 us (0.985)
  waiting for transfers between devices: 179 us -> 246 us
  starting transfers between devices: 156 us -> 127 us
  local copies, waits for them, and re-layouts: 41.9 us -> 20.7 us
  blocking collectives: 13.4 us -> 0 us
  Pallas kernels: 132 us -> 121 us
    ppermute x35, waiting for transfers between devices: 170 us -> 231 us  [send(): return lax.ppermute(piece, owner_axes, hops)]
    ppermute x35, starting transfers between devices: 152 us -> 113 us  [send(): return lax.ppermute(piece, owner_axes, hops)]
    unnamed x120 -> x68, local copies, waits for them, and re-layouts: 29.2 us -> 10.4 us
    pallas_call x4, Pallas kernels: 54.8 us -> 37.5 us  [coeffs_and_gram(): pl.pallas_call(functools.partial(coeff_kernel, sec_count, sec_local, freq...]
    all_to_all x1 -> x0, blocking collectives: 13.4 us -> none  [local(): gram = lax.all_to_all(gram, axes, split_axis=0, concat_axis=0, tiled=True)]
    all_to_all x0 -> x1, starting transfers between devices: none -> 8.79 us  [local(): gram = lax.all_to_all(gram, axes, split_axis=0, concat_axis=0, tiled=True)]
    all_to_all x0 -> x1, waiting for transfers between devices: none -> 8.2 us  [local(): gram = lax.all_to_all(gram, axes, split_axis=0, concat_axis=0, tiled=True)]
  transfers between devices with their start and end apart: 36 -> 37, of which waited for: 9 -> 13; matrix products, arithmetic and copies ran while one was open for 3% -> 3% of each run, Pallas kernels for 21% -> 20%
where the time goes in v5:
time: 526 us; the launch traced here: 524 us
  waiting for transfers between devices  246 us (47%)
  starting transfers between devices  127 us (24%)
  Pallas kernels  121 us (23%)
  local copies, waits for them, and re-layouts  20.7 us (4%)
  other arithmetic  6.63 us (1%)
    ppermute x35, waiting for transfers between devices, send(): return lax.ppermute(piece, owner_axes, hops)  231 us
    ppermute x35, starting transfers between devices, send(): return lax.ppermute(piece, owner_axes, hops)  113 us
    pallas_call x32, Pallas kernels, take(): pl.pallas_call(take_kernel, grid_spec=pltpu.PrefetchScalarGridSpec(num_sc...  41.3 us
    pallas_call x4, Pallas kernels, coeffs_and_gram(): pl.pallas_call(functools.partial(coeff_kernel, sec_count, sec_local, freq...  37.5 us
    pallas_call x8, Pallas kernels, mix(): pl.pallas_call(functools.partial(mix_kernel, orders, parts), grid_spec=pl...  24 us
    pallas_call x8, Pallas kernels, unpack(): pl.pallas_call(unpack_kernel, grid_spec=pltpu.PrefetchScalarGridSpec(num_...  14.3 us
  transfers between devices with their start and end apart: 37, of which 13 were waited for; matrix products, arithmetic and copies ran while one was open for 3% of the time, Pallas kernels for 20%

profile of v5, /device:TPU:16, one launch (start us, length us, event | category | flops | bytes accessed | tf_op | source)
XLA Modules:
  0.0 523.7 jit_solution(3309234322985249171)
XLA Ops:
  8.9 2.0 take.36
  12.7 2.0 take.37
  14.7 2.2 collective-permute-start.4
  23.6 2.0 take.41
  35.4 51.7 %collective-permute-done.2.refs_3_ = bf16[4,296,256]{2,1,0:T(8,128)(2,1)} collective-permute-done((bf16[4,296,256]{2,1,0:T(8,128)(2,1)}, bf16[4,296,256]{2,1,0:T(8,128)(2,1)}, u32[]{:S(2)}, u32[]{:S(2)}) %collective-permute-start.2) | collective-permute-done | bytes 606240 | tf_op jit(solution)/shard_map/ppermute | solution.py:398
  88.6 13.0 %collective-permute-start.8 = (bf16[4,296,256]{2,1,0:T(8,128)(2,1)}, bf16[4,296,256]{2,1,0:T(8,128)(2,1)}, u32[]{:S(2)}, u32[]{:S(2)}) collective-permute-start(bf16[4,296,256]{2,1,0:T(8,128)(2,1)} %take.42), channel_id=1, source_target_pairs={{0,8},{4,12},{8,16},{12,20},{16,24},{20,28},{24,0},{28,4},{1,9},{5... | collective-permute-start | bytes 1818632 | tf_op jit(solution)/shard_map/ppermute | solution.py:398
  101.8 2.9 multiply_bitcast_fusion
  104.7 10.8 %collective-permute-start.9 = (bf16[4,296,256]{2,1,0:T(8,128)(2,1)}, bf16[4,296,256]{2,1,0:T(8,128)(2,1)}, u32[]{:S(2)}, u32[]{:S(2)}) collective-permute-start(bf16[4,296,256]{2,1,0:T(8,128)(2,1)} %copy-done.2), channel_id=1, source_target_pairs={{0,12},{4,8},{8,20},{12,16},{16,28},{20,24},{24,4},{28,0},{1,13},{... | collective-permute-start | bytes 1818632 | tf_op jit(solution)/shard_map/ppermute | solution.py:398
  115.6 34.0 %collective-permute-done.6.refs_7_ = bf16[4,296,256]{2,1,0:T(8,128)(2,1)} collective-permute-done((bf16[4,296,256]{2,1,0:T(8,128)(2,1)}, bf16[4,296,256]{2,1,0:T(8,128)(2,1)}, u32[]{:S(2)}, u32[]{:S(2)}) %collective-permute-start.6) | collective-permute-done | bytes 606240 | tf_op jit(solution)/shard_map/ppermute | solution.py:398
  149.6 2.5 collective-permute-start.12
  159.8 5.1 reshape.543.azimuth_ref
  167.6 10.3 %coeffs_and_gram.4 = (bf16[32,256,256]{2,1,0:T(8,128)(2,1)}, f32[32,16,128]{2,1,0:T(8,128)S(1)}) custom-call(s32[2]{0:T(128)S(1)} %pad_add_fusion.place_ref, bf16[2,2,256,168]{3,2,1,0:T(8,128)(2,1)S(1)} %copy.43.time_ref, bf16[128,256]{1,0:T(8,128)(2,1)S(1)} %reshape.543.azimuth_ref, f32[1,256]{1,0:T(1,128)S(1)} %bitcast.98, ...), custom_call_target="tpu_custom_call" | custom-call | flops 3556769792 | bytes 9043968 | tf_op jit(solution)/shard_map/coeffs_and_gram/pallas_call | solution.py:153
  182.8 22.9 %collective-permute-start.15 = (bf16[4,296,128]{2,1,0:T(8,128)(2,1)S(1)}, bf16[4,296,128]{2,1,0:T(8,128)(2,1)S(1)}, u32[]{:S(2)}, u32[]{:S(2)}) collective-permute-start(bf16[4,296,128]{2,1,0:T(8,128)(2,1)S(1)} %take.50), channel_id=1, source_target_pairs={{0,8},{4,12},{8,16},{12,20},{16,24},{20,28},{24,0},{28,4},{1,9},{5... | collective-permute-start | bytes 909320 | tf_op jit(solution)/shard_map/ppermute | solution.py:398
  205.7 13.9 %collective-permute-start.16 = (bf16[4,296,128]{2,1,0:T(8,128)(2,1)S(1)}, bf16[4,296,128]{2,1,0:T(8,128)(2,1)S(1)}, u32[]{:S(2)}, u32[]{:S(2)}) collective-permute-start(bf16[4,296,128]{2,1,0:T(8,128)(2,1)S(1)} %take.51), channel_id=1, source_target_pairs={{0,12},{4,8},{8,20},{12,16},{16,28},{20,24},{24,4},{28,0},{1,13},{... | collective-permute-start | bytes 909320 | tf_op jit(solution)/shard_map/ppermute | solution.py:398
  219.6 14.9 %collective-permute-done.13.refs_7_ = bf16[4,296,256]{2,1,0:T(8,128)(2,1)} collective-permute-done((bf16[4,296,256]{2,1,0:T(8,128)(2,1)S(1)}, bf16[4,296,256]{2,1,0:T(8,128)(2,1)}, u32[]{:S(2)}, u32[]{:S(2)}) %collective-permute-start.13) | collective-permute-done | bytes 606240 | tf_op jit(solution)/shard_map/ppermute | solution.py:398
  234.5 10.4 %coeffs_and_gram.5 = (bf16[32,256,256]{2,1,0:T(8,128)(2,1)}, f32[32,16,128]{2,1,0:T(8,128)S(1)}) custom-call(s32[2]{0:T(128)S(1)} %pad_add_fusion.place_ref, bf16[2,2,256,168]{3,2,1,0:T(8,128)(2,1)S(1)} %copy.43.time_ref, bf16[128,256]{1,0:T(8,128)(2,1)S(1)} %copy-done.8, f32[1,256]{1,0:T(1,128)S(1)} %bitcast.99, ...), custom_call_target="tpu_custom_call" | custom-call | flops 3556769792 | bytes 9043968 | tf_op jit(solution)/shard_map/coeffs_and_gram/pallas_call | solution.py:153
  250.8 2.5 collective-permute-start.19
  264.1 17.8 %collective-permute-start.23 = (bf16[4,296,128]{2,1,0:T(8,128)(2,1)S(1)}, bf16[4,296,128]{2,1,0:T(8,128)(2,1)S(1)}, u32[]{:S(2)}, u32[]{:S(2)}) collective-permute-start(bf16[4,296,128]{2,1,0:T(8,128)(2,1)S(1)} %take.59), channel_id=1, source_target_pairs={{0,12},{4,8},{8,20},{12,16},{16,28},{20,24},{24,4},{28,0},{1,13},{... | collective-permute-start | bytes 909320 | tf_op jit(solution)/shard_map/ppermute | solution.py:398
  281.9 14.7 %collective-permute-done.20.refs_7_ = bf16[4,296,128]{2,1,0:T(8,128)(2,1)} collective-permute-done((bf16[4,296,128]{2,1,0:T(8,128)(2,1)S(1)}, bf16[4,296,128]{2,1,0:T(8,128)(2,1)}, u32[]{:S(2)}, u32[]{:S(2)}) %collective-permute-start.20) | collective-permute-done | bytes 303136 | tf_op jit(solution)/shard_map/ppermute | solution.py:398
  296.6 2.5 collective-permute-start.26
  303.5 8.7 %coeffs_and_gram.6 = (bf16[32,256,128]{2,1,0:T(8,128)(2,1)S(1)}, f32[32,16,128]{2,1,0:T(8,128)S(1)}) custom-call(s32[2]{0:T(128)S(1)} %copy-done.30, bf16[2,2,256,168]{3,2,1,0:T(8,128)(2,1)S(1)} %copy.43.time_ref, bf16[128,256]{1,0:T(8,128)(2,1)S(1)} %copy-done.9, f32[1,128]{1,0:T(1,128)S(1)} %get-tuple-element.32.weight_ref, ...), custom_call_target="tpu_custom_call" | custom-call | flops 1778384896 | bytes 4521984 | tf_op jit(solution)/shard_map/coeffs_and_gram/pallas_call | solution.py:153
  312.2 7.4 %collective-permute-done.23.refs_3_ = bf16[4,296,128]{2,1,0:T(8,128)(2,1)S(1)} collective-permute-done((bf16[4,296,128]{2,1,0:T(8,128)(2,1)S(1)}, bf16[4,296,128]{2,1,0:T(8,128)(2,1)S(1)}, u32[]{:S(2)}, u32[]{:S(2)}) %collective-permute-start.23) | collective-permute-done | bytes 303136 | tf_op jit(solution)/shard_map/ppermute | solution.py:398
  319.7 3.0 collective-permute-done.26.refs_6_
  322.7 5.8 %collective-permute-done.27.refs_7_ = bf16[4,296,128]{2,1,0:T(8,128)(2,1)S(1)} collective-permute-done((bf16[4,296,128]{2,1,0:T(8,128)(2,1)S(1)}, bf16[4,296,128]{2,1,0:T(8,128)(2,1)S(1)}, u32[]{:S(2)}, u32[]{:S(2)}) %collective-permute-start.27) | collective-permute-done | bytes 303136 | tf_op jit(solution)/shard_map/ppermute | solution.py:398
  328.4 8.1 %coeffs_and_gram.7 = (bf16[32,256,128]{2,1,0:T(8,128)(2,1)S(1)}, f32[32,16,128]{2,1,0:T(8,128)}) custom-call(s32[2]{0:T(128)S(1)} %copy-done.30, bf16[2,2,256,168]{3,2,1,0:T(8,128)(2,1)S(1)} %copy.43.time_ref, bf16[128,256]{1,0:T(8,128)(2,1)S(1)} %copy-done.9, f32[1,128]{1,0:T(1,128)S(1)} %get-tuple-element.33.weight_ref, ...), custom_call_target="tpu_custom_call" | custom-call | flops 1778384896 | bytes 4521984 | tf_op jit(solution)/shard_map/coeffs_and_gram/pallas_call | solution.py:153
  337.8 8.8 %all-to-all-start = ((f32[32,1,16,128]{3,2,1,0:T(8,128)}), f32[32,1,16,128]{3,2,1,0:T(8,128)S(1)}, u32[]{:S(2)}, u32[]{:S(2)}) async-start(f32[32,1,16,128]{3,2,1,0:T(8,128)} %bitcast.39), calls=%async_computation | async-start | bytes 524288 | tf_op jit(solution)/shard_map/all_to_all | solution.py:458
  346.6 8.2 %all-to-all-done = f32[32,1,16,128]{3,2,1,0:T(8,128)S(1)} async-done(((f32[32,1,16,128]{3,2,1,0:T(8,128)}), f32[32,1,16,128]{3,2,1,0:T(8,128)S(1)}, u32[]{:S(2)}, u32[]{:S(2)}) %all-to-all-start) | async-done | bytes 262176 | tf_op jit(solution)/shard_map/all_to_all | solution.py:458
  355.7 4.0 subspace.1
  362.5 4.9 all-to-all-start.1
  367.9 6.9 %all-to-all-done.1 = bf16[32,1,18,128]{3,2,1,0:T(8,128)(2,1)S(1)} async-done(((bf16[32,1,18,128]{3,2,1,0:T(8,128)(2,1)}), bf16[32,1,18,128]{3,2,1,0:T(8,128)(2,1)S(1)}, u32[]{:S(2)}, u32[]{:S(2)}) %all-to-all-start.1) | async-done | bytes 147488 | tf_op jit(solution)/shard_map/all_to_all | solution.py:475
  377.0 3.0 mix.8.refs_4_
  381.8 3.2 mix.9.refs_4_
  386.2 3.1 mix.10.refs_4_
  390.7 2.2 mix.11.refs_4_
  392.9 3.1 mix.12.refs_4_
  397.2 3.1 mix.13.refs_4_
  400.4 2.5 collective-permute-start.32
  402.8 63.8 %collective-permute-done.28 = bf16[3,4,128,256]{3,2,1,0:T(8,128)(2,1)} collective-permute-done((bf16[3,4,128,256]{3,2,1,0:T(8,128)(2,1)}, bf16[3,4,128,256]{3,2,1,0:T(8,128)(2,1)}, u32[]{:S(2)}, u32[]{:S(2)}) %collective-permute-start.28) | collective-permute-done | bytes 786464 | tf_op jit(solution)/shard_map/ppermute | solution.py:398
  466.6 2.1 unpack.8.refs_5_.refs_0_
  468.7 3.1 mix.14.refs_4_
  471.8 11.7 %collective-permute-done.29 = bf16[3,4,128,256]{3,2,1,0:T(8,128)(2,1)} collective-permute-done((bf16[3,4,128,256]{3,2,1,0:T(8,128)(2,1)}, bf16[3,4,128,256]{3,2,1,0:T(8,128)(2,1)}, u32[]{:S(2)}, u32[]{:S(2)}) %collective-permute-start.29) | collective-permute-done | bytes 786464 | tf_op jit(solution)/shard_map/ppermute | solution.py:398
  483.5 2.1 unpack.9.refs_5_.refs_0_
  485.6 3.2 mix.15
  489.6 2.1 unpack.10.refs_0_
  492.6 2.1 unpack.12.refs_0_
  494.7 23.9 %collective-permute-done.32 = bf16[3,4,128,256]{3,2,1,0:T(8,128)(2,1)} collective-permute-done((bf16[3,4,128,256]{3,2,1,0:T(8,128)(2,1)}, bf16[3,4,128,256]{3,2,1,0:T(8,128)(2,1)}, u32[]{:S(2)}, u32[]{:S(2)}) %collective-permute-start.32) | collective-permute-done | bytes 786464 | tf_op jit(solution)/shard_map/ppermute | solution.py:398
  518.6 2.1 unpack.13.refs_0_
  520.7 2.1 unpack.14.refs_0_
  (196 shorter events, 80.1 us)
Async XLA Ops:
  1.8 31.4 %collective-permute-start = (bf16[4,296,256]{2,1,0:T(8,128)(2,1)S(1)}, bf16[4,296,256]{2,1,0:T(8,128)(2,1)}, u32[]{:S(2)}, u32[]{:S(2)}) collective-permute-start(bf16[4,296,256]{2,1,0:T(8,128)(2,1)S(1)} %take.33), channel_id=1, source_target_pairs={{0,4},{4,0},{8,12},{12,8},{16,20},{20,16},{24,28},{28,24},{1,5},{5... | collective-permute-start | bytes 1818632 | tf_op jit(solution)/shard_map/ppermute | solution.py:398
  5.3 29.7 %collective-permute-start.1 = (bf16[4,296,256]{2,1,0:T(8,128)(2,1)}, bf16[4,296,256]{2,1,0:T(8,128)(2,1)}, u32[]{:S(2)}, u32[]{:S(2)}) collective-permute-start(bf16[4,296,256]{2,1,0:T(8,128)(2,1)} %take.34), channel_id=1, source_target_pairs={{0,8},{4,12},{8,16},{12,20},{16,24},{20,28},{24,0},{28,4},{1,9},{5... | collective-permute-start | bytes 1818632 | tf_op jit(solution)/shard_map/ppermute | solution.py:398
  8.9 78.3 %collective-permute-start.2 = (bf16[4,296,256]{2,1,0:T(8,128)(2,1)}, bf16[4,296,256]{2,1,0:T(8,128)(2,1)}, u32[]{:S(2)}, u32[]{:S(2)}) collective-permute-start(bf16[4,296,256]{2,1,0:T(8,128)(2,1)} %take.35), channel_id=1, source_target_pairs={{0,12},{4,8},{8,20},{12,16},{16,28},{20,24},{24,4},{28,0},{1,13},{... | collective-permute-start | bytes 1818632 | tf_op jit(solution)/shard_map/ppermute | solution.py:398
  10.9 77.8 %collective-permute-start.3 = (bf16[4,296,256]{2,1,0:T(8,128)(2,1)}, bf16[4,296,256]{2,1,0:T(8,128)(2,1)}, u32[]{:S(2)}, u32[]{:S(2)}) collective-permute-start(bf16[4,296,256]{2,1,0:T(8,128)(2,1)} %take.36), channel_id=1, source_target_pairs={{0,16},{4,20},{8,24},{12,28},{16,0},{20,4},{24,8},{28,12},{1,17},{... | collective-permute-start | bytes 1818632 | tf_op jit(solution)/shard_map/ppermute | solution.py:398
  14.7 90.0 %collective-permute-start.4 = (bf16[4,296,256]{2,1,0:T(8,128)(2,1)}, bf16[4,296,256]{2,1,0:T(8,128)(2,1)}, u32[]{:S(2)}, u32[]{:S(2)}) collective-permute-start(bf16[4,296,256]{2,1,0:T(8,128)(2,1)} %take.37), channel_id=1, source_target_pairs={{0,20},{4,16},{8,28},{12,24},{16,4},{20,0},{24,12},{28,8},{1,21},{... | collective-permute-start | bytes 1818632 | tf_op jit(solution)/shard_map/ppermute | solution.py:398
  33.2 82.4 %collective-permute-start.5 = (bf16[4,296,256]{2,1,0:T(8,128)(2,1)}, bf16[4,296,256]{2,1,0:T(8,128)(2,1)}, u32[]{:S(2)}, u32[]{:S(2)}) collective-permute-start(bf16[4,296,256]{2,1,0:T(8,128)(2,1)} %take.38), channel_id=1, source_target_pairs={{0,24},{4,28},{8,0},{12,4},{16,8},{20,12},{24,16},{28,20},{1,25},{... | collective-permute-start | bytes 1818632 | tf_op jit(solution)/shard_map/ppermute | solution.py:398
  35.0 114.6 %collective-permute-start.6 = (bf16[4,296,256]{2,1,0:T(8,128)(2,1)}, bf16[4,296,256]{2,1,0:T(8,128)(2,1)}, u32[]{:S(2)}, u32[]{:S(2)}) collective-permute-start(bf16[4,296,256]{2,1,0:T(8,128)(2,1)} %take.39), channel_id=1, source_target_pairs={{0,28},{4,24},{8,4},{12,0},{16,12},{20,8},{24,20},{28,16},{1,29},{... | collective-permute-start | bytes 1818632 | tf_op jit(solution)/shard_map/ppermute | solution.py:398
  87.1 62.5 %collective-permute-start.7 = (bf16[4,296,256]{2,1,0:T(8,128)(2,1)}, bf16[4,296,256]{2,1,0:T(8,128)(2,1)S(1)}, u32[]{:S(2)}, u32[]{:S(2)}) collective-permute-start(bf16[4,296,256]{2,1,0:T(8,128)(2,1)} %take.41), channel_id=1, source_target_pairs={{0,4},{4,0},{8,12},{12,8},{16,20},{20,16},{24,28},{28,24},{1,5},{5... | collective-permute-start | bytes 1818632 | tf_op jit(solution)/shard_map/ppermute | solution.py:398
  88.6 63.5 %collective-permute-start.8 = (bf16[4,296,256]{2,1,0:T(8,128)(2,1)}, bf16[4,296,256]{2,1,0:T(8,128)(2,1)}, u32[]{:S(2)}, u32[]{:S(2)}) collective-permute-start(bf16[4,296,256]{2,1,0:T(8,128)(2,1)} %take.42), channel_id=1, source_target_pairs={{0,8},{4,12},{8,16},{12,20},{16,24},{20,28},{24,0},{28,4},{1,9},{5... | collective-permute-start | bytes 1818632 | tf_op jit(solution)/shard_map/ppermute | solution.py:398
  104.7 77.4 %collective-permute-start.9 = (bf16[4,296,256]{2,1,0:T(8,128)(2,1)}, bf16[4,296,256]{2,1,0:T(8,128)(2,1)}, u32[]{:S(2)}, u32[]{:S(2)}) collective-permute-start(bf16[4,296,256]{2,1,0:T(8,128)(2,1)} %copy-done.2), channel_id=1, source_target_pairs={{0,12},{4,8},{8,20},{12,16},{16,28},{20,24},{24,4},{28,0},{1,13},{... | collective-permute-start | bytes 1818632 | tf_op jit(solution)/shard_map/ppermute | solution.py:398
  115.6 67.2 %collective-permute-start.10 = (bf16[4,296,256]{2,1,0:T(8,128)(2,1)S(1)}, bf16[4,296,256]{2,1,0:T(8,128)(2,1)}, u32[]{:S(2)}, u32[]{:S(2)}) collective-permute-start(bf16[4,296,256]{2,1,0:T(8,128)(2,1)S(1)} %take.44), channel_id=1, source_target_pairs={{0,16},{4,20},{8,24},{12,28},{16,0},{20,4},{24,8},{28,12},{1,17},{... | collective-permute-start | bytes 1818632 | tf_op jit(solution)/shard_map/ppermute | solution.py:398
  149.6 56.0 %collective-permute-start.11 = (bf16[4,296,256]{2,1,0:T(8,128)(2,1)S(1)}, bf16[4,296,256]{2,1,0:T(8,128)(2,1)}, u32[]{:S(2)}, u32[]{:S(2)}) collective-permute-start(bf16[4,296,256]{2,1,0:T(8,128)(2,1)S(1)} %take.45), channel_id=1, source_target_pairs={{0,20},{4,16},{8,28},{12,24},{16,4},{20,0},{24,12},{28,8},{1,21},{... | collective-permute-start | bytes 1818632 | tf_op jit(solution)/shard_map/ppermute | solution.py:398
  149.6 70.0 %collective-permute-start.12 = (bf16[4,296,256]{2,1,0:T(8,128)(2,1)S(1)}, bf16[4,296,256]{2,1,0:T(8,128)(2,1)}, u32[]{:S(2)}, u32[]{:S(2)}) collective-permute-start(bf16[4,296,256]{2,1,0:T(8,128)(2,1)S(1)} %take.46), channel_id=1, source_target_pairs={{0,24},{4,28},{8,0},{12,4},{16,8},{20,12},{24,16},{28,20},{1,25},{... | collective-permute-start | bytes 1818632 | tf_op jit(solution)/shard_map/ppermute | solution.py:398
  152.1 82.3 %collective-permute-start.13 = (bf16[4,296,256]{2,1,0:T(8,128)(2,1)S(1)}, bf16[4,296,256]{2,1,0:T(8,128)(2,1)}, u32[]{:S(2)}, u32[]{:S(2)}) collective-permute-start(bf16[4,296,256]{2,1,0:T(8,128)(2,1)S(1)} %take.47), channel_id=1, source_target_pairs={{0,28},{4,24},{8,4},{12,0},{16,12},{20,8},{24,20},{28,16},{1,29},{... | collective-permute-start | bytes 1818632 | tf_op jit(solution)/shard_map/ppermute | solution.py:398
  165.8 68.7 %copy-start.29 = (s32[2]{0:T(128)}, s32[2]{0:T(128)S(1)}, u32[]{:S(2)}) copy-start(s32[2]{0:T(128)S(1)} %pad_add_fusion.place_ref) | copy-start | bytes 28
  166.5 67.9 %copy-start.10 = (f32[256]{0:T(256)}, f32[256]{0:T(256)S(1)}, u32[]{:S(2)}) copy-start(f32[256]{0:T(256)S(1)} %select_reduce_fusion) | copy-start | bytes 3076
  181.0 53.5 %copy-start.4 = (bf16[4,296,256]{2,1,0:T(8,128)(2,1)S(1)}, bf16[4,296,256]{2,1,0:T(8,128)(2,1)}, u32[]{:S(2)}) copy-start(bf16[4,296,256]{2,1,0:T(8,128)(2,1)} %copy-done.3) | copy-start | bytes 1818628
  181.0 53.5 %copy-start.8 = (bf16[128,256]{1,0:T(8,128)(2,1)S(1)}, bf16[128,256]{1,0:T(8,128)(2,1)}, u32[]{:S(2)}) copy-start(bf16[128,256]{1,0:T(8,128)(2,1)} %copy-done.7) | copy-start | bytes 196612
  181.0 53.5 %copy-start.14 = (bf16[4,296,256]{2,1,0:T(8,128)(2,1)S(1)}, bf16[4,296,256]{2,1,0:T(8,128)(2,1)}, u32[]{:S(2)}) copy-start(bf16[4,296,256]{2,1,0:T(8,128)(2,1)} %copy-done.13) | copy-start | bytes 1818628
  182.1 67.9 %collective-permute-start.14 = (bf16[4,296,128]{2,1,0:T(8,128)(2,1)S(1)}, bf16[4,296,128]{2,1,0:T(8,128)(2,1)S(1)}, u32[]{:S(2)}, u32[]{:S(2)}) collective-permute-start(bf16[4,296,128]{2,1,0:T(8,128)(2,1)S(1)} %take.49), channel_id=1, source_target_pairs={{0,4},{4,0},{8,12},{12,8},{16,20},{20,16},{24,28},{28,24},{1,5},{5... | collective-permute-start | bytes 909320 | tf_op jit(solution)/shard_map/ppermute | solution.py:398
  182.8 70.5 %collective-permute-start.15 = (bf16[4,296,128]{2,1,0:T(8,128)(2,1)S(1)}, bf16[4,296,128]{2,1,0:T(8,128)(2,1)S(1)}, u32[]{:S(2)}, u32[]{:S(2)}) collective-permute-start(bf16[4,296,128]{2,1,0:T(8,128)(2,1)S(1)} %take.50), channel_id=1, source_target_pairs={{0,8},{4,12},{8,16},{12,20},{16,24},{20,28},{24,0},{28,4},{1,9},{5... | collective-permute-start | bytes 909320 | tf_op jit(solution)/shard_map/ppermute | solution.py:398
  205.7 50.2 %collective-permute-start.16 = (bf16[4,296,128]{2,1,0:T(8,128)(2,1)S(1)}, bf16[4,296,128]{2,1,0:T(8,128)(2,1)S(1)}, u32[]{:S(2)}, u32[]{:S(2)}) collective-permute-start(bf16[4,296,128]{2,1,0:T(8,128)(2,1)S(1)} %take.51), channel_id=1, source_target_pairs={{0,12},{4,8},{8,20},{12,16},{16,28},{20,24},{24,4},{28,0},{1,13},{... | collective-permute-start | bytes 909320 | tf_op jit(solution)/shard_map/ppermute | solution.py:398
  219.6 37.5 %collective-permute-start.17 = (bf16[4,296,128]{2,1,0:T(8,128)(2,1)S(1)}, bf16[4,296,128]{2,1,0:T(8,128)(2,1)S(1)}, u32[]{:S(2)}, u32[]{:S(2)}) collective-permute-start(bf16[4,296,128]{2,1,0:T(8,128)(2,1)S(1)} %take.52), channel_id=1, source_target_pairs={{0,16},{4,20},{8,24},{12,28},{16,0},{20,4},{24,8},{28,12},{1,17},{... | collective-permute-start | bytes 909320 | tf_op jit(solution)/shard_map/ppermute | solution.py:398
  250.0 14.2 %collective-permute-start.18 = (bf16[4,296,128]{2,1,0:T(8,128)(2,1)S(1)}, bf16[4,296,128]{2,1,0:T(8,128)(2,1)S(1)}, u32[]{:S(2)}, u32[]{:S(2)}) collective-permute-start(bf16[4,296,128]{2,1,0:T(8,128)(2,1)S(1)} %take.53), channel_id=1, source_target_pairs={{0,20},{4,16},{8,28},{12,24},{16,4},{20,0},{24,12},{28,8},{1,21},{... | collective-permute-start | bytes 909320 | tf_op jit(solution)/shard_map/ppermute | solution.py:398
  250.8 31.1 %collective-permute-start.19 = (bf16[4,296,128]{2,1,0:T(8,128)(2,1)S(1)}, bf16[4,296,128]{2,1,0:T(8,128)(2,1)}, u32[]{:S(2)}, u32[]{:S(2)}) collective-permute-start(bf16[4,296,128]{2,1,0:T(8,128)(2,1)S(1)} %take.54), channel_id=1, source_target_pairs={{0,24},{4,28},{8,0},{12,4},{16,8},{20,12},{24,16},{28,20},{1,25},{... | collective-permute-start | bytes 909320 | tf_op jit(solution)/shard_map/ppermute | solution.py:398
  254.0 42.6 %collective-permute-start.20 = (bf16[4,296,128]{2,1,0:T(8,128)(2,1)S(1)}, bf16[4,296,128]{2,1,0:T(8,128)(2,1)}, u32[]{:S(2)}, u32[]{:S(2)}) collective-permute-start(bf16[4,296,128]{2,1,0:T(8,128)(2,1)S(1)} %take.55), channel_id=1, source_target_pairs={{0,28},{4,24},{8,4},{12,0},{16,12},{20,8},{24,20},{28,16},{1,29},{... | collective-permute-start | bytes 909320 | tf_op jit(solution)/shard_map/ppermute | solution.py:398
  256.6 40.0 %collective-permute-start.21 = (bf16[4,296,128]{2,1,0:T(8,128)(2,1)S(1)}, bf16[4,296,128]{2,1,0:T(8,128)(2,1)S(1)}, u32[]{:S(2)}, u32[]{:S(2)}) collective-permute-start(bf16[4,296,128]{2,1,0:T(8,128)(2,1)S(1)} %take.57), channel_id=1, source_target_pairs={{0,4},{4,0},{8,12},{12,8},{16,20},{20,16},{24,28},{28,24},{1,5},{5... | collective-permute-start | bytes 909320 | tf_op jit(solution)/shard_map/ppermute | solution.py:398
  257.8 41.3 %collective-permute-start.22 = (bf16[4,296,128]{2,1,0:T(8,128)(2,1)S(1)}, bf16[4,296,128]{2,1,0:T(8,128)(2,1)S(1)}, u32[]{:S(2)}, u32[]{:S(2)}) collective-permute-start(bf16[4,296,128]{2,1,0:T(8,128)(2,1)S(1)} %take.58), channel_id=1, source_target_pairs={{0,8},{4,12},{8,16},{12,20},{16,24},{20,28},{24,0},{28,4},{1,9},{5... | collective-permute-start | bytes 909320 | tf_op jit(solution)/shard_map/ppermute | solution.py:398
  263.0 38.0 %copy-start.11 = (f32[256]{0:T(256)S(1)}, f32[256]{0:T(256)}, u32[]{:S(2)}) copy-start(f32[256]{0:T(256)} %copy-done.10) | copy-start | bytes 3076
  264.1 37.9 %copy-start.27 = (bf16[4,296,128]{2,1,0:T(8,128)(2,1)}, bf16[4,296,128]{2,1,0:T(8,128)(2,1)S(1)}, u32[]{:S(2)}) copy-start(bf16[4,296,128]{2,1,0:T(8,128)(2,1)S(1)} %collective-permute-done.18.refs_5_) | copy-start | bytes 909316
  264.1 55.5 %collective-permute-start.23 = (bf16[4,296,128]{2,1,0:T(8,128)(2,1)S(1)}, bf16[4,296,128]{2,1,0:T(8,128)(2,1)S(1)}, u32[]{:S(2)}, u32[]{:S(2)}) collective-permute-start(bf16[4,296,128]{2,1,0:T(8,128)(2,1)S(1)} %take.59), channel_id=1, source_target_pairs={{0,12},{4,8},{8,20},{12,16},{16,28},{20,24},{24,4},{28,0},{1,13},{... | collective-permute-start | bytes 909320 | tf_op jit(solution)/shard_map/ppermute | solution.py:398
  281.9 37.8 %collective-permute-start.24 = (bf16[4,296,128]{2,1,0:T(8,128)(2,1)S(1)}, bf16[4,296,128]{2,1,0:T(8,128)(2,1)S(1)}, u32[]{:S(2)}, u32[]{:S(2)}) collective-permute-start(bf16[4,296,128]{2,1,0:T(8,128)(2,1)S(1)} %take.60), channel_id=1, source_target_pairs={{0,16},{4,20},{8,24},{12,28},{16,0},{20,4},{24,8},{28,12},{1,17},{... | collective-permute-start | bytes 909320 | tf_op jit(solution)/shard_map/ppermute | solution.py:398
  296.6 23.1 %collective-permute-start.25 = (bf16[4,296,128]{2,1,0:T(8,128)(2,1)S(1)}, bf16[4,296,128]{2,1,0:T(8,128)(2,1)S(1)}, u32[]{:S(2)}, u32[]{:S(2)}) collective-permute-start(bf16[4,296,128]{2,1,0:T(8,128)(2,1)S(1)} %take.61), channel_id=1, source_target_pairs={{0,20},{4,16},{8,28},{12,24},{16,4},{20,0},{24,12},{28,8},{1,21},{... | collective-permute-start | bytes 909320 | tf_op jit(solution)/shard_map/ppermute | solution.py:398
  296.6 26.1 %collective-permute-start.26 = (bf16[4,296,128]{2,1,0:T(8,128)(2,1)S(1)}, bf16[4,296,128]{2,1,0:T(8,128)(2,1)S(1)}, u32[]{:S(2)}, u32[]{:S(2)}) collective-permute-start(bf16[4,296,128]{2,1,0:T(8,128)(2,1)S(1)} %take.62), channel_id=1, source_target_pairs={{0,24},{4,28},{8,0},{12,4},{16,8},{20,12},{24,16},{28,20},{1,25},{... | collective-permute-start | bytes 909320 | tf_op jit(solution)/shard_map/ppermute | solution.py:398
  299.1 29.3 %collective-permute-start.27 = (bf16[4,296,128]{2,1,0:T(8,128)(2,1)S(1)}, bf16[4,296,128]{2,1,0:T(8,128)(2,1)S(1)}, u32[]{:S(2)}, u32[]{:S(2)}) collective-permute-start(bf16[4,296,128]{2,1,0:T(8,128)(2,1)S(1)} %take.63), channel_id=1, source_target_pairs={{0,28},{4,24},{8,4},{12,0},{16,12},{20,8},{24,20},{28,16},{1,29},{... | collective-permute-start | bytes 909320 | tf_op jit(solution)/shard_map/ppermute | solution.py:398
  303.2 25.2 %copy-start.24 = (bf16[4,296,128]{2,1,0:T(8,128)(2,1)S(1)}, bf16[4,296,128]{2,1,0:T(8,128)(2,1)}, u32[]{:S(2)}) copy-start(bf16[4,296,128]{2,1,0:T(8,128)(2,1)} %copy-done.23) | copy-start | bytes 909316
  303.2 25.2 %copy-start.26 = (bf16[4,296,128]{2,1,0:T(8,128)(2,1)S(1)}, bf16[4,296,128]{2,1,0:T(8,128)(2,1)}, u32[]{:S(2)}) copy-start(bf16[4,296,128]{2,1,0:T(8,128)(2,1)} %copy-done.25) | copy-start | bytes 909316
  312.2 34.3 %copy-start.12 = (f32[256]{0:T(256)S(1)}, f32[256]{0:T(256)}, u32[]{:S(2)}) copy-start(f32[256]{0:T(256)} %copy-done.10) | copy-start | bytes 3076
  312.2 55.3 %copy-start.31 = (bf16[2,2,2]{2,1,0:T(2,128)(2,1)S(1)}, bf16[2,2,2]{2,1,0:T(2,128)(2,1)}, u32[]{:S(2)}) copy-start(bf16[2,2,2]{2,1,0:T(2,128)(2,1)} %constant.299.clone) | copy-start | bytes 52
  337.8 17.0 %all-to-all-start = ((f32[32,1,16,128]{3,2,1,0:T(8,128)}), f32[32,1,16,128]{3,2,1,0:T(8,128)S(1)}, u32[]{:S(2)}, u32[]{:S(2)}) async-start(f32[32,1,16,128]{3,2,1,0:T(8,128)} %bitcast.39), calls=%async_computation | async-start | bytes 524288 | tf_op jit(solution)/shard_map/all_to_all | solution.py:458
  362.5 12.3 %all-to-all-start.1 = ((bf16[32,1,18,128]{3,2,1,0:T(8,128)(2,1)}), bf16[32,1,18,128]{3,2,1,0:T(8,128)(2,1)S(1)}, u32[]{:S(2)}, u32[]{:S(2)}) async-start(bf16[32,1,18,128]{3,2,1,0:T(8,128)(2,1)} %broadcast_in_dim.27), calls=%async_computation.1 | async-start | bytes 393216 | tf_op jit(solution)/shard_map/all_to_all | solution.py:475
  380.0 86.6 %collective-permute-start.28 = (bf16[3,4,128,256]{3,2,1,0:T(8,128)(2,1)}, bf16[3,4,128,256]{3,2,1,0:T(8,128)(2,1)}, u32[]{:S(2)}, u32[]{:S(2)}) collective-permute-start(bf16[3,4,128,256]{3,2,1,0:T(8,128)(2,1)} %mix.8.refs_4_), channel_id=1, source_target_pairs={{0,16},{4,20},{8,24},{12,28},{16,0},{20,4},{24,8},{28,12},{1,17},{... | collective-permute-start | bytes 2359304 | tf_op jit(solution)/shard_map/ppermute | solution.py:398
  385.0 98.5 %collective-permute-start.29 = (bf16[3,4,128,256]{3,2,1,0:T(8,128)(2,1)}, bf16[3,4,128,256]{3,2,1,0:T(8,128)(2,1)}, u32[]{:S(2)}, u32[]{:S(2)}) collective-permute-start(bf16[3,4,128,256]{3,2,1,0:T(8,128)(2,1)} %mix.9.refs_4_), channel_id=1, source_target_pairs={{0,20},{4,16},{8,28},{12,24},{16,4},{20,0},{24,12},{28,8},{1,21},{... | collective-permute-start | bytes 2359304 | tf_op jit(solution)/shard_map/ppermute | solution.py:398
  389.3 100.3 %collective-permute-start.34 = (bf16[3,4,128,256]{3,2,1,0:T(8,128)(2,1)}, bf16[3,4,128,256]{3,2,1,0:T(8,128)(2,1)}, u32[]{:S(2)}, u32[]{:S(2)}) collective-permute-start(bf16[3,4,128,256]{3,2,1,0:T(8,128)(2,1)} %mix.10.refs_4_), channel_id=1, source_target_pairs={{0,4},{4,0},{8,12},{12,8},{16,20},{20,16},{24,28},{28,24},{1,5},{5... | collective-permute-start | bytes 2359304 | tf_op jit(solution)/shard_map/ppermute | solution.py:398
  396.0 96.6 %collective-permute-start.33 = (bf16[3,4,128,256]{3,2,1,0:T(8,128)(2,1)}, bf16[3,4,128,256]{3,2,1,0:T(8,128)(2,1)}, u32[]{:S(2)}, u32[]{:S(2)}) collective-permute-start(bf16[3,4,128,256]{3,2,1,0:T(8,128)(2,1)} %mix.12.refs_4_), channel_id=1, source_target_pairs={{0,8},{4,12},{8,16},{12,20},{16,24},{20,28},{24,0},{28,4},{1,9},{5... | collective-permute-start | bytes 2359304 | tf_op jit(solution)/shard_map/ppermute | solution.py:398
  400.4 118.3 %collective-permute-start.32 = (bf16[3,4,128,256]{3,2,1,0:T(8,128)(2,1)}, bf16[3,4,128,256]{3,2,1,0:T(8,128)(2,1)}, u32[]{:S(2)}, u32[]{:S(2)}) collective-permute-start(bf16[3,4,128,256]{3,2,1,0:T(8,128)(2,1)} %mix.13.refs_4_), channel_id=1, source_target_pairs={{0,12},{4,8},{8,20},{12,16},{16,28},{20,24},{24,4},{28,0},{1,13},{... | collective-permute-start | bytes 2359304 | tf_op jit(solution)/shard_map/ppermute | solution.py:398
  471.8 48.9 %collective-permute-start.31 = (bf16[3,4,128,256]{3,2,1,0:T(8,128)(2,1)}, bf16[3,4,128,256]{3,2,1,0:T(8,128)(2,1)}, u32[]{:S(2)}, u32[]{:S(2)}) collective-permute-start(bf16[3,4,128,256]{3,2,1,0:T(8,128)(2,1)} %mix.14.refs_4_), channel_id=1, source_target_pairs={{0,24},{4,28},{8,0},{12,4},{16,8},{20,12},{24,16},{28,20},{1,25},{... | collective-permute-start | bytes 2359304 | tf_op jit(solution)/shard_map/ppermute | solution.py:398
  488.7 34.0 %collective-permute-start.30 = (bf16[3,4,128,256]{3,2,1,0:T(8,128)(2,1)}, bf16[3,4,128,256]{3,2,1,0:T(8,128)(2,1)S(1)}, u32[]{:S(2)}, u32[]{:S(2)}) collective-permute-start(bf16[3,4,128,256]{3,2,1,0:T(8,128)(2,1)} %mix.15), channel_id=1, source_target_pairs={{0,28},{4,24},{8,4},{12,0},{16,12},{20,8},{24,20},{28,16},{1,29},{... | collective-permute-start | bytes 2359304 | tf_op jit(solution)/shard_map/ppermute | solution.py:398
  (22 other events, 50.8 us)

commit v6 on v5

--- a/solution.py
+++ b/solution.py
@@ -70,31 +70,23 @@
     sectors = spectra.shape[0]
     rows = spectra.shape[2] // NFREQ
 
-    beside = 2 if columns == LANES and sec_count % 2 == 0 else 1
-
     @pl.when(step < sec_local)
     def _():
-        for shift in range(0, sec_count, beside):
+        for shift in range(sec_count):
+            source = lax.rem(place_ref[0] + sec_count - shift, sec_count)
+            own = record_refs[shift * tm_count:(shift + 1) * tm_count]
             for h in range(halves):
                 first = h * (rec_len - span) // (halves - 1)
                 parts = []
                 for j in range(tm_count):
-                    row = []
-                    for n in range(beside):
-                        own = record_refs[(shift + n) * tm_count:(shift + n + 1) * tm_count]
-                        piece = own[0][0, first:first + span]
-                        for x in range(1, tm_count):
-                            here = lax.rem(place_ref[1] + tm_count - x, tm_count) == j
-                            piece = jnp.where(here, own[x][0, first:first + span], piece)
-                        row.append(piece)
-                    wide_piece = row[0] if beside == 1 else jnp.concatenate(row, 1)
-                    part = jnp.dot(time_ref[j, h], wide_piece, preferred_element_type=jnp.float32)
-                    parts.append(part.reshape(NFREQ, rows // tm_count, beside * columns))
-                joined = jnp.stack(parts, 1).reshape(NFREQ * rows, beside * columns)
-                joined = joined.astype(jnp.bfloat16)
-                for n in range(beside):
-                    source = lax.rem(place_ref[0] + sec_count - shift - n, sec_count)
-                    spectra[source * sec_local + step, h] = joined[:, n * columns:(n + 1) * columns]
+                    piece = own[0][0, first:first + span]
+                    for x in range(1, tm_count):
+                        here = lax.rem(place_ref[1] + tm_count - x, tm_count) == j
+                        piece = jnp.where(here, own[x][0, first:first + span], piece)
+                    part = jnp.dot(time_ref[j, h], piece, preferred_element_type=jnp.float32)
+                    parts.append(part.reshape(NFREQ, rows // tm_count, columns))
+                joined = jnp.stack(parts, 1).reshape(NFREQ * rows, columns)
+                spectra[source * sec_local + step, h] = joined.astype(jnp.bfloat16)
 
     @pl.when(step >= sec_local)
     def _():
@@ -111,15 +103,9 @@
                 spectra[:, h, pl.ds(at, rows), :].reshape(sectors * rows, columns)
                 for h in range(halves)
             ]
-            if beside == halves:
-                both = jnp.dot(
-                    azimuth_ref[...], jnp.concatenate(own, 1), preferred_element_type=jnp.float32
-                )
-                parts = [both[:, h * columns:(h + 1) * columns] for h in range(halves)]
-            else:
-                parts = [
-                    jnp.dot(azimuth_ref[...], x, preferred_element_type=jnp.float32) for x in own
-                ]
+            parts = [
+                jnp.dot(azimuth_ref[...], x, preferred_element_type=jnp.float32) for x in own
+            ]
             parts = [x.reshape(2 * orders, depth, columns) for x in parts]
             coeffs = jnp.stack(parts, 1).reshape(2 * wide, columns).astype(jnp.bfloat16)
             coeff_ref[n] = coeffs
@@ -238,8 +224,8 @@
     )(packed)
 
 
-def mix_kernel(orders, parts, owner_ref, mixing_ref, spread_ref, factor_ref, root_ref, *refs):
-    coeff_refs, out_ref = refs[:len(parts)], refs[-1]
+def mix_kernel(orders, fields, owner_ref, mixing_ref, spread_ref, factor_ref, root_ref, *refs):
+    out_ref = refs[-1]
     freqs, own_rows, _ = mixing_ref.shape
     rows = 2 * own_rows
     total = spread_ref.shape[2]
@@ -256,20 +242,20 @@
             0,
         )
         wide = jnp.where(row == column, wide, 0.0).astype(jnp.bfloat16)
-        for (k, low, high), coeff_ref in zip(parts, coeff_refs):
-            fields = jnp.dot(wide, coeff_ref[n], preferred_element_type=jnp.float32)
-            scaled = fields * (factor[:, n:n + 1] * root_ref[:, low:high])
-            out_ref[k, n, :, low:high] = scaled.astype(jnp.bfloat16)
-
-
-def mix(owner, coeffs, parts, mixing, spread, factor, root_weight, owners, orders, fields, after):
+        scale = factor[:, n:n + 1] * root_ref[...]
+        for k in range(fields):
+            mixed = jnp.dot(wide, refs[k][n], preferred_element_type=jnp.float32)
+            out_ref[k, n] = (mixed * scale).astype(jnp.bfloat16)
+
+
+def mix(owner, coeffs, mixing, spread, factor, root_weight, owners, orders, after):
     rows = coeffs[0].shape[1]
     own_rows, depth = mixing.shape[1:]
     out_rows = 2 * own_rows
     columns = root_weight.shape[1]
-    freqs = NFREQ // owners
+    freqs, fields = NFREQ // owners, len(coeffs)
     return pl.pallas_call(
-        functools.partial(mix_kernel, orders, parts),
+        functools.partial(mix_kernel, orders, fields),
         grid_spec=pltpu.PrefetchScalarGridSpec(
             num_scalar_prefetch=1,
             grid=(1,),
@@ -294,18 +280,15 @@
     )(jnp.reshape(owner, (1,)), mixing, spread, factor, root_weight, *coeffs, *after)
 
 
-def take_kernel(place_ref, record_ref, *refs):
-    out_ref = refs[-1]
+def take_kernel(place_ref, record_ref, out_ref):
     out_ref[...] = record_ref[:, 0]
 
 
-def take(by_field, owner, owners, part, after):
+def take(by_field, k, owner, owners):
     sec_local, _, rec_len, cells = by_field.shape
-    k, low, high = part
-    count = high - low
-    own = cells // owners
+    count = cells // owners
     if count % LANES:
-        return lax.dynamic_slice_in_dim(by_field[:, k], owner * own + low, count, 2)
+        return lax.dynamic_slice_in_dim(by_field[:, k], owner * count, count, 2)
     return pl.pallas_call(
         take_kernel,
         grid_spec=pltpu.PrefetchScalarGridSpec(
@@ -313,7 +296,7 @@
             grid=(1,),
             in_specs=[
                 pl.BlockSpec((sec_local, 1, rec_len, count), lambda i, at: (0, k, 0, at[0]))
-            ] + [pl.BlockSpec(memory_space=pl.ANY)] * len(after),
+            ],
             out_specs=pl.BlockSpec((sec_local, rec_len, count), lambda i, at: (0, 0, 0)),
         ),
         out_shape=jax.ShapeDtypeStruct((sec_local, rec_len, count), by_field.dtype),
@@ -322,7 +305,7 @@
             flops=0, bytes_accessed=4 * sec_local * rec_len * count, transcendentals=0
         ),
         name="take",
-    )(jnp.reshape(owner * (own // count) + low // count, (1,)), by_field, *after)
+    )(jnp.reshape(owner, (1,)), by_field)
 
 
 def unpack_kernel(owner_ref, piece_ref, *refs):
@@ -380,9 +363,8 @@
     sec_at, tm_at = lax.axis_index("sector"), lax.axis_index("tm")
     shifts = [(z, x) for z in range(sec_count) for x in range(tm_count)]
     in_order = sorted(
-        [r for r in shifts if r[0] > 0], key=lambda r: (abs(2 * r[0] - sec_count), r)
+        [r for r in shifts if r != (0, 0)], key=lambda r: (r[0] == 0, abs(2 * r[0] - sec_count), r)
     )
-    in_order[2:2] = [r for r in shifts if r[0] == 0 and r[1] > 0] + [(0, 0)]
 
     def owner_after(z, x):
         return (sec_at + z) % sec_count * tm_count + (tm_at + x) % tm_count
@@ -397,9 +379,11 @@
         ]
         return lax.ppermute(piece, owner_axes, hops)
 
-    parts = [(k, 0, part) for k in range(fields)]
-    if part % (2 * LANES) == 0:
-        parts[-1:] = [(fields - 1, 0, part // 2), (fields - 1, part // 2, part)]
+    arrived = []
+    for k in range(fields):
+        got = {r: send(take(by_field, k, owner_after(*r), owners), *r) for r in in_order + [(0, 0)]}
+        arrived.append([got[r] for r in shifts])
+
     time_basis = placed_time_basis(block_start, tm_count)
     half, _ = half_span(blocks // tm_count)
     halves = blocks // tm_count // half
@@ -426,25 +410,11 @@
 
     gram = jnp.zeros((NFREQ, blocks, orders * blocks), jnp.float32)
 
-    def coeffs_of(n, pieces, gram):
-        _, low, high = parts[n]
-        return coeffs_and_gram(
-            jnp.stack([sec_at, tm_at]), pieces, sec_count, time_basis, azimuth, weight[:, low:high], gram
+    coeffs = []
+    for k in range(fields):
+        own, gram = coeffs_and_gram(
+            jnp.stack([sec_at, tm_at]), arrived[k], sec_count, time_basis, azimuth, weight, gram
         )
-
-    coeffs = []
-    arrived = []
-    for own_part in parts:
-        if len(arrived) > 1:
-            own, gram = coeffs_of(len(coeffs), arrived[len(coeffs)], gram)
-            coeffs.append(own)
-            after = (gram,)
-        else:
-            after = ()
-        got = {r: send(take(by_field, owner_after(*r), owners, own_part, after), *r) for r in in_order}
-        arrived.append([got[r] for r in shifts])
-    while len(coeffs) < len(parts):
-        own, gram = coeffs_of(len(coeffs), arrived[len(coeffs)], gram)
         coeffs.append(own)
 
     if own_freqs % space_count == 0:
@@ -489,31 +459,18 @@
         (2, 2, blocks, 2, orders, blocks),
     ).reshape(2, depth, depth * orders)
 
-    mode_fields = None
     sent = []
-    unpacked = 0
-    in_flight = 5
-
-    def unpack_next(mode_fields):
-        owner, piece = sent[unpacked]
-        piece = piece.reshape(fields, own_freqs, 2, orders, MODES, part)
-        return unpack(owner, piece, owners, mode_fields)
-
     before = ()
-    for z, x in in_order:
-        if len(sent) > in_flight and part % LANES == 0:
-            mode_fields = unpack_next(mode_fields)
-            unpacked += 1
-            before = before + (mode_fields,)
+    for z, x in in_order + [(0, 0)]:
         piece = mix(
-            owner_after(z, x), coeffs, parts, mixing, spread, factor, root_weight, owners, orders,
-            fields, before,
+            owner_after(z, x), coeffs, mixing, spread, factor, root_weight, owners, orders, before
         )
         before = (piece,)
         sent.append((owner_after(-z, -x), send(piece, z, x)))
-    while unpacked < len(sent):
-        mode_fields = unpack_next(mode_fields)
-        unpacked += 1
+    mode_fields = None
+    for owner, piece in sent[-1:] + sent[:-1]:
+        piece = piece.reshape(fields, own_freqs, 2, orders, MODES, part)
+        mode_fields = unpack(owner, piece, owners, mode_fields)
     mode_fields = jnp.transpose(mode_fields, (0, 1, 2, 4, 3, 5))
     own_energy = lax.dynamic_slice_in_dim(energy, me * own_freqs, own_freqs)
     return (mode_fields, jnp.transpose(own_energy, (1, 0, 2)))

time: 526 us -> 515 us (0.979)
  waiting for transfers between devices: 246 us -> 317 us
  starting transfers between devices: 127 us -> 61.3 us
  Pallas kernels: 121 us -> 98.1 us
  local copies, waits for them, and re-layouts: 20.7 us -> 29.2 us
    ppermute x35 -> x28, waiting for transfers between devices: 231 us -> 302 us  [send(): return lax.ppermute(piece, owner_axes, hops)]
    ppermute x35 -> x28, starting transfers between devices: 113 us -> 48.9 us  [send(): return lax.ppermute(piece, owner_axes, hops)]
    pallas_call x32 -> x24, Pallas kernels: 41.3 us -> 31.2 us  [take(): pl.pallas_call(take_kernel, grid_spec=pltpu.PrefetchScalarGridSpec(num_sc...]
    unnamed x68 -> x46, local copies, waits for them, and re-layouts: 10.4 us -> 17.7 us
    pallas_call x4 -> x3, Pallas kernels: 37.5 us -> 30.5 us  [coeffs_and_gram(): pl.pallas_call(functools.partial(coeff_kernel, sec_count, sec_local, freq...]
  transfers between devices with their start and end apart: 37 -> 30, of which waited for: 13 -> 17; matrix products, arithmetic and copies ran while one was open for 3% -> 3% of each run, Pallas kernels for 20% -> 15%
where the time goes in v6:
time: 515 us; the launch traced here: 512 us
  waiting for transfers between devices  317 us (62%)
  Pallas kernels  98.1 us (19%)
  starting transfers between devices  61.3 us (12%)
  local copies, waits for them, and re-layouts  29.2 us (6%)
  other arithmetic  5.44 us (1%)
    ppermute x28, waiting for transfers between devices, send(): return lax.ppermute(piece, owner_axes, hops)  302 us
    ppermute x28, starting transfers between devices, send(): return lax.ppermute(piece, owner_axes, hops)  48.9 us
    pallas_call x24, Pallas kernels, take(): pl.pallas_call(take_kernel, grid_spec=pltpu.PrefetchScalarGridSpec(num_sc...  31.2 us
    pallas_call x3, Pallas kernels, coeffs_and_gram(): pl.pallas_call(functools.partial(coeff_kernel, sec_count, sec_local, freq...  30.5 us
    pallas_call x8, Pallas kernels, mix(): pl.pallas_call(functools.partial(mix_kernel, orders, fields), grid_spec=p...  19.2 us
    unnamed x46, local copies, waits for them, and re-layouts  17.7 us
    pallas_call x8, Pallas kernels, unpack(): pl.pallas_call(unpack_kernel, grid_spec=pltpu.PrefetchScalarGridSpec(num_...  13.2 us
  transfers between devices with their start and end apart: 30, of which 17 were waited for; matrix products, arithmetic and copies ran while one was open for 3% of the time, Pallas kernels for 15%

profile of v6, /device:TPU:16, one launch (start us, length us, event | category | flops | bytes accessed | tf_op | source)
XLA Modules:
  0.0 512.2 jit_solution(8670078297901258842)
XLA Ops:
  11.4 2.6 collective-permute-start.4
  14.2 2.0 take.36
  18.1 2.0 take.34
  26.2 18.4 %collective-permute-done.1.refs_2_ = bf16[4,296,256]{2,1,0:T(8,128)(2,1)} collective-permute-done((bf16[4,296,256]{2,1,0:T(8,128)(2,1)S(1)}, bf16[4,296,256]{2,1,0:T(8,128)(2,1)}, u32[]{:S(2)}, u32[]{:S(2)}) %collective-permute-start.1) | collective-permute-done | bytes 606240 | tf_op jit(solution)/shard_map/ppermute | solution.py:380
  44.6 2.9 multiply_bitcast_fusion
  49.0 32.2 %collective-permute-done.5.refs_6_ = bf16[4,296,256]{2,1,0:T(8,128)(2,1)} collective-permute-done((bf16[4,296,256]{2,1,0:T(8,128)(2,1)S(1)}, bf16[4,296,256]{2,1,0:T(8,128)(2,1)}, u32[]{:S(2)}, u32[]{:S(2)}) %collective-permute-start.5) | collective-permute-done | bytes 606240 | tf_op jit(solution)/shard_map/ppermute | solution.py:380
  81.2 42.2 %collective-permute-done.2.refs_3_ = bf16[4,296,256]{2,1,0:T(8,128)(2,1)} collective-permute-done((bf16[4,296,256]{2,1,0:T(8,128)(2,1)S(1)}, bf16[4,296,256]{2,1,0:T(8,128)(2,1)}, u32[]{:S(2)}, u32[]{:S(2)}) %collective-permute-start.2) | collective-permute-done | bytes 606240 | tf_op jit(solution)/shard_map/ppermute | solution.py:380
  123.4 14.4 %collective-permute-start.8 = (bf16[4,296,256]{2,1,0:T(8,128)(2,1)}, bf16[4,296,256]{2,1,0:T(8,128)(2,1)}, u32[]{:S(2)}, u32[]{:S(2)}) collective-permute-start(bf16[4,296,256]{2,1,0:T(8,128)(2,1)} %take.34), channel_id=1, source_target_pairs={{0,8},{4,12},{8,16},{12,20},{16,24},{20,28},{24,0},{28,4},{1,9},{5... | collective-permute-start | bytes 1818632 | tf_op jit(solution)/shard_map/ppermute | solution.py:380
  160.3 5.7 %reshape.503.azimuth_ref = bf16[128,256]{1,0:T(8,128)(2,1)} reshape(bf16[2,8,2,4,16,2,2,4]{7,6,5,4,3,2,1,0:T(2,128)(2,1)} %multiply_bitcast_fusion) | data formatting | bytes 131072 | tf_op jit(solution)/shard_map/reshape | solution.py:395
  166.2 2.4 collective-permute-start.13
  169.2 3.1 collective-permute-done.12.refs_6_
  173.8 13.7 %collective-permute-done.8.refs_2_ = bf16[4,296,256]{2,1,0:T(8,128)(2,1)} collective-permute-done((bf16[4,296,256]{2,1,0:T(8,128)(2,1)}, bf16[4,296,256]{2,1,0:T(8,128)(2,1)}, u32[]{:S(2)}, u32[]{:S(2)}) %collective-permute-start.8) | collective-permute-done | bytes 606240 | tf_op jit(solution)/shard_map/ppermute | solution.py:380
  187.5 36.8 %collective-permute-done.11.refs_5_ = bf16[4,296,256]{2,1,0:T(8,128)(2,1)} collective-permute-done((bf16[4,296,256]{2,1,0:T(8,128)(2,1)}, bf16[4,296,256]{2,1,0:T(8,128)(2,1)}, u32[]{:S(2)}, u32[]{:S(2)}) %collective-permute-start.11) | collective-permute-done | bytes 606240 | tf_op jit(solution)/shard_map/ppermute | solution.py:380
  224.3 4.3 collective-permute-start.17
  231.4 5.9 %collective-permute-done.13.refs_7_ = bf16[4,296,256]{2,1,0:T(8,128)(2,1)} collective-permute-done((bf16[4,296,256]{2,1,0:T(8,128)(2,1)}, bf16[4,296,256]{2,1,0:T(8,128)(2,1)}, u32[]{:S(2)}, u32[]{:S(2)}) %collective-permute-start.13) | collective-permute-done | bytes 606240 | tf_op jit(solution)/shard_map/ppermute | solution.py:380
  237.3 3.4 collective-permute-start.19
  240.7 2.4 collective-permute-start.18
  243.9 6.4 %collective-permute-done.17.refs_4_ = bf16[4,296,256]{2,1,0:T(8,128)(2,1)} collective-permute-done((bf16[4,296,256]{2,1,0:T(8,128)(2,1)}, bf16[4,296,256]{2,1,0:T(8,128)(2,1)}, u32[]{:S(2)}, u32[]{:S(2)}) %collective-permute-start.17) | collective-permute-done | bytes 606240 | tf_op jit(solution)/shard_map/ppermute | solution.py:380
  254.8 10.2 %coeffs_and_gram.3 = (bf16[32,256,256]{2,1,0:T(8,128)(2,1)}, f32[32,16,128]{2,1,0:T(8,128)S(1)}) custom-call(s32[2]{0:T(128)S(1)} %pad_add_fusion.place_ref, bf16[2,2,256,168]{3,2,1,0:T(8,128)(2,1)S(1)} %copy.40.time_ref, bf16[128,256]{1,0:T(8,128)(2,1)S(1)} %copy-done.16, f32[1,256]{1,0:T(1,128)S(1)} %bitcast.83, ...), custom_call_target="tpu_custom_call" | custom-call | flops 3556769792 | bytes 9043968 | tf_op jit(solution)/shard_map/coeffs_and_gram/pallas_call | solution.py:139
  265.1 10.4 %coeffs_and_gram.4 = (bf16[32,256,256]{2,1,0:T(8,128)(2,1)}, f32[32,16,128]{2,1,0:T(8,128)S(1)}) custom-call(s32[2]{0:T(128)S(1)} %pad_add_fusion.place_ref, bf16[2,2,256,168]{3,2,1,0:T(8,128)(2,1)S(1)} %copy.40.time_ref, bf16[128,256]{1,0:T(8,128)(2,1)S(1)} %copy-done.16, f32[1,256]{1,0:T(1,128)S(1)} %bitcast.84, ...), custom_call_target="tpu_custom_call" | custom-call | flops 3556769792 | bytes 9043968 | tf_op jit(solution)/shard_map/coeffs_and_gram/pallas_call | solution.py:139
  275.4 13.9 %collective-permute-done.19.refs_6_ = bf16[4,296,256]{2,1,0:T(8,128)(2,1)S(1)} collective-permute-done((bf16[4,296,256]{2,1,0:T(8,128)(2,1)}, bf16[4,296,256]{2,1,0:T(8,128)(2,1)S(1)}, u32[]{:S(2)}, u32[]{:S(2)}) %collective-permute-start.19) | collective-permute-done | bytes 606240 | tf_op jit(solution)/shard_map/ppermute | solution.py:380
  289.3 16.3 %collective-permute-done.16.refs_3_ = bf16[4,296,256]{2,1,0:T(8,128)(2,1)S(1)} collective-permute-done((bf16[4,296,256]{2,1,0:T(8,128)(2,1)S(1)}, bf16[4,296,256]{2,1,0:T(8,128)(2,1)S(1)}, u32[]{:S(2)}, u32[]{:S(2)}) %collective-permute-start.16) | collective-permute-done | bytes 606240 | tf_op jit(solution)/shard_map/ppermute | solution.py:380
  305.6 9.5 %collective-permute-done.20.refs_7_ = bf16[4,296,256]{2,1,0:T(8,128)(2,1)S(1)} collective-permute-done((bf16[4,296,256]{2,1,0:T(8,128)(2,1)S(1)}, bf16[4,296,256]{2,1,0:T(8,128)(2,1)S(1)}, u32[]{:S(2)}, u32[]{:S(2)}) %collective-permute-start.20) | collective-permute-done | bytes 606240 | tf_op jit(solution)/shard_map/ppermute | solution.py:380
  315.1 9.9 %coeffs_and_gram.5 = (bf16[32,256,256]{2,1,0:T(8,128)(2,1)}, f32[32,16,128]{2,1,0:T(8,128)}) custom-call(s32[2]{0:T(128)S(1)} %pad_add_fusion.place_ref, bf16[2,2,256,168]{3,2,1,0:T(8,128)(2,1)S(1)} %copy.40.time_ref, bf16[128,256]{1,0:T(8,128)(2,1)S(1)} %copy-done.16, f32[1,256]{1,0:T(1,128)S(1)} %bitcast.85, ...), custom_call_target="tpu_custom_call" | custom-call | flops 3556769792 | bytes 9043968 | tf_op jit(solution)/shard_map/coeffs_and_gram/pallas_call | solution.py:139
  325.0 7.5 %all-to-all-start = ((f32[32,1,16,128]{3,2,1,0:T(8,128)}), f32[32,1,16,128]{3,2,1,0:T(8,128)S(1)}, u32[]{:S(2)}, u32[]{:S(2)}) async-start(f32[32,1,16,128]{3,2,1,0:T(8,128)} %bitcast.23), calls=%async_computation | async-start | bytes 524288 | tf_op jit(solution)/shard_map/all_to_all | solution.py:428
  333.1 7.5 %all-to-all-done = f32[32,1,16,128]{3,2,1,0:T(8,128)S(1)} async-done(((f32[32,1,16,128]{3,2,1,0:T(8,128)}), f32[32,1,16,128]{3,2,1,0:T(8,128)S(1)}, u32[]{:S(2)}, u32[]{:S(2)}) %all-to-all-start) | async-done | bytes 262176 | tf_op jit(solution)/shard_map/all_to_all | solution.py:428
  341.6 4.0 subspace.1
  348.4 4.9 all-to-all-start.1
  353.8 6.9 %all-to-all-done.1 = bf16[32,1,18,128]{3,2,1,0:T(8,128)(2,1)S(1)} async-done(((bf16[32,1,18,128]{3,2,1,0:T(8,128)(2,1)}), bf16[32,1,18,128]{3,2,1,0:T(8,128)(2,1)S(1)}, u32[]{:S(2)}, u32[]{:S(2)}) %all-to-all-start.1) | async-done | bytes 147488 | tf_op jit(solution)/shard_map/all_to_all | solution.py:445
  361.3 2.2 copy-done
  363.5 2.0 mix.8.refs_3_
  367.4 2.2 mix.9.refs_3_
  370.9 3.1 mix.10.refs_3_
  375.2 3.1 mix.11.refs_3_
  378.3 2.8 collective-permute-start.24
  381.2 2.2 mix.12.refs_3_
  383.4 2.2 mix.13.refs_3_
  385.6 66.2 %collective-permute-done.27 = bf16[3,4,128,256]{3,2,1,0:T(8,128)(2,1)S(1)} collective-permute-done((bf16[3,4,128,256]{3,2,1,0:T(8,128)(2,1)S(1)}, bf16[3,4,128,256]{3,2,1,0:T(8,128)(2,1)S(1)}, u32[]{:S(2)}, u32[]{:S(2)}) %collective-permute-start.27) | collective-permute-done | bytes 786464 | tf_op jit(solution)/shard_map/ppermute | solution.py:380
  452.7 2.2 mix.14.refs_3_
  454.9 13.8 %collective-permute-done.26 = bf16[3,4,128,256]{3,2,1,0:T(8,128)(2,1)S(1)} collective-permute-done((bf16[3,4,128,256]{3,2,1,0:T(8,128)(2,1)S(1)}, bf16[3,4,128,256]{3,2,1,0:T(8,128)(2,1)S(1)}, u32[]{:S(2)}, u32[]{:S(2)}) %collective-permute-start.26) | collective-permute-done | bytes 786464 | tf_op jit(solution)/shard_map/ppermute | solution.py:380
  470.7 2.2 mix.15
  478.2 9.2 %collective-permute-done.25 = bf16[3,4,128,256]{3,2,1,0:T(8,128)(2,1)} collective-permute-done((bf16[3,4,128,256]{3,2,1,0:T(8,128)(2,1)}, bf16[3,4,128,256]{3,2,1,0:T(8,128)(2,1)}, u32[]{:S(2)}, u32[]{:S(2)}) %collective-permute-start.25) | collective-permute-done | bytes 786464 | tf_op jit(solution)/shard_map/ppermute | solution.py:380
  487.4 2.1 unpack.11.refs_0_
  489.5 14.4 %collective-permute-done.24 = bf16[3,4,128,256]{3,2,1,0:T(8,128)(2,1)} collective-permute-done((bf16[3,4,128,256]{3,2,1,0:T(8,128)(2,1)}, bf16[3,4,128,256]{3,2,1,0:T(8,128)(2,1)}, u32[]{:S(2)}, u32[]{:S(2)}) %collective-permute-start.24) | collective-permute-done | bytes 786464 | tf_op jit(solution)/shard_map/ppermute | solution.py:380
  503.9 2.1 unpack.12.refs_0_
  506.0 2.1 unpack.13.refs_0_
  508.0 2.1 unpack.14.refs_0_
  510.1 2.1 unpack.15
  (150 shorter events, 71.0 us)
Async XLA Ops:
  1.8 42.7 %collective-permute-start.1 = (bf16[4,296,256]{2,1,0:T(8,128)(2,1)S(1)}, bf16[4,296,256]{2,1,0:T(8,128)(2,1)}, u32[]{:S(2)}, u32[]{:S(2)}) collective-permute-start(bf16[4,296,256]{2,1,0:T(8,128)(2,1)S(1)} %take.26), channel_id=1, source_target_pairs={{0,8},{4,12},{8,16},{12,20},{16,24},{20,28},{24,0},{28,4},{1,9},{5... | collective-permute-start | bytes 1818632 | tf_op jit(solution)/shard_map/ppermute | solution.py:380
  4.6 42.9 %collective-permute-start.3 = (bf16[4,296,256]{2,1,0:T(8,128)(2,1)S(1)}, bf16[4,296,256]{2,1,0:T(8,128)(2,1)}, u32[]{:S(2)}, u32[]{:S(2)}) collective-permute-start(bf16[4,296,256]{2,1,0:T(8,128)(2,1)S(1)} %take.28), channel_id=1, source_target_pairs={{0,16},{4,20},{8,24},{12,28},{16,0},{20,4},{24,8},{28,12},{1,17},{... | collective-permute-start | bytes 1818632 | tf_op jit(solution)/shard_map/ppermute | solution.py:380
  6.1 75.1 %collective-permute-start.5 = (bf16[4,296,256]{2,1,0:T(8,128)(2,1)S(1)}, bf16[4,296,256]{2,1,0:T(8,128)(2,1)}, u32[]{:S(2)}, u32[]{:S(2)}) collective-permute-start(bf16[4,296,256]{2,1,0:T(8,128)(2,1)S(1)} %take.30), channel_id=1, source_target_pairs={{0,24},{4,28},{8,0},{12,4},{16,8},{20,12},{24,16},{28,20},{1,25},{... | collective-permute-start | bytes 1818632 | tf_op jit(solution)/shard_map/ppermute | solution.py:380
  8.4 115.0 %collective-permute-start.2 = (bf16[4,296,256]{2,1,0:T(8,128)(2,1)S(1)}, bf16[4,296,256]{2,1,0:T(8,128)(2,1)}, u32[]{:S(2)}, u32[]{:S(2)}) collective-permute-start(bf16[4,296,256]{2,1,0:T(8,128)(2,1)S(1)} %take.27), channel_id=1, source_target_pairs={{0,12},{4,8},{8,20},{12,16},{16,28},{20,24},{24,4},{28,0},{1,13},{... | collective-permute-start | bytes 1818632 | tf_op jit(solution)/shard_map/ppermute | solution.py:380
  11.4 112.0 %collective-permute-start.4 = (bf16[4,296,256]{2,1,0:T(8,128)(2,1)S(1)}, bf16[4,296,256]{2,1,0:T(8,128)(2,1)}, u32[]{:S(2)}, u32[]{:S(2)}) collective-permute-start(bf16[4,296,256]{2,1,0:T(8,128)(2,1)S(1)} %take.29), channel_id=1, source_target_pairs={{0,20},{4,16},{8,28},{12,24},{16,4},{20,0},{24,12},{28,8},{1,21},{... | collective-permute-start | bytes 1818632 | tf_op jit(solution)/shard_map/ppermute | solution.py:380
  23.1 0.8 copy-start.15
  44.5 93.3 %collective-permute-start.6 = (bf16[4,296,256]{2,1,0:T(8,128)(2,1)}, bf16[4,296,256]{2,1,0:T(8,128)(2,1)S(1)}, u32[]{:S(2)}, u32[]{:S(2)}) collective-permute-start(bf16[4,296,256]{2,1,0:T(8,128)(2,1)} %copy-done.15), channel_id=1, source_target_pairs={{0,28},{4,24},{8,4},{12,0},{16,12},{20,8},{24,20},{28,16},{1,29},{... | collective-permute-start | bytes 1818632 | tf_op jit(solution)/shard_map/ppermute | solution.py:380
  47.5 118.7 %collective-permute-start = (bf16[4,296,256]{2,1,0:T(8,128)(2,1)}, bf16[4,296,256]{2,1,0:T(8,128)(2,1)}, u32[]{:S(2)}, u32[]{:S(2)}) collective-permute-start(bf16[4,296,256]{2,1,0:T(8,128)(2,1)} %take.25), channel_id=1, source_target_pairs={{0,4},{4,0},{8,12},{12,8},{16,20},{20,16},{24,28},{28,24},{1,5},{5... | collective-permute-start | bytes 1818632 | tf_op jit(solution)/shard_map/ppermute | solution.py:380
  81.2 87.4 %collective-permute-start.10 = (bf16[4,296,256]{2,1,0:T(8,128)(2,1)}, bf16[4,296,256]{2,1,0:T(8,128)(2,1)}, u32[]{:S(2)}, u32[]{:S(2)}) collective-permute-start(bf16[4,296,256]{2,1,0:T(8,128)(2,1)} %take.36), channel_id=1, source_target_pairs={{0,16},{4,20},{8,24},{12,28},{16,0},{20,4},{24,8},{28,12},{1,17},{... | collective-permute-start | bytes 1818632 | tf_op jit(solution)/shard_map/ppermute | solution.py:380
  123.4 48.9 %collective-permute-start.12 = (bf16[4,296,256]{2,1,0:T(8,128)(2,1)}, bf16[4,296,256]{2,1,0:T(8,128)(2,1)}, u32[]{:S(2)}, u32[]{:S(2)}) collective-permute-start(bf16[4,296,256]{2,1,0:T(8,128)(2,1)} %take.38), channel_id=1, source_target_pairs={{0,24},{4,28},{8,0},{12,4},{16,8},{20,12},{24,16},{28,20},{1,25},{... | collective-permute-start | bytes 1818632 | tf_op jit(solution)/shard_map/ppermute | solution.py:380
  123.4 64.1 %collective-permute-start.8 = (bf16[4,296,256]{2,1,0:T(8,128)(2,1)}, bf16[4,296,256]{2,1,0:T(8,128)(2,1)}, u32[]{:S(2)}, u32[]{:S(2)}) collective-permute-start(bf16[4,296,256]{2,1,0:T(8,128)(2,1)} %take.34), channel_id=1, source_target_pairs={{0,8},{4,12},{8,16},{12,20},{16,24},{20,28},{24,0},{28,4},{1,9},{5... | collective-permute-start | bytes 1818632 | tf_op jit(solution)/shard_map/ppermute | solution.py:380
  137.9 0.9 copy-start.18
  138.7 85.6 %collective-permute-start.11 = (bf16[4,296,256]{2,1,0:T(8,128)(2,1)}, bf16[4,296,256]{2,1,0:T(8,128)(2,1)}, u32[]{:S(2)}, u32[]{:S(2)}) collective-permute-start(bf16[4,296,256]{2,1,0:T(8,128)(2,1)} %take.37), channel_id=1, source_target_pairs={{0,20},{4,16},{8,28},{12,24},{16,4},{20,0},{24,12},{28,8},{1,21},{... | collective-permute-start | bytes 1818632 | tf_op jit(solution)/shard_map/ppermute | solution.py:380
  143.8 0.9 copy-start.12
  145.8 0.8 copy-start.8
  147.8 0.9 copy-start.6
  151.7 0.9 copy-start.10
  159.1 6.8 %copy-start.21 = (s32[16]{0:T(128)S(1)}, s32[16]{0:T(128)}, u32[]{:S(2)}) copy-start(s32[16]{0:T(128)} %param.6) | copy-start | bytes 196
  166.2 71.1 %collective-permute-start.13 = (bf16[4,296,256]{2,1,0:T(8,128)(2,1)}, bf16[4,296,256]{2,1,0:T(8,128)(2,1)}, u32[]{:S(2)}, u32[]{:S(2)}) collective-permute-start(bf16[4,296,256]{2,1,0:T(8,128)(2,1)} %copy-done.14), channel_id=1, source_target_pairs={{0,28},{4,24},{8,4},{12,0},{16,12},{20,8},{24,20},{28,16},{1,29},{... | collective-permute-start | bytes 1818632 | tf_op jit(solution)/shard_map/ppermute | solution.py:380
  168.6 72.1 %collective-permute-start.9 = (bf16[4,296,256]{2,1,0:T(8,128)(2,1)}, bf16[4,296,256]{2,1,0:T(8,128)(2,1)}, u32[]{:S(2)}, u32[]{:S(2)}) collective-permute-start(bf16[4,296,256]{2,1,0:T(8,128)(2,1)} %copy-done.13), channel_id=1, source_target_pairs={{0,12},{4,8},{8,20},{12,16},{16,28},{20,24},{24,4},{28,0},{1,13},{... | collective-permute-start | bytes 1818632 | tf_op jit(solution)/shard_map/ppermute | solution.py:380
  172.3 68.4 %collective-permute-start.7 = (bf16[4,296,256]{2,1,0:T(8,128)(2,1)}, bf16[4,296,256]{2,1,0:T(8,128)(2,1)}, u32[]{:S(2)}, u32[]{:S(2)}) collective-permute-start(bf16[4,296,256]{2,1,0:T(8,128)(2,1)} %copy-done.12), channel_id=1, source_target_pairs={{0,4},{4,0},{8,12},{12,8},{16,20},{20,16},{24,28},{28,24},{1,5},{5... | collective-permute-start | bytes 1818632 | tf_op jit(solution)/shard_map/ppermute | solution.py:380
  187.5 55.6 %collective-permute-start.15 = (bf16[4,296,256]{2,1,0:T(8,128)(2,1)}, bf16[4,296,256]{2,1,0:T(8,128)(2,1)}, u32[]{:S(2)}, u32[]{:S(2)}) collective-permute-start(bf16[4,296,256]{2,1,0:T(8,128)(2,1)} %copy-done.11), channel_id=1, source_target_pairs={{0,8},{4,12},{8,16},{12,20},{16,24},{20,28},{24,0},{28,4},{1,9},{5... | collective-permute-start | bytes 1818632 | tf_op jit(solution)/shard_map/ppermute | solution.py:380
  224.3 26.0 %collective-permute-start.17 = (bf16[4,296,256]{2,1,0:T(8,128)(2,1)}, bf16[4,296,256]{2,1,0:T(8,128)(2,1)}, u32[]{:S(2)}, u32[]{:S(2)}) collective-permute-start(bf16[4,296,256]{2,1,0:T(8,128)(2,1)} %copy-done.10), channel_id=1, source_target_pairs={{0,16},{4,20},{8,24},{12,28},{16,0},{20,4},{24,8},{28,12},{1,17},{... | collective-permute-start | bytes 1818632 | tf_op jit(solution)/shard_map/ppermute | solution.py:380
  231.4 83.7 %copy-start.17 = (f32[256]{0:T(256)}, f32[256]{0:T(256)S(1)}, u32[]{:S(2)}) copy-start(f32[256]{0:T(256)S(1)} %select_reduce_fusion) | copy-start | bytes 3076
  237.3 52.0 %collective-permute-start.19 = (bf16[4,296,256]{2,1,0:T(8,128)(2,1)}, bf16[4,296,256]{2,1,0:T(8,128)(2,1)S(1)}, u32[]{:S(2)}, u32[]{:S(2)}) collective-permute-start(bf16[4,296,256]{2,1,0:T(8,128)(2,1)} %copy-done.5), channel_id=1, source_target_pairs={{0,24},{4,28},{8,0},{12,4},{16,8},{20,12},{24,16},{28,20},{1,25},{... | collective-permute-start | bytes 1818632 | tf_op jit(solution)/shard_map/ppermute | solution.py:380
  240.7 64.9 %collective-permute-start.16 = (bf16[4,296,256]{2,1,0:T(8,128)(2,1)S(1)}, bf16[4,296,256]{2,1,0:T(8,128)(2,1)S(1)}, u32[]{:S(2)}, u32[]{:S(2)}) collective-permute-start(bf16[4,296,256]{2,1,0:T(8,128)(2,1)S(1)} %take.43), channel_id=1, source_target_pairs={{0,12},{4,8},{8,20},{12,16},{16,28},{20,24},{24,4},{28,0},{1,13},{... | collective-permute-start | bytes 1818632 | tf_op jit(solution)/shard_map/ppermute | solution.py:380
  240.7 64.9 %collective-permute-start.18 = (bf16[4,296,256]{2,1,0:T(8,128)(2,1)S(1)}, bf16[4,296,256]{2,1,0:T(8,128)(2,1)S(1)}, u32[]{:S(2)}, u32[]{:S(2)}) collective-permute-start(bf16[4,296,256]{2,1,0:T(8,128)(2,1)S(1)} %take.45), channel_id=1, source_target_pairs={{0,20},{4,16},{8,28},{12,24},{16,4},{20,0},{24,12},{28,8},{1,21},{... | collective-permute-start | bytes 1818632 | tf_op jit(solution)/shard_map/ppermute | solution.py:380
  243.1 72.0 %collective-permute-start.20 = (bf16[4,296,256]{2,1,0:T(8,128)(2,1)S(1)}, bf16[4,296,256]{2,1,0:T(8,128)(2,1)S(1)}, u32[]{:S(2)}, u32[]{:S(2)}) collective-permute-start(bf16[4,296,256]{2,1,0:T(8,128)(2,1)S(1)} %take.47), channel_id=1, source_target_pairs={{0,28},{4,24},{8,4},{12,0},{16,12},{20,8},{24,20},{28,16},{1,29},{... | collective-permute-start | bytes 1818632 | tf_op jit(solution)/shard_map/ppermute | solution.py:380
  250.3 64.8 %collective-permute-start.14 = (bf16[4,296,256]{2,1,0:T(8,128)(2,1)S(1)}, bf16[4,296,256]{2,1,0:T(8,128)(2,1)S(1)}, u32[]{:S(2)}, u32[]{:S(2)}) collective-permute-start(bf16[4,296,256]{2,1,0:T(8,128)(2,1)S(1)} %take.41), channel_id=1, source_target_pairs={{0,4},{4,0},{8,12},{12,8},{16,20},{20,16},{24,28},{28,24},{1,5},{5... | collective-permute-start | bytes 1818632 | tf_op jit(solution)/shard_map/ppermute | solution.py:380
  251.9 1.1 copy-start.9
  252.9 0.8 copy-start.16
  253.8 1.1 copy-start.19
  254.8 10.3 %copy-start.7 = (bf16[4,296,256]{2,1,0:T(8,128)(2,1)S(1)}, bf16[4,296,256]{2,1,0:T(8,128)(2,1)}, u32[]{:S(2)}) copy-start(bf16[4,296,256]{2,1,0:T(8,128)(2,1)} %copy-done.6) | copy-start | bytes 1818628
  315.1 38.3 %copy-start.20 = (bf16[2,2,2]{2,1,0:T(2,128)(2,1)S(1)}, bf16[2,2,2]{2,1,0:T(2,128)(2,1)}, u32[]{:S(2)}) copy-start(bf16[2,2,2]{2,1,0:T(2,128)(2,1)} %constant.267.clone) | copy-start | bytes 52
  325.0 15.7 %all-to-all-start = ((f32[32,1,16,128]{3,2,1,0:T(8,128)}), f32[32,1,16,128]{3,2,1,0:T(8,128)S(1)}, u32[]{:S(2)}, u32[]{:S(2)}) async-start(f32[32,1,16,128]{3,2,1,0:T(8,128)} %bitcast.23), calls=%async_computation | async-start | bytes 524288 | tf_op jit(solution)/shard_map/all_to_all | solution.py:428
  348.4 12.3 %all-to-all-start.1 = ((bf16[32,1,18,128]{3,2,1,0:T(8,128)(2,1)}), bf16[32,1,18,128]{3,2,1,0:T(8,128)(2,1)S(1)}, u32[]{:S(2)}, u32[]{:S(2)}) async-start(bf16[32,1,18,128]{3,2,1,0:T(8,128)(2,1)} %broadcast_in_dim.27), calls=%async_computation.1 | async-start | bytes 393216 | tf_op jit(solution)/shard_map/all_to_all | solution.py:445
  361.3 2.2 copy-start
  365.5 86.3 %collective-permute-start.27 = (bf16[3,4,128,256]{3,2,1,0:T(8,128)(2,1)S(1)}, bf16[3,4,128,256]{3,2,1,0:T(8,128)(2,1)S(1)}, u32[]{:S(2)}, u32[]{:S(2)}) collective-permute-start(bf16[3,4,128,256]{3,2,1,0:T(8,128)(2,1)S(1)} %mix.8.refs_3_), channel_id=1, source_target_pairs={{0,16},{4,20},{8,24},{12,28},{16,0},{20,4},{24,8},{28,12},{1,17},{... | collective-permute-start | bytes 2359304 | tf_op jit(solution)/shard_map/ppermute | solution.py:380
  369.6 99.1 %collective-permute-start.26 = (bf16[3,4,128,256]{3,2,1,0:T(8,128)(2,1)S(1)}, bf16[3,4,128,256]{3,2,1,0:T(8,128)(2,1)S(1)}, u32[]{:S(2)}, u32[]{:S(2)}) collective-permute-start(bf16[3,4,128,256]{3,2,1,0:T(8,128)(2,1)S(1)} %mix.9.refs_3_), channel_id=1, source_target_pairs={{0,20},{4,16},{8,28},{12,24},{16,4},{20,0},{24,12},{28,8},{1,21},{... | collective-permute-start | bytes 2359304 | tf_op jit(solution)/shard_map/ppermute | solution.py:380
  374.0 113.5 %collective-permute-start.25 = (bf16[3,4,128,256]{3,2,1,0:T(8,128)(2,1)}, bf16[3,4,128,256]{3,2,1,0:T(8,128)(2,1)}, u32[]{:S(2)}, u32[]{:S(2)}) collective-permute-start(bf16[3,4,128,256]{3,2,1,0:T(8,128)(2,1)} %mix.10.refs_3_), channel_id=1, source_target_pairs={{0,8},{4,12},{8,16},{12,20},{16,24},{20,28},{24,0},{28,4},{1,9},{5... | collective-permute-start | bytes 2359304 | tf_op jit(solution)/shard_map/ppermute | solution.py:380
  378.3 125.6 %collective-permute-start.24 = (bf16[3,4,128,256]{3,2,1,0:T(8,128)(2,1)}, bf16[3,4,128,256]{3,2,1,0:T(8,128)(2,1)}, u32[]{:S(2)}, u32[]{:S(2)}) collective-permute-start(bf16[3,4,128,256]{3,2,1,0:T(8,128)(2,1)} %mix.11.refs_3_), channel_id=1, source_target_pairs={{0,12},{4,8},{8,20},{12,16},{16,28},{20,24},{24,4},{28,0},{1,13},{... | collective-permute-start | bytes 2359304 | tf_op jit(solution)/shard_map/ppermute | solution.py:380
  383.4 122.6 %collective-permute-start.23 = (bf16[3,4,128,256]{3,2,1,0:T(8,128)(2,1)S(1)}, bf16[3,4,128,256]{3,2,1,0:T(8,128)(2,1)}, u32[]{:S(2)}, u32[]{:S(2)}) collective-permute-start(bf16[3,4,128,256]{3,2,1,0:T(8,128)(2,1)S(1)} %mix.12.refs_3_), channel_id=1, source_target_pairs={{0,24},{4,28},{8,0},{12,4},{16,8},{20,12},{24,16},{28,20},{1,25},{... | collective-permute-start | bytes 2359304 | tf_op jit(solution)/shard_map/ppermute | solution.py:380
  451.9 0.9 copy-start.1
  452.7 55.3 %collective-permute-start.22 = (bf16[3,4,128,256]{3,2,1,0:T(8,128)(2,1)S(1)}, bf16[3,4,128,256]{3,2,1,0:T(8,128)(2,1)}, u32[]{:S(2)}, u32[]{:S(2)}) collective-permute-start(bf16[3,4,128,256]{3,2,1,0:T(8,128)(2,1)S(1)} %mix.13.refs_3_), channel_id=1, source_target_pairs={{0,28},{4,24},{8,4},{12,0},{16,12},{20,8},{24,20},{28,16},{1,29},{... | collective-permute-start | bytes 2359304 | tf_op jit(solution)/shard_map/ppermute | solution.py:380
  468.8 0.9 copy-start.3
  469.6 40.5 %collective-permute-start.21 = (bf16[3,4,128,256]{3,2,1,0:T(8,128)(2,1)S(1)}, bf16[3,4,128,256]{3,2,1,0:T(8,128)(2,1)}, u32[]{:S(2)}, u32[]{:S(2)}) collective-permute-start(bf16[3,4,128,256]{3,2,1,0:T(8,128)(2,1)S(1)} %mix.14.refs_3_), channel_id=1, source_target_pairs={{0,4},{4,0},{8,12},{12,8},{16,20},{20,16},{24,28},{28,24},{1,5},{5... | collective-permute-start | bytes 2359304 | tf_op jit(solution)/shard_map/ppermute | solution.py:380
  474.7 1.1 copy-start.2
  475.8 1.4 copy-start.4
  (4 other events, 3.3 us)

commit v7 on v6

--- a/solution.py
+++ b/solution.py
@@ -66,7 +66,7 @@
     record_refs, (coeff_ref, gram_ref, spectra) = refs[:-3], refs[-3:]
     step = pl.program_id(0)
     tm_count, halves, _, span = time_ref.shape
-    rec_len, columns = record_refs[0].shape[1:]
+    rec_len, columns = record_refs[0].shape[2:]
     sectors = spectra.shape[0]
     rows = spectra.shape[2] // NFREQ
 
@@ -79,10 +79,10 @@
                 first = h * (rec_len - span) // (halves - 1)
                 parts = []
                 for j in range(tm_count):
-                    piece = own[0][0, first:first + span]
+                    piece = own[0][0, 0, first:first + span]
                     for x in range(1, tm_count):
                         here = lax.rem(place_ref[1] + tm_count - x, tm_count) == j
-                        piece = jnp.where(here, own[x][0, first:first + span], piece)
+                        piece = jnp.where(here, own[x][0, 0, first:first + span], piece)
                     part = jnp.dot(time_ref[j, h], piece, preferred_element_type=jnp.float32)
                     parts.append(part.reshape(NFREQ, rows // tm_count, columns))
                 joined = jnp.stack(parts, 1).reshape(NFREQ * rows, columns)
@@ -122,10 +122,10 @@
             gram_ref[n] = before_ref[n] + own
 
 
-def coeffs_and_gram(place, arrived, sec_count, time_basis, azimuth, weight, before):
-    sec_local, rec_len, columns = arrived[0].shape
+def coeffs_and_gram(place, arrived, k, sec_count, time_basis, azimuth, weight, before):
+    sec_local, _, rec_len, columns = arrived[0].shape
     sectors = sec_count * sec_local
-    halves = time_basis.shape[1]
+    tm_count, halves = time_basis.shape[:2]
     blocks, wide = before.shape[1:]
     rows = azimuth.shape[1] // sectors
     steps = 4
@@ -135,7 +135,7 @@
     flops = 2 * columns * (
         sectors * time_basis.size + NFREQ * halves * azimuth.size + NFREQ * 4 * wide * wide
     )
-    piece = pl.BlockSpec((1, rec_len, columns), lambda i, _: (early(i), 0, 0))
+    piece = pl.BlockSpec((1, 1, rec_len, columns), lambda i, _: (early(i), k, 0, 0))
     return pl.pallas_call(
         functools.partial(coeff_kernel, sec_count, sec_local, freqs, wide // blocks),
         grid_spec=pltpu.PrefetchScalarGridSpec(
@@ -154,13 +154,13 @@
             scratch_shapes=[pltpu.VMEM((sectors, halves, NFREQ * rows, columns), jnp.bfloat16)],
         ),
         out_shape=[
-            jax.ShapeDtypeStruct((NFREQ, 2 * wide, columns), jnp.bfloat16),
+            pltpu.HBM((NFREQ, 2 * wide, columns), jnp.bfloat16),
             jax.ShapeDtypeStruct(before.shape, jnp.float32),
         ],
         compiler_params=pltpu.CompilerParams(vmem_limit_bytes=VMEM_LIMIT),
         cost_estimate=pl.CostEstimate(
             flops=flops,
-            bytes_accessed=2 * (len(arrived) * arrived[0].size + NFREQ * 2 * wide * columns),
+            bytes_accessed=2 * columns * (sectors * tm_count * rec_len + NFREQ * 2 * wide),
             transcendentals=0,
         ),
         name="coeffs_and_gram",
@@ -281,28 +281,27 @@
 
 
 def take_kernel(place_ref, record_ref, out_ref):
-    out_ref[...] = record_ref[:, 0]
-
-
-def take(by_field, k, owner, owners):
+    out_ref[...] = record_ref[...]
+
+
+def take(by_field, first, fields, owner, owners):
     sec_local, _, rec_len, cells = by_field.shape
     count = cells // owners
     if count % LANES:
-        return lax.dynamic_slice_in_dim(by_field[:, k], owner * count, count, 2)
+        return lax.dynamic_slice_in_dim(by_field[:, first:first + fields], owner * count, count, 3)
+    shape = (sec_local, fields, rec_len, count)
     return pl.pallas_call(
         take_kernel,
         grid_spec=pltpu.PrefetchScalarGridSpec(
             num_scalar_prefetch=1,
             grid=(1,),
-            in_specs=[
-                pl.BlockSpec((sec_local, 1, rec_len, count), lambda i, at: (0, k, 0, at[0]))
-            ],
-            out_specs=pl.BlockSpec((sec_local, rec_len, count), lambda i, at: (0, 0, 0)),
-        ),
-        out_shape=jax.ShapeDtypeStruct((sec_local, rec_len, count), by_field.dtype),
+            in_specs=[pl.BlockSpec(shape, lambda i, at: (0, first // fields, 0, at[0]))],
+            out_specs=pl.BlockSpec(shape, lambda i, at: (0, 0, 0, 0)),
+        ),
+        out_shape=jax.ShapeDtypeStruct(shape, by_field.dtype),
         compiler_params=pltpu.CompilerParams(vmem_limit_bytes=VMEM_LIMIT),
         cost_estimate=pl.CostEstimate(
-            flops=0, bytes_accessed=4 * sec_local * rec_len * count, transcendentals=0
+            flops=0, bytes_accessed=4 * math.prod(shape), transcendentals=0
         ),
         name="take",
     )(jnp.reshape(owner, (1,)), by_field)
@@ -380,9 +379,11 @@
         return lax.ppermute(piece, owner_axes, hops)
 
     arrived = []
-    for k in range(fields):
-        got = {r: send(take(by_field, k, owner_after(*r), owners), *r) for r in in_order + [(0, 0)]}
-        arrived.append([got[r] for r in shifts])
+    for first, count in ((0, fields - 1), (fields - 1, 1)):
+        got = {}
+        for z, x in in_order + [(0, 0)]:
+            got[z, x] = send(take(by_field, first, count, owner_after(z, x), owners), z, x)
+        arrived += [([got[r] for r in shifts], k) for k in range(count)]
 
     time_basis = placed_time_basis(block_start, tm_count)
     half, _ = half_span(blocks // tm_count)
@@ -413,7 +414,7 @@
     coeffs = []
     for k in range(fields):
         own, gram = coeffs_and_gram(
-            jnp.stack([sec_at, tm_at]), arrived[k], sec_count, time_basis, azimuth, weight, gram
+            jnp.stack([sec_at, tm_at]), *arrived[k], sec_count, time_basis, azimuth, weight, gram
         )
         coeffs.append(own)
 

time: 515 us -> 530 us (1.029)
  starting transfers between devices: 61.3 us -> 109 us
  waiting for transfers between devices: 317 us -> 297 us
  Pallas kernels: 98.1 us -> 90.1 us
    ppermute x28 -> x21, starting transfers between devices: 48.9 us -> 84.4 us  [send(): return lax.ppermute(piece, owner_axes, hops)]
    ppermute x28 -> x21, waiting for transfers between devices: 302 us -> 282 us  [send(): return lax.ppermute(piece, owner_axes, hops)]
    all_to_all x1, starting transfers between devices: 7.48 us -> 19.3 us  [local(): gram = lax.all_to_all(gram, axes, split_axis=0, concat_axis=0, tiled=True)]
    pallas_call x24 -> x16, Pallas kernels: 31.2 us -> 23 us  [take(): pl.pallas_call(take_kernel, grid_spec=pltpu.PrefetchScalarGridSpec(num_sc...]
    unnamed x46 -> x44, local copies, waits for them, and re-layouts: 17.7 us -> 14.5 us
  transfers between devices with their start and end apart: 30 -> 23, of which waited for: 17 -> 13; matrix products, arithmetic and copies ran while one was open for 3% -> 3% of each run, Pallas kernels for 15% -> 13%
where the time goes in v7:
time: 530 us; the launch traced here: 528 us
  waiting for transfers between devices  297 us (56%)
  starting transfers between devices  109 us (21%)
  Pallas kernels  90.1 us (17%)
  local copies, waits for them, and re-layouts  26 us (5%)
  other arithmetic  5.44 us (1%)
    ppermute x21, waiting for transfers between devices, send(): return lax.ppermute(piece, owner_axes, hops)  282 us
    ppermute x21, starting transfers between devices, send(): return lax.ppermute(piece, owner_axes, hops)  84.4 us
    pallas_call x3, Pallas kernels, coeffs_and_gram(): pl.pallas_call(functools.partial(coeff_kernel, sec_count, sec_local, freq...  30.5 us
    pallas_call x16, Pallas kernels, take(): pl.pallas_call(take_kernel, grid_spec=pltpu.PrefetchScalarGridSpec(num_sc...  23 us
    pallas_call x8, Pallas kernels, mix(): pl.pallas_call(functools.partial(mix_kernel, orders, fields), grid_spec=p...  19.5 us
    all_to_all x1, starting transfers between devices, local(): gram = lax.all_to_all(gram, axes, split_axis=0, concat_axis=0, tiled=True)  19.3 us
    unnamed x44, local copies, waits for them, and re-layouts  14.5 us
    pallas_call x8, Pallas kernels, unpack(): pl.pallas_call(unpack_kernel, grid_spec=pltpu.PrefetchScalarGridSpec(num_...  13.2 us
  transfers between devices with their start and end apart: 23, of which 13 were waited for; matrix products, arithmetic and copies ran while one was open for 3% of the time, Pallas kernels for 13%

profile of v7, /device:TPU:16, one launch (start us, length us, event | category | flops | bytes accessed | tf_op | source)
XLA Modules:
  0.0 528.4 jit_solution(13259787900529710467)
XLA Ops:
  0.7 1.4 take.18
  2.1 1.6 collective-permute-start.1
  3.7 2.5 take.20
  6.5 1.4 take.22
  9.1 2.0 take.28
  11.1 2.8 collective-permute-start.10
  13.9 2.0 take.30
  18.0 1.4 take.21
  39.5 2.9 multiply_bitcast_fusion
  42.3 5.7 %reshape.495.azimuth_ref = bf16[128,256]{1,0:T(8,128)(2,1)} reshape(bf16[2,8,2,4,16,2,2,4]{7,6,5,4,3,2,1,0:T(2,128)(2,1)} %multiply_bitcast_fusion) | data formatting | bytes 131072 | tf_op jit(solution)/shard_map/reshape | solution.py:396
  48.2 85.4 %collective-permute-done.10.refs_4_ = bf16[4,1,296,256]{3,2,1,0:T(8,128)(2,1)} collective-permute-done((bf16[4,1,296,256]{3,2,1,0:T(8,128)(2,1)}, bf16[4,1,296,256]{3,2,1,0:T(8,128)(2,1)}, u32[]{:S(2)}, u32[]{:S(2)}) %collective-permute-start.10) | collective-permute-done | bytes 606240 | tf_op jit(solution)/shard_map/ppermute | solution.py:379
  133.6 16.6 %collective-permute-start.2 = (bf16[4,2,296,256]{3,2,1,0:T(8,128)(2,1)}, bf16[4,2,296,256]{3,2,1,0:T(8,128)(2,1)}, u32[]{:S(2)}, u32[]{:S(2)}) collective-permute-start(bf16[4,2,296,256]{3,2,1,0:T(8,128)(2,1)} %copy-done.6), channel_id=1, source_target_pairs={{0,12},{4,8},{8,20},{12,16},{16,28},{20,24},{24,4},{28,0},{1,13},{... | collective-permute-start | bytes 3637256 | tf_op jit(solution)/shard_map/ppermute | solution.py:379
  150.2 1.4 collective-permute-start.6
  151.6 1.5 collective-permute-start
  156.7 70.1 %collective-permute-done.2.refs_3_ = bf16[4,2,296,256]{3,2,1,0:T(8,128)(2,1)} collective-permute-done((bf16[4,2,296,256]{3,2,1,0:T(8,128)(2,1)}, bf16[4,2,296,256]{3,2,1,0:T(8,128)(2,1)}, u32[]{:S(2)}, u32[]{:S(2)}) %collective-permute-start.2) | collective-permute-done | bytes 1212448 | tf_op jit(solution)/shard_map/ppermute | solution.py:379
  227.8 38.9 %collective-permute-start.13 = (bf16[4,1,296,256]{3,2,1,0:T(8,128)(2,1)}, bf16[4,1,296,256]{3,2,1,0:T(8,128)(2,1)S(1)}, u32[]{:S(2)}, u32[]{:S(2)}) collective-permute-start(bf16[4,1,296,256]{3,2,1,0:T(8,128)(2,1)} %copy-done.13), channel_id=1, source_target_pairs={{0,28},{4,24},{8,4},{12,0},{16,12},{20,8},{24,20},{28,16},{1,29},{... | collective-permute-start | bytes 1818632 | tf_op jit(solution)/shard_map/ppermute | solution.py:379
  266.7 15.0 %collective-permute-done.6.refs_7_ = bf16[4,2,296,256]{3,2,1,0:T(8,128)(2,1)} collective-permute-done((bf16[4,2,296,256]{3,2,1,0:T(8,128)(2,1)}, bf16[4,2,296,256]{3,2,1,0:T(8,128)(2,1)}, u32[]{:S(2)}, u32[]{:S(2)}) %collective-permute-start.6) | collective-permute-done | bytes 1212448 | tf_op jit(solution)/shard_map/ppermute | solution.py:379
  281.8 10.9 %collective-permute-start.7 = (bf16[4,1,296,256]{3,2,1,0:T(8,128)(2,1)}, bf16[4,1,296,256]{3,2,1,0:T(8,128)(2,1)S(1)}, u32[]{:S(2)}, u32[]{:S(2)}) collective-permute-start(bf16[4,1,296,256]{3,2,1,0:T(8,128)(2,1)} %copy-done.11), channel_id=1, source_target_pairs={{0,4},{4,0},{8,12},{12,8},{16,20},{20,16},{24,28},{28,24},{1,5},{5... | collective-permute-start | bytes 1818632 | tf_op jit(solution)/shard_map/ppermute | solution.py:379
  293.5 10.3 %coeffs_and_gram.3 = (bf16[32,256,256]{2,1,0:T(8,128)(2,1)}, f32[32,16,128]{2,1,0:T(8,128)S(1)}) custom-call(s32[2]{0:T(128)S(1)} %pad_add_fusion.place_ref, bf16[2,2,256,168]{3,2,1,0:T(8,128)(2,1)S(1)} %copy.40.time_ref, bf16[128,256]{1,0:T(8,128)(2,1)S(1)} %copy-done.16, f32[1,256]{1,0:T(1,128)S(1)} %bitcast.83, ...), custom_call_target="tpu_custom_call" | custom-call | flops 3556769792 | bytes 9043968 | tf_op jit(solution)/shard_map/coeffs_and_gram/pallas_call | solution.py:139
  303.8 10.4 %coeffs_and_gram.4 = (bf16[32,256,256]{2,1,0:T(8,128)(2,1)}, f32[32,16,128]{2,1,0:T(8,128)S(1)}) custom-call(s32[2]{0:T(128)S(1)} %pad_add_fusion.place_ref, bf16[2,2,256,168]{3,2,1,0:T(8,128)(2,1)S(1)} %copy.40.time_ref, bf16[128,256]{1,0:T(8,128)(2,1)S(1)} %copy-done.16, f32[1,256]{1,0:T(1,128)S(1)} %bitcast.84, ...), custom_call_target="tpu_custom_call" | custom-call | flops 3556769792 | bytes 9043968 | tf_op jit(solution)/shard_map/coeffs_and_gram/pallas_call | solution.py:139
  314.2 2.9 collective-permute-done.13.refs_7_
  317.5 2.0 collective-permute-done.7.refs_1_
  319.5 9.8 %coeffs_and_gram.5 = (bf16[32,256,256]{2,1,0:T(8,128)(2,1)}, f32[32,16,128]{2,1,0:T(8,128)}) custom-call(s32[2]{0:T(128)S(1)} %pad_add_fusion.place_ref, bf16[2,2,256,168]{3,2,1,0:T(8,128)(2,1)S(1)} %copy.40.time_ref, bf16[128,256]{1,0:T(8,128)(2,1)S(1)} %copy-done.17, f32[1,256]{1,0:T(1,128)S(1)} %bitcast.85, ...), custom_call_target="tpu_custom_call" | custom-call | flops 3556769792 | bytes 9043968 | tf_op jit(solution)/shard_map/coeffs_and_gram/pallas_call | solution.py:139
  329.3 19.3 %all-to-all-start = ((f32[32,1,16,128]{3,2,1,0:T(8,128)}), f32[32,1,16,128]{3,2,1,0:T(8,128)S(1)}, u32[]{:S(2)}, u32[]{:S(2)}) async-start(f32[32,1,16,128]{3,2,1,0:T(8,128)} %bitcast.23), calls=%async_computation | async-start | bytes 524288 | tf_op jit(solution)/shard_map/all_to_all | solution.py:429
  349.4 7.5 %all-to-all-done = f32[32,1,16,128]{3,2,1,0:T(8,128)S(1)} async-done(((f32[32,1,16,128]{3,2,1,0:T(8,128)}), f32[32,1,16,128]{3,2,1,0:T(8,128)S(1)}, u32[]{:S(2)}, u32[]{:S(2)}) %all-to-all-start) | async-done | bytes 262176 | tf_op jit(solution)/shard_map/all_to_all | solution.py:429
  357.8 4.0 subspace.1
  364.7 4.9 all-to-all-start.1
  370.0 6.9 %all-to-all-done.1 = bf16[32,1,18,128]{3,2,1,0:T(8,128)(2,1)S(1)} async-done(((bf16[32,1,18,128]{3,2,1,0:T(8,128)(2,1)}), bf16[32,1,18,128]{3,2,1,0:T(8,128)(2,1)S(1)}, u32[]{:S(2)}, u32[]{:S(2)}) %all-to-all-start.1) | async-done | bytes 147488 | tf_op jit(solution)/shard_map/all_to_all | solution.py:446
  377.5 2.2 copy-done
  379.7 2.0 mix.8.refs_3_
  381.8 1.9 collective-permute-start.20
  383.7 2.2 mix.9.refs_3_
  387.1 3.1 mix.10.refs_3_
  391.5 3.1 mix.11.refs_3_
  394.6 2.8 collective-permute-start.17
  397.4 2.2 mix.12.refs_3_
  399.7 2.2 mix.13.refs_3_
  401.9 66.2 %collective-permute-done.20 = bf16[3,4,128,256]{3,2,1,0:T(8,128)(2,1)S(1)} collective-permute-done((bf16[3,4,128,256]{3,2,1,0:T(8,128)(2,1)S(1)}, bf16[3,4,128,256]{3,2,1,0:T(8,128)(2,1)S(1)}, u32[]{:S(2)}, u32[]{:S(2)}) %collective-permute-start.20) | collective-permute-done | bytes 786464 | tf_op jit(solution)/shard_map/ppermute | solution.py:379
  468.1 2.5 mix.14.refs_3_
  470.6 14.4 %collective-permute-done.19 = bf16[3,4,128,256]{3,2,1,0:T(8,128)(2,1)S(1)} collective-permute-done((bf16[3,4,128,256]{3,2,1,0:T(8,128)(2,1)S(1)}, bf16[3,4,128,256]{3,2,1,0:T(8,128)(2,1)S(1)}, u32[]{:S(2)}, u32[]{:S(2)}) %collective-permute-start.19) | collective-permute-done | bytes 786464 | tf_op jit(solution)/shard_map/ppermute | solution.py:379
  486.9 2.2 mix.15
  493.3 10.4 %collective-permute-done.18 = bf16[3,4,128,256]{3,2,1,0:T(8,128)(2,1)} collective-permute-done((bf16[3,4,128,256]{3,2,1,0:T(8,128)(2,1)}, bf16[3,4,128,256]{3,2,1,0:T(8,128)(2,1)}, u32[]{:S(2)}, u32[]{:S(2)}) %collective-permute-start.18) | collective-permute-done | bytes 786464 | tf_op jit(solution)/shard_map/ppermute | solution.py:379
  503.7 2.1 unpack.11.refs_0_
  505.8 14.4 %collective-permute-done.17 = bf16[3,4,128,256]{3,2,1,0:T(8,128)(2,1)} collective-permute-done((bf16[3,4,128,256]{3,2,1,0:T(8,128)(2,1)}, bf16[3,4,128,256]{3,2,1,0:T(8,128)(2,1)}, u32[]{:S(2)}, u32[]{:S(2)}) %collective-permute-start.17) | collective-permute-done | bytes 786464 | tf_op jit(solution)/shard_map/ppermute | solution.py:379
  520.1 2.1 unpack.12.refs_0_
  522.2 2.1 unpack.13.refs_0_
  524.3 2.1 unpack.14.refs_0_
  526.3 2.1 unpack.15
  (126 shorter events, 43.5 us)
Async XLA Ops:
  2.1 148.1 %collective-permute-start.1 = (bf16[4,2,296,256]{3,2,1,0:T(8,128)(2,1)S(1)}, bf16[4,2,296,256]{3,2,1,0:T(8,128)(2,1)}, u32[]{:S(2)}, u32[]{:S(2)}) collective-permute-start(bf16[4,2,296,256]{3,2,1,0:T(8,128)(2,1)S(1)} %take.18), channel_id=1, source_target_pairs={{0,8},{4,12},{8,16},{12,20},{16,24},{20,28},{24,0},{28,4},{1,9},{5... | collective-permute-start | bytes 3637256 | tf_op jit(solution)/shard_map/ppermute | solution.py:379
  6.1 145.5 %collective-permute-start.3 = (bf16[4,2,296,256]{3,2,1,0:T(8,128)(2,1)}, bf16[4,2,296,256]{3,2,1,0:T(8,128)(2,1)}, u32[]{:S(2)}, u32[]{:S(2)}) collective-permute-start(bf16[4,2,296,256]{3,2,1,0:T(8,128)(2,1)} %take.20), channel_id=1, source_target_pairs={{0,16},{4,20},{8,24},{12,28},{16,0},{20,4},{24,8},{28,12},{1,17},{... | collective-permute-start | bytes 3637256 | tf_op jit(solution)/shard_map/ppermute | solution.py:379
  7.9 148.2 %collective-permute-start.5 = (bf16[4,2,296,256]{3,2,1,0:T(8,128)(2,1)S(1)}, bf16[4,2,296,256]{3,2,1,0:T(8,128)(2,1)}, u32[]{:S(2)}, u32[]{:S(2)}) collective-permute-start(bf16[4,2,296,256]{3,2,1,0:T(8,128)(2,1)S(1)} %take.22), channel_id=1, source_target_pairs={{0,24},{4,28},{8,0},{12,4},{16,8},{20,12},{24,16},{28,20},{1,25},{... | collective-permute-start | bytes 3637256 | tf_op jit(solution)/shard_map/ppermute | solution.py:379
  11.1 122.5 %collective-permute-start.10 = (bf16[4,1,296,256]{3,2,1,0:T(8,128)(2,1)}, bf16[4,1,296,256]{3,2,1,0:T(8,128)(2,1)}, u32[]{:S(2)}, u32[]{:S(2)}) collective-permute-start(bf16[4,1,296,256]{3,2,1,0:T(8,128)(2,1)} %take.28), channel_id=1, source_target_pairs={{0,16},{4,20},{8,24},{12,28},{16,0},{20,4},{24,8},{28,12},{1,17},{... | collective-permute-start | bytes 1818632 | tf_op jit(solution)/shard_map/ppermute | solution.py:379
  15.8 134.4 %collective-permute-start.12 = (bf16[4,1,296,256]{3,2,1,0:T(8,128)(2,1)}, bf16[4,1,296,256]{3,2,1,0:T(8,128)(2,1)}, u32[]{:S(2)}, u32[]{:S(2)}) collective-permute-start(bf16[4,1,296,256]{3,2,1,0:T(8,128)(2,1)} %take.30), channel_id=1, source_target_pairs={{0,24},{4,28},{8,0},{12,4},{16,8},{20,12},{24,16},{28,20},{1,25},{... | collective-permute-start | bytes 1818632 | tf_op jit(solution)/shard_map/ppermute | solution.py:379
  17.2 0.8 copy-start.15
  19.4 1.1 copy-start.5
  21.6 0.8 copy-start.14
  23.8 1.0 copy-start.4
  26.0 0.8 copy-start.13
  28.2 1.0 copy-start.6
  30.4 0.8 copy-start.12
  32.6 1.1 copy-start.3
  34.8 0.8 copy-start.11
  37.0 1.0 copy-start.1
  39.5 8.6 %copy-start.20 = (s32[16]{0:T(128)S(1)}, s32[16]{0:T(128)}, u32[]{:S(2)}) copy-start(s32[16]{0:T(128)} %param.6) | copy-start | bytes 196
  133.6 93.3 %collective-permute-start.2 = (bf16[4,2,296,256]{3,2,1,0:T(8,128)(2,1)}, bf16[4,2,296,256]{3,2,1,0:T(8,128)(2,1)}, u32[]{:S(2)}, u32[]{:S(2)}) collective-permute-start(bf16[4,2,296,256]{3,2,1,0:T(8,128)(2,1)} %copy-done.6), channel_id=1, source_target_pairs={{0,12},{4,8},{8,20},{12,16},{16,28},{20,24},{24,4},{28,0},{1,13},{... | collective-permute-start | bytes 3637256 | tf_op jit(solution)/shard_map/ppermute | solution.py:379
  150.2 77.6 %collective-permute-start.4 = (bf16[4,2,296,256]{3,2,1,0:T(8,128)(2,1)}, bf16[4,2,296,256]{3,2,1,0:T(8,128)(2,1)}, u32[]{:S(2)}, u32[]{:S(2)}) collective-permute-start(bf16[4,2,296,256]{3,2,1,0:T(8,128)(2,1)} %copy-done.5), channel_id=1, source_target_pairs={{0,20},{4,16},{8,28},{12,24},{16,4},{20,0},{24,12},{28,8},{1,21},{... | collective-permute-start | bytes 3637256 | tf_op jit(solution)/shard_map/ppermute | solution.py:379
  150.2 142.5 %copy-start.2 = (bf16[4,2,296,256]{3,2,1,0:T(8,128)(2,1)S(1)}, bf16[4,2,296,256]{3,2,1,0:T(8,128)(2,1)}, u32[]{:S(2)}) copy-start(bf16[4,2,296,256]{3,2,1,0:T(8,128)(2,1)} %copy-done.1) | copy-start | bytes 3637252
  150.2 131.5 %collective-permute-start.6 = (bf16[4,2,296,256]{3,2,1,0:T(8,128)(2,1)}, bf16[4,2,296,256]{3,2,1,0:T(8,128)(2,1)}, u32[]{:S(2)}, u32[]{:S(2)}) collective-permute-start(bf16[4,2,296,256]{3,2,1,0:T(8,128)(2,1)} %copy-done.4), channel_id=1, source_target_pairs={{0,28},{4,24},{8,4},{12,0},{16,12},{20,8},{24,20},{28,16},{1,29},{... | collective-permute-start | bytes 3637256 | tf_op jit(solution)/shard_map/ppermute | solution.py:379
  151.6 130.1 %collective-permute-start = (bf16[4,2,296,256]{3,2,1,0:T(8,128)(2,1)}, bf16[4,2,296,256]{3,2,1,0:T(8,128)(2,1)}, u32[]{:S(2)}, u32[]{:S(2)}) collective-permute-start(bf16[4,2,296,256]{3,2,1,0:T(8,128)(2,1)} %copy-done.3), channel_id=1, source_target_pairs={{0,4},{4,0},{8,12},{12,8},{16,20},{20,16},{24,28},{28,24},{1,5},{5... | collective-permute-start | bytes 3637256 | tf_op jit(solution)/shard_map/ppermute | solution.py:379
  156.1 163.5 %copy-start.18 = (f32[256]{0:T(256)}, f32[256]{0:T(256)S(1)}, u32[]{:S(2)}) copy-start(f32[256]{0:T(256)S(1)} %select_reduce_fusion) | copy-start | bytes 3076
  156.1 158.1 %collective-permute-start.8 = (bf16[4,1,296,256]{3,2,1,0:T(8,128)(2,1)}, bf16[4,1,296,256]{3,2,1,0:T(8,128)(2,1)S(1)}, u32[]{:S(2)}, u32[]{:S(2)}) collective-permute-start(bf16[4,1,296,256]{3,2,1,0:T(8,128)(2,1)} %copy-done.15), channel_id=1, source_target_pairs={{0,8},{4,12},{8,16},{12,20},{16,24},{20,28},{24,0},{28,4},{1,9},{5... | collective-permute-start | bytes 1818632 | tf_op jit(solution)/shard_map/ppermute | solution.py:379
  226.8 87.4 %collective-permute-start.11 = (bf16[4,1,296,256]{3,2,1,0:T(8,128)(2,1)}, bf16[4,1,296,256]{3,2,1,0:T(8,128)(2,1)S(1)}, u32[]{:S(2)}, u32[]{:S(2)}) collective-permute-start(bf16[4,1,296,256]{3,2,1,0:T(8,128)(2,1)} %copy-done.14), channel_id=1, source_target_pairs={{0,20},{4,16},{8,28},{12,24},{16,4},{20,0},{24,12},{28,8},{1,21},{... | collective-permute-start | bytes 1818632 | tf_op jit(solution)/shard_map/ppermute | solution.py:379
  227.8 89.4 %collective-permute-start.13 = (bf16[4,1,296,256]{3,2,1,0:T(8,128)(2,1)}, bf16[4,1,296,256]{3,2,1,0:T(8,128)(2,1)S(1)}, u32[]{:S(2)}, u32[]{:S(2)}) collective-permute-start(bf16[4,1,296,256]{3,2,1,0:T(8,128)(2,1)} %copy-done.13), channel_id=1, source_target_pairs={{0,28},{4,24},{8,4},{12,0},{16,12},{20,8},{24,20},{28,16},{1,29},{... | collective-permute-start | bytes 1818632 | tf_op jit(solution)/shard_map/ppermute | solution.py:379
  281.7 35.7 %collective-permute-start.9 = (bf16[4,1,296,256]{3,2,1,0:T(8,128)(2,1)}, bf16[4,1,296,256]{3,2,1,0:T(8,128)(2,1)S(1)}, u32[]{:S(2)}, u32[]{:S(2)}) collective-permute-start(bf16[4,1,296,256]{3,2,1,0:T(8,128)(2,1)} %copy-done.12), channel_id=1, source_target_pairs={{0,12},{4,8},{8,20},{12,16},{16,28},{20,24},{24,4},{28,0},{1,13},{... | collective-permute-start | bytes 1818632 | tf_op jit(solution)/shard_map/ppermute | solution.py:379
  281.8 37.8 %collective-permute-start.7 = (bf16[4,1,296,256]{3,2,1,0:T(8,128)(2,1)}, bf16[4,1,296,256]{3,2,1,0:T(8,128)(2,1)S(1)}, u32[]{:S(2)}, u32[]{:S(2)}) collective-permute-start(bf16[4,1,296,256]{3,2,1,0:T(8,128)(2,1)} %copy-done.11), channel_id=1, source_target_pairs={{0,4},{4,0},{8,12},{12,8},{16,20},{20,16},{24,28},{28,24},{1,5},{5... | collective-permute-start | bytes 1818632 | tf_op jit(solution)/shard_map/ppermute | solution.py:379
  292.7 0.8 copy-start.16
  303.8 15.7 %copy-start.17 = (bf16[128,256]{1,0:T(8,128)(2,1)S(1)}, bf16[128,256]{1,0:T(8,128)(2,1)}, u32[]{:S(2)}) copy-start(bf16[128,256]{1,0:T(8,128)(2,1)} %reshape.495.azimuth_ref) | copy-start | bytes 196612
  329.3 40.3 %copy-start.19 = (bf16[2,2,2]{2,1,0:T(2,128)(2,1)S(1)}, bf16[2,2,2]{2,1,0:T(2,128)(2,1)}, u32[]{:S(2)}) copy-start(bf16[2,2,2]{2,1,0:T(2,128)(2,1)} %constant.235.clone) | copy-start | bytes 52
  329.3 27.6 %all-to-all-start = ((f32[32,1,16,128]{3,2,1,0:T(8,128)}), f32[32,1,16,128]{3,2,1,0:T(8,128)S(1)}, u32[]{:S(2)}, u32[]{:S(2)}) async-start(f32[32,1,16,128]{3,2,1,0:T(8,128)} %bitcast.23), calls=%async_computation | async-start | bytes 524288 | tf_op jit(solution)/shard_map/all_to_all | solution.py:429
  364.7 12.3 %all-to-all-start.1 = ((bf16[32,1,18,128]{3,2,1,0:T(8,128)(2,1)}), bf16[32,1,18,128]{3,2,1,0:T(8,128)(2,1)S(1)}, u32[]{:S(2)}, u32[]{:S(2)}) async-start(bf16[32,1,18,128]{3,2,1,0:T(8,128)(2,1)} %broadcast_in_dim.27), calls=%async_computation.1 | async-start | bytes 393216 | tf_op jit(solution)/shard_map/all_to_all | solution.py:446
  377.5 2.2 copy-start
  381.8 86.3 %collective-permute-start.20 = (bf16[3,4,128,256]{3,2,1,0:T(8,128)(2,1)S(1)}, bf16[3,4,128,256]{3,2,1,0:T(8,128)(2,1)S(1)}, u32[]{:S(2)}, u32[]{:S(2)}) collective-permute-start(bf16[3,4,128,256]{3,2,1,0:T(8,128)(2,1)S(1)} %mix.8.refs_3_), channel_id=1, source_target_pairs={{0,16},{4,20},{8,24},{12,28},{16,0},{20,4},{24,8},{28,12},{1,17},{... | collective-permute-start | bytes 2359304 | tf_op jit(solution)/shard_map/ppermute | solution.py:379
  385.9 99.1 %collective-permute-start.19 = (bf16[3,4,128,256]{3,2,1,0:T(8,128)(2,1)S(1)}, bf16[3,4,128,256]{3,2,1,0:T(8,128)(2,1)S(1)}, u32[]{:S(2)}, u32[]{:S(2)}) collective-permute-start(bf16[3,4,128,256]{3,2,1,0:T(8,128)(2,1)S(1)} %mix.9.refs_3_), channel_id=1, source_target_pairs={{0,20},{4,16},{8,28},{12,24},{16,4},{20,0},{24,12},{28,8},{1,21},{... | collective-permute-start | bytes 2359304 | tf_op jit(solution)/shard_map/ppermute | solution.py:379
  390.2 113.5 %collective-permute-start.18 = (bf16[3,4,128,256]{3,2,1,0:T(8,128)(2,1)}, bf16[3,4,128,256]{3,2,1,0:T(8,128)(2,1)}, u32[]{:S(2)}, u32[]{:S(2)}) collective-permute-start(bf16[3,4,128,256]{3,2,1,0:T(8,128)(2,1)} %mix.10.refs_3_), channel_id=1, source_target_pairs={{0,8},{4,12},{8,16},{12,20},{16,24},{20,28},{24,0},{28,4},{1,9},{5... | collective-permute-start | bytes 2359304 | tf_op jit(solution)/shard_map/ppermute | solution.py:379
  394.6 125.6 %collective-permute-start.17 = (bf16[3,4,128,256]{3,2,1,0:T(8,128)(2,1)}, bf16[3,4,128,256]{3,2,1,0:T(8,128)(2,1)}, u32[]{:S(2)}, u32[]{:S(2)}) collective-permute-start(bf16[3,4,128,256]{3,2,1,0:T(8,128)(2,1)} %mix.11.refs_3_), channel_id=1, source_target_pairs={{0,12},{4,8},{8,20},{12,16},{16,28},{20,24},{24,4},{28,0},{1,13},{... | collective-permute-start | bytes 2359304 | tf_op jit(solution)/shard_map/ppermute | solution.py:379
  399.6 122.6 %collective-permute-start.16 = (bf16[3,4,128,256]{3,2,1,0:T(8,128)(2,1)S(1)}, bf16[3,4,128,256]{3,2,1,0:T(8,128)(2,1)}, u32[]{:S(2)}, u32[]{:S(2)}) collective-permute-start(bf16[3,4,128,256]{3,2,1,0:T(8,128)(2,1)S(1)} %mix.12.refs_3_), channel_id=1, source_target_pairs={{0,24},{4,28},{8,0},{12,4},{16,8},{20,12},{24,16},{28,20},{1,25},{... | collective-permute-start | bytes 2359304 | tf_op jit(solution)/shard_map/ppermute | solution.py:379
  468.1 2.5 copy-start.7
  468.1 56.2 %collective-permute-start.15 = (bf16[3,4,128,256]{3,2,1,0:T(8,128)(2,1)S(1)}, bf16[3,4,128,256]{3,2,1,0:T(8,128)(2,1)}, u32[]{:S(2)}, u32[]{:S(2)}) collective-permute-start(bf16[3,4,128,256]{3,2,1,0:T(8,128)(2,1)S(1)} %mix.13.refs_3_), channel_id=1, source_target_pairs={{0,28},{4,24},{8,4},{12,0},{16,12},{20,8},{24,20},{28,16},{1,29},{... | collective-permute-start | bytes 2359304 | tf_op jit(solution)/shard_map/ppermute | solution.py:379
  485.0 0.9 copy-start.9
  485.9 40.5 %collective-permute-start.14 = (bf16[3,4,128,256]{3,2,1,0:T(8,128)(2,1)S(1)}, bf16[3,4,128,256]{3,2,1,0:T(8,128)(2,1)}, u32[]{:S(2)}, u32[]{:S(2)}) collective-permute-start(bf16[3,4,128,256]{3,2,1,0:T(8,128)(2,1)S(1)} %mix.14.refs_3_), channel_id=1, source_target_pairs={{0,4},{4,0},{8,12},{12,8},{16,20},{20,16},{24,28},{28,24},{1,5},{5... | collective-permute-start | bytes 2359304 | tf_op jit(solution)/shard_map/ppermute | solution.py:379
  489.1 1.8 copy-start.8
  491.0 1.4 copy-start.10

commit v8 on v6

--- a/solution.py
+++ b/solution.py
@@ -311,9 +311,8 @@
 def unpack_kernel(owner_ref, piece_ref, *refs):
     out_ref = refs[-1]
     for k in range(piece_ref.shape[0]):
-        for f in range(piece_ref.shape[1]):
-            for d in range(piece_ref.shape[2]):
-                out_ref[:, f, d, k] = piece_ref[k, f, d]
+        for d in range(piece_ref.shape[2]):
+            out_ref[:, 0, d, k] = piece_ref[k, 0, d]
 
 
 def unpack(owner, piece, owners, whole):
@@ -325,16 +324,18 @@
         return lax.dynamic_update_slice_in_dim(whole, piece, owner * part, 5)
     inputs = [piece] if whole is None else [piece, whole]
     in_specs = [
-        pl.BlockSpec(piece.shape, lambda i, at: (0, 0, 0, 0, 0, 0)),
+        pl.BlockSpec((fields, 1) + piece.shape[2:], lambda i, at: (0, i, 0, 0, 0, 0)),
         pl.BlockSpec(memory_space=pl.ANY),
     ]
     return pl.pallas_call(
         unpack_kernel,
         grid_spec=pltpu.PrefetchScalarGridSpec(
             num_scalar_prefetch=1,
-            grid=(1,),
+            grid=(freqs,),
             in_specs=in_specs[:len(inputs)],
-            out_specs=pl.BlockSpec(shape[:5] + (part,), lambda i, at: (0, 0, 0, 0, 0, at[0])),
+            out_specs=pl.BlockSpec(
+                (orders, 1) + shape[2:5] + (part,), lambda i, at: (0, i, 0, 0, 0, at[0])
+            ),
         ),
         out_shape=jax.ShapeDtypeStruct(shape, piece.dtype),
         input_output_aliases={} if whole is None else {2: 0},
@@ -459,16 +460,18 @@
         (2, 2, blocks, 2, orders, blocks),
     ).reshape(2, depth, depth * orders)
 
-    sent = []
+    coeffs = [pltpu.with_memory_space_constraint(x, pltpu.HBM) for x in coeffs]
+    sent = {}
     before = ()
     for z, x in in_order + [(0, 0)]:
         piece = mix(
             owner_after(z, x), coeffs, mixing, spread, factor, root_weight, owners, orders, before
         )
         before = (piece,)
-        sent.append((owner_after(-z, -x), send(piece, z, x)))
+        sent[z, x] = owner_after(-z, -x), send(piece, z, x)
     mode_fields = None
-    for owner, piece in sent[-1:] + sent[:-1]:
+    for r in sorted(sent, key=lambda r: (r != (0, 0), r[0] == 0, r[0] == 1, in_order.index(r) if r in in_order else 0)):
+        owner, piece = sent[r]
         piece = piece.reshape(fields, own_freqs, 2, orders, MODES, part)
         mode_fields = unpack(owner, piece, owners, mode_fields)
     mode_fields = jnp.transpose(mode_fields, (0, 1, 2, 4, 3, 5))

time: 515 us -> 518 us (level)
  Pallas kernels: 98.1 us -> 106 us
    pallas_call x8, Pallas kernels: 13.2 us -> 20.9 us  [unpack(): pl.pallas_call(unpack_kernel, grid_spec=pltpu.PrefetchScalarGridSpec(num_...]
    unnamed x46 -> x44, local copies, waits for them, and re-layouts: 17.7 us -> 15 us
  transfers between devices with their start and end apart: 30 -> 30, of which waited for: 17 -> 17; matrix products, arithmetic and copies ran while one was open for 3% -> 3% of each run, Pallas kernels for 15% -> 17%
where the time goes in v8:
time: 518 us; the launch traced here: 514 us
  waiting for transfers between devices  312 us (60%)
  Pallas kernels  106 us (20%)
  starting transfers between devices  61.5 us (12%)
  local copies, waits for them, and re-layouts  26.6 us (5%)
  other arithmetic  5.44 us (1%)
    ppermute x28, waiting for transfers between devices, send(): return lax.ppermute(piece, owner_axes, hops)  298 us
    ppermute x28, starting transfers between devices, send(): return lax.ppermute(piece, owner_axes, hops)  49.1 us
    pallas_call x24, Pallas kernels, take(): pl.pallas_call(take_kernel, grid_spec=pltpu.PrefetchScalarGridSpec(num_sc...  31.3 us
    pallas_call x3, Pallas kernels, coeffs_and_gram(): pl.pallas_call(functools.partial(coeff_kernel, sec_count, sec_local, freq...  30.4 us
    pallas_call x8, Pallas kernels, unpack(): pl.pallas_call(unpack_kernel, grid_spec=pltpu.PrefetchScalarGridSpec(num_...  20.9 us
    pallas_call x8, Pallas kernels, mix(): pl.pallas_call(functools.partial(mix_kernel, orders, fields), grid_spec=p...  19.4 us
    unnamed x44, local copies, waits for them, and re-layouts  15 us
  transfers between devices with their start and end apart: 30, of which 17 were waited for; matrix products, arithmetic and copies ran while one was open for 3% of the time, Pallas kernels for 17%

profile of v8, /device:TPU:16, one launch (start us, length us, event | category | flops | bytes accessed | tf_op | source)
XLA Modules:
  0.0 513.6 jit_solution(12683385798462156924)
XLA Ops:
  11.4 2.6 collective-permute-start.4
  14.2 2.0 take.36
  16.2 2.0 take.38
  18.1 2.0 take.34
  26.2 18.3 %collective-permute-done.1.refs_2_ = bf16[4,296,256]{2,1,0:T(8,128)(2,1)} collective-permute-done((bf16[4,296,256]{2,1,0:T(8,128)(2,1)S(1)}, bf16[4,296,256]{2,1,0:T(8,128)(2,1)}, u32[]{:S(2)}, u32[]{:S(2)}) %collective-permute-start.1) | collective-permute-done | bytes 606240 | tf_op jit(solution)/shard_map/ppermute | solution.py:381
  44.6 2.9 multiply_bitcast_fusion
  49.0 32.2 %collective-permute-done.5.refs_6_ = bf16[4,296,256]{2,1,0:T(8,128)(2,1)} collective-permute-done((bf16[4,296,256]{2,1,0:T(8,128)(2,1)S(1)}, bf16[4,296,256]{2,1,0:T(8,128)(2,1)}, u32[]{:S(2)}, u32[]{:S(2)}) %collective-permute-start.5) | collective-permute-done | bytes 606240 | tf_op jit(solution)/shard_map/ppermute | solution.py:381
  81.2 42.2 %collective-permute-done.2.refs_3_ = bf16[4,296,256]{2,1,0:T(8,128)(2,1)} collective-permute-done((bf16[4,296,256]{2,1,0:T(8,128)(2,1)S(1)}, bf16[4,296,256]{2,1,0:T(8,128)(2,1)}, u32[]{:S(2)}, u32[]{:S(2)}) %collective-permute-start.2) | collective-permute-done | bytes 606240 | tf_op jit(solution)/shard_map/ppermute | solution.py:381
  123.4 14.4 %collective-permute-start.8 = (bf16[4,296,256]{2,1,0:T(8,128)(2,1)}, bf16[4,296,256]{2,1,0:T(8,128)(2,1)}, u32[]{:S(2)}, u32[]{:S(2)}) collective-permute-start(bf16[4,296,256]{2,1,0:T(8,128)(2,1)} %take.34), channel_id=1, source_target_pairs={{0,8},{4,12},{8,16},{12,20},{16,24},{20,28},{24,0},{28,4},{1,9},{5... | collective-permute-start | bytes 1818632 | tf_op jit(solution)/shard_map/ppermute | solution.py:381
  160.3 5.7 %reshape.503.azimuth_ref = bf16[128,256]{1,0:T(8,128)(2,1)} reshape(bf16[2,8,2,4,16,2,2,4]{7,6,5,4,3,2,1,0:T(2,128)(2,1)} %multiply_bitcast_fusion) | data formatting | bytes 131072 | tf_op jit(solution)/shard_map/reshape | solution.py:396
  166.2 2.4 collective-permute-start.13
  169.2 3.1 collective-permute-done.12.refs_6_
  173.8 13.7 %collective-permute-done.8.refs_2_ = bf16[4,296,256]{2,1,0:T(8,128)(2,1)} collective-permute-done((bf16[4,296,256]{2,1,0:T(8,128)(2,1)}, bf16[4,296,256]{2,1,0:T(8,128)(2,1)}, u32[]{:S(2)}, u32[]{:S(2)}) %collective-permute-start.8) | collective-permute-done | bytes 606240 | tf_op jit(solution)/shard_map/ppermute | solution.py:381
  187.5 36.8 %collective-permute-done.11.refs_5_ = bf16[4,296,256]{2,1,0:T(8,128)(2,1)} collective-permute-done((bf16[4,296,256]{2,1,0:T(8,128)(2,1)}, bf16[4,296,256]{2,1,0:T(8,128)(2,1)}, u32[]{:S(2)}, u32[]{:S(2)}) %collective-permute-start.11) | collective-permute-done | bytes 606240 | tf_op jit(solution)/shard_map/ppermute | solution.py:381
  224.3 4.3 collective-permute-start.17
  231.4 5.9 %collective-permute-done.13.refs_7_ = bf16[4,296,256]{2,1,0:T(8,128)(2,1)} collective-permute-done((bf16[4,296,256]{2,1,0:T(8,128)(2,1)}, bf16[4,296,256]{2,1,0:T(8,128)(2,1)}, u32[]{:S(2)}, u32[]{:S(2)}) %collective-permute-start.13) | collective-permute-done | bytes 606240 | tf_op jit(solution)/shard_map/ppermute | solution.py:381
  237.3 3.4 collective-permute-start.19
  240.7 2.4 collective-permute-start.18
  243.9 6.5 %collective-permute-done.17.refs_4_ = bf16[4,296,256]{2,1,0:T(8,128)(2,1)} collective-permute-done((bf16[4,296,256]{2,1,0:T(8,128)(2,1)}, bf16[4,296,256]{2,1,0:T(8,128)(2,1)}, u32[]{:S(2)}, u32[]{:S(2)}) %collective-permute-start.17) | collective-permute-done | bytes 606240 | tf_op jit(solution)/shard_map/ppermute | solution.py:381
  254.8 10.2 %coeffs_and_gram.3 = (bf16[32,256,256]{2,1,0:T(8,128)(2,1)}, f32[32,16,128]{2,1,0:T(8,128)S(1)}) custom-call(s32[2]{0:T(128)S(1)} %pad_add_fusion.place_ref, bf16[2,2,256,168]{3,2,1,0:T(8,128)(2,1)S(1)} %copy.40.time_ref, bf16[128,256]{1,0:T(8,128)(2,1)S(1)} %copy-done.15, f32[1,256]{1,0:T(1,128)S(1)} %bitcast.83, ...), custom_call_target="tpu_custom_call" | custom-call | flops 3556769792 | bytes 9043968 | tf_op jit(solution)/shard_map/coeffs_and_gram/pallas_call | solution.py:139
  265.1 10.3 %coeffs_and_gram.4 = (bf16[32,256,256]{2,1,0:T(8,128)(2,1)}, f32[32,16,128]{2,1,0:T(8,128)S(1)}) custom-call(s32[2]{0:T(128)S(1)} %pad_add_fusion.place_ref, bf16[2,2,256,168]{3,2,1,0:T(8,128)(2,1)S(1)} %copy.40.time_ref, bf16[128,256]{1,0:T(8,128)(2,1)S(1)} %copy-done.15, f32[1,256]{1,0:T(1,128)S(1)} %bitcast.84, ...), custom_call_target="tpu_custom_call" | custom-call | flops 3556769792 | bytes 9043968 | tf_op jit(solution)/shard_map/coeffs_and_gram/pallas_call | solution.py:139
  275.4 13.9 %collective-permute-done.19.refs_6_ = bf16[4,296,256]{2,1,0:T(8,128)(2,1)S(1)} collective-permute-done((bf16[4,296,256]{2,1,0:T(8,128)(2,1)}, bf16[4,296,256]{2,1,0:T(8,128)(2,1)S(1)}, u32[]{:S(2)}, u32[]{:S(2)}) %collective-permute-start.19) | collective-permute-done | bytes 606240 | tf_op jit(solution)/shard_map/ppermute | solution.py:381
  289.3 16.3 %collective-permute-done.16.refs_3_ = bf16[4,296,256]{2,1,0:T(8,128)(2,1)S(1)} collective-permute-done((bf16[4,296,256]{2,1,0:T(8,128)(2,1)S(1)}, bf16[4,296,256]{2,1,0:T(8,128)(2,1)S(1)}, u32[]{:S(2)}, u32[]{:S(2)}) %collective-permute-start.16) | collective-permute-done | bytes 606240 | tf_op jit(solution)/shard_map/ppermute | solution.py:381
  305.6 9.5 %collective-permute-done.20.refs_7_ = bf16[4,296,256]{2,1,0:T(8,128)(2,1)S(1)} collective-permute-done((bf16[4,296,256]{2,1,0:T(8,128)(2,1)S(1)}, bf16[4,296,256]{2,1,0:T(8,128)(2,1)S(1)}, u32[]{:S(2)}, u32[]{:S(2)}) %collective-permute-start.20) | collective-permute-done | bytes 606240 | tf_op jit(solution)/shard_map/ppermute | solution.py:381
  315.1 9.9 %coeffs_and_gram.5 = (bf16[32,256,256]{2,1,0:T(8,128)(2,1)}, f32[32,16,128]{2,1,0:T(8,128)}) custom-call(s32[2]{0:T(128)S(1)} %pad_add_fusion.place_ref, bf16[2,2,256,168]{3,2,1,0:T(8,128)(2,1)S(1)} %copy.40.time_ref, bf16[128,256]{1,0:T(8,128)(2,1)S(1)} %copy-done.15, f32[1,256]{1,0:T(1,128)S(1)} %bitcast.85, ...), custom_call_target="tpu_custom_call" | custom-call | flops 3556769792 | bytes 9043968 | tf_op jit(solution)/shard_map/coeffs_and_gram/pallas_call | solution.py:139
  325.0 7.5 %all-to-all-start = ((f32[32,1,16,128]{3,2,1,0:T(8,128)}), f32[32,1,16,128]{3,2,1,0:T(8,128)S(1)}, u32[]{:S(2)}, u32[]{:S(2)}) async-start(f32[32,1,16,128]{3,2,1,0:T(8,128)} %bitcast.23), calls=%async_computation | async-start | bytes 524288 | tf_op jit(solution)/shard_map/all_to_all | solution.py:429
  333.1 7.5 %all-to-all-done = f32[32,1,16,128]{3,2,1,0:T(8,128)S(1)} async-done(((f32[32,1,16,128]{3,2,1,0:T(8,128)}), f32[32,1,16,128]{3,2,1,0:T(8,128)S(1)}, u32[]{:S(2)}, u32[]{:S(2)}) %all-to-all-start) | async-done | bytes 262176 | tf_op jit(solution)/shard_map/all_to_all | solution.py:429
  341.6 4.0 subspace.1
  348.4 4.9 all-to-all-start.1
  353.8 6.9 %all-to-all-done.1 = bf16[32,1,18,128]{3,2,1,0:T(8,128)(2,1)S(1)} async-done(((bf16[32,1,18,128]{3,2,1,0:T(8,128)(2,1)}), bf16[32,1,18,128]{3,2,1,0:T(8,128)(2,1)S(1)}, u32[]{:S(2)}, u32[]{:S(2)}) %all-to-all-start.1) | async-done | bytes 147488 | tf_op jit(solution)/shard_map/all_to_all | solution.py:446
  361.3 2.2 mix.8.refs_3_
  365.4 2.2 mix.9.refs_3_
  368.9 2.2 mix.10.refs_3_
  372.4 2.2 mix.11.refs_3_
  374.6 3.1 collective-permute-start.22
  377.7 3.1 mix.12.refs_3_
  380.8 3.1 mix.13.refs_3_
  383.9 65.9 %collective-permute-done.27 = bf16[3,4,128,256]{3,2,1,0:T(8,128)(2,1)S(1)} collective-permute-done((bf16[3,4,128,256]{3,2,1,0:T(8,128)(2,1)S(1)}, bf16[3,4,128,256]{3,2,1,0:T(8,128)(2,1)S(1)}, u32[]{:S(2)}, u32[]{:S(2)}) %collective-permute-start.27) | collective-permute-done | bytes 786464 | tf_op jit(solution)/shard_map/ppermute | solution.py:381
  450.7 2.2 mix.14.refs_3_
  452.9 13.8 %collective-permute-done.26 = bf16[3,4,128,256]{3,2,1,0:T(8,128)(2,1)S(1)} collective-permute-done((bf16[3,4,128,256]{3,2,1,0:T(8,128)(2,1)S(1)}, bf16[3,4,128,256]{3,2,1,0:T(8,128)(2,1)S(1)}, u32[]{:S(2)}, u32[]{:S(2)}) %collective-permute-start.26) | collective-permute-done | bytes 786464 | tf_op jit(solution)/shard_map/ppermute | solution.py:381
  468.7 2.2 mix.15
  477.5 6.2 %collective-permute-done.25 = bf16[3,4,128,256]{3,2,1,0:T(8,128)(2,1)} collective-permute-done((bf16[3,4,128,256]{3,2,1,0:T(8,128)(2,1)}, bf16[3,4,128,256]{3,2,1,0:T(8,128)(2,1)}, u32[]{:S(2)}, u32[]{:S(2)}) %collective-permute-start.25) | collective-permute-done | bytes 786464 | tf_op jit(solution)/shard_map/ppermute | solution.py:381
  483.7 3.3 unpack.11.refs_0_
  487.0 13.6 %collective-permute-done.24 = bf16[3,4,128,256]{3,2,1,0:T(8,128)(2,1)} collective-permute-done((bf16[3,4,128,256]{3,2,1,0:T(8,128)(2,1)}, bf16[3,4,128,256]{3,2,1,0:T(8,128)(2,1)}, u32[]{:S(2)}, u32[]{:S(2)}) %collective-permute-start.24) | collective-permute-done | bytes 786464 | tf_op jit(solution)/shard_map/ppermute | solution.py:381
  500.5 3.3 unpack.12.refs_0_
  503.8 3.3 unpack.13.refs_0_
  507.1 3.3 unpack.14.refs_0_
  510.3 3.3 unpack.15
  (148 shorter events, 70.4 us)
Async XLA Ops:
  1.8 42.7 %collective-permute-start.1 = (bf16[4,296,256]{2,1,0:T(8,128)(2,1)S(1)}, bf16[4,296,256]{2,1,0:T(8,128)(2,1)}, u32[]{:S(2)}, u32[]{:S(2)}) collective-permute-start(bf16[4,296,256]{2,1,0:T(8,128)(2,1)S(1)} %take.26), channel_id=1, source_target_pairs={{0,8},{4,12},{8,16},{12,20},{16,24},{20,28},{24,0},{28,4},{1,9},{5... | collective-permute-start | bytes 1818632 | tf_op jit(solution)/shard_map/ppermute | solution.py:381
  4.6 42.9 %collective-permute-start.3 = (bf16[4,296,256]{2,1,0:T(8,128)(2,1)S(1)}, bf16[4,296,256]{2,1,0:T(8,128)(2,1)}, u32[]{:S(2)}, u32[]{:S(2)}) collective-permute-start(bf16[4,296,256]{2,1,0:T(8,128)(2,1)S(1)} %take.28), channel_id=1, source_target_pairs={{0,16},{4,20},{8,24},{12,28},{16,0},{20,4},{24,8},{28,12},{1,17},{... | collective-permute-start | bytes 1818632 | tf_op jit(solution)/shard_map/ppermute | solution.py:381
  6.1 75.1 %collective-permute-start.5 = (bf16[4,296,256]{2,1,0:T(8,128)(2,1)S(1)}, bf16[4,296,256]{2,1,0:T(8,128)(2,1)}, u32[]{:S(2)}, u32[]{:S(2)}) collective-permute-start(bf16[4,296,256]{2,1,0:T(8,128)(2,1)S(1)} %take.30), channel_id=1, source_target_pairs={{0,24},{4,28},{8,0},{12,4},{16,8},{20,12},{24,16},{28,20},{1,25},{... | collective-permute-start | bytes 1818632 | tf_op jit(solution)/shard_map/ppermute | solution.py:381
  8.4 115.0 %collective-permute-start.2 = (bf16[4,296,256]{2,1,0:T(8,128)(2,1)S(1)}, bf16[4,296,256]{2,1,0:T(8,128)(2,1)}, u32[]{:S(2)}, u32[]{:S(2)}) collective-permute-start(bf16[4,296,256]{2,1,0:T(8,128)(2,1)S(1)} %take.27), channel_id=1, source_target_pairs={{0,12},{4,8},{8,20},{12,16},{16,28},{20,24},{24,4},{28,0},{1,13},{... | collective-permute-start | bytes 1818632 | tf_op jit(solution)/shard_map/ppermute | solution.py:381
  11.4 112.0 %collective-permute-start.4 = (bf16[4,296,256]{2,1,0:T(8,128)(2,1)S(1)}, bf16[4,296,256]{2,1,0:T(8,128)(2,1)}, u32[]{:S(2)}, u32[]{:S(2)}) collective-permute-start(bf16[4,296,256]{2,1,0:T(8,128)(2,1)S(1)} %take.29), channel_id=1, source_target_pairs={{0,20},{4,16},{8,28},{12,24},{16,4},{20,0},{24,12},{28,8},{1,21},{... | collective-permute-start | bytes 1818632 | tf_op jit(solution)/shard_map/ppermute | solution.py:381
  23.2 0.8 copy-start.14
  44.5 93.3 %collective-permute-start.6 = (bf16[4,296,256]{2,1,0:T(8,128)(2,1)}, bf16[4,296,256]{2,1,0:T(8,128)(2,1)S(1)}, u32[]{:S(2)}, u32[]{:S(2)}) collective-permute-start(bf16[4,296,256]{2,1,0:T(8,128)(2,1)} %copy-done.14), channel_id=1, source_target_pairs={{0,28},{4,24},{8,4},{12,0},{16,12},{20,8},{24,20},{28,16},{1,29},{... | collective-permute-start | bytes 1818632 | tf_op jit(solution)/shard_map/ppermute | solution.py:381
  47.5 118.7 %collective-permute-start = (bf16[4,296,256]{2,1,0:T(8,128)(2,1)}, bf16[4,296,256]{2,1,0:T(8,128)(2,1)}, u32[]{:S(2)}, u32[]{:S(2)}) collective-permute-start(bf16[4,296,256]{2,1,0:T(8,128)(2,1)} %take.25), channel_id=1, source_target_pairs={{0,4},{4,0},{8,12},{12,8},{16,20},{20,16},{24,28},{28,24},{1,5},{5... | collective-permute-start | bytes 1818632 | tf_op jit(solution)/shard_map/ppermute | solution.py:381
  81.2 87.4 %collective-permute-start.10 = (bf16[4,296,256]{2,1,0:T(8,128)(2,1)}, bf16[4,296,256]{2,1,0:T(8,128)(2,1)}, u32[]{:S(2)}, u32[]{:S(2)}) collective-permute-start(bf16[4,296,256]{2,1,0:T(8,128)(2,1)} %take.36), channel_id=1, source_target_pairs={{0,16},{4,20},{8,24},{12,28},{16,0},{20,4},{24,8},{28,12},{1,17},{... | collective-permute-start | bytes 1818632 | tf_op jit(solution)/shard_map/ppermute | solution.py:381
  123.4 48.9 %collective-permute-start.12 = (bf16[4,296,256]{2,1,0:T(8,128)(2,1)}, bf16[4,296,256]{2,1,0:T(8,128)(2,1)}, u32[]{:S(2)}, u32[]{:S(2)}) collective-permute-start(bf16[4,296,256]{2,1,0:T(8,128)(2,1)} %take.38), channel_id=1, source_target_pairs={{0,24},{4,28},{8,0},{12,4},{16,8},{20,12},{24,16},{28,20},{1,25},{... | collective-permute-start | bytes 1818632 | tf_op jit(solution)/shard_map/ppermute | solution.py:381
  123.4 64.1 %collective-permute-start.8 = (bf16[4,296,256]{2,1,0:T(8,128)(2,1)}, bf16[4,296,256]{2,1,0:T(8,128)(2,1)}, u32[]{:S(2)}, u32[]{:S(2)}) collective-permute-start(bf16[4,296,256]{2,1,0:T(8,128)(2,1)} %take.34), channel_id=1, source_target_pairs={{0,8},{4,12},{8,16},{12,20},{16,24},{20,28},{24,0},{28,4},{1,9},{5... | collective-permute-start | bytes 1818632 | tf_op jit(solution)/shard_map/ppermute | solution.py:381
  137.9 0.9 copy-start.17
  138.7 85.6 %collective-permute-start.11 = (bf16[4,296,256]{2,1,0:T(8,128)(2,1)}, bf16[4,296,256]{2,1,0:T(8,128)(2,1)}, u32[]{:S(2)}, u32[]{:S(2)}) collective-permute-start(bf16[4,296,256]{2,1,0:T(8,128)(2,1)} %take.37), channel_id=1, source_target_pairs={{0,20},{4,16},{8,28},{12,24},{16,4},{20,0},{24,12},{28,8},{1,21},{... | collective-permute-start | bytes 1818632 | tf_op jit(solution)/shard_map/ppermute | solution.py:381
  143.8 0.9 copy-start.11
  145.8 0.8 copy-start.7
  147.8 0.9 copy-start.5
  149.8 0.8 copy-start.10
  151.8 0.8 copy-start.9
  159.1 6.8 %copy-start.20 = (s32[16]{0:T(128)S(1)}, s32[16]{0:T(128)}, u32[]{:S(2)}) copy-start(s32[16]{0:T(128)} %param.6) | copy-start | bytes 196
  166.2 71.1 %collective-permute-start.13 = (bf16[4,296,256]{2,1,0:T(8,128)(2,1)}, bf16[4,296,256]{2,1,0:T(8,128)(2,1)}, u32[]{:S(2)}, u32[]{:S(2)}) collective-permute-start(bf16[4,296,256]{2,1,0:T(8,128)(2,1)} %copy-done.13), channel_id=1, source_target_pairs={{0,28},{4,24},{8,4},{12,0},{16,12},{20,8},{24,20},{28,16},{1,29},{... | collective-permute-start | bytes 1818632 | tf_op jit(solution)/shard_map/ppermute | solution.py:381
  168.6 72.1 %collective-permute-start.9 = (bf16[4,296,256]{2,1,0:T(8,128)(2,1)}, bf16[4,296,256]{2,1,0:T(8,128)(2,1)}, u32[]{:S(2)}, u32[]{:S(2)}) collective-permute-start(bf16[4,296,256]{2,1,0:T(8,128)(2,1)} %copy-done.12), channel_id=1, source_target_pairs={{0,12},{4,8},{8,20},{12,16},{16,28},{20,24},{24,4},{28,0},{1,13},{... | collective-permute-start | bytes 1818632 | tf_op jit(solution)/shard_map/ppermute | solution.py:381
  172.3 68.4 %collective-permute-start.7 = (bf16[4,296,256]{2,1,0:T(8,128)(2,1)}, bf16[4,296,256]{2,1,0:T(8,128)(2,1)}, u32[]{:S(2)}, u32[]{:S(2)}) collective-permute-start(bf16[4,296,256]{2,1,0:T(8,128)(2,1)} %copy-done.11), channel_id=1, source_target_pairs={{0,4},{4,0},{8,12},{12,8},{16,20},{20,16},{24,28},{28,24},{1,5},{5... | collective-permute-start | bytes 1818632 | tf_op jit(solution)/shard_map/ppermute | solution.py:381
  187.5 55.6 %collective-permute-start.15 = (bf16[4,296,256]{2,1,0:T(8,128)(2,1)}, bf16[4,296,256]{2,1,0:T(8,128)(2,1)}, u32[]{:S(2)}, u32[]{:S(2)}) collective-permute-start(bf16[4,296,256]{2,1,0:T(8,128)(2,1)} %copy-done.10), channel_id=1, source_target_pairs={{0,8},{4,12},{8,16},{12,20},{16,24},{20,28},{24,0},{28,4},{1,9},{5... | collective-permute-start | bytes 1818632 | tf_op jit(solution)/shard_map/ppermute | solution.py:381
  224.3 26.0 %collective-permute-start.17 = (bf16[4,296,256]{2,1,0:T(8,128)(2,1)}, bf16[4,296,256]{2,1,0:T(8,128)(2,1)}, u32[]{:S(2)}, u32[]{:S(2)}) collective-permute-start(bf16[4,296,256]{2,1,0:T(8,128)(2,1)} %copy-done.9), channel_id=1, source_target_pairs={{0,16},{4,20},{8,24},{12,28},{16,0},{20,4},{24,8},{28,12},{1,17},{... | collective-permute-start | bytes 1818632 | tf_op jit(solution)/shard_map/ppermute | solution.py:381
  231.4 83.7 %copy-start.16 = (f32[256]{0:T(256)}, f32[256]{0:T(256)S(1)}, u32[]{:S(2)}) copy-start(f32[256]{0:T(256)S(1)} %select_reduce_fusion) | copy-start | bytes 3076
  237.3 52.0 %collective-permute-start.19 = (bf16[4,296,256]{2,1,0:T(8,128)(2,1)}, bf16[4,296,256]{2,1,0:T(8,128)(2,1)S(1)}, u32[]{:S(2)}, u32[]{:S(2)}) collective-permute-start(bf16[4,296,256]{2,1,0:T(8,128)(2,1)} %copy-done.4), channel_id=1, source_target_pairs={{0,24},{4,28},{8,0},{12,4},{16,8},{20,12},{24,16},{28,20},{1,25},{... | collective-permute-start | bytes 1818632 | tf_op jit(solution)/shard_map/ppermute | solution.py:381
  240.7 64.9 %collective-permute-start.16 = (bf16[4,296,256]{2,1,0:T(8,128)(2,1)S(1)}, bf16[4,296,256]{2,1,0:T(8,128)(2,1)S(1)}, u32[]{:S(2)}, u32[]{:S(2)}) collective-permute-start(bf16[4,296,256]{2,1,0:T(8,128)(2,1)S(1)} %take.43), channel_id=1, source_target_pairs={{0,12},{4,8},{8,20},{12,16},{16,28},{20,24},{24,4},{28,0},{1,13},{... | collective-permute-start | bytes 1818632 | tf_op jit(solution)/shard_map/ppermute | solution.py:381
  240.7 64.9 %collective-permute-start.18 = (bf16[4,296,256]{2,1,0:T(8,128)(2,1)S(1)}, bf16[4,296,256]{2,1,0:T(8,128)(2,1)S(1)}, u32[]{:S(2)}, u32[]{:S(2)}) collective-permute-start(bf16[4,296,256]{2,1,0:T(8,128)(2,1)S(1)} %take.45), channel_id=1, source_target_pairs={{0,20},{4,16},{8,28},{12,24},{16,4},{20,0},{24,12},{28,8},{1,21},{... | collective-permute-start | bytes 1818632 | tf_op jit(solution)/shard_map/ppermute | solution.py:381
  243.1 72.0 %collective-permute-start.20 = (bf16[4,296,256]{2,1,0:T(8,128)(2,1)S(1)}, bf16[4,296,256]{2,1,0:T(8,128)(2,1)S(1)}, u32[]{:S(2)}, u32[]{:S(2)}) collective-permute-start(bf16[4,296,256]{2,1,0:T(8,128)(2,1)S(1)} %take.47), channel_id=1, source_target_pairs={{0,28},{4,24},{8,4},{12,0},{16,12},{20,8},{24,20},{28,16},{1,29},{... | collective-permute-start | bytes 1818632 | tf_op jit(solution)/shard_map/ppermute | solution.py:381
  250.3 64.8 %collective-permute-start.14 = (bf16[4,296,256]{2,1,0:T(8,128)(2,1)S(1)}, bf16[4,296,256]{2,1,0:T(8,128)(2,1)S(1)}, u32[]{:S(2)}, u32[]{:S(2)}) collective-permute-start(bf16[4,296,256]{2,1,0:T(8,128)(2,1)S(1)} %take.41), channel_id=1, source_target_pairs={{0,4},{4,0},{8,12},{12,8},{16,20},{20,16},{24,28},{28,24},{1,5},{5... | collective-permute-start | bytes 1818632 | tf_op jit(solution)/shard_map/ppermute | solution.py:381
  251.9 1.1 copy-start.8
  252.9 0.8 copy-start.15
  253.8 1.1 copy-start.18
  254.8 10.3 %copy-start.6 = (bf16[4,296,256]{2,1,0:T(8,128)(2,1)S(1)}, bf16[4,296,256]{2,1,0:T(8,128)(2,1)}, u32[]{:S(2)}) copy-start(bf16[4,296,256]{2,1,0:T(8,128)(2,1)} %copy-done.5) | copy-start | bytes 1818628
  315.1 38.3 %copy-start.19 = (bf16[2,2,2]{2,1,0:T(2,128)(2,1)S(1)}, bf16[2,2,2]{2,1,0:T(2,128)(2,1)}, u32[]{:S(2)}) copy-start(bf16[2,2,2]{2,1,0:T(2,128)(2,1)} %constant.267.clone) | copy-start | bytes 52
  325.0 15.7 %all-to-all-start = ((f32[32,1,16,128]{3,2,1,0:T(8,128)}), f32[32,1,16,128]{3,2,1,0:T(8,128)S(1)}, u32[]{:S(2)}, u32[]{:S(2)}) async-start(f32[32,1,16,128]{3,2,1,0:T(8,128)} %bitcast.23), calls=%async_computation | async-start | bytes 524288 | tf_op jit(solution)/shard_map/all_to_all | solution.py:429
  348.4 12.3 %all-to-all-start.1 = ((bf16[32,1,18,128]{3,2,1,0:T(8,128)(2,1)}), bf16[32,1,18,128]{3,2,1,0:T(8,128)(2,1)S(1)}, u32[]{:S(2)}, u32[]{:S(2)}) async-start(bf16[32,1,18,128]{3,2,1,0:T(8,128)(2,1)} %broadcast_in_dim.27), calls=%async_computation.1 | async-start | bytes 393216 | tf_op jit(solution)/shard_map/all_to_all | solution.py:446
  363.5 86.3 %collective-permute-start.27 = (bf16[3,4,128,256]{3,2,1,0:T(8,128)(2,1)S(1)}, bf16[3,4,128,256]{3,2,1,0:T(8,128)(2,1)S(1)}, u32[]{:S(2)}, u32[]{:S(2)}) collective-permute-start(bf16[3,4,128,256]{3,2,1,0:T(8,128)(2,1)S(1)} %mix.8.refs_3_), channel_id=1, source_target_pairs={{0,16},{4,20},{8,24},{12,28},{16,0},{20,4},{24,8},{28,12},{1,17},{... | collective-permute-start | bytes 2359304 | tf_op jit(solution)/shard_map/ppermute | solution.py:381
  367.6 99.1 %collective-permute-start.26 = (bf16[3,4,128,256]{3,2,1,0:T(8,128)(2,1)S(1)}, bf16[3,4,128,256]{3,2,1,0:T(8,128)(2,1)S(1)}, u32[]{:S(2)}, u32[]{:S(2)}) collective-permute-start(bf16[3,4,128,256]{3,2,1,0:T(8,128)(2,1)S(1)} %mix.9.refs_3_), channel_id=1, source_target_pairs={{0,20},{4,16},{8,28},{12,24},{16,4},{20,0},{24,12},{28,8},{1,21},{... | collective-permute-start | bytes 2359304 | tf_op jit(solution)/shard_map/ppermute | solution.py:381
  371.1 132.7 %collective-permute-start.23 = (bf16[3,4,128,256]{3,2,1,0:T(8,128)(2,1)S(1)}, bf16[3,4,128,256]{3,2,1,0:T(8,128)(2,1)}, u32[]{:S(2)}, u32[]{:S(2)}) collective-permute-start(bf16[3,4,128,256]{3,2,1,0:T(8,128)(2,1)S(1)} %mix.10.refs_3_), channel_id=1, source_target_pairs={{0,8},{4,12},{8,16},{12,20},{16,24},{20,28},{24,0},{28,4},{1,9},{5... | collective-permute-start | bytes 2359304 | tf_op jit(solution)/shard_map/ppermute | solution.py:381
  374.6 132.5 %collective-permute-start.22 = (bf16[3,4,128,256]{3,2,1,0:T(8,128)(2,1)S(1)}, bf16[3,4,128,256]{3,2,1,0:T(8,128)(2,1)}, u32[]{:S(2)}, u32[]{:S(2)}) collective-permute-start(bf16[3,4,128,256]{3,2,1,0:T(8,128)(2,1)S(1)} %mix.11.refs_3_), channel_id=1, source_target_pairs={{0,12},{4,8},{8,20},{12,16},{16,28},{20,24},{24,4},{28,0},{1,13},{... | collective-permute-start | bytes 2359304 | tf_op jit(solution)/shard_map/ppermute | solution.py:381
  380.8 102.9 %collective-permute-start.25 = (bf16[3,4,128,256]{3,2,1,0:T(8,128)(2,1)}, bf16[3,4,128,256]{3,2,1,0:T(8,128)(2,1)}, u32[]{:S(2)}, u32[]{:S(2)}) collective-permute-start(bf16[3,4,128,256]{3,2,1,0:T(8,128)(2,1)} %mix.12.refs_3_), channel_id=1, source_target_pairs={{0,24},{4,28},{8,0},{12,4},{16,8},{20,12},{24,16},{28,20},{1,25},{... | collective-permute-start | bytes 2359304 | tf_op jit(solution)/shard_map/ppermute | solution.py:381
  449.8 0.9 copy-start
  450.7 49.8 %collective-permute-start.24 = (bf16[3,4,128,256]{3,2,1,0:T(8,128)(2,1)}, bf16[3,4,128,256]{3,2,1,0:T(8,128)(2,1)}, u32[]{:S(2)}, u32[]{:S(2)}) collective-permute-start(bf16[3,4,128,256]{3,2,1,0:T(8,128)(2,1)} %mix.13.refs_3_), channel_id=1, source_target_pairs={{0,28},{4,24},{8,4},{12,0},{16,12},{20,8},{24,20},{28,16},{1,29},{... | collective-permute-start | bytes 2359304 | tf_op jit(solution)/shard_map/ppermute | solution.py:381
  466.7 0.9 copy-start.2
  467.6 42.7 %collective-permute-start.21 = (bf16[3,4,128,256]{3,2,1,0:T(8,128)(2,1)S(1)}, bf16[3,4,128,256]{3,2,1,0:T(8,128)(2,1)}, u32[]{:S(2)}, u32[]{:S(2)}) collective-permute-start(bf16[3,4,128,256]{3,2,1,0:T(8,128)(2,1)S(1)} %mix.14.refs_3_), channel_id=1, source_target_pairs={{0,4},{4,0},{8,12},{12,8},{16,20},{20,16},{24,28},{28,24},{1,5},{5... | collective-permute-start | bytes 2359304 | tf_op jit(solution)/shard_map/ppermute | solution.py:381
  473.3 1.1 copy-start.1
  474.4 1.5 copy-start.3
  (3 other events, 2.5 us)

commit v9 on v8

--- a/solution.py
+++ b/solution.py
@@ -66,7 +66,7 @@
     record_refs, (coeff_ref, gram_ref, spectra) = refs[:-3], refs[-3:]
     step = pl.program_id(0)
     tm_count, halves, _, span = time_ref.shape
-    rec_len, columns = record_refs[0].shape[1:]
+    rec_len, columns = record_refs[0].shape[2:]
     sectors = spectra.shape[0]
     rows = spectra.shape[2] // NFREQ
 
@@ -79,10 +79,10 @@
                 first = h * (rec_len - span) // (halves - 1)
                 parts = []
                 for j in range(tm_count):
-                    piece = own[0][0, first:first + span]
+                    piece = own[0][0, 0, first:first + span]
                     for x in range(1, tm_count):
                         here = lax.rem(place_ref[1] + tm_count - x, tm_count) == j
-                        piece = jnp.where(here, own[x][0, first:first + span], piece)
+                        piece = jnp.where(here, own[x][0, 0, first:first + span], piece)
                     part = jnp.dot(time_ref[j, h], piece, preferred_element_type=jnp.float32)
                     parts.append(part.reshape(NFREQ, rows // tm_count, columns))
                 joined = jnp.stack(parts, 1).reshape(NFREQ * rows, columns)
@@ -123,9 +123,9 @@
 
 
 def coeffs_and_gram(place, arrived, sec_count, time_basis, azimuth, weight, before):
-    sec_local, rec_len, columns = arrived[0].shape
+    senders, sec_local, rec_len, columns = arrived[0].shape
     sectors = sec_count * sec_local
-    halves = time_basis.shape[1]
+    tm_count, halves = time_basis.shape[:2]
     blocks, wide = before.shape[1:]
     rows = azimuth.shape[1] // sectors
     steps = 4
@@ -135,7 +135,18 @@
     flops = 2 * columns * (
         sectors * time_basis.size + NFREQ * halves * azimuth.size + NFREQ * 4 * wide * wide
     )
-    piece = pl.BlockSpec((1, rec_len, columns), lambda i, _: (early(i), 0, 0))
+
+    def piece(z, x):
+        def index(i, place):
+            sender = lax.rem(place[0] + sec_count - z, sec_count) * tm_count
+            sender += lax.rem(place[1] + tm_count - x, tm_count)
+            return (sender if senders > 1 else 0, early(i), 0, 0)
+
+        return pl.BlockSpec((1, 1, rec_len, columns), index)
+
+    pieces = [piece(z, x) for z in range(sec_count) for x in range(tm_count)]
+    if senders > 1:
+        arrived = arrived * len(pieces)
     return pl.pallas_call(
         functools.partial(coeff_kernel, sec_count, sec_local, freqs, wide // blocks),
         grid_spec=pltpu.PrefetchScalarGridSpec(
@@ -146,7 +157,7 @@
                 pl.BlockSpec(azimuth.shape, lambda i, _: (0, 0)),
                 pl.BlockSpec(weight.shape, lambda i, _: (0, 0)),
                 pl.BlockSpec((freqs, blocks, wide), lambda i, _: (later(i), 0, 0)),
-            ] + [piece] * len(arrived),
+            ] + pieces,
             out_specs=[
                 pl.BlockSpec((freqs, 2 * wide, columns), lambda i, _: (later(i), 0, 0)),
                 pl.BlockSpec((freqs, blocks, wide), lambda i, _: (later(i), 0, 0)),
@@ -160,7 +171,7 @@
         compiler_params=pltpu.CompilerParams(vmem_limit_bytes=VMEM_LIMIT),
         cost_estimate=pl.CostEstimate(
             flops=flops,
-            bytes_accessed=2 * (len(arrived) * arrived[0].size + NFREQ * 2 * wide * columns),
+            bytes_accessed=2 * columns * (sectors * tm_count * rec_len + NFREQ * 2 * wide),
             transcendentals=0,
         ),
         name="coeffs_and_gram",
@@ -280,6 +291,29 @@
     )(jnp.reshape(owner, (1,)), mixing, spread, factor, root_weight, *coeffs, *after)
 
 
+def pack_kernel(record_ref, out_ref):
+    owners, _, _, part = out_ref.shape
+    for d in range(owners):
+        out_ref[d, 0] = record_ref[0, 0, :, d * part:(d + 1) * part]
+
+
+def pack(by_field, k, owners):
+    sec_local, _, rec_len, cells = by_field.shape
+    part = cells // owners
+    return pl.pallas_call(
+        pack_kernel,
+        grid=(sec_local,),
+        in_specs=[pl.BlockSpec((1, 1, rec_len, cells), lambda i: (i, k, 0, 0))],
+        out_specs=pl.BlockSpec((owners, 1, rec_len, part), lambda i: (0, i, 0, 0)),
+        out_shape=jax.ShapeDtypeStruct((owners, sec_local, rec_len, part), by_field.dtype),
+        compiler_params=pltpu.CompilerParams(vmem_limit_bytes=VMEM_LIMIT),
+        cost_estimate=pl.CostEstimate(
+            flops=0, bytes_accessed=4 * sec_local * rec_len * cells, transcendentals=0
+        ),
+        name="pack",
+    )(by_field)
+
+
 def take_kernel(place_ref, record_ref, out_ref):
     out_ref[...] = record_ref[:, 0]
 
@@ -308,41 +342,49 @@
     )(jnp.reshape(owner, (1,)), by_field)
 
 
-def unpack_kernel(owner_ref, piece_ref, *refs):
+def unpack_kernel(count, owner_ref, *refs):
     out_ref = refs[-1]
-    for k in range(piece_ref.shape[0]):
-        for d in range(piece_ref.shape[2]):
-            out_ref[:, 0, d, k] = piece_ref[k, 0, d]
-
-
-def unpack(owner, piece, owners, whole):
-    fields, freqs, two, orders, modes, part = piece.shape
+    step = pl.program_id(0)
+    for n in range(count):
+
+        @pl.when(step == n)
+        def _():
+            for k in range(refs[n].shape[0]):
+                for f in range(refs[n].shape[1]):
+                    for d in range(refs[n].shape[2]):
+                        out_ref[:, f, d, k] = refs[n][k, f, d]
+
+
+def unpack(sources, pieces, owners, whole):
+    fields, freqs, two, orders, modes, part = pieces[0].shape
     shape = (orders, freqs, two, fields, modes, owners * part)
     if part % LANES:
-        whole = jnp.zeros(shape, piece.dtype) if whole is None else whole
-        piece = jnp.transpose(piece, (3, 1, 2, 0, 4, 5))
-        return lax.dynamic_update_slice_in_dim(whole, piece, owner * part, 5)
-    inputs = [piece] if whole is None else [piece, whole]
+        whole = jnp.zeros(shape, pieces[0].dtype) if whole is None else whole
+        for owner, piece in zip(sources, pieces):
+            piece = jnp.transpose(piece, (3, 1, 2, 0, 4, 5))
+            whole = lax.dynamic_update_slice_in_dim(whole, piece, owner * part, 5)
+        return whole
+    count = len(pieces)
+    inputs = list(pieces) if whole is None else list(pieces) + [whole]
     in_specs = [
-        pl.BlockSpec((fields, 1) + piece.shape[2:], lambda i, at: (0, i, 0, 0, 0, 0)),
-        pl.BlockSpec(memory_space=pl.ANY),
-    ]
+        pl.BlockSpec(pieces[0].shape, lambda i, at: (0, 0, 0, 0, 0, 0)) for _ in pieces
+    ] + [pl.BlockSpec(memory_space=pl.ANY)]
     return pl.pallas_call(
-        unpack_kernel,
+        functools.partial(unpack_kernel, count),
         grid_spec=pltpu.PrefetchScalarGridSpec(
             num_scalar_prefetch=1,
-            grid=(freqs,),
+            grid=(count,),
             in_specs=in_specs[:len(inputs)],
-            out_specs=pl.BlockSpec(
-                (orders, 1) + shape[2:5] + (part,), lambda i, at: (0, i, 0, 0, 0, at[0])
-            ),
-        ),
-        out_shape=jax.ShapeDtypeStruct(shape, piece.dtype),
-        input_output_aliases={} if whole is None else {2: 0},
+            out_specs=pl.BlockSpec(shape[:5] + (part,), lambda i, at: (0, 0, 0, 0, 0, at[i])),
+        ),
+        out_shape=jax.ShapeDtypeStruct(shape, pieces[0].dtype),
+        input_output_aliases={} if whole is None else {1 + count: 0},
         compiler_params=pltpu.CompilerParams(vmem_limit_bytes=VMEM_LIMIT),
-        cost_estimate=pl.CostEstimate(flops=0, bytes_accessed=4 * piece.size, transcendentals=0),
+        cost_estimate=pl.CostEstimate(
+            flops=0, bytes_accessed=4 * count * pieces[0].size, transcendentals=0
+        ),
         name="unpack",
-    )(jnp.reshape(owner, (1,)), *inputs)
+    )(jnp.stack(sources), *inputs)
 
 
 def local(records, block_start, slab_index, weight_table):
@@ -382,8 +424,14 @@
 
     arrived = []
     for k in range(fields):
-        got = {r: send(take(by_field, k, owner_after(*r), owners), *r) for r in in_order + [(0, 0)]}
-        arrived.append([got[r] for r in shifts])
+        if k % 2:
+            got = {r: send(take(by_field, k, owner_after(*r), owners), *r) for r in in_order + [(0, 0)]}
+            arrived.append([got[r][None] for r in shifts])
+        else:
+            got = pack(by_field, k, owners)
+            arrived.append(
+                [lax.all_to_all(got, owner_axes, split_axis=0, concat_axis=0, tiled=True)]
+            )
 
     time_basis = placed_time_basis(block_start, tm_count)
     half, _ = half_span(blocks // tm_count)
@@ -469,11 +517,12 @@
         )
         before = (piece,)
         sent[z, x] = owner_after(-z, -x), send(piece, z, x)
+    late = [r for r in in_order if r[0] in (0, 1) and r[1] > 0 or r == in_order[-tm_count]]
+    groups = [[(0, 0)]] + [[r] for r in in_order if r not in late] + [late]
     mode_fields = None
-    for r in sorted(sent, key=lambda r: (r != (0, 0), r[0] == 0, r[0] == 1, in_order.index(r) if r in in_order else 0)):
-        owner, piece = sent[r]
-        piece = piece.reshape(fields, own_freqs, 2, orders, MODES, part)
-        mode_fields = unpack(owner, piece, owners, mode_fields)
+    for group in groups:
+        pieces = [sent[r][1].reshape(fields, own_freqs, 2, orders, MODES, part) for r in group]
+        mode_fields = unpack([sent[r][0] for r in group], pieces, owners, mode_fields)
     mode_fields = jnp.transpose(mode_fields, (0, 1, 2, 4, 3, 5))
     own_energy = lax.dynamic_slice_in_dim(energy, me * own_freqs, own_freqs)
     return (mode_fields, jnp.transpose(own_energy, (1, 0, 2)))

time: 518 us -> 539 us (1.041)
  waiting for transfers between devices: 312 us -> 358 us
  Pallas kernels: 106 us -> 81.6 us
    all_to_all x0 -> x2, waiting for transfers between devices: none -> 98.4 us  [local(): lax.all_to_all(got, owner_axes, split_axis=0, concat_axis=0, tiled=True)]
    ppermute x28 -> x14, waiting for transfers between devices: 298 us -> 245 us  [send(): return lax.ppermute(piece, owner_axes, hops)]
    pallas_call x24 -> x8, Pallas kernels: 31.3 us -> 9.06 us  [take(): pl.pallas_call(take_kernel, grid_spec=pltpu.PrefetchScalarGridSpec(num_sc...]
    all_to_all x0 -> x2, starting transfers between devices: none -> 14 us  [local(): lax.all_to_all(got, owner_axes, split_axis=0, concat_axis=0, tiled=True)]
    ppermute x28 -> x14, starting transfers between devices: 49.1 us -> 40.1 us  [send(): return lax.ppermute(piece, owner_axes, hops)]
    unnamed x44 -> x32, local copies, waits for them, and re-layouts: 15 us -> 14.3 us
  transfers between devices with their start and end apart: 30 -> 18, of which waited for: 17 -> 13; matrix products, arithmetic and copies ran while one was open for 3% -> 2% of each run, Pallas kernels for 17% -> 11%
where the time goes in v9:
time: 539 us; the launch traced here: 536 us
  waiting for transfers between devices  358 us (66%)
  Pallas kernels  81.6 us (15%)
  starting transfers between devices  64.4 us (12%)
  local copies, waits for them, and re-layouts  24.8 us (5%)
    ppermute x14, waiting for transfers between devices, send(): return lax.ppermute(piece, owner_axes, hops)  245 us
    all_to_all x2, waiting for transfers between devices, local(): lax.all_to_all(got, owner_axes, split_axis=0, concat_axis=0, tiled=True)  98.4 us
    ppermute x14, starting transfers between devices, send(): return lax.ppermute(piece, owner_axes, hops)  40.1 us
    pallas_call x3, Pallas kernels, coeffs_and_gram(): pl.pallas_call(functools.partial(coeff_kernel, sec_count, sec_local, freq...  31.3 us
    pallas_call x8, Pallas kernels, mix(): pl.pallas_call(functools.partial(mix_kernel, orders, fields), grid_spec=p...  19.4 us
    unnamed x32, local copies, waits for them, and re-layouts  14.3 us
    all_to_all x2, starting transfers between devices, local(): lax.all_to_all(got, owner_axes, split_axis=0, concat_axis=0, tiled=True)  14 us
    pallas_call x6, Pallas kernels, unpack(): pl.pallas_call(functools.partial(unpack_kernel, count), grid_spec=pltpu.P...  11 us
  transfers between devices with their start and end apart: 18, of which 13 were waited for; matrix products, arithmetic and copies ran while one was open for 2% of the time, Pallas kernels for 11%

profile of v9, /device:TPU:16, one launch (start us, length us, event | category | flops | bytes accessed | tf_op | source)
XLA Modules:
  0.0 535.5 jit_solution(7099751576485037761)
XLA Ops:
  0.6 3.4 pack.2
  4.0 2.2 copy-done.3
  6.3 6.1 %all-to-all-start = ((bf16[8,4,296,256]{3,2,1,0:T(8,128)(2,1)}), bf16[8,4,296,256]{3,2,1,0:T(8,128)(2,1)}, u32[]{:S(2)}, u32[]{:S(2)}) async-start(bf16[8,4,296,256]{3,2,1,0:T(8,128)(2,1)} %copy-done.3), calls=%async_computation | async-start | bytes 9699328 | tf_op jit(solution)/shard_map/all_to_all | solution.py:433
  12.4 3.4 pack.3
  15.8 2.2 copy-done.2
  18.0 98.4 %all-to-all-done.refs_0_.refs_1_.refs_2_.refs_3_.refs_4_.refs_5_.refs_6_.refs_7_ = bf16[8,4,296,256]{3,2,1,0:T(8,128)(2,1)} async-done(((bf16[8,4,296,256]{3,2,1,0:T(8,128)(2,1)}), bf16[8,4,296,256]{3,2,1,0:T(8,128)(2,1)}, u32[]{:S(2)}, u32[]{:S(2)}) %all-to-all-start) | async-done | bytes 4849696 | tf_op jit(solution)/shard_map/all_to_all | solution.py:433
  116.3 7.9 %all-to-all-start.1 = ((bf16[8,4,296,256]{3,2,1,0:T(8,128)(2,1)}), bf16[8,4,296,256]{3,2,1,0:T(8,128)(2,1)}, u32[]{:S(2)}, u32[]{:S(2)}) async-start(bf16[8,4,296,256]{3,2,1,0:T(8,128)(2,1)} %copy-done.2), calls=%async_computation.1 | async-start | bytes 9699328 | tf_op jit(solution)/shard_map/all_to_all | solution.py:433
  126.7 2.8 collective-permute-start.5
  130.7 2.4 collective-permute-start.4
  135.4 2.0 collective-permute-start.1
  142.3 2.9 multiply_bitcast_fusion
  145.2 136.3 %collective-permute-done.3 = bf16[4,296,256]{2,1,0:T(8,128)(2,1)} collective-permute-done((bf16[4,296,256]{2,1,0:T(8,128)(2,1)S(1)}, bf16[4,296,256]{2,1,0:T(8,128)(2,1)}, u32[]{:S(2)}, u32[]{:S(2)}) %collective-permute-start.3) | collective-permute-done | bytes 606240 | tf_op jit(solution)/shard_map/ppermute | solution.py:423
  281.9 12.6 %collective-permute-done.5 = bf16[4,296,256]{2,1,0:T(8,128)(2,1)} collective-permute-done((bf16[4,296,256]{2,1,0:T(8,128)(2,1)S(1)}, bf16[4,296,256]{2,1,0:T(8,128)(2,1)}, u32[]{:S(2)}, u32[]{:S(2)}) %collective-permute-start.5) | collective-permute-done | bytes 606240 | tf_op jit(solution)/shard_map/ppermute | solution.py:423
  294.5 2.8 collective-permute-start.2
  298.9 5.3 reshape.464.azimuth_ref
  305.8 10.1 %coeffs_and_gram.3 = (bf16[32,256,256]{2,1,0:T(8,128)(2,1)S(1)}, f32[32,16,128]{2,1,0:T(8,128)S(1)}) custom-call(s32[2]{0:T(128)S(1)} %pad_add_fusion.1.place_ref, bf16[2,2,256,168]{3,2,1,0:T(8,128)(2,1)S(1)} %copy.38.time_ref, bf16[128,256]{1,0:T(8,128)(2,1)S(1)} %reshape.464.azimuth_ref, f32[1,256]{1,0:T(1,128)S(1)} %bitcast.92, ...), custom_call_target="tpu_custom_call" | custom-call | flops 3556769792 | bytes 9043968 | tf_op jit(solution)/shard_map/coeffs_and_gram/pallas_call | solution.py:150
  316.0 2.1 copy-done
  318.0 2.4 collective-permute-done.4
  320.5 10.9 %collective-permute-done.6 = bf16[4,296,256]{2,1,0:T(8,128)(2,1)} collective-permute-done((bf16[4,296,256]{2,1,0:T(8,128)(2,1)S(1)}, bf16[4,296,256]{2,1,0:T(8,128)(2,1)}, u32[]{:S(2)}, u32[]{:S(2)}) %collective-permute-start.6) | collective-permute-done | bytes 606240 | tf_op jit(solution)/shard_map/ppermute | solution.py:423
  331.4 2.4 collective-permute-done.2
  333.8 10.3 %coeffs_and_gram.4 = (bf16[32,256,256]{2,1,0:T(8,128)(2,1)}, f32[32,16,128]{2,1,0:T(8,128)S(1)}) custom-call(s32[2]{0:T(128)S(1)} %pad_add_fusion.1.place_ref, bf16[2,2,256,168]{3,2,1,0:T(8,128)(2,1)S(1)} %copy.38.time_ref, bf16[128,256]{1,0:T(8,128)(2,1)S(1)} %reshape.464.azimuth_ref, f32[1,256]{1,0:T(1,128)S(1)} %bitcast.93, ...), custom_call_target="tpu_custom_call" | custom-call | flops 3556769792 | bytes 9043968 | tf_op jit(solution)/shard_map/coeffs_and_gram/pallas_call | solution.py:150
  344.1 10.8 %coeffs_and_gram.5 = (bf16[32,256,256]{2,1,0:T(8,128)(2,1)S(1)}, f32[32,16,128]{2,1,0:T(8,128)}) custom-call(s32[2]{0:T(128)S(1)} %pad_add_fusion.1.place_ref, bf16[2,2,256,168]{3,2,1,0:T(8,128)(2,1)S(1)} %copy.38.time_ref, bf16[128,256]{1,0:T(8,128)(2,1)S(1)} %reshape.464.azimuth_ref, f32[1,256]{1,0:T(1,128)S(1)} %bitcast.94, ...), custom_call_target="tpu_custom_call" | custom-call | flops 3556769792 | bytes 9043968 | tf_op jit(solution)/shard_map/coeffs_and_gram/pallas_call | solution.py:150
  355.0 2.0 copy-done.1
  356.9 5.3 all-to-all-start.2
  362.2 8.2 %all-to-all-done.2 = f32[32,1,16,128]{3,2,1,0:T(8,128)S(1)} async-done(((f32[32,1,16,128]{3,2,1,0:T(8,128)}), f32[32,1,16,128]{3,2,1,0:T(8,128)S(1)}, u32[]{:S(2)}, u32[]{:S(2)}) %all-to-all-start.2) | async-done | bytes 262176 | tf_op jit(solution)/shard_map/all_to_all | solution.py:477
  371.3 4.1 subspace.1
  378.2 4.9 all-to-all-start.3
  383.6 6.9 %all-to-all-done.3 = bf16[32,1,18,128]{3,2,1,0:T(8,128)(2,1)S(1)} async-done(((bf16[32,1,18,128]{3,2,1,0:T(8,128)(2,1)}), bf16[32,1,18,128]{3,2,1,0:T(8,128)(2,1)S(1)}, u32[]{:S(2)}, u32[]{:S(2)}) %all-to-all-start.3) | async-done | bytes 147488 | tf_op jit(solution)/shard_map/all_to_all | solution.py:494
  391.1 2.2 mix.8.refs_3_
  393.3 1.9 collective-permute-start.13
  395.2 2.2 mix.9.refs_3_
  397.4 1.3 collective-permute-start.12
  398.6 2.2 mix.10.refs_3_
  400.8 1.3 collective-permute-start.11
  402.1 2.2 mix.11.refs_3_
  404.3 3.1 mix.12.refs_3_
  408.2 2.2 mix.13.refs_3_
  410.4 3.1 mix.14.refs_3_
  413.5 2.2 collective-permute-start.8
  415.7 47.0 %collective-permute-done.13 = bf16[3,4,128,256]{3,2,1,0:T(8,128)(2,1)S(1)} collective-permute-done((bf16[3,4,128,256]{3,2,1,0:T(8,128)(2,1)S(1)}, bf16[3,4,128,256]{3,2,1,0:T(8,128)(2,1)S(1)}, u32[]{:S(2)}, u32[]{:S(2)}) %collective-permute-start.13) | collective-permute-done | bytes 786464 | tf_op jit(solution)/shard_map/ppermute | solution.py:423
  464.7 14.9 %collective-permute-done.12 = bf16[3,4,128,256]{3,2,1,0:T(8,128)(2,1)S(1)} collective-permute-done((bf16[3,4,128,256]{3,2,1,0:T(8,128)(2,1)S(1)}, bf16[3,4,128,256]{3,2,1,0:T(8,128)(2,1)S(1)}, u32[]{:S(2)}, u32[]{:S(2)}) %collective-permute-start.12) | collective-permute-done | bytes 786464 | tf_op jit(solution)/shard_map/ppermute | solution.py:423
  480.6 20.9 %collective-permute-start.7 = (bf16[3,4,128,256]{3,2,1,0:T(8,128)(2,1)S(1)}, bf16[3,4,128,256]{3,2,1,0:T(8,128)(2,1)}, u32[]{:S(2)}, u32[]{:S(2)}) collective-permute-start(bf16[3,4,128,256]{3,2,1,0:T(8,128)(2,1)S(1)} %mix.11.refs_3_), channel_id=1, source_target_pairs={{0,12},{4,8},{8,20},{12,16},{16,28},{20,24},{24,4},{28,0},{1,13},{... | collective-permute-start | bytes 2359304 | tf_op jit(solution)/shard_map/ppermute | solution.py:423
  501.5 2.2 mix.15
  509.1 6.1 %collective-permute-done.11 = bf16[3,4,128,256]{3,2,1,0:T(8,128)(2,1)} collective-permute-done((bf16[3,4,128,256]{3,2,1,0:T(8,128)(2,1)S(1)}, bf16[3,4,128,256]{3,2,1,0:T(8,128)(2,1)}, u32[]{:S(2)}, u32[]{:S(2)}) %collective-permute-start.11) | collective-permute-done | bytes 786464 | tf_op jit(solution)/shard_map/ppermute | solution.py:423
  515.1 2.1 unpack.9.refs_1_
  517.2 2.1 unpack.10.refs_3_
  519.3 11.3 %collective-permute-done.8 = bf16[3,4,128,256]{3,2,1,0:T(8,128)(2,1)} collective-permute-done((bf16[3,4,128,256]{3,2,1,0:T(8,128)(2,1)S(1)}, bf16[3,4,128,256]{3,2,1,0:T(8,128)(2,1)}, u32[]{:S(2)}, u32[]{:S(2)}) %collective-permute-start.8) | collective-permute-done | bytes 786464 | tf_op jit(solution)/shard_map/ppermute | solution.py:423
  531.5 4.1 unpack.11
  (97 shorter events, 28.8 us)
Async XLA Ops:
  4.0 2.2 copy-start.3
  6.3 110.1 %all-to-all-start = ((bf16[8,4,296,256]{3,2,1,0:T(8,128)(2,1)}), bf16[8,4,296,256]{3,2,1,0:T(8,128)(2,1)}, u32[]{:S(2)}, u32[]{:S(2)}) async-start(bf16[8,4,296,256]{3,2,1,0:T(8,128)(2,1)} %copy-done.3), calls=%async_computation | async-start | bytes 9699328 | tf_op jit(solution)/shard_map/all_to_all | solution.py:433
  15.8 2.2 copy-start.2
  116.3 227.8 %all-to-all-start.1 = ((bf16[8,4,296,256]{3,2,1,0:T(8,128)(2,1)}), bf16[8,4,296,256]{3,2,1,0:T(8,128)(2,1)}, u32[]{:S(2)}, u32[]{:S(2)}) async-start(bf16[8,4,296,256]{3,2,1,0:T(8,128)(2,1)} %copy-done.2), calls=%async_computation.1 | async-start | bytes 9699328 | tf_op jit(solution)/shard_map/all_to_all | solution.py:433
  125.4 156.1 %collective-permute-start.3 = (bf16[4,296,256]{2,1,0:T(8,128)(2,1)S(1)}, bf16[4,296,256]{2,1,0:T(8,128)(2,1)}, u32[]{:S(2)}, u32[]{:S(2)}) collective-permute-start(bf16[4,296,256]{2,1,0:T(8,128)(2,1)S(1)} %take.12), channel_id=1, source_target_pairs={{0,16},{4,20},{8,24},{12,28},{16,0},{20,4},{24,8},{28,12},{1,17},{... | collective-permute-start | bytes 1818632 | tf_op jit(solution)/shard_map/ppermute | solution.py:423
  126.7 167.8 %collective-permute-start.5 = (bf16[4,296,256]{2,1,0:T(8,128)(2,1)S(1)}, bf16[4,296,256]{2,1,0:T(8,128)(2,1)}, u32[]{:S(2)}, u32[]{:S(2)}) collective-permute-start(bf16[4,296,256]{2,1,0:T(8,128)(2,1)S(1)} %take.14), channel_id=1, source_target_pairs={{0,24},{4,28},{8,0},{12,4},{16,8},{20,12},{24,16},{28,20},{1,25},{... | collective-permute-start | bytes 1818632 | tf_op jit(solution)/shard_map/ppermute | solution.py:423
  130.7 189.8 %collective-permute-start.4 = (bf16[4,296,256]{2,1,0:T(8,128)(2,1)S(1)}, bf16[4,296,256]{2,1,0:T(8,128)(2,1)}, u32[]{:S(2)}, u32[]{:S(2)}) collective-permute-start(bf16[4,296,256]{2,1,0:T(8,128)(2,1)S(1)} %take.13), channel_id=1, source_target_pairs={{0,20},{4,16},{8,28},{12,24},{16,4},{20,0},{24,12},{28,8},{1,21},{... | collective-permute-start | bytes 1818632 | tf_op jit(solution)/shard_map/ppermute | solution.py:423
  134.2 197.1 %collective-permute-start.6 = (bf16[4,296,256]{2,1,0:T(8,128)(2,1)S(1)}, bf16[4,296,256]{2,1,0:T(8,128)(2,1)}, u32[]{:S(2)}, u32[]{:S(2)}) collective-permute-start(bf16[4,296,256]{2,1,0:T(8,128)(2,1)S(1)} %take.15), channel_id=1, source_target_pairs={{0,28},{4,24},{8,4},{12,0},{16,12},{20,8},{24,20},{28,16},{1,29},{... | collective-permute-start | bytes 1818632 | tf_op jit(solution)/shard_map/ppermute | solution.py:423
  135.4 195.9 %collective-permute-start.1 = (bf16[4,296,256]{2,1,0:T(8,128)(2,1)S(1)}, bf16[4,296,256]{2,1,0:T(8,128)(2,1)}, u32[]{:S(2)}, u32[]{:S(2)}) collective-permute-start(bf16[4,296,256]{2,1,0:T(8,128)(2,1)S(1)} %take.10), channel_id=1, source_target_pairs={{0,8},{4,12},{8,16},{12,20},{16,24},{20,28},{24,0},{28,4},{1,9},{5... | collective-permute-start | bytes 1818632 | tf_op jit(solution)/shard_map/ppermute | solution.py:423
  138.6 0.8 copy-start.9
  139.5 2.0 copy-start.13
  140.6 0.8 copy-start.8
  281.5 49.9 %collective-permute-start = (bf16[4,296,256]{2,1,0:T(8,128)(2,1)}, bf16[4,296,256]{2,1,0:T(8,128)(2,1)}, u32[]{:S(2)}, u32[]{:S(2)}) collective-permute-start(bf16[4,296,256]{2,1,0:T(8,128)(2,1)} %copy-done.9), channel_id=1, source_target_pairs={{0,4},{4,0},{8,12},{12,8},{16,20},{20,16},{24,28},{28,24},{1,5},{5... | collective-permute-start | bytes 1818632 | tf_op jit(solution)/shard_map/ppermute | solution.py:423
  294.5 39.3 %collective-permute-start.2 = (bf16[4,296,256]{2,1,0:T(8,128)(2,1)}, bf16[4,296,256]{2,1,0:T(8,128)(2,1)}, u32[]{:S(2)}, u32[]{:S(2)}) collective-permute-start(bf16[4,296,256]{2,1,0:T(8,128)(2,1)} %copy-done.8), channel_id=1, source_target_pairs={{0,12},{4,8},{8,20},{12,16},{16,28},{20,24},{24,4},{28,0},{1,13},{... | collective-permute-start | bytes 1818632 | tf_op jit(solution)/shard_map/ppermute | solution.py:423
  297.8 7.9 %copy-start.14 = (f32[16]{0:T(128)S(1)}, f32[16]{0:T(128)}, u32[]{:S(2)}) copy-start(f32[16]{0:T(128)} %param.8) | copy-start | bytes 196
  298.9 6.9 %copy-start.10 = (bf16[4,296,256]{2,1,0:T(8,128)(2,1)}, bf16[4,296,256]{2,1,0:T(8,128)(2,1)S(1)}, u32[]{:S(2)}) copy-start(bf16[4,296,256]{2,1,0:T(8,128)(2,1)S(1)} %take.8) | copy-start | bytes 1818628
  305.8 28.0 %copy-start.11 = (bf16[4,296,256]{2,1,0:T(8,128)(2,1)S(1)}, bf16[4,296,256]{2,1,0:T(8,128)(2,1)}, u32[]{:S(2)}) copy-start(bf16[4,296,256]{2,1,0:T(8,128)(2,1)} %copy-done.10) | copy-start | bytes 1818628
  316.0 2.1 copy-start
  344.1 39.0 %copy-start.12 = (bf16[2,2,2]{2,1,0:T(2,128)(2,1)S(1)}, bf16[2,2,2]{2,1,0:T(2,128)(2,1)}, u32[]{:S(2)}) copy-start(bf16[2,2,2]{2,1,0:T(2,128)(2,1)} %constant.203.clone) | copy-start | bytes 52
  355.0 2.0 copy-start.1
  356.9 13.5 %all-to-all-start.2 = ((f32[32,1,16,128]{3,2,1,0:T(8,128)}), f32[32,1,16,128]{3,2,1,0:T(8,128)S(1)}, u32[]{:S(2)}, u32[]{:S(2)}) async-start(f32[32,1,16,128]{3,2,1,0:T(8,128)} %bitcast.33), calls=%async_computation.2 | async-start | bytes 524288 | tf_op jit(solution)/shard_map/all_to_all | solution.py:477
  378.2 12.3 %all-to-all-start.3 = ((bf16[32,1,18,128]{3,2,1,0:T(8,128)(2,1)}), bf16[32,1,18,128]{3,2,1,0:T(8,128)(2,1)S(1)}, u32[]{:S(2)}, u32[]{:S(2)}) async-start(bf16[32,1,18,128]{3,2,1,0:T(8,128)(2,1)} %broadcast_in_dim.80), calls=%async_computation.3 | async-start | bytes 393216 | tf_op jit(solution)/shard_map/all_to_all | solution.py:494
  393.3 69.5 %collective-permute-start.13 = (bf16[3,4,128,256]{3,2,1,0:T(8,128)(2,1)S(1)}, bf16[3,4,128,256]{3,2,1,0:T(8,128)(2,1)S(1)}, u32[]{:S(2)}, u32[]{:S(2)}) collective-permute-start(bf16[3,4,128,256]{3,2,1,0:T(8,128)(2,1)S(1)} %mix.8.refs_3_), channel_id=1, source_target_pairs={{0,16},{4,20},{8,24},{12,28},{16,0},{20,4},{24,8},{28,12},{1,17},{... | collective-permute-start | bytes 2359304 | tf_op jit(solution)/shard_map/ppermute | solution.py:423
  397.4 82.3 %collective-permute-start.12 = (bf16[3,4,128,256]{3,2,1,0:T(8,128)(2,1)S(1)}, bf16[3,4,128,256]{3,2,1,0:T(8,128)(2,1)S(1)}, u32[]{:S(2)}, u32[]{:S(2)}) collective-permute-start(bf16[3,4,128,256]{3,2,1,0:T(8,128)(2,1)S(1)} %mix.9.refs_3_), channel_id=1, source_target_pairs={{0,20},{4,16},{8,28},{12,24},{16,4},{20,0},{24,12},{28,8},{1,21},{... | collective-permute-start | bytes 2359304 | tf_op jit(solution)/shard_map/ppermute | solution.py:423
  400.8 114.3 %collective-permute-start.11 = (bf16[3,4,128,256]{3,2,1,0:T(8,128)(2,1)S(1)}, bf16[3,4,128,256]{3,2,1,0:T(8,128)(2,1)}, u32[]{:S(2)}, u32[]{:S(2)}) collective-permute-start(bf16[3,4,128,256]{3,2,1,0:T(8,128)(2,1)S(1)} %mix.10.refs_3_), channel_id=1, source_target_pairs={{0,8},{4,12},{8,16},{12,20},{16,24},{20,28},{24,0},{28,4},{1,9},{5... | collective-permute-start | bytes 2359304 | tf_op jit(solution)/shard_map/ppermute | solution.py:423
  407.5 109.7 %collective-permute-start.10 = (bf16[3,4,128,256]{3,2,1,0:T(8,128)(2,1)}, bf16[3,4,128,256]{3,2,1,0:T(8,128)(2,1)}, u32[]{:S(2)}, u32[]{:S(2)}) collective-permute-start(bf16[3,4,128,256]{3,2,1,0:T(8,128)(2,1)} %mix.12.refs_3_), channel_id=1, source_target_pairs={{0,24},{4,28},{8,0},{12,4},{16,8},{20,12},{24,16},{28,20},{1,25},{... | collective-permute-start | bytes 2359304 | tf_op jit(solution)/shard_map/ppermute | solution.py:423
  413.5 117.0 %collective-permute-start.8 = (bf16[3,4,128,256]{3,2,1,0:T(8,128)(2,1)S(1)}, bf16[3,4,128,256]{3,2,1,0:T(8,128)(2,1)}, u32[]{:S(2)}, u32[]{:S(2)}) collective-permute-start(bf16[3,4,128,256]{3,2,1,0:T(8,128)(2,1)S(1)} %mix.13.refs_3_), channel_id=1, source_target_pairs={{0,28},{4,24},{8,4},{12,0},{16,12},{20,8},{24,20},{28,16},{1,29},{... | collective-permute-start | bytes 2359304 | tf_op jit(solution)/shard_map/ppermute | solution.py:423
  462.8 0.9 copy-start.4
  463.7 55.6 %collective-permute-start.9 = (bf16[3,4,128,256]{3,2,1,0:T(8,128)(2,1)}, bf16[3,4,128,256]{3,2,1,0:T(8,128)(2,1)}, u32[]{:S(2)}, u32[]{:S(2)}) collective-permute-start(bf16[3,4,128,256]{3,2,1,0:T(8,128)(2,1)} %mix.14.refs_3_), channel_id=1, source_target_pairs={{0,4},{4,0},{8,12},{12,8},{16,20},{20,16},{24,28},{28,24},{1,5},{5... | collective-permute-start | bytes 2359304 | tf_op jit(solution)/shard_map/ppermute | solution.py:423
  479.7 0.9 copy-start.6
  480.6 50.9 %collective-permute-start.7 = (bf16[3,4,128,256]{3,2,1,0:T(8,128)(2,1)S(1)}, bf16[3,4,128,256]{3,2,1,0:T(8,128)(2,1)}, u32[]{:S(2)}, u32[]{:S(2)}) collective-permute-start(bf16[3,4,128,256]{3,2,1,0:T(8,128)(2,1)S(1)} %mix.11.refs_3_), channel_id=1, source_target_pairs={{0,12},{4,8},{8,20},{12,16},{16,28},{20,24},{24,4},{28,0},{1,13},{... | collective-permute-start | bytes 2359304 | tf_op jit(solution)/shard_map/ppermute | solution.py:423
  505.6 1.1 copy-start.5
  506.7 1.4 copy-start.7

commit v10 on v9

--- a/solution.py
+++ b/solution.py
@@ -66,7 +66,7 @@
     record_refs, (coeff_ref, gram_ref, spectra) = refs[:-3], refs[-3:]
     step = pl.program_id(0)
     tm_count, halves, _, span = time_ref.shape
-    rec_len, columns = record_refs[0].shape[2:]
+    rec_len, columns = record_refs[0].shape[1:]
     sectors = spectra.shape[0]
     rows = spectra.shape[2] // NFREQ
 
@@ -79,10 +79,10 @@
                 first = h * (rec_len - span) // (halves - 1)
                 parts = []
                 for j in range(tm_count):
-                    piece = own[0][0, 0, first:first + span]
+                    piece = own[0][0, first:first + span]
                     for x in range(1, tm_count):
                         here = lax.rem(place_ref[1] + tm_count - x, tm_count) == j
-                        piece = jnp.where(here, own[x][0, 0, first:first + span], piece)
+                        piece = jnp.where(here, own[x][0, first:first + span], piece)
                     part = jnp.dot(time_ref[j, h], piece, preferred_element_type=jnp.float32)
                     parts.append(part.reshape(NFREQ, rows // tm_count, columns))
                 joined = jnp.stack(parts, 1).reshape(NFREQ * rows, columns)
@@ -123,7 +123,7 @@
 
 
 def coeffs_and_gram(place, arrived, sec_count, time_basis, azimuth, weight, before):
-    senders, sec_local, rec_len, columns = arrived[0].shape
+    sec_local, rec_len, columns = arrived[0].shape
     sectors = sec_count * sec_local
     tm_count, halves = time_basis.shape[:2]
     blocks, wide = before.shape[1:]
@@ -135,18 +135,7 @@
     flops = 2 * columns * (
         sectors * time_basis.size + NFREQ * halves * azimuth.size + NFREQ * 4 * wide * wide
     )
-
-    def piece(z, x):
-        def index(i, place):
-            sender = lax.rem(place[0] + sec_count - z, sec_count) * tm_count
-            sender += lax.rem(place[1] + tm_count - x, tm_count)
-            return (sender if senders > 1 else 0, early(i), 0, 0)
-
-        return pl.BlockSpec((1, 1, rec_len, columns), index)
-
-    pieces = [piece(z, x) for z in range(sec_count) for x in range(tm_count)]
-    if senders > 1:
-        arrived = arrived * len(pieces)
+    piece = pl.BlockSpec((1, rec_len, columns), lambda i, _: (early(i), 0, 0))
     return pl.pallas_call(
         functools.partial(coeff_kernel, sec_count, sec_local, freqs, wide // blocks),
         grid_spec=pltpu.PrefetchScalarGridSpec(
@@ -157,7 +146,7 @@
                 pl.BlockSpec(azimuth.shape, lambda i, _: (0, 0)),
                 pl.BlockSpec(weight.shape, lambda i, _: (0, 0)),
                 pl.BlockSpec((freqs, blocks, wide), lambda i, _: (later(i), 0, 0)),
-            ] + pieces,
+            ] + [piece] * len(arrived),
             out_specs=[
                 pl.BlockSpec((freqs, 2 * wide, columns), lambda i, _: (later(i), 0, 0)),
                 pl.BlockSpec((freqs, blocks, wide), lambda i, _: (later(i), 0, 0)),
@@ -291,29 +280,6 @@
     )(jnp.reshape(owner, (1,)), mixing, spread, factor, root_weight, *coeffs, *after)
 
 
-def pack_kernel(record_ref, out_ref):
-    owners, _, _, part = out_ref.shape
-    for d in range(owners):
-        out_ref[d, 0] = record_ref[0, 0, :, d * part:(d + 1) * part]
-
-
-def pack(by_field, k, owners):
-    sec_local, _, rec_len, cells = by_field.shape
-    part = cells // owners
-    return pl.pallas_call(
-        pack_kernel,
-        grid=(sec_local,),
-        in_specs=[pl.BlockSpec((1, 1, rec_len, cells), lambda i: (i, k, 0, 0))],
-        out_specs=pl.BlockSpec((owners, 1, rec_len, part), lambda i: (0, i, 0, 0)),
-        out_shape=jax.ShapeDtypeStruct((owners, sec_local, rec_len, part), by_field.dtype),
-        compiler_params=pltpu.CompilerParams(vmem_limit_bytes=VMEM_LIMIT),
-        cost_estimate=pl.CostEstimate(
-            flops=0, bytes_accessed=4 * sec_local * rec_len * cells, transcendentals=0
-        ),
-        name="pack",
-    )(by_field)
-
-
 def take_kernel(place_ref, record_ref, out_ref):
     out_ref[...] = record_ref[:, 0]
 
@@ -424,14 +390,8 @@
 
     arrived = []
     for k in range(fields):
-        if k % 2:
-            got = {r: send(take(by_field, k, owner_after(*r), owners), *r) for r in in_order + [(0, 0)]}
-            arrived.append([got[r][None] for r in shifts])
-        else:
-            got = pack(by_field, k, owners)
-            arrived.append(
-                [lax.all_to_all(got, owner_axes, split_axis=0, concat_axis=0, tiled=True)]
-            )
+        got = {r: send(take(by_field, k, owner_after(*r), owners), *r) for r in in_order + [(0, 0)]}
+        arrived.append([got[r] for r in shifts])
 
     time_basis = placed_time_basis(block_start, tm_count)
     half, _ = half_span(blocks // tm_count)

time: 539 us -> 510 us (0.946)
  waiting for transfers between devices: 358 us -> 244 us
  starting transfers between devices: 64.4 us -> 132 us
  Pallas kernels: 81.6 us -> 96.1 us
    all_to_all x2 -> x0, waiting for transfers between devices: 98.4 us -> none  [local(): lax.all_to_all(got, owner_axes, split_axis=0, concat_axis=0, tiled=True)]
    ppermute x14 -> x28, starting transfers between devices: 40.1 us -> 122 us  [send(): return lax.ppermute(piece, owner_axes, hops)]
    pallas_call x8 -> x24, Pallas kernels: 9.06 us -> 31.3 us  [take(): pl.pallas_call(take_kernel, grid_spec=pltpu.PrefetchScalarGridSpec(num_sc...]
    ppermute x14 -> x28, waiting for transfers between devices: 245 us -> 229 us  [send(): return lax.ppermute(piece, owner_axes, hops)]
    all_to_all x2 -> x0, starting transfers between devices: 14 us -> none  [local(): lax.all_to_all(got, owner_axes, split_axis=0, concat_axis=0, tiled=True)]
    pallas_call x2 -> x0, Pallas kernels: 6.76 us -> none  [pack(): pl.pallas_call(pack_kernel, grid=(sec_local,), in_specs=[pl.BlockSpec((1,...]
    unnamed x32 -> x44, local copies, waits for them, and re-layouts: 14.3 us -> 15.5 us
  transfers between devices with their start and end apart: 18 -> 30, of which waited for: 13 -> 18; matrix products, arithmetic and copies ran while one was open for 2% -> 3% of each run, Pallas kernels for 11% -> 15%
where the time goes in v10:
time: 510 us; the launch traced here: 506 us
  waiting for transfers between devices  244 us (48%)
  starting transfers between devices  132 us (26%)
  Pallas kernels  96.1 us (19%)
  local copies, waits for them, and re-layouts  27.1 us (5%)
  other arithmetic  5.52 us (1%)
    ppermute x28, waiting for transfers between devices, send(): return lax.ppermute(piece, owner_axes, hops)  229 us
    ppermute x28, starting transfers between devices, send(): return lax.ppermute(piece, owner_axes, hops)  122 us
    pallas_call x24, Pallas kernels, take(): pl.pallas_call(take_kernel, grid_spec=pltpu.PrefetchScalarGridSpec(num_sc...  31.3 us
    pallas_call x3, Pallas kernels, coeffs_and_gram(): pl.pallas_call(functools.partial(coeff_kernel, sec_count, sec_local, freq...  30.4 us
    pallas_call x8, Pallas kernels, mix(): pl.pallas_call(functools.partial(mix_kernel, orders, fields), grid_spec=p...  19.4 us
    unnamed x44, local copies, waits for them, and re-layouts  15.5 us
    pallas_call x6, Pallas kernels, unpack(): pl.pallas_call(functools.partial(unpack_kernel, count), grid_spec=pltpu.P...  11 us
  transfers between devices with their start and end apart: 30, of which 18 were waited for; matrix products, arithmetic and copies ran while one was open for 3% of the time, Pallas kernels for 15%

profile of v10, /device:TPU:16, one launch (start us, length us, event | category | flops | bytes accessed | tf_op | source)
XLA Modules:
  0.0 506.2 jit_solution(542547426863182185)
XLA Ops:
  3.0 3.1 collective-permute-start.5
  7.2 2.2 collective-permute-start.4
  26.0 3.3 collective-permute-done.3.refs_4_
  29.3 2.2 collective-permute-start
  31.6 2.9 multiply_bitcast_fusion
  34.4 20.5 %collective-permute-done.5.refs_6_ = bf16[4,296,256]{2,1,0:T(8,128)(2,1)} collective-permute-done((bf16[4,296,256]{2,1,0:T(8,128)(2,1)S(1)}, bf16[4,296,256]{2,1,0:T(8,128)(2,1)}, u32[]{:S(2)}, u32[]{:S(2)}) %collective-permute-start.5) | collective-permute-done | bytes 606240 | tf_op jit(solution)/shard_map/ppermute | solution.py:389
  54.9 21.3 %collective-permute-start.2 = (bf16[4,296,256]{2,1,0:T(8,128)(2,1)}, bf16[4,296,256]{2,1,0:T(8,128)(2,1)}, u32[]{:S(2)}, u32[]{:S(2)}) collective-permute-start(bf16[4,296,256]{2,1,0:T(8,128)(2,1)} %take.27), channel_id=1, source_target_pairs={{0,12},{4,8},{8,20},{12,16},{16,28},{20,24},{24,4},{28,0},{1,13},{... | collective-permute-start | bytes 1818632 | tf_op jit(solution)/shard_map/ppermute | solution.py:389
  76.3 30.6 %collective-permute-done.4.refs_5_ = bf16[4,296,256]{2,1,0:T(8,128)(2,1)} collective-permute-done((bf16[4,296,256]{2,1,0:T(8,128)(2,1)S(1)}, bf16[4,296,256]{2,1,0:T(8,128)(2,1)}, u32[]{:S(2)}, u32[]{:S(2)}) %collective-permute-start.4) | collective-permute-done | bytes 606240 | tf_op jit(solution)/shard_map/ppermute | solution.py:389
  106.9 4.8 collective-permute-start.10
  111.7 8.2 %collective-permute-done.6.refs_7_ = bf16[4,296,256]{2,1,0:T(8,128)(2,1)} collective-permute-done((bf16[4,296,256]{2,1,0:T(8,128)(2,1)S(1)}, bf16[4,296,256]{2,1,0:T(8,128)(2,1)}, u32[]{:S(2)}, u32[]{:S(2)}) %collective-permute-start.6) | collective-permute-done | bytes 606240 | tf_op jit(solution)/shard_map/ppermute | solution.py:389
  119.9 3.9 collective-permute-start.12
  146.7 5.7 %reshape.480.azimuth_ref = bf16[128,256]{1,0:T(8,128)(2,1)} reshape(bf16[2,8,2,4,16,2,2,4]{7,6,5,4,3,2,1,0:T(2,128)(2,1)} %multiply_bitcast_fusion) | data formatting | bytes 131072 | tf_op jit(solution)/shard_map/reshape | solution.py:404
  155.6 3.4 collective-permute-done.12.refs_6_
  159.0 18.4 %collective-permute-start.9 = (bf16[4,296,256]{2,1,0:T(8,128)(2,1)}, bf16[4,296,256]{2,1,0:T(8,128)(2,1)}, u32[]{:S(2)}, u32[]{:S(2)}) collective-permute-start(bf16[4,296,256]{2,1,0:T(8,128)(2,1)} %copy-done.11), channel_id=1, source_target_pairs={{0,12},{4,8},{8,20},{12,16},{16,28},{20,24},{24,4},{28,0},{1,13},{... | collective-permute-start | bytes 1818632 | tf_op jit(solution)/shard_map/ppermute | solution.py:389
  177.4 33.5 %collective-permute-done.11.refs_5_ = bf16[4,296,256]{2,1,0:T(8,128)(2,1)} collective-permute-done((bf16[4,296,256]{2,1,0:T(8,128)(2,1)}, bf16[4,296,256]{2,1,0:T(8,128)(2,1)}, u32[]{:S(2)}, u32[]{:S(2)}) %collective-permute-start.11) | collective-permute-done | bytes 606240 | tf_op jit(solution)/shard_map/ppermute | solution.py:389
  211.0 4.7 collective-permute-start.17
  215.6 8.3 %collective-permute-done.13.refs_7_ = bf16[4,296,256]{2,1,0:T(8,128)(2,1)} collective-permute-done((bf16[4,296,256]{2,1,0:T(8,128)(2,1)}, bf16[4,296,256]{2,1,0:T(8,128)(2,1)}, u32[]{:S(2)}, u32[]{:S(2)}) %collective-permute-start.13) | collective-permute-done | bytes 606240 | tf_op jit(solution)/shard_map/ppermute | solution.py:389
  224.0 3.8 collective-permute-start.19
  232.3 6.5 %collective-permute-done.17.refs_4_ = bf16[4,296,256]{2,1,0:T(8,128)(2,1)} collective-permute-done((bf16[4,296,256]{2,1,0:T(8,128)(2,1)}, bf16[4,296,256]{2,1,0:T(8,128)(2,1)}, u32[]{:S(2)}, u32[]{:S(2)}) %collective-permute-start.17) | collective-permute-done | bytes 606240 | tf_op jit(solution)/shard_map/ppermute | solution.py:389
  238.8 3.0 collective-permute-start.14
  241.8 21.2 %collective-permute-done.19.refs_6_ = bf16[4,296,256]{2,1,0:T(8,128)(2,1)} collective-permute-done((bf16[4,296,256]{2,1,0:T(8,128)(2,1)}, bf16[4,296,256]{2,1,0:T(8,128)(2,1)}, u32[]{:S(2)}, u32[]{:S(2)}) %collective-permute-start.19) | collective-permute-done | bytes 606240 | tf_op jit(solution)/shard_map/ppermute | solution.py:389
  263.0 18.4 %collective-permute-start.16 = (bf16[4,296,256]{2,1,0:T(8,128)(2,1)S(1)}, bf16[4,296,256]{2,1,0:T(8,128)(2,1)S(1)}, u32[]{:S(2)}, u32[]{:S(2)}) collective-permute-start(bf16[4,296,256]{2,1,0:T(8,128)(2,1)S(1)} %take.43), channel_id=1, source_target_pairs={{0,12},{4,8},{8,20},{12,16},{16,28},{20,24},{24,4},{28,0},{1,13},{... | collective-permute-start | bytes 1818632 | tf_op jit(solution)/shard_map/ppermute | solution.py:389
  284.4 10.2 %coeffs_and_gram.3 = (bf16[32,256,256]{2,1,0:T(8,128)(2,1)}, f32[32,16,128]{2,1,0:T(8,128)S(1)}) custom-call(s32[2]{0:T(128)S(1)} %pad_add_fusion.1.place_ref, bf16[2,2,256,168]{3,2,1,0:T(8,128)(2,1)S(1)} %copy.38.time_ref, bf16[128,256]{1,0:T(8,128)(2,1)S(1)} %copy-done.15, f32[1,256]{1,0:T(1,128)S(1)} %bitcast.83, ...), custom_call_target="tpu_custom_call" | custom-call | flops 3556769792 | bytes 9043968 | tf_op jit(solution)/shard_map/coeffs_and_gram/pallas_call | solution.py:139
  294.6 10.3 %coeffs_and_gram.4 = (bf16[32,256,256]{2,1,0:T(8,128)(2,1)}, f32[32,16,128]{2,1,0:T(8,128)S(1)}) custom-call(s32[2]{0:T(128)S(1)} %pad_add_fusion.1.place_ref, bf16[2,2,256,168]{3,2,1,0:T(8,128)(2,1)S(1)} %copy.38.time_ref, bf16[128,256]{1,0:T(8,128)(2,1)S(1)} %copy-done.15, f32[1,256]{1,0:T(1,128)S(1)} %bitcast.84, ...), custom_call_target="tpu_custom_call" | custom-call | flops 3556769792 | bytes 9043968 | tf_op jit(solution)/shard_map/coeffs_and_gram/pallas_call | solution.py:139
  305.0 9.1 %collective-permute-done.20.refs_7_ = bf16[4,296,256]{2,1,0:T(8,128)(2,1)S(1)} collective-permute-done((bf16[4,296,256]{2,1,0:T(8,128)(2,1)S(1)}, bf16[4,296,256]{2,1,0:T(8,128)(2,1)S(1)}, u32[]{:S(2)}, u32[]{:S(2)}) %collective-permute-start.20) | collective-permute-done | bytes 606240 | tf_op jit(solution)/shard_map/ppermute | solution.py:389
  314.1 4.2 collective-permute-done.16.refs_3_
  318.2 9.8 %coeffs_and_gram.5 = (bf16[32,256,256]{2,1,0:T(8,128)(2,1)}, f32[32,16,128]{2,1,0:T(8,128)}) custom-call(s32[2]{0:T(128)S(1)} %pad_add_fusion.1.place_ref, bf16[2,2,256,168]{3,2,1,0:T(8,128)(2,1)S(1)} %copy.38.time_ref, bf16[128,256]{1,0:T(8,128)(2,1)S(1)} %copy-done.15, f32[1,256]{1,0:T(1,128)S(1)} %bitcast.85, ...), custom_call_target="tpu_custom_call" | custom-call | flops 3556769792 | bytes 9043968 | tf_op jit(solution)/shard_map/coeffs_and_gram/pallas_call | solution.py:139
  328.1 4.8 all-to-all-start
  333.6 7.5 %all-to-all-done = f32[32,1,16,128]{3,2,1,0:T(8,128)S(1)} async-done(((f32[32,1,16,128]{3,2,1,0:T(8,128)}), f32[32,1,16,128]{3,2,1,0:T(8,128)S(1)}, u32[]{:S(2)}, u32[]{:S(2)}) %all-to-all-start) | async-done | bytes 262176 | tf_op jit(solution)/shard_map/all_to_all | solution.py:437
  342.0 4.0 subspace.1
  348.9 4.9 all-to-all-start.1
  354.3 6.9 %all-to-all-done.1 = bf16[32,1,18,128]{3,2,1,0:T(8,128)(2,1)S(1)} async-done(((bf16[32,1,18,128]{3,2,1,0:T(8,128)(2,1)}), bf16[32,1,18,128]{3,2,1,0:T(8,128)(2,1)S(1)}, u32[]{:S(2)}, u32[]{:S(2)}) %all-to-all-start.1) | async-done | bytes 147488 | tf_op jit(solution)/shard_map/all_to_all | solution.py:454
  361.8 2.2 mix.8.refs_3_
  365.9 2.2 mix.9.refs_3_
  369.3 2.2 mix.10.refs_3_
  372.9 2.2 mix.11.refs_3_
  375.1 3.1 mix.12.refs_3_
  378.9 2.2 mix.13.refs_3_
  381.1 3.1 mix.14.refs_3_
  384.2 2.2 collective-permute-start.22
  386.4 47.1 %collective-permute-done.27 = bf16[3,4,128,256]{3,2,1,0:T(8,128)(2,1)S(1)} collective-permute-done((bf16[3,4,128,256]{3,2,1,0:T(8,128)(2,1)S(1)}, bf16[3,4,128,256]{3,2,1,0:T(8,128)(2,1)S(1)}, u32[]{:S(2)}, u32[]{:S(2)}) %collective-permute-start.27) | collective-permute-done | bytes 786464 | tf_op jit(solution)/shard_map/ppermute | solution.py:389
  435.5 15.0 %collective-permute-done.26 = bf16[3,4,128,256]{3,2,1,0:T(8,128)(2,1)S(1)} collective-permute-done((bf16[3,4,128,256]{3,2,1,0:T(8,128)(2,1)S(1)}, bf16[3,4,128,256]{3,2,1,0:T(8,128)(2,1)S(1)}, u32[]{:S(2)}, u32[]{:S(2)}) %collective-permute-start.26) | collective-permute-done | bytes 786464 | tf_op jit(solution)/shard_map/ppermute | solution.py:389
  451.3 20.9 %collective-permute-start.21 = (bf16[3,4,128,256]{3,2,1,0:T(8,128)(2,1)S(1)}, bf16[3,4,128,256]{3,2,1,0:T(8,128)(2,1)}, u32[]{:S(2)}, u32[]{:S(2)}) collective-permute-start(bf16[3,4,128,256]{3,2,1,0:T(8,128)(2,1)S(1)} %mix.11.refs_3_), channel_id=1, source_target_pairs={{0,12},{4,8},{8,20},{12,16},{16,28},{20,24},{24,4},{28,0},{1,13},{... | collective-permute-start | bytes 2359304 | tf_op jit(solution)/shard_map/ppermute | solution.py:389
  472.2 2.2 mix.15
  479.7 6.1 %collective-permute-done.25 = bf16[3,4,128,256]{3,2,1,0:T(8,128)(2,1)} collective-permute-done((bf16[3,4,128,256]{3,2,1,0:T(8,128)(2,1)S(1)}, bf16[3,4,128,256]{3,2,1,0:T(8,128)(2,1)}, u32[]{:S(2)}, u32[]{:S(2)}) %collective-permute-start.25) | collective-permute-done | bytes 786464 | tf_op jit(solution)/shard_map/ppermute | solution.py:389
  487.9 2.1 unpack.10.refs_3_
  490.0 11.3 %collective-permute-done.22 = bf16[3,4,128,256]{3,2,1,0:T(8,128)(2,1)} collective-permute-done((bf16[3,4,128,256]{3,2,1,0:T(8,128)(2,1)S(1)}, bf16[3,4,128,256]{3,2,1,0:T(8,128)(2,1)}, u32[]{:S(2)}, u32[]{:S(2)}) %collective-permute-start.22) | collective-permute-done | bytes 786464 | tf_op jit(solution)/shard_map/ppermute | solution.py:389
  502.2 4.1 unpack.11
  (147 shorter events, 75.3 us)
Async XLA Ops:
  1.8 27.5 %collective-permute-start.3 = (bf16[4,296,256]{2,1,0:T(8,128)(2,1)S(1)}, bf16[4,296,256]{2,1,0:T(8,128)(2,1)}, u32[]{:S(2)}, u32[]{:S(2)}) collective-permute-start(bf16[4,296,256]{2,1,0:T(8,128)(2,1)S(1)} %take.28), channel_id=1, source_target_pairs={{0,16},{4,20},{8,24},{12,28},{16,0},{20,4},{24,8},{28,12},{1,17},{... | collective-permute-start | bytes 1818632 | tf_op jit(solution)/shard_map/ppermute | solution.py:389
  3.0 51.9 %collective-permute-start.5 = (bf16[4,296,256]{2,1,0:T(8,128)(2,1)S(1)}, bf16[4,296,256]{2,1,0:T(8,128)(2,1)}, u32[]{:S(2)}, u32[]{:S(2)}) collective-permute-start(bf16[4,296,256]{2,1,0:T(8,128)(2,1)S(1)} %take.30), channel_id=1, source_target_pairs={{0,24},{4,28},{8,0},{12,4},{16,8},{20,12},{24,16},{28,20},{1,25},{... | collective-permute-start | bytes 1818632 | tf_op jit(solution)/shard_map/ppermute | solution.py:389
  7.2 99.7 %collective-permute-start.4 = (bf16[4,296,256]{2,1,0:T(8,128)(2,1)S(1)}, bf16[4,296,256]{2,1,0:T(8,128)(2,1)}, u32[]{:S(2)}, u32[]{:S(2)}) collective-permute-start(bf16[4,296,256]{2,1,0:T(8,128)(2,1)S(1)} %take.29), channel_id=1, source_target_pairs={{0,20},{4,16},{8,28},{12,24},{16,4},{20,0},{24,12},{28,8},{1,21},{... | collective-permute-start | bytes 1818632 | tf_op jit(solution)/shard_map/ppermute | solution.py:389
  10.6 109.3 %collective-permute-start.6 = (bf16[4,296,256]{2,1,0:T(8,128)(2,1)S(1)}, bf16[4,296,256]{2,1,0:T(8,128)(2,1)}, u32[]{:S(2)}, u32[]{:S(2)}) collective-permute-start(bf16[4,296,256]{2,1,0:T(8,128)(2,1)S(1)} %take.31), channel_id=1, source_target_pairs={{0,28},{4,24},{8,4},{12,0},{16,12},{20,8},{24,20},{28,16},{1,29},{... | collective-permute-start | bytes 1818632 | tf_op jit(solution)/shard_map/ppermute | solution.py:389
  11.8 112.0 %collective-permute-start.1 = (bf16[4,296,256]{2,1,0:T(8,128)(2,1)S(1)}, bf16[4,296,256]{2,1,0:T(8,128)(2,1)}, u32[]{:S(2)}, u32[]{:S(2)}) collective-permute-start(bf16[4,296,256]{2,1,0:T(8,128)(2,1)S(1)} %take.26), channel_id=1, source_target_pairs={{0,8},{4,12},{8,16},{12,20},{16,24},{20,28},{24,0},{28,4},{1,9},{5... | collective-permute-start | bytes 1818632 | tf_op jit(solution)/shard_map/ppermute | solution.py:389
  22.9 0.8 copy-start.14
  29.3 94.4 %collective-permute-start = (bf16[4,296,256]{2,1,0:T(8,128)(2,1)}, bf16[4,296,256]{2,1,0:T(8,128)(2,1)S(1)}, u32[]{:S(2)}, u32[]{:S(2)}) collective-permute-start(bf16[4,296,256]{2,1,0:T(8,128)(2,1)} %copy-done.14), channel_id=1, source_target_pairs={{0,4},{4,0},{8,12},{12,8},{16,20},{20,16},{24,28},{28,24},{1,5},{5... | collective-permute-start | bytes 1818632 | tf_op jit(solution)/shard_map/ppermute | solution.py:389
  54.9 97.7 %collective-permute-start.2 = (bf16[4,296,256]{2,1,0:T(8,128)(2,1)}, bf16[4,296,256]{2,1,0:T(8,128)(2,1)}, u32[]{:S(2)}, u32[]{:S(2)}) collective-permute-start(bf16[4,296,256]{2,1,0:T(8,128)(2,1)} %take.27), channel_id=1, source_target_pairs={{0,12},{4,8},{8,20},{12,16},{16,28},{20,24},{24,4},{28,0},{1,13},{... | collective-permute-start | bytes 1818632 | tf_op jit(solution)/shard_map/ppermute | solution.py:389
  106.9 46.9 %collective-permute-start.10 = (bf16[4,296,256]{2,1,0:T(8,128)(2,1)}, bf16[4,296,256]{2,1,0:T(8,128)(2,1)}, u32[]{:S(2)}, u32[]{:S(2)}) collective-permute-start(bf16[4,296,256]{2,1,0:T(8,128)(2,1)} %take.36), channel_id=1, source_target_pairs={{0,16},{4,20},{8,24},{12,28},{16,0},{20,4},{24,8},{28,12},{1,17},{... | collective-permute-start | bytes 1818632 | tf_op jit(solution)/shard_map/ppermute | solution.py:389
  119.9 39.1 %collective-permute-start.12 = (bf16[4,296,256]{2,1,0:T(8,128)(2,1)}, bf16[4,296,256]{2,1,0:T(8,128)(2,1)}, u32[]{:S(2)}, u32[]{:S(2)}) collective-permute-start(bf16[4,296,256]{2,1,0:T(8,128)(2,1)} %take.38), channel_id=1, source_target_pairs={{0,24},{4,28},{8,0},{12,4},{16,8},{20,12},{24,16},{28,20},{1,25},{... | collective-permute-start | bytes 1818632 | tf_op jit(solution)/shard_map/ppermute | solution.py:389
  123.8 87.2 %collective-permute-start.11 = (bf16[4,296,256]{2,1,0:T(8,128)(2,1)}, bf16[4,296,256]{2,1,0:T(8,128)(2,1)}, u32[]{:S(2)}, u32[]{:S(2)}) collective-permute-start(bf16[4,296,256]{2,1,0:T(8,128)(2,1)} %take.37), channel_id=1, source_target_pairs={{0,20},{4,16},{8,28},{12,24},{16,4},{20,0},{24,12},{28,8},{1,21},{... | collective-permute-start | bytes 1818632 | tf_op jit(solution)/shard_map/ppermute | solution.py:389
  123.8 0.9 copy-start.17
  124.6 99.3 %collective-permute-start.13 = (bf16[4,296,256]{2,1,0:T(8,128)(2,1)}, bf16[4,296,256]{2,1,0:T(8,128)(2,1)}, u32[]{:S(2)}, u32[]{:S(2)}) collective-permute-start(bf16[4,296,256]{2,1,0:T(8,128)(2,1)} %take.39), channel_id=1, source_target_pairs={{0,28},{4,24},{8,4},{12,0},{16,12},{20,8},{24,20},{28,16},{1,29},{... | collective-permute-start | bytes 1818632 | tf_op jit(solution)/shard_map/ppermute | solution.py:389
  128.2 0.9 copy-start.12
  132.2 0.8 copy-start.7
  134.2 0.9 copy-start.5
  136.2 0.8 copy-start.10
  138.2 0.8 copy-start.9
  145.5 6.8 %copy-start.20 = (s32[16]{0:T(128)S(1)}, s32[16]{0:T(128)}, u32[]{:S(2)}) copy-start(s32[16]{0:T(128)} %param.6) | copy-start | bytes 196
  152.6 77.9 %collective-permute-start.8 = (bf16[4,296,256]{2,1,0:T(8,128)(2,1)}, bf16[4,296,256]{2,1,0:T(8,128)(2,1)}, u32[]{:S(2)}, u32[]{:S(2)}) collective-permute-start(bf16[4,296,256]{2,1,0:T(8,128)(2,1)} %copy-done.13), channel_id=1, source_target_pairs={{0,8},{4,12},{8,16},{12,20},{16,24},{20,28},{24,0},{28,4},{1,9},{5... | collective-permute-start | bytes 1818632 | tf_op jit(solution)/shard_map/ppermute | solution.py:389
  153.8 76.8 %collective-permute-start.7 = (bf16[4,296,256]{2,1,0:T(8,128)(2,1)}, bf16[4,296,256]{2,1,0:T(8,128)(2,1)}, u32[]{:S(2)}, u32[]{:S(2)}) collective-permute-start(bf16[4,296,256]{2,1,0:T(8,128)(2,1)} %copy-done.12), channel_id=1, source_target_pairs={{0,4},{4,0},{8,12},{12,8},{16,20},{20,16},{24,28},{28,24},{1,5},{5... | collective-permute-start | bytes 1818632 | tf_op jit(solution)/shard_map/ppermute | solution.py:389
  159.0 72.2 %collective-permute-start.9 = (bf16[4,296,256]{2,1,0:T(8,128)(2,1)}, bf16[4,296,256]{2,1,0:T(8,128)(2,1)}, u32[]{:S(2)}, u32[]{:S(2)}) collective-permute-start(bf16[4,296,256]{2,1,0:T(8,128)(2,1)} %copy-done.11), channel_id=1, source_target_pairs={{0,12},{4,8},{8,20},{12,16},{16,28},{20,24},{24,4},{28,0},{1,13},{... | collective-permute-start | bytes 1818632 | tf_op jit(solution)/shard_map/ppermute | solution.py:389
  211.0 27.8 %collective-permute-start.17 = (bf16[4,296,256]{2,1,0:T(8,128)(2,1)}, bf16[4,296,256]{2,1,0:T(8,128)(2,1)}, u32[]{:S(2)}, u32[]{:S(2)}) collective-permute-start(bf16[4,296,256]{2,1,0:T(8,128)(2,1)} %copy-done.10), channel_id=1, source_target_pairs={{0,16},{4,20},{8,24},{12,28},{16,0},{20,4},{24,8},{28,12},{1,17},{... | collective-permute-start | bytes 1818632 | tf_op jit(solution)/shard_map/ppermute | solution.py:389
  224.0 39.0 %collective-permute-start.19 = (bf16[4,296,256]{2,1,0:T(8,128)(2,1)}, bf16[4,296,256]{2,1,0:T(8,128)(2,1)}, u32[]{:S(2)}, u32[]{:S(2)}) collective-permute-start(bf16[4,296,256]{2,1,0:T(8,128)(2,1)} %copy-done.9), channel_id=1, source_target_pairs={{0,24},{4,28},{8,0},{12,4},{16,8},{20,12},{24,16},{28,20},{1,25},{... | collective-permute-start | bytes 1818632 | tf_op jit(solution)/shard_map/ppermute | solution.py:389
  230.5 87.8 %copy-start.16 = (f32[256]{0:T(256)}, f32[256]{0:T(256)S(1)}, u32[]{:S(2)}) copy-start(f32[256]{0:T(256)S(1)} %select_reduce_fusion) | copy-start | bytes 3076
  230.5 74.5 %collective-permute-start.18 = (bf16[4,296,256]{2,1,0:T(8,128)(2,1)}, bf16[4,296,256]{2,1,0:T(8,128)(2,1)S(1)}, u32[]{:S(2)}, u32[]{:S(2)}) collective-permute-start(bf16[4,296,256]{2,1,0:T(8,128)(2,1)} %copy-done.4), channel_id=1, source_target_pairs={{0,20},{4,16},{8,28},{12,24},{16,4},{20,0},{24,12},{28,8},{1,21},{... | collective-permute-start | bytes 1818632 | tf_op jit(solution)/shard_map/ppermute | solution.py:389
  230.6 83.5 %collective-permute-start.20 = (bf16[4,296,256]{2,1,0:T(8,128)(2,1)S(1)}, bf16[4,296,256]{2,1,0:T(8,128)(2,1)S(1)}, u32[]{:S(2)}, u32[]{:S(2)}) collective-permute-start(bf16[4,296,256]{2,1,0:T(8,128)(2,1)S(1)} %take.47), channel_id=1, source_target_pairs={{0,28},{4,24},{8,4},{12,0},{16,12},{20,8},{24,20},{28,16},{1,29},{... | collective-permute-start | bytes 1818632 | tf_op jit(solution)/shard_map/ppermute | solution.py:389
  231.2 82.9 %collective-permute-start.15 = (bf16[4,296,256]{2,1,0:T(8,128)(2,1)S(1)}, bf16[4,296,256]{2,1,0:T(8,128)(2,1)S(1)}, u32[]{:S(2)}, u32[]{:S(2)}) collective-permute-start(bf16[4,296,256]{2,1,0:T(8,128)(2,1)S(1)} %take.42), channel_id=1, source_target_pairs={{0,8},{4,12},{8,16},{12,20},{16,24},{20,28},{24,0},{28,4},{1,9},{5... | collective-permute-start | bytes 1818632 | tf_op jit(solution)/shard_map/ppermute | solution.py:389
  238.8 75.3 %collective-permute-start.14 = (bf16[4,296,256]{2,1,0:T(8,128)(2,1)S(1)}, bf16[4,296,256]{2,1,0:T(8,128)(2,1)S(1)}, u32[]{:S(2)}, u32[]{:S(2)}) collective-permute-start(bf16[4,296,256]{2,1,0:T(8,128)(2,1)S(1)} %take.41), channel_id=1, source_target_pairs={{0,4},{4,0},{8,12},{12,8},{16,20},{20,16},{24,28},{28,24},{1,5},{5... | collective-permute-start | bytes 1818632 | tf_op jit(solution)/shard_map/ppermute | solution.py:389
  263.0 55.3 %collective-permute-start.16 = (bf16[4,296,256]{2,1,0:T(8,128)(2,1)S(1)}, bf16[4,296,256]{2,1,0:T(8,128)(2,1)S(1)}, u32[]{:S(2)}, u32[]{:S(2)}) collective-permute-start(bf16[4,296,256]{2,1,0:T(8,128)(2,1)S(1)} %take.43), channel_id=1, source_target_pairs={{0,12},{4,8},{8,20},{12,16},{16,28},{20,24},{24,4},{28,0},{1,13},{... | collective-permute-start | bytes 1818632 | tf_op jit(solution)/shard_map/ppermute | solution.py:389
  281.4 1.1 copy-start.8
  282.5 0.8 copy-start.15
  283.3 1.1 copy-start.18
  284.4 10.2 %copy-start.6 = (bf16[4,296,256]{2,1,0:T(8,128)(2,1)S(1)}, bf16[4,296,256]{2,1,0:T(8,128)(2,1)}, u32[]{:S(2)}) copy-start(bf16[4,296,256]{2,1,0:T(8,128)(2,1)} %copy-done.5) | copy-start | bytes 1818628
  318.2 35.6 %copy-start.19 = (bf16[2,2,2]{2,1,0:T(2,128)(2,1)S(1)}, bf16[2,2,2]{2,1,0:T(2,128)(2,1)}, u32[]{:S(2)}) copy-start(bf16[2,2,2]{2,1,0:T(2,128)(2,1)} %constant.267.clone) | copy-start | bytes 52
  328.1 13.1 %all-to-all-start = ((f32[32,1,16,128]{3,2,1,0:T(8,128)}), f32[32,1,16,128]{3,2,1,0:T(8,128)S(1)}, u32[]{:S(2)}, u32[]{:S(2)}) async-start(f32[32,1,16,128]{3,2,1,0:T(8,128)} %bitcast.25), calls=%async_computation | async-start | bytes 524288 | tf_op jit(solution)/shard_map/all_to_all | solution.py:437
  348.9 12.3 %all-to-all-start.1 = ((bf16[32,1,18,128]{3,2,1,0:T(8,128)(2,1)}), bf16[32,1,18,128]{3,2,1,0:T(8,128)(2,1)S(1)}, u32[]{:S(2)}, u32[]{:S(2)}) async-start(bf16[32,1,18,128]{3,2,1,0:T(8,128)(2,1)} %broadcast_in_dim.27), calls=%async_computation.1 | async-start | bytes 393216 | tf_op jit(solution)/shard_map/all_to_all | solution.py:454
  364.0 69.5 %collective-permute-start.27 = (bf16[3,4,128,256]{3,2,1,0:T(8,128)(2,1)S(1)}, bf16[3,4,128,256]{3,2,1,0:T(8,128)(2,1)S(1)}, u32[]{:S(2)}, u32[]{:S(2)}) collective-permute-start(bf16[3,4,128,256]{3,2,1,0:T(8,128)(2,1)S(1)} %mix.8.refs_3_), channel_id=1, source_target_pairs={{0,16},{4,20},{8,24},{12,28},{16,0},{20,4},{24,8},{28,12},{1,17},{... | collective-permute-start | bytes 2359304 | tf_op jit(solution)/shard_map/ppermute | solution.py:389
  368.1 82.3 %collective-permute-start.26 = (bf16[3,4,128,256]{3,2,1,0:T(8,128)(2,1)S(1)}, bf16[3,4,128,256]{3,2,1,0:T(8,128)(2,1)S(1)}, u32[]{:S(2)}, u32[]{:S(2)}) collective-permute-start(bf16[3,4,128,256]{3,2,1,0:T(8,128)(2,1)S(1)} %mix.9.refs_3_), channel_id=1, source_target_pairs={{0,20},{4,16},{8,28},{12,24},{16,4},{20,0},{24,12},{28,8},{1,21},{... | collective-permute-start | bytes 2359304 | tf_op jit(solution)/shard_map/ppermute | solution.py:389
  371.5 114.3 %collective-permute-start.25 = (bf16[3,4,128,256]{3,2,1,0:T(8,128)(2,1)S(1)}, bf16[3,4,128,256]{3,2,1,0:T(8,128)(2,1)}, u32[]{:S(2)}, u32[]{:S(2)}) collective-permute-start(bf16[3,4,128,256]{3,2,1,0:T(8,128)(2,1)S(1)} %mix.10.refs_3_), channel_id=1, source_target_pairs={{0,8},{4,12},{8,16},{12,20},{16,24},{20,28},{24,0},{28,4},{1,9},{5... | collective-permute-start | bytes 2359304 | tf_op jit(solution)/shard_map/ppermute | solution.py:389
  378.2 109.8 %collective-permute-start.24 = (bf16[3,4,128,256]{3,2,1,0:T(8,128)(2,1)}, bf16[3,4,128,256]{3,2,1,0:T(8,128)(2,1)}, u32[]{:S(2)}, u32[]{:S(2)}) collective-permute-start(bf16[3,4,128,256]{3,2,1,0:T(8,128)(2,1)} %mix.12.refs_3_), channel_id=1, source_target_pairs={{0,24},{4,28},{8,0},{12,4},{16,8},{20,12},{24,16},{28,20},{1,25},{... | collective-permute-start | bytes 2359304 | tf_op jit(solution)/shard_map/ppermute | solution.py:389
  384.2 117.1 %collective-permute-start.22 = (bf16[3,4,128,256]{3,2,1,0:T(8,128)(2,1)S(1)}, bf16[3,4,128,256]{3,2,1,0:T(8,128)(2,1)}, u32[]{:S(2)}, u32[]{:S(2)}) collective-permute-start(bf16[3,4,128,256]{3,2,1,0:T(8,128)(2,1)S(1)} %mix.13.refs_3_), channel_id=1, source_target_pairs={{0,28},{4,24},{8,4},{12,0},{16,12},{20,8},{24,20},{28,16},{1,29},{... | collective-permute-start | bytes 2359304 | tf_op jit(solution)/shard_map/ppermute | solution.py:389
  433.5 0.9 copy-start
  434.4 55.6 %collective-permute-start.23 = (bf16[3,4,128,256]{3,2,1,0:T(8,128)(2,1)}, bf16[3,4,128,256]{3,2,1,0:T(8,128)(2,1)}, u32[]{:S(2)}, u32[]{:S(2)}) collective-permute-start(bf16[3,4,128,256]{3,2,1,0:T(8,128)(2,1)} %mix.14.refs_3_), channel_id=1, source_target_pairs={{0,4},{4,0},{8,12},{12,8},{16,20},{20,16},{24,28},{28,24},{1,5},{5... | collective-permute-start | bytes 2359304 | tf_op jit(solution)/shard_map/ppermute | solution.py:389
  450.4 0.9 copy-start.2
  451.3 50.9 %collective-permute-start.21 = (bf16[3,4,128,256]{3,2,1,0:T(8,128)(2,1)S(1)}, bf16[3,4,128,256]{3,2,1,0:T(8,128)(2,1)}, u32[]{:S(2)}, u32[]{:S(2)}) collective-permute-start(bf16[3,4,128,256]{3,2,1,0:T(8,128)(2,1)S(1)} %mix.11.refs_3_), channel_id=1, source_target_pairs={{0,12},{4,8},{8,20},{12,16},{16,28},{20,24},{24,4},{28,0},{1,13},{... | collective-permute-start | bytes 2359304 | tf_op jit(solution)/shard_map/ppermute | solution.py:389
  476.3 1.1 copy-start.1
  477.4 1.4 copy-start.3
  (3 other events, 2.5 us)

commit v11 on v10

--- a/solution.py
+++ b/solution.py
@@ -468,19 +468,31 @@
         (2, 2, blocks, 2, orders, blocks),
     ).reshape(2, depth, depth * orders)
 
+    paired = not (sec_count & (sec_count - 1) or tm_count & (tm_count - 1))
+
+    def exchange(piece, z, x):
+        if not paired or (z, x) == (0, 0):
+            return owner_after(-z, -x), send(piece, z, x)
+        hops = [
+            (a * tm_count + j, (a ^ z) * tm_count + (j ^ x))
+            for a in range(sec_count)
+            for j in range(tm_count)
+        ]
+        return (sec_at ^ z) * tm_count + (tm_at ^ x), lax.ppermute(piece, owner_axes, hops)
+
     coeffs = [pltpu.with_memory_space_constraint(x, pltpu.HBM) for x in coeffs]
+    far = [r for r in shifts if r[0] >= max(sec_count // 2, 1)]
+    near = sorted([r for r in shifts if r not in far and r != (0, 0)], key=lambda r: (r[0] == 0, r))
     sent = {}
     before = ()
-    for z, x in in_order + [(0, 0)]:
-        piece = mix(
-            owner_after(z, x), coeffs, mixing, spread, factor, root_weight, owners, orders, before
-        )
+    in_turn = near[:1] + far[:1] + near[1:] + far[1:]
+    for z, x in in_turn + [(0, 0)]:
+        owner = (sec_at ^ z) * tm_count + (tm_at ^ x) if paired else owner_after(z, x)
+        piece = mix(owner, coeffs, mixing, spread, factor, root_weight, owners, orders, before)
         before = (piece,)
-        sent[z, x] = owner_after(-z, -x), send(piece, z, x)
-    late = [r for r in in_order if r[0] in (0, 1) and r[1] > 0 or r == in_order[-tm_count]]
-    groups = [[(0, 0)]] + [[r] for r in in_order if r not in late] + [late]
+        sent[z, x] = exchange(piece, z, x)
     mode_fields = None
-    for group in groups:
+    for group in ([(0, 0)], in_turn[:1], in_turn[1:2], in_turn[2:]):
         pieces = [sent[r][1].reshape(fields, own_freqs, 2, orders, MODES, part) for r in group]
         mode_fields = unpack([sent[r][0] for r in group], pieces, owners, mode_fields)
     mode_fields = jnp.transpose(mode_fields, (0, 1, 2, 4, 3, 5))

time: 510 us -> 513 us (level)
  waiting for transfers between devices: 244 us -> 270 us
  starting transfers between devices: 132 us -> 113 us
    ppermute x0 -> x7, waiting for transfers between devices: none -> 106 us  [exchange(): lax.ppermute(piece, owner_axes, hops)]
    ppermute x28 -> x21, waiting for transfers between devices: 229 us -> 149 us  [send(): return lax.ppermute(piece, owner_axes, hops)]
    ppermute x28 -> x21, starting transfers between devices: 122 us -> 90.8 us  [send(): return lax.ppermute(piece, owner_axes, hops)]
    ppermute x0 -> x7, starting transfers between devices: none -> 11 us  [exchange(): lax.ppermute(piece, owner_axes, hops)]
    unnamed x44 -> x36, local copies, waits for them, and re-layouts: 15.5 us -> 12.1 us
    pallas_call x6 -> x4, Pallas kernels: 11 us -> 10.3 us  [unpack(): pl.pallas_call(functools.partial(unpack_kernel, count), grid_spec=pltpu.P...]
  transfers between devices with their start and end apart: 30 -> 30, of which waited for: 18 -> 15; matrix products, arithmetic and copies ran while one was open for 3% -> 3% of each run, Pallas kernels for 15% -> 15%
where the time goes in v11:
time: 513 us; the launch traced here: 510 us
  waiting for transfers between devices  270 us (53%)
  starting transfers between devices  113 us (22%)
  Pallas kernels  97.2 us (19%)
  local copies, waits for them, and re-layouts  23.8 us (5%)
  other arithmetic  5.44 us (1%)
    ppermute x21, waiting for transfers between devices, send(): return lax.ppermute(piece, owner_axes, hops)  149 us
    ppermute x7, waiting for transfers between devices, exchange(): lax.ppermute(piece, owner_axes, hops)  106 us
    ppermute x21, starting transfers between devices, send(): return lax.ppermute(piece, owner_axes, hops)  90.8 us
    pallas_call x24, Pallas kernels, take(): pl.pallas_call(take_kernel, grid_spec=pltpu.PrefetchScalarGridSpec(num_sc...  31.3 us
    pallas_call x3, Pallas kernels, coeffs_and_gram(): pl.pallas_call(functools.partial(coeff_kernel, sec_count, sec_local, freq...  30.4 us
    pallas_call x8, Pallas kernels, mix(): pl.pallas_call(functools.partial(mix_kernel, orders, fields), grid_spec=p...  21.2 us
    unnamed x36, local copies, waits for them, and re-layouts  12.1 us
    ppermute x7, starting transfers between devices, exchange(): lax.ppermute(piece, owner_axes, hops)  11 us
  transfers between devices with their start and end apart: 30, of which 15 were waited for; matrix products, arithmetic and copies ran while one was open for 3% of the time, Pallas kernels for 15%

profile of v11, /device:TPU:16, one launch (start us, length us, event | category | flops | bytes accessed | tf_op | source)
XLA Modules:
  0.0 510.4 jit_solution(8572027373153619130)
XLA Ops:
  1.8 2.6 collective-permute-start.2
  7.0 2.3 collective-permute-start.6
  13.1 2.0 take.37
  15.0 2.0 take.39
  17.0 2.0 take.35
  20.9 1.9 take.36
  22.8 2.0 take.30
  25.1 20.4 %collective-permute-done.2.refs_3_ = bf16[4,296,256]{2,1,0:T(8,128)(2,1)} collective-permute-done((bf16[4,296,256]{2,1,0:T(8,128)(2,1)S(1)}, bf16[4,296,256]{2,1,0:T(8,128)(2,1)}, u32[]{:S(2)}, u32[]{:S(2)}) %collective-permute-start.2) | collective-permute-done | bytes 606240 | tf_op jit(solution)/shard_map/ppermute | solution.py:389
  45.5 2.9 multiply_bitcast_fusion
  48.4 29.0 %collective-permute-start.5 = (bf16[4,296,256]{2,1,0:T(8,128)(2,1)}, bf16[4,296,256]{2,1,0:T(8,128)(2,1)}, u32[]{:S(2)}, u32[]{:S(2)}) collective-permute-start(bf16[4,296,256]{2,1,0:T(8,128)(2,1)} %take.30), channel_id=1, source_target_pairs={{0,24},{4,28},{8,0},{12,4},{16,8},{20,12},{24,16},{28,20},{1,25},{... | collective-permute-start | bytes 1818632 | tf_op jit(solution)/shard_map/ppermute | solution.py:389
  77.4 4.7 collective-permute-done.6.refs_7_
  82.7 2.9 collective-permute-start.13
  85.6 37.9 %collective-permute-done.1.refs_2_ = bf16[4,296,256]{2,1,0:T(8,128)(2,1)} collective-permute-done((bf16[4,296,256]{2,1,0:T(8,128)(2,1)S(1)}, bf16[4,296,256]{2,1,0:T(8,128)(2,1)}, u32[]{:S(2)}, u32[]{:S(2)}) %collective-permute-start.1) | collective-permute-done | bytes 606240 | tf_op jit(solution)/shard_map/ppermute | solution.py:389
  146.7 5.7 %reshape.485.azimuth_ref = bf16[128,256]{1,0:T(8,128)(2,1)} reshape(bf16[2,8,2,4,16,2,2,4]{7,6,5,4,3,2,1,0:T(2,128)(2,1)} %multiply_bitcast_fusion) | data formatting | bytes 131072 | tf_op jit(solution)/shard_map/reshape | solution.py:404
  152.7 28.0 %collective-permute-start.12 = (bf16[4,296,256]{2,1,0:T(8,128)(2,1)}, bf16[4,296,256]{2,1,0:T(8,128)(2,1)}, u32[]{:S(2)}, u32[]{:S(2)}) collective-permute-start(bf16[4,296,256]{2,1,0:T(8,128)(2,1)} %copy-done.9), channel_id=1, source_target_pairs={{0,24},{4,28},{8,0},{12,4},{16,8},{20,12},{24,16},{28,20},{1,25},{... | collective-permute-start | bytes 1818632 | tf_op jit(solution)/shard_map/ppermute | solution.py:389
  180.8 7.7 %collective-permute-done.9.refs_3_ = bf16[4,296,256]{2,1,0:T(8,128)(2,1)} collective-permute-done((bf16[4,296,256]{2,1,0:T(8,128)(2,1)}, bf16[4,296,256]{2,1,0:T(8,128)(2,1)}, u32[]{:S(2)}, u32[]{:S(2)}) %collective-permute-start.9) | collective-permute-done | bytes 606240 | tf_op jit(solution)/shard_map/ppermute | solution.py:389
  188.4 36.8 %collective-permute-done.10.refs_4_ = bf16[4,296,256]{2,1,0:T(8,128)(2,1)} collective-permute-done((bf16[4,296,256]{2,1,0:T(8,128)(2,1)}, bf16[4,296,256]{2,1,0:T(8,128)(2,1)}, u32[]{:S(2)}, u32[]{:S(2)}) %collective-permute-start.10) | collective-permute-done | bytes 606240 | tf_op jit(solution)/shard_map/ppermute | solution.py:389
  225.3 3.5 collective-permute-start.18
  231.5 6.8 %collective-permute-done.12.refs_6_ = bf16[4,296,256]{2,1,0:T(8,128)(2,1)} collective-permute-done((bf16[4,296,256]{2,1,0:T(8,128)(2,1)}, bf16[4,296,256]{2,1,0:T(8,128)(2,1)}, u32[]{:S(2)}, u32[]{:S(2)}) %collective-permute-start.12) | collective-permute-done | bytes 606240 | tf_op jit(solution)/shard_map/ppermute | solution.py:389
  238.3 2.6 collective-permute-start.20
  242.8 8.5 %collective-permute-done.18.refs_5_ = bf16[4,296,256]{2,1,0:T(8,128)(2,1)} collective-permute-done((bf16[4,296,256]{2,1,0:T(8,128)(2,1)}, bf16[4,296,256]{2,1,0:T(8,128)(2,1)}, u32[]{:S(2)}, u32[]{:S(2)}) %collective-permute-start.18) | collective-permute-done | bytes 606240 | tf_op jit(solution)/shard_map/ppermute | solution.py:389
  251.3 14.7 %collective-permute-start.19 = (bf16[4,296,256]{2,1,0:T(8,128)(2,1)S(1)}, bf16[4,296,256]{2,1,0:T(8,128)(2,1)S(1)}, u32[]{:S(2)}, u32[]{:S(2)}) collective-permute-start(bf16[4,296,256]{2,1,0:T(8,128)(2,1)S(1)} %take.46), channel_id=1, source_target_pairs={{0,24},{4,28},{8,0},{12,4},{16,8},{20,12},{24,16},{28,20},{1,25},{... | collective-permute-start | bytes 1818632 | tf_op jit(solution)/shard_map/ppermute | solution.py:389
  269.0 10.2 %coeffs_and_gram.3 = (bf16[32,256,256]{2,1,0:T(8,128)(2,1)}, f32[32,16,128]{2,1,0:T(8,128)S(1)}) custom-call(s32[2]{0:T(128)S(1)} %pad_add_fusion.place_ref, bf16[2,2,256,168]{3,2,1,0:T(8,128)(2,1)S(1)} %copy.36.time_ref, bf16[128,256]{1,0:T(8,128)(2,1)S(1)} %copy-done.11, f32[1,256]{1,0:T(1,128)S(1)} %bitcast.83, ...), custom_call_target="tpu_custom_call" | custom-call | flops 3556769792 | bytes 9043968 | tf_op jit(solution)/shard_map/coeffs_and_gram/pallas_call | solution.py:139
  279.3 10.3 %coeffs_and_gram.4 = (bf16[32,256,256]{2,1,0:T(8,128)(2,1)}, f32[32,16,128]{2,1,0:T(8,128)S(1)}) custom-call(s32[2]{0:T(128)S(1)} %pad_add_fusion.place_ref, bf16[2,2,256,168]{3,2,1,0:T(8,128)(2,1)S(1)} %copy.36.time_ref, bf16[128,256]{1,0:T(8,128)(2,1)S(1)} %copy-done.11, f32[1,256]{1,0:T(1,128)S(1)} %bitcast.84, ...), custom_call_target="tpu_custom_call" | custom-call | flops 3556769792 | bytes 9043968 | tf_op jit(solution)/shard_map/coeffs_and_gram/pallas_call | solution.py:139
  290.4 15.0 %collective-permute-done.15.refs_2_ = bf16[4,296,256]{2,1,0:T(8,128)(2,1)S(1)} collective-permute-done((bf16[4,296,256]{2,1,0:T(8,128)(2,1)S(1)}, bf16[4,296,256]{2,1,0:T(8,128)(2,1)S(1)}, u32[]{:S(2)}, u32[]{:S(2)}) %collective-permute-start.15) | collective-permute-done | bytes 606240 | tf_op jit(solution)/shard_map/ppermute | solution.py:389
  305.4 10.8 %collective-permute-done.19.refs_6_ = bf16[4,296,256]{2,1,0:T(8,128)(2,1)S(1)} collective-permute-done((bf16[4,296,256]{2,1,0:T(8,128)(2,1)S(1)}, bf16[4,296,256]{2,1,0:T(8,128)(2,1)S(1)}, u32[]{:S(2)}, u32[]{:S(2)}) %collective-permute-start.19) | collective-permute-done | bytes 606240 | tf_op jit(solution)/shard_map/ppermute | solution.py:389
  316.1 9.8 %coeffs_and_gram.5 = (bf16[32,256,256]{2,1,0:T(8,128)(2,1)}, f32[32,16,128]{2,1,0:T(8,128)}) custom-call(s32[2]{0:T(128)S(1)} %pad_add_fusion.place_ref, bf16[2,2,256,168]{3,2,1,0:T(8,128)(2,1)S(1)} %copy.36.time_ref, bf16[128,256]{1,0:T(8,128)(2,1)S(1)} %copy-done.11, f32[1,256]{1,0:T(1,128)S(1)} %bitcast.85, ...), custom_call_target="tpu_custom_call" | custom-call | flops 3556769792 | bytes 9043968 | tf_op jit(solution)/shard_map/coeffs_and_gram/pallas_call | solution.py:139
  326.0 6.0 %all-to-all-start = ((f32[32,1,16,128]{3,2,1,0:T(8,128)}), f32[32,1,16,128]{3,2,1,0:T(8,128)S(1)}, u32[]{:S(2)}, u32[]{:S(2)}) async-start(f32[32,1,16,128]{3,2,1,0:T(8,128)} %bitcast.27), calls=%async_computation | async-start | bytes 524288 | tf_op jit(solution)/shard_map/all_to_all | solution.py:437
  332.6 7.5 %all-to-all-done = f32[32,1,16,128]{3,2,1,0:T(8,128)S(1)} async-done(((f32[32,1,16,128]{3,2,1,0:T(8,128)}), f32[32,1,16,128]{3,2,1,0:T(8,128)S(1)}, u32[]{:S(2)}, u32[]{:S(2)}) %all-to-all-start) | async-done | bytes 262176 | tf_op jit(solution)/shard_map/all_to_all | solution.py:437
  341.0 4.0 subspace.1
  347.9 4.9 all-to-all-start.1
  353.3 6.9 %all-to-all-done.1 = bf16[32,1,18,128]{3,2,1,0:T(8,128)(2,1)S(1)} async-done(((bf16[32,1,18,128]{3,2,1,0:T(8,128)(2,1)}), bf16[32,1,18,128]{3,2,1,0:T(8,128)(2,1)S(1)}, u32[]{:S(2)}, u32[]{:S(2)}) %all-to-all-start.1) | async-done | bytes 147488 | tf_op jit(solution)/shard_map/all_to_all | solution.py:454
  360.8 2.2 mix.8.refs_3_
  364.3 3.1 mix.9.refs_3_
  367.4 1.6 collective-permute-start.26
  369.0 2.2 mix.10.refs_3_
  371.2 2.2 mix.11.refs_3_
  373.4 3.1 mix.12.refs_3_
  378.0 3.1 mix.13.refs_3_
  382.5 3.1 mix.14.refs_3_
  386.9 6.9 %collective-permute-done.27 = bf16[3,4,128,256]{3,2,1,0:T(8,128)(2,1)} collective-permute-done((bf16[3,4,128,256]{3,2,1,0:T(8,128)(2,1)S(1)}, bf16[3,4,128,256]{3,2,1,0:T(8,128)(2,1)}, u32[]{:S(2)}, u32[]{:S(2)}) %collective-permute-start.27) | collective-permute-done | bytes 786464 | tf_op jit(solution)/shard_map/ppermute | solution.py:481
  395.0 59.7 %collective-permute-done.26 = bf16[3,4,128,256]{3,2,1,0:T(8,128)(2,1)} collective-permute-done((bf16[3,4,128,256]{3,2,1,0:T(8,128)(2,1)}, bf16[3,4,128,256]{3,2,1,0:T(8,128)(2,1)}, u32[]{:S(2)}, u32[]{:S(2)}) %collective-permute-start.26) | collective-permute-done | bytes 786464 | tf_op jit(solution)/shard_map/ppermute | solution.py:481
  454.7 2.7 collective-permute-start.21
  457.5 2.2 mix.15
  461.5 2.1 unpack.5.refs_1_
  463.6 2.1 unpack.6.refs_5_
  465.6 39.5 %collective-permute-done.25 = bf16[3,4,128,256]{3,2,1,0:T(8,128)(2,1)} collective-permute-done((bf16[3,4,128,256]{3,2,1,0:T(8,128)(2,1)}, bf16[3,4,128,256]{3,2,1,0:T(8,128)(2,1)}, u32[]{:S(2)}, u32[]{:S(2)}) %collective-permute-start.25) | collective-permute-done | bytes 786464 | tf_op jit(solution)/shard_map/ppermute | solution.py:481
  505.2 5.3 %unpack.7 = bf16[8,4,2,3,8,2048]{5,4,3,2,1,0:T(8,128)(2,1)} custom-call(s32[5]{0:T(128)S(1)} %stack.65.owner_ref, bf16[3,4,2,8,8,256]{5,4,3,2,1,0:T(8,128)(2,1)} %bitcast.37.refs_0_, bf16[3,4,2,8,8,256]{5,4,3,2,1,0:T(8,128)(2,1)S(1)} %bitcast.82, bf16[3,4,2,8,8,256]{5,4,3,2,1,0:T(8,128)(2,1)} %bitcast.39.refs_2_, ...), custom_call_target="tpu_custom_call", output_to_operand_aliasing={{}: (6, {})} | custom-call | bytes 7864320 | tf_op jit(solution)/shard_map/unpack/pallas_call | solution.py:338
  (137 shorter events, 56.3 us)
Async XLA Ops:
  1.8 43.7 %collective-permute-start.2 = (bf16[4,296,256]{2,1,0:T(8,128)(2,1)S(1)}, bf16[4,296,256]{2,1,0:T(8,128)(2,1)}, u32[]{:S(2)}, u32[]{:S(2)}) collective-permute-start(bf16[4,296,256]{2,1,0:T(8,128)(2,1)S(1)} %take.27), channel_id=1, source_target_pairs={{0,12},{4,8},{8,20},{12,16},{16,28},{20,24},{24,4},{28,0},{1,13},{... | collective-permute-start | bytes 1818632 | tf_op jit(solution)/shard_map/ppermute | solution.py:389
  5.5 42.9 %collective-permute-start.4 = (bf16[4,296,256]{2,1,0:T(8,128)(2,1)S(1)}, bf16[4,296,256]{2,1,0:T(8,128)(2,1)}, u32[]{:S(2)}, u32[]{:S(2)}) collective-permute-start(bf16[4,296,256]{2,1,0:T(8,128)(2,1)S(1)} %take.29), channel_id=1, source_target_pairs={{0,20},{4,16},{8,28},{12,24},{16,4},{20,0},{24,12},{28,8},{1,21},{... | collective-permute-start | bytes 1818632 | tf_op jit(solution)/shard_map/ppermute | solution.py:389
  7.0 75.1 %collective-permute-start.6 = (bf16[4,296,256]{2,1,0:T(8,128)(2,1)S(1)}, bf16[4,296,256]{2,1,0:T(8,128)(2,1)}, u32[]{:S(2)}, u32[]{:S(2)}) collective-permute-start(bf16[4,296,256]{2,1,0:T(8,128)(2,1)S(1)} %take.31), channel_id=1, source_target_pairs={{0,28},{4,24},{8,4},{12,0},{16,12},{20,8},{24,20},{28,16},{1,29},{... | collective-permute-start | bytes 1818632 | tf_op jit(solution)/shard_map/ppermute | solution.py:389
  10.4 72.3 %collective-permute-start = (bf16[4,296,256]{2,1,0:T(8,128)(2,1)S(1)}, bf16[4,296,256]{2,1,0:T(8,128)(2,1)}, u32[]{:S(2)}, u32[]{:S(2)}) collective-permute-start(bf16[4,296,256]{2,1,0:T(8,128)(2,1)S(1)} %take.25), channel_id=1, source_target_pairs={{0,4},{4,0},{8,12},{12,8},{16,20},{20,16},{24,28},{28,24},{1,5},{5... | collective-permute-start | bytes 1818632 | tf_op jit(solution)/shard_map/ppermute | solution.py:389
  12.0 111.4 %collective-permute-start.1 = (bf16[4,296,256]{2,1,0:T(8,128)(2,1)S(1)}, bf16[4,296,256]{2,1,0:T(8,128)(2,1)}, u32[]{:S(2)}, u32[]{:S(2)}) collective-permute-start(bf16[4,296,256]{2,1,0:T(8,128)(2,1)S(1)} %take.26), channel_id=1, source_target_pairs={{0,8},{4,12},{8,16},{12,20},{16,24},{20,28},{24,0},{28,4},{1,9},{5... | collective-permute-start | bytes 1818632 | tf_op jit(solution)/shard_map/ppermute | solution.py:389
  20.1 0.8 copy-start.10
  45.5 78.0 %collective-permute-start.3 = (bf16[4,296,256]{2,1,0:T(8,128)(2,1)}, bf16[4,296,256]{2,1,0:T(8,128)(2,1)S(1)}, u32[]{:S(2)}, u32[]{:S(2)}) collective-permute-start(bf16[4,296,256]{2,1,0:T(8,128)(2,1)} %copy-done.10), channel_id=1, source_target_pairs={{0,16},{4,20},{8,24},{12,28},{16,0},{20,4},{24,8},{28,12},{1,17},{... | collective-permute-start | bytes 1818632 | tf_op jit(solution)/shard_map/ppermute | solution.py:389
  48.4 104.2 %collective-permute-start.5 = (bf16[4,296,256]{2,1,0:T(8,128)(2,1)}, bf16[4,296,256]{2,1,0:T(8,128)(2,1)}, u32[]{:S(2)}, u32[]{:S(2)}) collective-permute-start(bf16[4,296,256]{2,1,0:T(8,128)(2,1)} %take.30), channel_id=1, source_target_pairs={{0,24},{4,28},{8,0},{12,4},{16,8},{20,12},{24,16},{28,20},{1,25},{... | collective-permute-start | bytes 1818632 | tf_op jit(solution)/shard_map/ppermute | solution.py:389
  82.1 98.6 %collective-permute-start.11 = (bf16[4,296,256]{2,1,0:T(8,128)(2,1)}, bf16[4,296,256]{2,1,0:T(8,128)(2,1)}, u32[]{:S(2)}, u32[]{:S(2)}) collective-permute-start(bf16[4,296,256]{2,1,0:T(8,128)(2,1)} %take.37), channel_id=1, source_target_pairs={{0,20},{4,16},{8,28},{12,24},{16,4},{20,0},{24,12},{28,8},{1,21},{... | collective-permute-start | bytes 1818632 | tf_op jit(solution)/shard_map/ppermute | solution.py:389
  82.7 98.0 %collective-permute-start.13 = (bf16[4,296,256]{2,1,0:T(8,128)(2,1)}, bf16[4,296,256]{2,1,0:T(8,128)(2,1)}, u32[]{:S(2)}, u32[]{:S(2)}) collective-permute-start(bf16[4,296,256]{2,1,0:T(8,128)(2,1)} %take.39), channel_id=1, source_target_pairs={{0,28},{4,24},{8,4},{12,0},{16,12},{20,8},{24,20},{28,16},{1,29},{... | collective-permute-start | bytes 1818632 | tf_op jit(solution)/shard_map/ppermute | solution.py:389
  123.5 65.0 %collective-permute-start.9 = (bf16[4,296,256]{2,1,0:T(8,128)(2,1)}, bf16[4,296,256]{2,1,0:T(8,128)(2,1)}, u32[]{:S(2)}, u32[]{:S(2)}) collective-permute-start(bf16[4,296,256]{2,1,0:T(8,128)(2,1)} %take.35), channel_id=1, source_target_pairs={{0,12},{4,8},{8,20},{12,16},{16,28},{20,24},{24,4},{28,0},{1,13},{... | collective-permute-start | bytes 1818632 | tf_op jit(solution)/shard_map/ppermute | solution.py:389
  123.5 0.9 copy-start.13
  124.4 100.9 %collective-permute-start.10 = (bf16[4,296,256]{2,1,0:T(8,128)(2,1)}, bf16[4,296,256]{2,1,0:T(8,128)(2,1)}, u32[]{:S(2)}, u32[]{:S(2)}) collective-permute-start(bf16[4,296,256]{2,1,0:T(8,128)(2,1)} %take.36), channel_id=1, source_target_pairs={{0,16},{4,20},{8,24},{12,28},{16,0},{20,4},{24,8},{28,12},{1,17},{... | collective-permute-start | bytes 1818632 | tf_op jit(solution)/shard_map/ppermute | solution.py:389
  126.4 0.8 copy-start.9
  128.3 0.9 copy-start.8
  130.3 0.8 copy-start.7
  132.3 0.8 copy-start.3
  134.2 0.9 copy-start
  136.2 0.8 copy-start.6
  138.2 0.8 copy-start.5
  140.2 0.8 copy-start.2
  145.6 6.8 %copy-start.16 = (s32[16]{0:T(128)S(1)}, s32[16]{0:T(128)}, u32[]{:S(2)}) copy-start(s32[16]{0:T(128)} %param.6) | copy-start | bytes 196
  152.7 85.6 %collective-permute-start.12 = (bf16[4,296,256]{2,1,0:T(8,128)(2,1)}, bf16[4,296,256]{2,1,0:T(8,128)(2,1)}, u32[]{:S(2)}, u32[]{:S(2)}) collective-permute-start(bf16[4,296,256]{2,1,0:T(8,128)(2,1)} %copy-done.9), channel_id=1, source_target_pairs={{0,24},{4,28},{8,0},{12,4},{16,8},{20,12},{24,16},{28,20},{1,25},{... | collective-permute-start | bytes 1818632 | tf_op jit(solution)/shard_map/ppermute | solution.py:389
  180.7 60.1 %collective-permute-start.7 = (bf16[4,296,256]{2,1,0:T(8,128)(2,1)}, bf16[4,296,256]{2,1,0:T(8,128)(2,1)}, u32[]{:S(2)}, u32[]{:S(2)}) collective-permute-start(bf16[4,296,256]{2,1,0:T(8,128)(2,1)} %copy-done.8), channel_id=1, source_target_pairs={{0,4},{4,0},{8,12},{12,8},{16,20},{20,16},{24,28},{28,24},{1,5},{5... | collective-permute-start | bytes 1818632 | tf_op jit(solution)/shard_map/ppermute | solution.py:389
  180.7 61.5 %collective-permute-start.8 = (bf16[4,296,256]{2,1,0:T(8,128)(2,1)}, bf16[4,296,256]{2,1,0:T(8,128)(2,1)}, u32[]{:S(2)}, u32[]{:S(2)}) collective-permute-start(bf16[4,296,256]{2,1,0:T(8,128)(2,1)} %copy-done.7), channel_id=1, source_target_pairs={{0,8},{4,12},{8,16},{12,20},{16,24},{20,28},{24,0},{28,4},{1,9},{5... | collective-permute-start | bytes 1818632 | tf_op jit(solution)/shard_map/ppermute | solution.py:389
  188.4 53.8 %collective-permute-start.16 = (bf16[4,296,256]{2,1,0:T(8,128)(2,1)}, bf16[4,296,256]{2,1,0:T(8,128)(2,1)}, u32[]{:S(2)}, u32[]{:S(2)}) collective-permute-start(bf16[4,296,256]{2,1,0:T(8,128)(2,1)} %copy-done.6), channel_id=1, source_target_pairs={{0,12},{4,8},{8,20},{12,16},{16,28},{20,24},{24,4},{28,0},{1,13},{... | collective-permute-start | bytes 1818632 | tf_op jit(solution)/shard_map/ppermute | solution.py:389
  225.3 26.1 %collective-permute-start.18 = (bf16[4,296,256]{2,1,0:T(8,128)(2,1)}, bf16[4,296,256]{2,1,0:T(8,128)(2,1)}, u32[]{:S(2)}, u32[]{:S(2)}) collective-permute-start(bf16[4,296,256]{2,1,0:T(8,128)(2,1)} %copy-done.5), channel_id=1, source_target_pairs={{0,20},{4,16},{8,28},{12,24},{16,4},{20,0},{24,12},{28,8},{1,21},{... | collective-permute-start | bytes 1818632 | tf_op jit(solution)/shard_map/ppermute | solution.py:389
  231.5 84.7 %copy-start.12 = (f32[256]{0:T(256)}, f32[256]{0:T(256)S(1)}, u32[]{:S(2)}) copy-start(f32[256]{0:T(256)S(1)} %select_reduce_fusion) | copy-start | bytes 3076
  238.3 52.1 %collective-permute-start.20 = (bf16[4,296,256]{2,1,0:T(8,128)(2,1)}, bf16[4,296,256]{2,1,0:T(8,128)(2,1)S(1)}, u32[]{:S(2)}, u32[]{:S(2)}) collective-permute-start(bf16[4,296,256]{2,1,0:T(8,128)(2,1)} %copy-done.2), channel_id=1, source_target_pairs={{0,28},{4,24},{8,4},{12,0},{16,12},{20,8},{24,20},{28,16},{1,29},{... | collective-permute-start | bytes 1818632 | tf_op jit(solution)/shard_map/ppermute | solution.py:389
  240.8 49.5 %collective-permute-start.14 = (bf16[4,296,256]{2,1,0:T(8,128)(2,1)S(1)}, bf16[4,296,256]{2,1,0:T(8,128)(2,1)S(1)}, u32[]{:S(2)}, u32[]{:S(2)}) collective-permute-start(bf16[4,296,256]{2,1,0:T(8,128)(2,1)S(1)} %take.41), channel_id=1, source_target_pairs={{0,4},{4,0},{8,12},{12,8},{16,20},{20,16},{24,28},{28,24},{1,5},{5... | collective-permute-start | bytes 1818632 | tf_op jit(solution)/shard_map/ppermute | solution.py:389
  242.2 63.1 %collective-permute-start.15 = (bf16[4,296,256]{2,1,0:T(8,128)(2,1)S(1)}, bf16[4,296,256]{2,1,0:T(8,128)(2,1)S(1)}, u32[]{:S(2)}, u32[]{:S(2)}) collective-permute-start(bf16[4,296,256]{2,1,0:T(8,128)(2,1)S(1)} %take.42), channel_id=1, source_target_pairs={{0,8},{4,12},{8,16},{12,20},{16,24},{20,28},{24,0},{28,4},{1,9},{5... | collective-permute-start | bytes 1818632 | tf_op jit(solution)/shard_map/ppermute | solution.py:389
  242.2 63.1 %collective-permute-start.17 = (bf16[4,296,256]{2,1,0:T(8,128)(2,1)S(1)}, bf16[4,296,256]{2,1,0:T(8,128)(2,1)S(1)}, u32[]{:S(2)}, u32[]{:S(2)}) collective-permute-start(bf16[4,296,256]{2,1,0:T(8,128)(2,1)S(1)} %take.44), channel_id=1, source_target_pairs={{0,16},{4,20},{8,24},{12,28},{16,0},{20,4},{24,8},{28,12},{1,17},{... | collective-permute-start | bytes 1818632 | tf_op jit(solution)/shard_map/ppermute | solution.py:389
  251.3 64.8 %collective-permute-start.19 = (bf16[4,296,256]{2,1,0:T(8,128)(2,1)S(1)}, bf16[4,296,256]{2,1,0:T(8,128)(2,1)S(1)}, u32[]{:S(2)}, u32[]{:S(2)}) collective-permute-start(bf16[4,296,256]{2,1,0:T(8,128)(2,1)S(1)} %take.46), channel_id=1, source_target_pairs={{0,24},{4,28},{8,0},{12,4},{16,8},{20,12},{24,16},{28,20},{1,25},{... | collective-permute-start | bytes 1818632 | tf_op jit(solution)/shard_map/ppermute | solution.py:389
  266.1 1.1 copy-start.4
  267.1 0.8 copy-start.11
  268.0 1.1 copy-start.14
  269.0 10.3 %copy-start.1 = (bf16[4,296,256]{2,1,0:T(8,128)(2,1)S(1)}, bf16[4,296,256]{2,1,0:T(8,128)(2,1)}, u32[]{:S(2)}) copy-start(bf16[4,296,256]{2,1,0:T(8,128)(2,1)} %copy-done) | copy-start | bytes 1818628
  316.1 36.8 %copy-start.15 = (bf16[2,2,2]{2,1,0:T(2,128)(2,1)S(1)}, bf16[2,2,2]{2,1,0:T(2,128)(2,1)}, u32[]{:S(2)}) copy-start(bf16[2,2,2]{2,1,0:T(2,128)(2,1)} %constant.194.clone) | copy-start | bytes 52
  326.0 14.2 %all-to-all-start = ((f32[32,1,16,128]{3,2,1,0:T(8,128)}), f32[32,1,16,128]{3,2,1,0:T(8,128)S(1)}, u32[]{:S(2)}, u32[]{:S(2)}) async-start(f32[32,1,16,128]{3,2,1,0:T(8,128)} %bitcast.27), calls=%async_computation | async-start | bytes 524288 | tf_op jit(solution)/shard_map/all_to_all | solution.py:437
  347.9 12.3 %all-to-all-start.1 = ((bf16[32,1,18,128]{3,2,1,0:T(8,128)(2,1)}), bf16[32,1,18,128]{3,2,1,0:T(8,128)(2,1)S(1)}, u32[]{:S(2)}, u32[]{:S(2)}) async-start(bf16[32,1,18,128]{3,2,1,0:T(8,128)(2,1)} %broadcast_in_dim.27), calls=%async_computation.1 | async-start | bytes 393216 | tf_op jit(solution)/shard_map/all_to_all | solution.py:454
  363.0 30.8 %collective-permute-start.27 = (bf16[3,4,128,256]{3,2,1,0:T(8,128)(2,1)S(1)}, bf16[3,4,128,256]{3,2,1,0:T(8,128)(2,1)}, u32[]{:S(2)}, u32[]{:S(2)}) collective-permute-start(bf16[3,4,128,256]{3,2,1,0:T(8,128)(2,1)S(1)} %mix.8.refs_3_), channel_id=1, source_target_pairs={{0,8},{4,12},{8,0},{12,4},{16,24},{20,28},{24,16},{28,20},{1,9},{5... | collective-permute-start | bytes 2359304 | tf_op jit(solution)/shard_map/ppermute | solution.py:481
  367.4 87.4 %collective-permute-start.26 = (bf16[3,4,128,256]{3,2,1,0:T(8,128)(2,1)}, bf16[3,4,128,256]{3,2,1,0:T(8,128)(2,1)}, u32[]{:S(2)}, u32[]{:S(2)}) collective-permute-start(bf16[3,4,128,256]{3,2,1,0:T(8,128)(2,1)} %mix.9.refs_3_), channel_id=1, source_target_pairs={{0,16},{4,20},{8,24},{12,28},{16,0},{20,4},{24,8},{28,12},{1,17},{... | collective-permute-start | bytes 2359304 | tf_op jit(solution)/shard_map/ppermute | solution.py:481
  376.5 128.6 %collective-permute-start.23 = (bf16[3,4,128,256]{3,2,1,0:T(8,128)(2,1)}, bf16[3,4,128,256]{3,2,1,0:T(8,128)(2,1)}, u32[]{:S(2)}, u32[]{:S(2)}) collective-permute-start(bf16[3,4,128,256]{3,2,1,0:T(8,128)(2,1)} %mix.12.refs_3_), channel_id=1, source_target_pairs={{0,20},{4,16},{8,28},{12,24},{16,4},{20,0},{24,12},{28,8},{1,21},{... | collective-permute-start | bytes 2359304 | tf_op jit(solution)/shard_map/ppermute | solution.py:481
  381.1 124.1 %collective-permute-start.24 = (bf16[3,4,128,256]{3,2,1,0:T(8,128)(2,1)}, bf16[3,4,128,256]{3,2,1,0:T(8,128)(2,1)}, u32[]{:S(2)}, u32[]{:S(2)}) collective-permute-start(bf16[3,4,128,256]{3,2,1,0:T(8,128)(2,1)} %mix.13.refs_3_), channel_id=1, source_target_pairs={{0,24},{4,28},{8,16},{12,20},{16,8},{20,12},{24,0},{28,4},{1,25},{... | collective-permute-start | bytes 2359304 | tf_op jit(solution)/shard_map/ppermute | solution.py:481
  385.6 119.6 %collective-permute-start.25 = (bf16[3,4,128,256]{3,2,1,0:T(8,128)(2,1)}, bf16[3,4,128,256]{3,2,1,0:T(8,128)(2,1)}, u32[]{:S(2)}, u32[]{:S(2)}) collective-permute-start(bf16[3,4,128,256]{3,2,1,0:T(8,128)(2,1)} %mix.14.refs_3_), channel_id=1, source_target_pairs={{0,28},{4,24},{8,20},{12,16},{16,12},{20,8},{24,4},{28,0},{1,29},{... | collective-permute-start | bytes 2359304 | tf_op jit(solution)/shard_map/ppermute | solution.py:481
  393.8 111.4 %collective-permute-start.22 = (bf16[3,4,128,256]{3,2,1,0:T(8,128)(2,1)S(1)}, bf16[3,4,128,256]{3,2,1,0:T(8,128)(2,1)S(1)}, u32[]{:S(2)}, u32[]{:S(2)}) collective-permute-start(bf16[3,4,128,256]{3,2,1,0:T(8,128)(2,1)S(1)} %mix.11.refs_3_), channel_id=1, source_target_pairs={{0,4},{4,0},{8,12},{12,8},{16,20},{20,16},{24,28},{28,24},{1,5},{5... | collective-permute-start | bytes 2359304 | tf_op jit(solution)/shard_map/ppermute | solution.py:481
  454.7 50.4 %collective-permute-start.21 = (bf16[3,4,128,256]{3,2,1,0:T(8,128)(2,1)S(1)}, bf16[3,4,128,256]{3,2,1,0:T(8,128)(2,1)}, u32[]{:S(2)}, u32[]{:S(2)}) collective-permute-start(bf16[3,4,128,256]{3,2,1,0:T(8,128)(2,1)S(1)} %mix.10.refs_3_), channel_id=1, source_target_pairs={{0,12},{4,8},{8,4},{12,0},{16,28},{20,24},{24,20},{28,16},{1,13},{... | collective-permute-start | bytes 2359304 | tf_op jit(solution)/shard_map/ppermute | solution.py:481

commit v12 on v10

--- a/solution.py
+++ b/solution.py
@@ -66,29 +66,30 @@
     record_refs, (coeff_ref, gram_ref, spectra) = refs[:-3], refs[-3:]
     step = pl.program_id(0)
     tm_count, halves, _, span = time_ref.shape
-    rec_len, columns = record_refs[0].shape[1:]
+    together, rec_len, columns = record_refs[0].shape
+    early_steps = sec_local // together
     sectors = spectra.shape[0]
     rows = spectra.shape[2] // NFREQ
 
-    @pl.when(step < sec_local)
+    @pl.when(step < early_steps)
     def _():
-        for shift in range(sec_count):
+        for shift, s in [(shift, s) for shift in range(sec_count) for s in range(together)]:
             source = lax.rem(place_ref[0] + sec_count - shift, sec_count)
             own = record_refs[shift * tm_count:(shift + 1) * tm_count]
             for h in range(halves):
                 first = h * (rec_len - span) // (halves - 1)
                 parts = []
                 for j in range(tm_count):
-                    piece = own[0][0, first:first + span]
+                    piece = own[0][s, first:first + span]
                     for x in range(1, tm_count):
                         here = lax.rem(place_ref[1] + tm_count - x, tm_count) == j
-                        piece = jnp.where(here, own[x][0, first:first + span], piece)
+                        piece = jnp.where(here, own[x][s, first:first + span], piece)
                     part = jnp.dot(time_ref[j, h], piece, preferred_element_type=jnp.float32)
                     parts.append(part.reshape(NFREQ, rows // tm_count, columns))
                 joined = jnp.stack(parts, 1).reshape(NFREQ * rows, columns)
-                spectra[source * sec_local + step, h] = joined.astype(jnp.bfloat16)
-
-    @pl.when(step >= sec_local)
+                spectra[source * sec_local + step * together + s, h] = joined.astype(jnp.bfloat16)
+
+    @pl.when(step >= early_steps)
     def _():
         half_rows = azimuth_ref.shape[0]
         depth = half_rows // (2 * orders)
@@ -98,7 +99,7 @@
         column = lax.broadcasted_iota(jnp.int32, (wide, wide), 1) % blocks
         owner = lax.broadcasted_iota(jnp.int32, (blocks, wide), 1) // blocks
         for n in range(freqs):
-            at = pl.multiple_of(((step - sec_local) * freqs + n) * rows, rows)
+            at = pl.multiple_of(((step - early_steps) * freqs + n) * rows, rows)
             own = [
                 spectra[:, h, pl.ds(at, rows), :].reshape(sectors * rows, columns)
                 for h in range(halves)
@@ -128,19 +129,21 @@
     tm_count, halves = time_basis.shape[:2]
     blocks, wide = before.shape[1:]
     rows = azimuth.shape[1] // sectors
-    steps = 4
+    together = 2 if sec_local % 2 == 0 else 1
+    early_steps = sec_local // together
+    steps = 2
     freqs = NFREQ // steps
-    later = lambda i: jnp.maximum(i - sec_local, 0)
-    early = lambda i: jnp.minimum(i, sec_local - 1)
+    later = lambda i: jnp.maximum(i - early_steps, 0)
+    early = lambda i: jnp.minimum(i, early_steps - 1)
     flops = 2 * columns * (
         sectors * time_basis.size + NFREQ * halves * azimuth.size + NFREQ * 4 * wide * wide
     )
-    piece = pl.BlockSpec((1, rec_len, columns), lambda i, _: (early(i), 0, 0))
+    piece = pl.BlockSpec((together, rec_len, columns), lambda i, _: (early(i), 0, 0))
     return pl.pallas_call(
         functools.partial(coeff_kernel, sec_count, sec_local, freqs, wide // blocks),
         grid_spec=pltpu.PrefetchScalarGridSpec(
             num_scalar_prefetch=1,
-            grid=(sec_local + steps,),
+            grid=(early_steps + steps,),
             in_specs=[
                 pl.BlockSpec(time_basis.shape, lambda i, _: (0, 0, 0, 0)),
                 pl.BlockSpec(azimuth.shape, lambda i, _: (0, 0)),

time: 510 us -> 509 us (level)
  transfers between devices with their start and end apart: 30 -> 30, of which waited for: 18 -> 18; matrix products, arithmetic and copies ran while one was open for 3% -> 3% of each run, Pallas kernels for 15% -> 14%
where the time goes in v12:
time: 509 us; the launch traced here: 505 us
  waiting for transfers between devices  246 us (48%)
  starting transfers between devices  132 us (26%)
  Pallas kernels  92.7 us (18%)
  local copies, waits for them, and re-layouts  27.1 us (5%)
  other arithmetic  5.52 us (1%)
    ppermute x28, waiting for transfers between devices, send(): return lax.ppermute(piece, owner_axes, hops)  232 us
    ppermute x28, starting transfers between devices, send(): return lax.ppermute(piece, owner_axes, hops)  122 us
    pallas_call x24, Pallas kernels, take(): pl.pallas_call(take_kernel, grid_spec=pltpu.PrefetchScalarGridSpec(num_sc...  31.3 us
    pallas_call x3, Pallas kernels, coeffs_and_gram(): pl.pallas_call(functools.partial(coeff_kernel, sec_count, sec_local, freq...  27 us
    pallas_call x8, Pallas kernels, mix(): pl.pallas_call(functools.partial(mix_kernel, orders, fields), grid_spec=p...  19.4 us
    unnamed x44, local copies, waits for them, and re-layouts  15.5 us
    pallas_call x6, Pallas kernels, unpack(): pl.pallas_call(functools.partial(unpack_kernel, count), grid_spec=pltpu.P...  11 us
  transfers between devices with their start and end apart: 30, of which 18 were waited for; matrix products, arithmetic and copies ran while one was open for 3% of the time, Pallas kernels for 14%

profile of v12, /device:TPU:16, one launch (start us, length us, event | category | flops | bytes accessed | tf_op | source)
XLA Modules:
  0.0 505.2 jit_solution(17149440685888477215)
XLA Ops:
  3.0 3.1 collective-permute-start.5
  7.2 2.2 collective-permute-start.4
  26.0 3.3 collective-permute-done.3.refs_4_
  29.3 2.2 collective-permute-start
  31.6 2.9 multiply_bitcast_fusion
  34.4 20.5 %collective-permute-done.5.refs_6_ = bf16[4,296,256]{2,1,0:T(8,128)(2,1)} collective-permute-done((bf16[4,296,256]{2,1,0:T(8,128)(2,1)S(1)}, bf16[4,296,256]{2,1,0:T(8,128)(2,1)}, u32[]{:S(2)}, u32[]{:S(2)}) %collective-permute-start.5) | collective-permute-done | bytes 606240 | tf_op jit(solution)/shard_map/ppermute | solution.py:392
  54.9 21.3 %collective-permute-start.2 = (bf16[4,296,256]{2,1,0:T(8,128)(2,1)}, bf16[4,296,256]{2,1,0:T(8,128)(2,1)}, u32[]{:S(2)}, u32[]{:S(2)}) collective-permute-start(bf16[4,296,256]{2,1,0:T(8,128)(2,1)} %take.27), channel_id=1, source_target_pairs={{0,12},{4,8},{8,20},{12,16},{16,28},{20,24},{24,4},{28,0},{1,13},{... | collective-permute-start | bytes 1818632 | tf_op jit(solution)/shard_map/ppermute | solution.py:392
  76.3 30.6 %collective-permute-done.4.refs_5_ = bf16[4,296,256]{2,1,0:T(8,128)(2,1)} collective-permute-done((bf16[4,296,256]{2,1,0:T(8,128)(2,1)S(1)}, bf16[4,296,256]{2,1,0:T(8,128)(2,1)}, u32[]{:S(2)}, u32[]{:S(2)}) %collective-permute-start.4) | collective-permute-done | bytes 606240 | tf_op jit(solution)/shard_map/ppermute | solution.py:392
  106.9 4.8 collective-permute-start.10
  111.7 8.2 %collective-permute-done.6.refs_7_ = bf16[4,296,256]{2,1,0:T(8,128)(2,1)} collective-permute-done((bf16[4,296,256]{2,1,0:T(8,128)(2,1)S(1)}, bf16[4,296,256]{2,1,0:T(8,128)(2,1)}, u32[]{:S(2)}, u32[]{:S(2)}) %collective-permute-start.6) | collective-permute-done | bytes 606240 | tf_op jit(solution)/shard_map/ppermute | solution.py:392
  119.9 3.9 collective-permute-start.12
  146.7 5.7 %reshape.480.azimuth_ref = bf16[128,256]{1,0:T(8,128)(2,1)} reshape(bf16[2,8,2,4,16,2,2,4]{7,6,5,4,3,2,1,0:T(2,128)(2,1)} %multiply_bitcast_fusion) | data formatting | bytes 131072 | tf_op jit(solution)/shard_map/reshape | solution.py:407
  155.6 3.4 collective-permute-done.12.refs_6_
  159.0 18.4 %collective-permute-start.9 = (bf16[4,296,256]{2,1,0:T(8,128)(2,1)}, bf16[4,296,256]{2,1,0:T(8,128)(2,1)}, u32[]{:S(2)}, u32[]{:S(2)}) collective-permute-start(bf16[4,296,256]{2,1,0:T(8,128)(2,1)} %copy-done.11), channel_id=1, source_target_pairs={{0,12},{4,8},{8,20},{12,16},{16,28},{20,24},{24,4},{28,0},{1,13},{... | collective-permute-start | bytes 1818632 | tf_op jit(solution)/shard_map/ppermute | solution.py:392
  177.4 33.5 %collective-permute-done.11.refs_5_ = bf16[4,296,256]{2,1,0:T(8,128)(2,1)} collective-permute-done((bf16[4,296,256]{2,1,0:T(8,128)(2,1)}, bf16[4,296,256]{2,1,0:T(8,128)(2,1)}, u32[]{:S(2)}, u32[]{:S(2)}) %collective-permute-start.11) | collective-permute-done | bytes 606240 | tf_op jit(solution)/shard_map/ppermute | solution.py:392
  211.0 4.7 collective-permute-start.17
  215.6 8.3 %collective-permute-done.13.refs_7_ = bf16[4,296,256]{2,1,0:T(8,128)(2,1)} collective-permute-done((bf16[4,296,256]{2,1,0:T(8,128)(2,1)}, bf16[4,296,256]{2,1,0:T(8,128)(2,1)}, u32[]{:S(2)}, u32[]{:S(2)}) %collective-permute-start.13) | collective-permute-done | bytes 606240 | tf_op jit(solution)/shard_map/ppermute | solution.py:392
  224.0 3.8 collective-permute-start.19
  232.3 6.5 %collective-permute-done.17.refs_4_ = bf16[4,296,256]{2,1,0:T(8,128)(2,1)} collective-permute-done((bf16[4,296,256]{2,1,0:T(8,128)(2,1)}, bf16[4,296,256]{2,1,0:T(8,128)(2,1)}, u32[]{:S(2)}, u32[]{:S(2)}) %collective-permute-start.17) | collective-permute-done | bytes 606240 | tf_op jit(solution)/shard_map/ppermute | solution.py:392
  238.8 3.0 collective-permute-start.14
  241.8 21.2 %collective-permute-done.19.refs_6_ = bf16[4,296,256]{2,1,0:T(8,128)(2,1)} collective-permute-done((bf16[4,296,256]{2,1,0:T(8,128)(2,1)}, bf16[4,296,256]{2,1,0:T(8,128)(2,1)}, u32[]{:S(2)}, u32[]{:S(2)}) %collective-permute-start.19) | collective-permute-done | bytes 606240 | tf_op jit(solution)/shard_map/ppermute | solution.py:392
  263.0 18.4 %collective-permute-start.16 = (bf16[4,296,256]{2,1,0:T(8,128)(2,1)S(1)}, bf16[4,296,256]{2,1,0:T(8,128)(2,1)S(1)}, u32[]{:S(2)}, u32[]{:S(2)}) collective-permute-start(bf16[4,296,256]{2,1,0:T(8,128)(2,1)S(1)} %take.43), channel_id=1, source_target_pairs={{0,12},{4,8},{8,20},{12,16},{16,28},{20,24},{24,4},{28,0},{1,13},{... | collective-permute-start | bytes 1818632 | tf_op jit(solution)/shard_map/ppermute | solution.py:392
  284.4 9.0 %coeffs_and_gram.3 = (bf16[32,256,256]{2,1,0:T(8,128)(2,1)}, f32[32,16,128]{2,1,0:T(8,128)S(1)}) custom-call(s32[2]{0:T(128)S(1)} %pad_add_fusion.1.place_ref, bf16[2,2,256,168]{3,2,1,0:T(8,128)(2,1)S(1)} %copy.38.time_ref, bf16[128,256]{1,0:T(8,128)(2,1)S(1)} %copy-done.15, f32[1,256]{1,0:T(1,128)S(1)} %bitcast.83, ...), custom_call_target="tpu_custom_call" | custom-call | flops 3556769792 | bytes 9043968 | tf_op jit(solution)/shard_map/coeffs_and_gram/pallas_call | solution.py:142
  293.4 9.2 %coeffs_and_gram.4 = (bf16[32,256,256]{2,1,0:T(8,128)(2,1)}, f32[32,16,128]{2,1,0:T(8,128)S(1)}) custom-call(s32[2]{0:T(128)S(1)} %pad_add_fusion.1.place_ref, bf16[2,2,256,168]{3,2,1,0:T(8,128)(2,1)S(1)} %copy.38.time_ref, bf16[128,256]{1,0:T(8,128)(2,1)S(1)} %copy-done.15, f32[1,256]{1,0:T(1,128)S(1)} %bitcast.84, ...), custom_call_target="tpu_custom_call" | custom-call | flops 3556769792 | bytes 9043968 | tf_op jit(solution)/shard_map/coeffs_and_gram/pallas_call | solution.py:142
  302.6 11.4 %collective-permute-done.20.refs_7_ = bf16[4,296,256]{2,1,0:T(8,128)(2,1)S(1)} collective-permute-done((bf16[4,296,256]{2,1,0:T(8,128)(2,1)S(1)}, bf16[4,296,256]{2,1,0:T(8,128)(2,1)S(1)}, u32[]{:S(2)}, u32[]{:S(2)}) %collective-permute-start.20) | collective-permute-done | bytes 606240 | tf_op jit(solution)/shard_map/ppermute | solution.py:392
  314.1 4.2 collective-permute-done.16.refs_3_
  318.2 8.8 %coeffs_and_gram.5 = (bf16[32,256,256]{2,1,0:T(8,128)(2,1)}, f32[32,16,128]{2,1,0:T(8,128)}) custom-call(s32[2]{0:T(128)S(1)} %pad_add_fusion.1.place_ref, bf16[2,2,256,168]{3,2,1,0:T(8,128)(2,1)S(1)} %copy.38.time_ref, bf16[128,256]{1,0:T(8,128)(2,1)S(1)} %copy-done.15, f32[1,256]{1,0:T(1,128)S(1)} %bitcast.85, ...), custom_call_target="tpu_custom_call" | custom-call | flops 3556769792 | bytes 9043968 | tf_op jit(solution)/shard_map/coeffs_and_gram/pallas_call | solution.py:142
  327.0 4.8 all-to-all-start
  332.5 7.5 %all-to-all-done = f32[32,1,16,128]{3,2,1,0:T(8,128)S(1)} async-done(((f32[32,1,16,128]{3,2,1,0:T(8,128)}), f32[32,1,16,128]{3,2,1,0:T(8,128)S(1)}, u32[]{:S(2)}, u32[]{:S(2)}) %all-to-all-start) | async-done | bytes 262176 | tf_op jit(solution)/shard_map/all_to_all | solution.py:440
  341.0 4.0 subspace.1
  347.8 4.9 all-to-all-start.1
  353.2 6.9 %all-to-all-done.1 = bf16[32,1,18,128]{3,2,1,0:T(8,128)(2,1)S(1)} async-done(((bf16[32,1,18,128]{3,2,1,0:T(8,128)(2,1)}), bf16[32,1,18,128]{3,2,1,0:T(8,128)(2,1)S(1)}, u32[]{:S(2)}, u32[]{:S(2)}) %all-to-all-start.1) | async-done | bytes 147488 | tf_op jit(solution)/shard_map/all_to_all | solution.py:457
  360.7 2.2 mix.8.refs_3_
  364.8 2.2 mix.9.refs_3_
  368.3 2.2 mix.10.refs_3_
  371.8 2.2 mix.11.refs_3_
  374.0 3.1 mix.12.refs_3_
  377.8 2.2 mix.13.refs_3_
  380.1 3.1 mix.14.refs_3_
  383.2 2.2 collective-permute-start.22
  385.3 47.1 %collective-permute-done.27 = bf16[3,4,128,256]{3,2,1,0:T(8,128)(2,1)S(1)} collective-permute-done((bf16[3,4,128,256]{3,2,1,0:T(8,128)(2,1)S(1)}, bf16[3,4,128,256]{3,2,1,0:T(8,128)(2,1)S(1)}, u32[]{:S(2)}, u32[]{:S(2)}) %collective-permute-start.27) | collective-permute-done | bytes 786464 | tf_op jit(solution)/shard_map/ppermute | solution.py:392
  434.4 15.0 %collective-permute-done.26 = bf16[3,4,128,256]{3,2,1,0:T(8,128)(2,1)S(1)} collective-permute-done((bf16[3,4,128,256]{3,2,1,0:T(8,128)(2,1)S(1)}, bf16[3,4,128,256]{3,2,1,0:T(8,128)(2,1)S(1)}, u32[]{:S(2)}, u32[]{:S(2)}) %collective-permute-start.26) | collective-permute-done | bytes 786464 | tf_op jit(solution)/shard_map/ppermute | solution.py:392
  450.2 20.9 %collective-permute-start.21 = (bf16[3,4,128,256]{3,2,1,0:T(8,128)(2,1)S(1)}, bf16[3,4,128,256]{3,2,1,0:T(8,128)(2,1)}, u32[]{:S(2)}, u32[]{:S(2)}) collective-permute-start(bf16[3,4,128,256]{3,2,1,0:T(8,128)(2,1)S(1)} %mix.11.refs_3_), channel_id=1, source_target_pairs={{0,12},{4,8},{8,20},{12,16},{16,28},{20,24},{24,4},{28,0},{1,13},{... | collective-permute-start | bytes 2359304 | tf_op jit(solution)/shard_map/ppermute | solution.py:392
  471.2 2.2 mix.15
  478.7 6.1 %collective-permute-done.25 = bf16[3,4,128,256]{3,2,1,0:T(8,128)(2,1)} collective-permute-done((bf16[3,4,128,256]{3,2,1,0:T(8,128)(2,1)S(1)}, bf16[3,4,128,256]{3,2,1,0:T(8,128)(2,1)}, u32[]{:S(2)}, u32[]{:S(2)}) %collective-permute-start.25) | collective-permute-done | bytes 786464 | tf_op jit(solution)/shard_map/ppermute | solution.py:392
  486.9 2.1 unpack.10.refs_3_
  488.9 11.3 %collective-permute-done.22 = bf16[3,4,128,256]{3,2,1,0:T(8,128)(2,1)} collective-permute-done((bf16[3,4,128,256]{3,2,1,0:T(8,128)(2,1)S(1)}, bf16[3,4,128,256]{3,2,1,0:T(8,128)(2,1)}, u32[]{:S(2)}, u32[]{:S(2)}) %collective-permute-start.22) | collective-permute-done | bytes 786464 | tf_op jit(solution)/shard_map/ppermute | solution.py:392
  501.1 4.1 unpack.11
  (147 shorter events, 75.3 us)
Async XLA Ops:
  1.8 27.5 %collective-permute-start.3 = (bf16[4,296,256]{2,1,0:T(8,128)(2,1)S(1)}, bf16[4,296,256]{2,1,0:T(8,128)(2,1)}, u32[]{:S(2)}, u32[]{:S(2)}) collective-permute-start(bf16[4,296,256]{2,1,0:T(8,128)(2,1)S(1)} %take.28), channel_id=1, source_target_pairs={{0,16},{4,20},{8,24},{12,28},{16,0},{20,4},{24,8},{28,12},{1,17},{... | collective-permute-start | bytes 1818632 | tf_op jit(solution)/shard_map/ppermute | solution.py:392
  3.0 51.9 %collective-permute-start.5 = (bf16[4,296,256]{2,1,0:T(8,128)(2,1)S(1)}, bf16[4,296,256]{2,1,0:T(8,128)(2,1)}, u32[]{:S(2)}, u32[]{:S(2)}) collective-permute-start(bf16[4,296,256]{2,1,0:T(8,128)(2,1)S(1)} %take.30), channel_id=1, source_target_pairs={{0,24},{4,28},{8,0},{12,4},{16,8},{20,12},{24,16},{28,20},{1,25},{... | collective-permute-start | bytes 1818632 | tf_op jit(solution)/shard_map/ppermute | solution.py:392
  7.2 99.7 %collective-permute-start.4 = (bf16[4,296,256]{2,1,0:T(8,128)(2,1)S(1)}, bf16[4,296,256]{2,1,0:T(8,128)(2,1)}, u32[]{:S(2)}, u32[]{:S(2)}) collective-permute-start(bf16[4,296,256]{2,1,0:T(8,128)(2,1)S(1)} %take.29), channel_id=1, source_target_pairs={{0,20},{4,16},{8,28},{12,24},{16,4},{20,0},{24,12},{28,8},{1,21},{... | collective-permute-start | bytes 1818632 | tf_op jit(solution)/shard_map/ppermute | solution.py:392
  10.6 109.3 %collective-permute-start.6 = (bf16[4,296,256]{2,1,0:T(8,128)(2,1)S(1)}, bf16[4,296,256]{2,1,0:T(8,128)(2,1)}, u32[]{:S(2)}, u32[]{:S(2)}) collective-permute-start(bf16[4,296,256]{2,1,0:T(8,128)(2,1)S(1)} %take.31), channel_id=1, source_target_pairs={{0,28},{4,24},{8,4},{12,0},{16,12},{20,8},{24,20},{28,16},{1,29},{... | collective-permute-start | bytes 1818632 | tf_op jit(solution)/shard_map/ppermute | solution.py:392
  11.8 112.0 %collective-permute-start.1 = (bf16[4,296,256]{2,1,0:T(8,128)(2,1)S(1)}, bf16[4,296,256]{2,1,0:T(8,128)(2,1)}, u32[]{:S(2)}, u32[]{:S(2)}) collective-permute-start(bf16[4,296,256]{2,1,0:T(8,128)(2,1)S(1)} %take.26), channel_id=1, source_target_pairs={{0,8},{4,12},{8,16},{12,20},{16,24},{20,28},{24,0},{28,4},{1,9},{5... | collective-permute-start | bytes 1818632 | tf_op jit(solution)/shard_map/ppermute | solution.py:392
  22.9 0.8 copy-start.14
  29.3 94.4 %collective-permute-start = (bf16[4,296,256]{2,1,0:T(8,128)(2,1)}, bf16[4,296,256]{2,1,0:T(8,128)(2,1)S(1)}, u32[]{:S(2)}, u32[]{:S(2)}) collective-permute-start(bf16[4,296,256]{2,1,0:T(8,128)(2,1)} %copy-done.14), channel_id=1, source_target_pairs={{0,4},{4,0},{8,12},{12,8},{16,20},{20,16},{24,28},{28,24},{1,5},{5... | collective-permute-start | bytes 1818632 | tf_op jit(solution)/shard_map/ppermute | solution.py:392
  54.9 97.7 %collective-permute-start.2 = (bf16[4,296,256]{2,1,0:T(8,128)(2,1)}, bf16[4,296,256]{2,1,0:T(8,128)(2,1)}, u32[]{:S(2)}, u32[]{:S(2)}) collective-permute-start(bf16[4,296,256]{2,1,0:T(8,128)(2,1)} %take.27), channel_id=1, source_target_pairs={{0,12},{4,8},{8,20},{12,16},{16,28},{20,24},{24,4},{28,0},{1,13},{... | collective-permute-start | bytes 1818632 | tf_op jit(solution)/shard_map/ppermute | solution.py:392
  106.9 46.9 %collective-permute-start.10 = (bf16[4,296,256]{2,1,0:T(8,128)(2,1)}, bf16[4,296,256]{2,1,0:T(8,128)(2,1)}, u32[]{:S(2)}, u32[]{:S(2)}) collective-permute-start(bf16[4,296,256]{2,1,0:T(8,128)(2,1)} %take.36), channel_id=1, source_target_pairs={{0,16},{4,20},{8,24},{12,28},{16,0},{20,4},{24,8},{28,12},{1,17},{... | collective-permute-start | bytes 1818632 | tf_op jit(solution)/shard_map/ppermute | solution.py:392
  119.9 39.1 %collective-permute-start.12 = (bf16[4,296,256]{2,1,0:T(8,128)(2,1)}, bf16[4,296,256]{2,1,0:T(8,128)(2,1)}, u32[]{:S(2)}, u32[]{:S(2)}) collective-permute-start(bf16[4,296,256]{2,1,0:T(8,128)(2,1)} %take.38), channel_id=1, source_target_pairs={{0,24},{4,28},{8,0},{12,4},{16,8},{20,12},{24,16},{28,20},{1,25},{... | collective-permute-start | bytes 1818632 | tf_op jit(solution)/shard_map/ppermute | solution.py:392
  123.8 87.2 %collective-permute-start.11 = (bf16[4,296,256]{2,1,0:T(8,128)(2,1)}, bf16[4,296,256]{2,1,0:T(8,128)(2,1)}, u32[]{:S(2)}, u32[]{:S(2)}) collective-permute-start(bf16[4,296,256]{2,1,0:T(8,128)(2,1)} %take.37), channel_id=1, source_target_pairs={{0,20},{4,16},{8,28},{12,24},{16,4},{20,0},{24,12},{28,8},{1,21},{... | collective-permute-start | bytes 1818632 | tf_op jit(solution)/shard_map/ppermute | solution.py:392
  123.8 0.9 copy-start.17
  124.6 99.3 %collective-permute-start.13 = (bf16[4,296,256]{2,1,0:T(8,128)(2,1)}, bf16[4,296,256]{2,1,0:T(8,128)(2,1)}, u32[]{:S(2)}, u32[]{:S(2)}) collective-permute-start(bf16[4,296,256]{2,1,0:T(8,128)(2,1)} %take.39), channel_id=1, source_target_pairs={{0,28},{4,24},{8,4},{12,0},{16,12},{20,8},{24,20},{28,16},{1,29},{... | collective-permute-start | bytes 1818632 | tf_op jit(solution)/shard_map/ppermute | solution.py:392
  128.2 0.9 copy-start.12
  132.2 0.8 copy-start.7
  134.2 0.9 copy-start.5
  136.2 0.8 copy-start.10
  138.2 0.8 copy-start.9
  145.5 6.8 %copy-start.20 = (s32[16]{0:T(128)S(1)}, s32[16]{0:T(128)}, u32[]{:S(2)}) copy-start(s32[16]{0:T(128)} %param.6) | copy-start | bytes 196
  152.6 77.9 %collective-permute-start.8 = (bf16[4,296,256]{2,1,0:T(8,128)(2,1)}, bf16[4,296,256]{2,1,0:T(8,128)(2,1)}, u32[]{:S(2)}, u32[]{:S(2)}) collective-permute-start(bf16[4,296,256]{2,1,0:T(8,128)(2,1)} %copy-done.13), channel_id=1, source_target_pairs={{0,8},{4,12},{8,16},{12,20},{16,24},{20,28},{24,0},{28,4},{1,9},{5... | collective-permute-start | bytes 1818632 | tf_op jit(solution)/shard_map/ppermute | solution.py:392
  153.8 76.8 %collective-permute-start.7 = (bf16[4,296,256]{2,1,0:T(8,128)(2,1)}, bf16[4,296,256]{2,1,0:T(8,128)(2,1)}, u32[]{:S(2)}, u32[]{:S(2)}) collective-permute-start(bf16[4,296,256]{2,1,0:T(8,128)(2,1)} %copy-done.12), channel_id=1, source_target_pairs={{0,4},{4,0},{8,12},{12,8},{16,20},{20,16},{24,28},{28,24},{1,5},{5... | collective-permute-start | bytes 1818632 | tf_op jit(solution)/shard_map/ppermute | solution.py:392
  159.0 72.2 %collective-permute-start.9 = (bf16[4,296,256]{2,1,0:T(8,128)(2,1)}, bf16[4,296,256]{2,1,0:T(8,128)(2,1)}, u32[]{:S(2)}, u32[]{:S(2)}) collective-permute-start(bf16[4,296,256]{2,1,0:T(8,128)(2,1)} %copy-done.11), channel_id=1, source_target_pairs={{0,12},{4,8},{8,20},{12,16},{16,28},{20,24},{24,4},{28,0},{1,13},{... | collective-permute-start | bytes 1818632 | tf_op jit(solution)/shard_map/ppermute | solution.py:392
  211.0 27.8 %collective-permute-start.17 = (bf16[4,296,256]{2,1,0:T(8,128)(2,1)}, bf16[4,296,256]{2,1,0:T(8,128)(2,1)}, u32[]{:S(2)}, u32[]{:S(2)}) collective-permute-start(bf16[4,296,256]{2,1,0:T(8,128)(2,1)} %copy-done.10), channel_id=1, source_target_pairs={{0,16},{4,20},{8,24},{12,28},{16,0},{20,4},{24,8},{28,12},{1,17},{... | collective-permute-start | bytes 1818632 | tf_op jit(solution)/shard_map/ppermute | solution.py:392
  224.0 39.0 %collective-permute-start.19 = (bf16[4,296,256]{2,1,0:T(8,128)(2,1)}, bf16[4,296,256]{2,1,0:T(8,128)(2,1)}, u32[]{:S(2)}, u32[]{:S(2)}) collective-permute-start(bf16[4,296,256]{2,1,0:T(8,128)(2,1)} %copy-done.9), channel_id=1, source_target_pairs={{0,24},{4,28},{8,0},{12,4},{16,8},{20,12},{24,16},{28,20},{1,25},{... | collective-permute-start | bytes 1818632 | tf_op jit(solution)/shard_map/ppermute | solution.py:392
  230.5 87.8 %copy-start.16 = (f32[256]{0:T(256)}, f32[256]{0:T(256)S(1)}, u32[]{:S(2)}) copy-start(f32[256]{0:T(256)S(1)} %select_reduce_fusion) | copy-start | bytes 3076
  230.5 72.1 %collective-permute-start.18 = (bf16[4,296,256]{2,1,0:T(8,128)(2,1)}, bf16[4,296,256]{2,1,0:T(8,128)(2,1)S(1)}, u32[]{:S(2)}, u32[]{:S(2)}) collective-permute-start(bf16[4,296,256]{2,1,0:T(8,128)(2,1)} %copy-done.4), channel_id=1, source_target_pairs={{0,20},{4,16},{8,28},{12,24},{16,4},{20,0},{24,12},{28,8},{1,21},{... | collective-permute-start | bytes 1818632 | tf_op jit(solution)/shard_map/ppermute | solution.py:392
  230.6 83.5 %collective-permute-start.20 = (bf16[4,296,256]{2,1,0:T(8,128)(2,1)S(1)}, bf16[4,296,256]{2,1,0:T(8,128)(2,1)S(1)}, u32[]{:S(2)}, u32[]{:S(2)}) collective-permute-start(bf16[4,296,256]{2,1,0:T(8,128)(2,1)S(1)} %take.47), channel_id=1, source_target_pairs={{0,28},{4,24},{8,4},{12,0},{16,12},{20,8},{24,20},{28,16},{1,29},{... | collective-permute-start | bytes 1818632 | tf_op jit(solution)/shard_map/ppermute | solution.py:392
  231.2 82.9 %collective-permute-start.15 = (bf16[4,296,256]{2,1,0:T(8,128)(2,1)S(1)}, bf16[4,296,256]{2,1,0:T(8,128)(2,1)S(1)}, u32[]{:S(2)}, u32[]{:S(2)}) collective-permute-start(bf16[4,296,256]{2,1,0:T(8,128)(2,1)S(1)} %take.42), channel_id=1, source_target_pairs={{0,8},{4,12},{8,16},{12,20},{16,24},{20,28},{24,0},{28,4},{1,9},{5... | collective-permute-start | bytes 1818632 | tf_op jit(solution)/shard_map/ppermute | solution.py:392
  238.8 75.3 %collective-permute-start.14 = (bf16[4,296,256]{2,1,0:T(8,128)(2,1)S(1)}, bf16[4,296,256]{2,1,0:T(8,128)(2,1)S(1)}, u32[]{:S(2)}, u32[]{:S(2)}) collective-permute-start(bf16[4,296,256]{2,1,0:T(8,128)(2,1)S(1)} %take.41), channel_id=1, source_target_pairs={{0,4},{4,0},{8,12},{12,8},{16,20},{20,16},{24,28},{28,24},{1,5},{5... | collective-permute-start | bytes 1818632 | tf_op jit(solution)/shard_map/ppermute | solution.py:392
  263.0 55.3 %collective-permute-start.16 = (bf16[4,296,256]{2,1,0:T(8,128)(2,1)S(1)}, bf16[4,296,256]{2,1,0:T(8,128)(2,1)S(1)}, u32[]{:S(2)}, u32[]{:S(2)}) collective-permute-start(bf16[4,296,256]{2,1,0:T(8,128)(2,1)S(1)} %take.43), channel_id=1, source_target_pairs={{0,12},{4,8},{8,20},{12,16},{16,28},{20,24},{24,4},{28,0},{1,13},{... | collective-permute-start | bytes 1818632 | tf_op jit(solution)/shard_map/ppermute | solution.py:392
  281.4 1.1 copy-start.8
  282.5 0.8 copy-start.15
  283.3 1.1 copy-start.18
  284.4 9.0 %copy-start.6 = (bf16[4,296,256]{2,1,0:T(8,128)(2,1)S(1)}, bf16[4,296,256]{2,1,0:T(8,128)(2,1)}, u32[]{:S(2)}) copy-start(bf16[4,296,256]{2,1,0:T(8,128)(2,1)} %copy-done.5) | copy-start | bytes 1818628
  318.2 34.6 %copy-start.19 = (bf16[2,2,2]{2,1,0:T(2,128)(2,1)S(1)}, bf16[2,2,2]{2,1,0:T(2,128)(2,1)}, u32[]{:S(2)}) copy-start(bf16[2,2,2]{2,1,0:T(2,128)(2,1)} %constant.267.clone) | copy-start | bytes 52
  327.0 13.1 %all-to-all-start = ((f32[32,1,16,128]{3,2,1,0:T(8,128)}), f32[32,1,16,128]{3,2,1,0:T(8,128)S(1)}, u32[]{:S(2)}, u32[]{:S(2)}) async-start(f32[32,1,16,128]{3,2,1,0:T(8,128)} %bitcast.25), calls=%async_computation | async-start | bytes 524288 | tf_op jit(solution)/shard_map/all_to_all | solution.py:440
  347.8 12.3 %all-to-all-start.1 = ((bf16[32,1,18,128]{3,2,1,0:T(8,128)(2,1)}), bf16[32,1,18,128]{3,2,1,0:T(8,128)(2,1)S(1)}, u32[]{:S(2)}, u32[]{:S(2)}) async-start(bf16[32,1,18,128]{3,2,1,0:T(8,128)(2,1)} %broadcast_in_dim.27), calls=%async_computation.1 | async-start | bytes 393216 | tf_op jit(solution)/shard_map/all_to_all | solution.py:457
  362.9 69.5 %collective-permute-start.27 = (bf16[3,4,128,256]{3,2,1,0:T(8,128)(2,1)S(1)}, bf16[3,4,128,256]{3,2,1,0:T(8,128)(2,1)S(1)}, u32[]{:S(2)}, u32[]{:S(2)}) collective-permute-start(bf16[3,4,128,256]{3,2,1,0:T(8,128)(2,1)S(1)} %mix.8.refs_3_), channel_id=1, source_target_pairs={{0,16},{4,20},{8,24},{12,28},{16,0},{20,4},{24,8},{28,12},{1,17},{... | collective-permute-start | bytes 2359304 | tf_op jit(solution)/shard_map/ppermute | solution.py:392
  367.0 82.3 %collective-permute-start.26 = (bf16[3,4,128,256]{3,2,1,0:T(8,128)(2,1)S(1)}, bf16[3,4,128,256]{3,2,1,0:T(8,128)(2,1)S(1)}, u32[]{:S(2)}, u32[]{:S(2)}) collective-permute-start(bf16[3,4,128,256]{3,2,1,0:T(8,128)(2,1)S(1)} %mix.9.refs_3_), channel_id=1, source_target_pairs={{0,20},{4,16},{8,28},{12,24},{16,4},{20,0},{24,12},{28,8},{1,21},{... | collective-permute-start | bytes 2359304 | tf_op jit(solution)/shard_map/ppermute | solution.py:392
  370.5 114.3 %collective-permute-start.25 = (bf16[3,4,128,256]{3,2,1,0:T(8,128)(2,1)S(1)}, bf16[3,4,128,256]{3,2,1,0:T(8,128)(2,1)}, u32[]{:S(2)}, u32[]{:S(2)}) collective-permute-start(bf16[3,4,128,256]{3,2,1,0:T(8,128)(2,1)S(1)} %mix.10.refs_3_), channel_id=1, source_target_pairs={{0,8},{4,12},{8,16},{12,20},{16,24},{20,28},{24,0},{28,4},{1,9},{5... | collective-permute-start | bytes 2359304 | tf_op jit(solution)/shard_map/ppermute | solution.py:392
  377.1 109.8 %collective-permute-start.24 = (bf16[3,4,128,256]{3,2,1,0:T(8,128)(2,1)}, bf16[3,4,128,256]{3,2,1,0:T(8,128)(2,1)}, u32[]{:S(2)}, u32[]{:S(2)}) collective-permute-start(bf16[3,4,128,256]{3,2,1,0:T(8,128)(2,1)} %mix.12.refs_3_), channel_id=1, source_target_pairs={{0,24},{4,28},{8,0},{12,4},{16,8},{20,12},{24,16},{28,20},{1,25},{... | collective-permute-start | bytes 2359304 | tf_op jit(solution)/shard_map/ppermute | solution.py:392
  383.2 117.1 %collective-permute-start.22 = (bf16[3,4,128,256]{3,2,1,0:T(8,128)(2,1)S(1)}, bf16[3,4,128,256]{3,2,1,0:T(8,128)(2,1)}, u32[]{:S(2)}, u32[]{:S(2)}) collective-permute-start(bf16[3,4,128,256]{3,2,1,0:T(8,128)(2,1)S(1)} %mix.13.refs_3_), channel_id=1, source_target_pairs={{0,28},{4,24},{8,4},{12,0},{16,12},{20,8},{24,20},{28,16},{1,29},{... | collective-permute-start | bytes 2359304 | tf_op jit(solution)/shard_map/ppermute | solution.py:392
  432.4 0.9 copy-start
  433.3 55.6 %collective-permute-start.23 = (bf16[3,4,128,256]{3,2,1,0:T(8,128)(2,1)}, bf16[3,4,128,256]{3,2,1,0:T(8,128)(2,1)}, u32[]{:S(2)}, u32[]{:S(2)}) collective-permute-start(bf16[3,4,128,256]{3,2,1,0:T(8,128)(2,1)} %mix.14.refs_3_), channel_id=1, source_target_pairs={{0,4},{4,0},{8,12},{12,8},{16,20},{20,16},{24,28},{28,24},{1,5},{5... | collective-permute-start | bytes 2359304 | tf_op jit(solution)/shard_map/ppermute | solution.py:392
  449.3 0.9 copy-start.2
  450.2 50.9 %collective-permute-start.21 = (bf16[3,4,128,256]{3,2,1,0:T(8,128)(2,1)S(1)}, bf16[3,4,128,256]{3,2,1,0:T(8,128)(2,1)}, u32[]{:S(2)}, u32[]{:S(2)}) collective-permute-start(bf16[3,4,128,256]{3,2,1,0:T(8,128)(2,1)S(1)} %mix.11.refs_3_), channel_id=1, source_target_pairs={{0,12},{4,8},{8,20},{12,16},{16,28},{20,24},{24,4},{28,0},{1,13},{... | collective-permute-start | bytes 2359304 | tf_op jit(solution)/shard_map/ppermute | solution.py:392
  475.2 1.1 copy-start.1
  476.3 1.4 copy-start.3
  (3 other events, 2.5 us)

commit v13 on v12

--- a/solution.py
+++ b/solution.py
@@ -480,7 +480,7 @@
         )
         before = (piece,)
         sent[z, x] = owner_after(-z, -x), send(piece, z, x)
-    late = [r for r in in_order if r[0] in (0, 1) and r[1] > 0 or r == in_order[-tm_count]]
+    late = [r for r in in_order if r[0] == 0 or r == in_order[-tm_count]]
     groups = [[(0, 0)]] + [[r] for r in in_order if r not in late] + [late]
     mode_fields = None
     for group in groups:

time: 509 us -> 511 us (level)
  waiting for transfers between devices: 246 us -> 290 us
  starting transfers between devices: 132 us -> 90.4 us
    ppermute x28, waiting for transfers between devices: 232 us -> 276 us  [send(): return lax.ppermute(piece, owner_axes, hops)]
    ppermute x28, starting transfers between devices: 122 us -> 78.6 us  [send(): return lax.ppermute(piece, owner_axes, hops)]
    pallas_call x6 -> x7, Pallas kernels: 11 us -> 12.2 us  [unpack(): pl.pallas_call(functools.partial(unpack_kernel, count), grid_spec=pltpu.P...]
  transfers between devices with their start and end apart: 30 -> 30, of which waited for: 18 -> 16; matrix products, arithmetic and copies ran while one was open for 3% -> 3% of each run, Pallas kernels for 14% -> 15%
where the time goes in v13:
time: 511 us; the launch traced here: 509 us
  waiting for transfers between devices  290 us (57%)
  Pallas kernels  93.9 us (18%)
  starting transfers between devices  90.4 us (18%)
  local copies, waits for them, and re-layouts  27.1 us (5%)
  other arithmetic  5.52 us (1%)
    ppermute x28, waiting for transfers between devices, send(): return lax.ppermute(piece, owner_axes, hops)  276 us
    ppermute x28, starting transfers between devices, send(): return lax.ppermute(piece, owner_axes, hops)  78.6 us
    pallas_call x24, Pallas kernels, take(): pl.pallas_call(take_kernel, grid_spec=pltpu.PrefetchScalarGridSpec(num_sc...  31.3 us
    pallas_call x3, Pallas kernels, coeffs_and_gram(): pl.pallas_call(functools.partial(coeff_kernel, sec_count, sec_local, freq...  27 us
    pallas_call x8, Pallas kernels, mix(): pl.pallas_call(functools.partial(mix_kernel, orders, fields), grid_spec=p...  19.4 us
    unnamed x44, local copies, waits for them, and re-layouts  15.5 us
    pallas_call x7, Pallas kernels, unpack(): pl.pallas_call(functools.partial(unpack_kernel, count), grid_spec=pltpu.P...  12.2 us
  transfers between devices with their start and end apart: 30, of which 16 were waited for; matrix products, arithmetic and copies ran while one was open for 3% of the time, Pallas kernels for 15%

profile of v13, /device:TPU:16, one launch (start us, length us, event | category | flops | bytes accessed | tf_op | source)
XLA Modules:
  0.0 508.5 jit_solution(6703413022521944457)
XLA Ops:
  6.1 2.6 collective-permute-start.2
  12.0 2.9 collective-permute-start.5
  15.1 2.0 take.36
  17.1 2.0 take.34
  19.0 2.0 take.37
  21.0 1.9 take.35
  27.1 4.4 collective-permute-done.1.refs_2_
  33.0 2.9 multiply_bitcast_fusion
  35.9 32.2 %collective-permute-done.3.refs_4_ = bf16[4,296,256]{2,1,0:T(8,128)(2,1)} collective-permute-done((bf16[4,296,256]{2,1,0:T(8,128)(2,1)S(1)}, bf16[4,296,256]{2,1,0:T(8,128)(2,1)}, u32[]{:S(2)}, u32[]{:S(2)}) %collective-permute-start.3) | collective-permute-done | bytes 606240 | tf_op jit(solution)/shard_map/ppermute | solution.py:392
  68.2 2.7 collective-permute-start.6
  70.9 26.9 %collective-permute-done.2.refs_3_ = bf16[4,296,256]{2,1,0:T(8,128)(2,1)} collective-permute-done((bf16[4,296,256]{2,1,0:T(8,128)(2,1)S(1)}, bf16[4,296,256]{2,1,0:T(8,128)(2,1)}, u32[]{:S(2)}, u32[]{:S(2)}) %collective-permute-start.2) | collective-permute-done | bytes 606240 | tf_op jit(solution)/shard_map/ppermute | solution.py:392
  97.8 27.4 %collective-permute-start.8 = (bf16[4,296,256]{2,1,0:T(8,128)(2,1)}, bf16[4,296,256]{2,1,0:T(8,128)(2,1)}, u32[]{:S(2)}, u32[]{:S(2)}) collective-permute-start(bf16[4,296,256]{2,1,0:T(8,128)(2,1)} %take.34), channel_id=1, source_target_pairs={{0,8},{4,12},{8,16},{12,20},{16,24},{20,28},{24,0},{28,4},{1,9},{5... | collective-permute-start | bytes 1818632 | tf_op jit(solution)/shard_map/ppermute | solution.py:392
  147.7 5.7 %reshape.480.azimuth_ref = bf16[128,256]{1,0:T(8,128)(2,1)} reshape(bf16[2,8,2,4,16,2,2,4]{7,6,5,4,3,2,1,0:T(2,128)(2,1)} %multiply_bitcast_fusion) | data formatting | bytes 131072 | tf_op jit(solution)/shard_map/reshape | solution.py:407
  155.3 17.0 %collective-permute-done.10.refs_4_ = bf16[4,296,256]{2,1,0:T(8,128)(2,1)} collective-permute-done((bf16[4,296,256]{2,1,0:T(8,128)(2,1)}, bf16[4,296,256]{2,1,0:T(8,128)(2,1)}, u32[]{:S(2)}, u32[]{:S(2)}) %collective-permute-start.10) | collective-permute-done | bytes 606240 | tf_op jit(solution)/shard_map/ppermute | solution.py:392
  173.8 11.5 %collective-permute-done.11.refs_5_ = bf16[4,296,256]{2,1,0:T(8,128)(2,1)} collective-permute-done((bf16[4,296,256]{2,1,0:T(8,128)(2,1)}, bf16[4,296,256]{2,1,0:T(8,128)(2,1)}, u32[]{:S(2)}, u32[]{:S(2)}) %collective-permute-start.11) | collective-permute-done | bytes 606240 | tf_op jit(solution)/shard_map/ppermute | solution.py:392
  185.3 17.9 %collective-permute-start.15 = (bf16[4,296,256]{2,1,0:T(8,128)(2,1)}, bf16[4,296,256]{2,1,0:T(8,128)(2,1)}, u32[]{:S(2)}, u32[]{:S(2)}) collective-permute-start(bf16[4,296,256]{2,1,0:T(8,128)(2,1)} %copy-done.10), channel_id=1, source_target_pairs={{0,8},{4,12},{8,16},{12,20},{16,24},{20,28},{24,0},{28,4},{1,9},{5... | collective-permute-start | bytes 1818632 | tf_op jit(solution)/shard_map/ppermute | solution.py:392
  203.2 11.6 %collective-permute-done.9.refs_3_ = bf16[4,296,256]{2,1,0:T(8,128)(2,1)} collective-permute-done((bf16[4,296,256]{2,1,0:T(8,128)(2,1)}, bf16[4,296,256]{2,1,0:T(8,128)(2,1)}, u32[]{:S(2)}, u32[]{:S(2)}) %collective-permute-start.9) | collective-permute-done | bytes 606240 | tf_op jit(solution)/shard_map/ppermute | solution.py:392
  220.2 43.7 %collective-permute-done.13.refs_7_ = bf16[4,296,256]{2,1,0:T(8,128)(2,1)} collective-permute-done((bf16[4,296,256]{2,1,0:T(8,128)(2,1)}, bf16[4,296,256]{2,1,0:T(8,128)(2,1)}, u32[]{:S(2)}, u32[]{:S(2)}) %collective-permute-start.13) | collective-permute-done | bytes 606240 | tf_op jit(solution)/shard_map/ppermute | solution.py:392
  264.0 3.0 collective-permute-start.19
  267.9 9.1 %collective-permute-done.17.refs_4_ = bf16[4,296,256]{2,1,0:T(8,128)(2,1)} collective-permute-done((bf16[4,296,256]{2,1,0:T(8,128)(2,1)}, bf16[4,296,256]{2,1,0:T(8,128)(2,1)}, u32[]{:S(2)}, u32[]{:S(2)}) %collective-permute-start.17) | collective-permute-done | bytes 606240 | tf_op jit(solution)/shard_map/ppermute | solution.py:392
  277.0 2.3 collective-permute-start.20
  282.3 9.0 %coeffs_and_gram.3 = (bf16[32,256,256]{2,1,0:T(8,128)(2,1)}, f32[32,16,128]{2,1,0:T(8,128)S(1)}) custom-call(s32[2]{0:T(128)S(1)} %pad_add_fusion.1.place_ref, bf16[2,2,256,168]{3,2,1,0:T(8,128)(2,1)S(1)} %copy.39.time_ref, bf16[128,256]{1,0:T(8,128)(2,1)S(1)} %copy-done.15, f32[1,256]{1,0:T(1,128)S(1)} %bitcast.83, ...), custom_call_target="tpu_custom_call" | custom-call | flops 3556769792 | bytes 9043968 | tf_op jit(solution)/shard_map/coeffs_and_gram/pallas_call | solution.py:142
  291.4 9.2 %coeffs_and_gram.4 = (bf16[32,256,256]{2,1,0:T(8,128)(2,1)}, f32[32,16,128]{2,1,0:T(8,128)S(1)}) custom-call(s32[2]{0:T(128)S(1)} %pad_add_fusion.1.place_ref, bf16[2,2,256,168]{3,2,1,0:T(8,128)(2,1)S(1)} %copy.39.time_ref, bf16[128,256]{1,0:T(8,128)(2,1)S(1)} %copy-done.15, f32[1,256]{1,0:T(1,128)S(1)} %bitcast.84, ...), custom_call_target="tpu_custom_call" | custom-call | flops 3556769792 | bytes 9043968 | tf_op jit(solution)/shard_map/coeffs_and_gram/pallas_call | solution.py:142
  300.6 5.2 %collective-permute-done.16.refs_3_ = bf16[4,296,256]{2,1,0:T(8,128)(2,1)S(1)} collective-permute-done((bf16[4,296,256]{2,1,0:T(8,128)(2,1)}, bf16[4,296,256]{2,1,0:T(8,128)(2,1)S(1)}, u32[]{:S(2)}, u32[]{:S(2)}) %collective-permute-start.16) | collective-permute-done | bytes 606240 | tf_op jit(solution)/shard_map/ppermute | solution.py:392
  305.8 2.3 collective-permute-done.14.refs_1_
  308.1 7.6 %collective-permute-done.20.refs_7_ = bf16[4,296,256]{2,1,0:T(8,128)(2,1)S(1)} collective-permute-done((bf16[4,296,256]{2,1,0:T(8,128)(2,1)S(1)}, bf16[4,296,256]{2,1,0:T(8,128)(2,1)S(1)}, u32[]{:S(2)}, u32[]{:S(2)}) %collective-permute-start.20) | collective-permute-done | bytes 606240 | tf_op jit(solution)/shard_map/ppermute | solution.py:392
  315.8 8.8 %coeffs_and_gram.5 = (bf16[32,256,256]{2,1,0:T(8,128)(2,1)}, f32[32,16,128]{2,1,0:T(8,128)}) custom-call(s32[2]{0:T(128)S(1)} %pad_add_fusion.1.place_ref, bf16[2,2,256,168]{3,2,1,0:T(8,128)(2,1)S(1)} %copy.39.time_ref, bf16[128,256]{1,0:T(8,128)(2,1)S(1)} %copy-done.15, f32[1,256]{1,0:T(1,128)S(1)} %bitcast.85, ...), custom_call_target="tpu_custom_call" | custom-call | flops 3556769792 | bytes 9043968 | tf_op jit(solution)/shard_map/coeffs_and_gram/pallas_call | solution.py:142
  324.6 6.9 %all-to-all-start = ((f32[32,1,16,128]{3,2,1,0:T(8,128)}), f32[32,1,16,128]{3,2,1,0:T(8,128)S(1)}, u32[]{:S(2)}, u32[]{:S(2)}) async-start(f32[32,1,16,128]{3,2,1,0:T(8,128)} %bitcast.24), calls=%async_computation | async-start | bytes 524288 | tf_op jit(solution)/shard_map/all_to_all | solution.py:440
  332.1 7.5 %all-to-all-done = f32[32,1,16,128]{3,2,1,0:T(8,128)S(1)} async-done(((f32[32,1,16,128]{3,2,1,0:T(8,128)}), f32[32,1,16,128]{3,2,1,0:T(8,128)S(1)}, u32[]{:S(2)}, u32[]{:S(2)}) %all-to-all-start) | async-done | bytes 262176 | tf_op jit(solution)/shard_map/all_to_all | solution.py:440
  340.6 4.0 subspace.1
  347.4 4.9 all-to-all-start.1
  352.8 6.9 %all-to-all-done.1 = bf16[32,1,18,128]{3,2,1,0:T(8,128)(2,1)S(1)} async-done(((bf16[32,1,18,128]{3,2,1,0:T(8,128)(2,1)}), bf16[32,1,18,128]{3,2,1,0:T(8,128)(2,1)S(1)}, u32[]{:S(2)}, u32[]{:S(2)}) %all-to-all-start.1) | async-done | bytes 147488 | tf_op jit(solution)/shard_map/all_to_all | solution.py:457
  360.3 2.2 mix.8.refs_3_
  364.4 2.2 mix.9.refs_3_
  367.9 3.1 mix.10.refs_3_
  372.2 3.1 mix.11.refs_3_
  375.3 2.8 collective-permute-start.24
  378.2 2.2 mix.12.refs_3_
  380.4 2.2 mix.13.refs_3_
  382.6 2.2 mix.14.refs_3_
  384.9 64.0 %collective-permute-done.27 = bf16[3,4,128,256]{3,2,1,0:T(8,128)(2,1)S(1)} collective-permute-done((bf16[3,4,128,256]{3,2,1,0:T(8,128)(2,1)S(1)}, bf16[3,4,128,256]{3,2,1,0:T(8,128)(2,1)S(1)}, u32[]{:S(2)}, u32[]{:S(2)}) %collective-permute-start.27) | collective-permute-done | bytes 786464 | tf_op jit(solution)/shard_map/ppermute | solution.py:392
  450.8 14.9 %collective-permute-done.26 = bf16[3,4,128,256]{3,2,1,0:T(8,128)(2,1)S(1)} collective-permute-done((bf16[3,4,128,256]{3,2,1,0:T(8,128)(2,1)S(1)}, bf16[3,4,128,256]{3,2,1,0:T(8,128)(2,1)S(1)}, u32[]{:S(2)}, u32[]{:S(2)}) %collective-permute-start.26) | collective-permute-done | bytes 786464 | tf_op jit(solution)/shard_map/ppermute | solution.py:392
  466.7 2.2 mix.15
  474.2 2.1 unpack.10.refs_1_
  476.3 25.0 %collective-permute-done.24 = bf16[3,4,128,256]{3,2,1,0:T(8,128)(2,1)} collective-permute-done((bf16[3,4,128,256]{3,2,1,0:T(8,128)(2,1)}, bf16[3,4,128,256]{3,2,1,0:T(8,128)(2,1)}, u32[]{:S(2)}, u32[]{:S(2)}) %collective-permute-start.24) | collective-permute-done | bytes 786464 | tf_op jit(solution)/shard_map/ppermute | solution.py:392
  501.3 2.1 unpack.11.refs_1_
  503.3 2.1 unpack.12.refs_2_
  505.4 3.1 unpack.13
  (148 shorter events, 67.7 us)
Async XLA Ops:
  1.8 29.7 %collective-permute-start.1 = (bf16[4,296,256]{2,1,0:T(8,128)(2,1)S(1)}, bf16[4,296,256]{2,1,0:T(8,128)(2,1)}, u32[]{:S(2)}, u32[]{:S(2)}) collective-permute-start(bf16[4,296,256]{2,1,0:T(8,128)(2,1)S(1)} %take.26), channel_id=1, source_target_pairs={{0,8},{4,12},{8,16},{12,20},{16,24},{20,28},{24,0},{28,4},{1,9},{5... | collective-permute-start | bytes 1818632 | tf_op jit(solution)/shard_map/ppermute | solution.py:392
  4.6 63.6 %collective-permute-start.3 = (bf16[4,296,256]{2,1,0:T(8,128)(2,1)S(1)}, bf16[4,296,256]{2,1,0:T(8,128)(2,1)}, u32[]{:S(2)}, u32[]{:S(2)}) collective-permute-start(bf16[4,296,256]{2,1,0:T(8,128)(2,1)S(1)} %take.28), channel_id=1, source_target_pairs={{0,16},{4,20},{8,24},{12,28},{16,0},{20,4},{24,8},{28,12},{1,17},{... | collective-permute-start | bytes 1818632 | tf_op jit(solution)/shard_map/ppermute | solution.py:392
  6.1 91.7 %collective-permute-start.2 = (bf16[4,296,256]{2,1,0:T(8,128)(2,1)S(1)}, bf16[4,296,256]{2,1,0:T(8,128)(2,1)}, u32[]{:S(2)}, u32[]{:S(2)}) collective-permute-start(bf16[4,296,256]{2,1,0:T(8,128)(2,1)S(1)} %take.27), channel_id=1, source_target_pairs={{0,12},{4,8},{8,20},{12,16},{16,28},{20,24},{24,4},{28,0},{1,13},{... | collective-permute-start | bytes 1818632 | tf_op jit(solution)/shard_map/ppermute | solution.py:392
  9.8 88.0 %collective-permute-start.4 = (bf16[4,296,256]{2,1,0:T(8,128)(2,1)S(1)}, bf16[4,296,256]{2,1,0:T(8,128)(2,1)}, u32[]{:S(2)}, u32[]{:S(2)}) collective-permute-start(bf16[4,296,256]{2,1,0:T(8,128)(2,1)S(1)} %take.29), channel_id=1, source_target_pairs={{0,20},{4,16},{8,28},{12,24},{16,4},{20,0},{24,12},{28,8},{1,21},{... | collective-permute-start | bytes 1818632 | tf_op jit(solution)/shard_map/ppermute | solution.py:392
  12.0 113.2 %collective-permute-start.5 = (bf16[4,296,256]{2,1,0:T(8,128)(2,1)S(1)}, bf16[4,296,256]{2,1,0:T(8,128)(2,1)}, u32[]{:S(2)}, u32[]{:S(2)}) collective-permute-start(bf16[4,296,256]{2,1,0:T(8,128)(2,1)S(1)} %take.30), channel_id=1, source_target_pairs={{0,24},{4,28},{8,0},{12,4},{16,8},{20,12},{24,16},{28,20},{1,25},{... | collective-permute-start | bytes 1818632 | tf_op jit(solution)/shard_map/ppermute | solution.py:392
  24.1 0.8 copy-start.14
  31.5 93.8 %collective-permute-start = (bf16[4,296,256]{2,1,0:T(8,128)(2,1)}, bf16[4,296,256]{2,1,0:T(8,128)(2,1)S(1)}, u32[]{:S(2)}, u32[]{:S(2)}) collective-permute-start(bf16[4,296,256]{2,1,0:T(8,128)(2,1)} %copy-done.14), channel_id=1, source_target_pairs={{0,4},{4,0},{8,12},{12,8},{16,20},{20,16},{24,28},{28,24},{1,5},{5... | collective-permute-start | bytes 1818632 | tf_op jit(solution)/shard_map/ppermute | solution.py:392
  68.2 85.4 %collective-permute-start.6 = (bf16[4,296,256]{2,1,0:T(8,128)(2,1)}, bf16[4,296,256]{2,1,0:T(8,128)(2,1)}, u32[]{:S(2)}, u32[]{:S(2)}) collective-permute-start(bf16[4,296,256]{2,1,0:T(8,128)(2,1)} %take.31), channel_id=1, source_target_pairs={{0,28},{4,24},{8,4},{12,0},{16,12},{20,8},{24,20},{28,16},{1,29},{... | collective-permute-start | bytes 1818632 | tf_op jit(solution)/shard_map/ppermute | solution.py:392
  97.8 74.5 %collective-permute-start.10 = (bf16[4,296,256]{2,1,0:T(8,128)(2,1)}, bf16[4,296,256]{2,1,0:T(8,128)(2,1)}, u32[]{:S(2)}, u32[]{:S(2)}) collective-permute-start(bf16[4,296,256]{2,1,0:T(8,128)(2,1)} %take.36), channel_id=1, source_target_pairs={{0,16},{4,20},{8,24},{12,28},{16,0},{20,4},{24,8},{28,12},{1,17},{... | collective-permute-start | bytes 1818632 | tf_op jit(solution)/shard_map/ppermute | solution.py:392
  97.8 76.0 %collective-permute-start.8 = (bf16[4,296,256]{2,1,0:T(8,128)(2,1)}, bf16[4,296,256]{2,1,0:T(8,128)(2,1)}, u32[]{:S(2)}, u32[]{:S(2)}) collective-permute-start(bf16[4,296,256]{2,1,0:T(8,128)(2,1)} %take.34), channel_id=1, source_target_pairs={{0,8},{4,12},{8,16},{12,20},{16,24},{20,28},{24,0},{28,4},{1,9},{5... | collective-permute-start | bytes 1818632 | tf_op jit(solution)/shard_map/ppermute | solution.py:392
  125.3 60.1 %collective-permute-start.11 = (bf16[4,296,256]{2,1,0:T(8,128)(2,1)}, bf16[4,296,256]{2,1,0:T(8,128)(2,1)}, u32[]{:S(2)}, u32[]{:S(2)}) collective-permute-start(bf16[4,296,256]{2,1,0:T(8,128)(2,1)} %take.37), channel_id=1, source_target_pairs={{0,20},{4,16},{8,28},{12,24},{16,4},{20,0},{24,12},{28,8},{1,21},{... | collective-permute-start | bytes 1818632 | tf_op jit(solution)/shard_map/ppermute | solution.py:392
  125.3 0.9 copy-start.17
  126.1 88.7 %collective-permute-start.9 = (bf16[4,296,256]{2,1,0:T(8,128)(2,1)}, bf16[4,296,256]{2,1,0:T(8,128)(2,1)}, u32[]{:S(2)}, u32[]{:S(2)}) collective-permute-start(bf16[4,296,256]{2,1,0:T(8,128)(2,1)} %take.35), channel_id=1, source_target_pairs={{0,12},{4,8},{8,20},{12,16},{16,28},{20,24},{24,4},{28,0},{1,13},{... | collective-permute-start | bytes 1818632 | tf_op jit(solution)/shard_map/ppermute | solution.py:392
  129.2 0.9 copy-start.12
  133.2 0.8 copy-start.7
  135.2 0.9 copy-start.5
  137.2 0.8 copy-start.10
  139.2 0.8 copy-start.9
  146.5 6.8 %copy-start.20 = (s32[16]{0:T(128)S(1)}, s32[16]{0:T(128)}, u32[]{:S(2)}) copy-start(s32[16]{0:T(128)} %param.6) | copy-start | bytes 196
  153.6 64.0 %collective-permute-start.12 = (bf16[4,296,256]{2,1,0:T(8,128)(2,1)}, bf16[4,296,256]{2,1,0:T(8,128)(2,1)}, u32[]{:S(2)}, u32[]{:S(2)}) collective-permute-start(bf16[4,296,256]{2,1,0:T(8,128)(2,1)} %copy-done.13), channel_id=1, source_target_pairs={{0,24},{4,28},{8,0},{12,4},{16,8},{20,12},{24,16},{28,20},{1,25},{... | collective-permute-start | bytes 1818632 | tf_op jit(solution)/shard_map/ppermute | solution.py:392
  172.3 46.3 %collective-permute-start.7 = (bf16[4,296,256]{2,1,0:T(8,128)(2,1)}, bf16[4,296,256]{2,1,0:T(8,128)(2,1)}, u32[]{:S(2)}, u32[]{:S(2)}) collective-permute-start(bf16[4,296,256]{2,1,0:T(8,128)(2,1)} %copy-done.12), channel_id=1, source_target_pairs={{0,4},{4,0},{8,12},{12,8},{16,20},{20,16},{24,28},{28,24},{1,5},{5... | collective-permute-start | bytes 1818632 | tf_op jit(solution)/shard_map/ppermute | solution.py:392
  173.8 90.2 %collective-permute-start.13 = (bf16[4,296,256]{2,1,0:T(8,128)(2,1)}, bf16[4,296,256]{2,1,0:T(8,128)(2,1)}, u32[]{:S(2)}, u32[]{:S(2)}) collective-permute-start(bf16[4,296,256]{2,1,0:T(8,128)(2,1)} %copy-done.11), channel_id=1, source_target_pairs={{0,28},{4,24},{8,4},{12,0},{16,12},{20,8},{24,20},{28,16},{1,29},{... | collective-permute-start | bytes 1818632 | tf_op jit(solution)/shard_map/ppermute | solution.py:392
  185.3 81.6 %collective-permute-start.15 = (bf16[4,296,256]{2,1,0:T(8,128)(2,1)}, bf16[4,296,256]{2,1,0:T(8,128)(2,1)}, u32[]{:S(2)}, u32[]{:S(2)}) collective-permute-start(bf16[4,296,256]{2,1,0:T(8,128)(2,1)} %copy-done.10), channel_id=1, source_target_pairs={{0,8},{4,12},{8,16},{12,20},{16,24},{20,28},{24,0},{28,4},{1,9},{5... | collective-permute-start | bytes 1818632 | tf_op jit(solution)/shard_map/ppermute | solution.py:392
  214.8 62.2 %collective-permute-start.17 = (bf16[4,296,256]{2,1,0:T(8,128)(2,1)}, bf16[4,296,256]{2,1,0:T(8,128)(2,1)}, u32[]{:S(2)}, u32[]{:S(2)}) collective-permute-start(bf16[4,296,256]{2,1,0:T(8,128)(2,1)} %copy-done.9), channel_id=1, source_target_pairs={{0,16},{4,20},{8,24},{12,28},{16,0},{20,4},{24,8},{28,12},{1,17},{... | collective-permute-start | bytes 1818632 | tf_op jit(solution)/shard_map/ppermute | solution.py:392
  217.6 98.2 %copy-start.16 = (f32[256]{0:T(256)}, f32[256]{0:T(256)S(1)}, u32[]{:S(2)}) copy-start(f32[256]{0:T(256)S(1)} %select_reduce_fusion) | copy-start | bytes 3076
  217.6 88.2 %collective-permute-start.16 = (bf16[4,296,256]{2,1,0:T(8,128)(2,1)}, bf16[4,296,256]{2,1,0:T(8,128)(2,1)S(1)}, u32[]{:S(2)}, u32[]{:S(2)}) collective-permute-start(bf16[4,296,256]{2,1,0:T(8,128)(2,1)} %copy-done.4), channel_id=1, source_target_pairs={{0,12},{4,8},{8,20},{12,16},{16,28},{20,24},{24,4},{28,0},{1,13},{... | collective-permute-start | bytes 1818632 | tf_op jit(solution)/shard_map/ppermute | solution.py:392
  218.6 87.2 %collective-permute-start.18 = (bf16[4,296,256]{2,1,0:T(8,128)(2,1)S(1)}, bf16[4,296,256]{2,1,0:T(8,128)(2,1)S(1)}, u32[]{:S(2)}, u32[]{:S(2)}) collective-permute-start(bf16[4,296,256]{2,1,0:T(8,128)(2,1)S(1)} %take.45), channel_id=1, source_target_pairs={{0,20},{4,16},{8,28},{12,24},{16,4},{20,0},{24,12},{28,8},{1,21},{... | collective-permute-start | bytes 1818632 | tf_op jit(solution)/shard_map/ppermute | solution.py:392
  264.0 41.8 %collective-permute-start.19 = (bf16[4,296,256]{2,1,0:T(8,128)(2,1)S(1)}, bf16[4,296,256]{2,1,0:T(8,128)(2,1)S(1)}, u32[]{:S(2)}, u32[]{:S(2)}) collective-permute-start(bf16[4,296,256]{2,1,0:T(8,128)(2,1)S(1)} %take.46), channel_id=1, source_target_pairs={{0,24},{4,28},{8,0},{12,4},{16,8},{20,12},{24,16},{28,20},{1,25},{... | collective-permute-start | bytes 1818632 | tf_op jit(solution)/shard_map/ppermute | solution.py:392
  266.9 41.2 %collective-permute-start.14 = (bf16[4,296,256]{2,1,0:T(8,128)(2,1)S(1)}, bf16[4,296,256]{2,1,0:T(8,128)(2,1)S(1)}, u32[]{:S(2)}, u32[]{:S(2)}) collective-permute-start(bf16[4,296,256]{2,1,0:T(8,128)(2,1)S(1)} %take.41), channel_id=1, source_target_pairs={{0,4},{4,0},{8,12},{12,8},{16,20},{20,16},{24,28},{28,24},{1,5},{5... | collective-permute-start | bytes 1818632 | tf_op jit(solution)/shard_map/ppermute | solution.py:392
  277.0 38.8 %collective-permute-start.20 = (bf16[4,296,256]{2,1,0:T(8,128)(2,1)S(1)}, bf16[4,296,256]{2,1,0:T(8,128)(2,1)S(1)}, u32[]{:S(2)}, u32[]{:S(2)}) collective-permute-start(bf16[4,296,256]{2,1,0:T(8,128)(2,1)S(1)} %take.47), channel_id=1, source_target_pairs={{0,28},{4,24},{8,4},{12,0},{16,12},{20,8},{24,20},{28,16},{1,29},{... | collective-permute-start | bytes 1818632 | tf_op jit(solution)/shard_map/ppermute | solution.py:392
  279.3 1.1 copy-start.8
  280.4 0.8 copy-start.15
  281.3 1.1 copy-start.18
  282.3 9.0 %copy-start.6 = (bf16[4,296,256]{2,1,0:T(8,128)(2,1)S(1)}, bf16[4,296,256]{2,1,0:T(8,128)(2,1)}, u32[]{:S(2)}) copy-start(bf16[4,296,256]{2,1,0:T(8,128)(2,1)} %copy-done.5) | copy-start | bytes 1818628
  315.8 36.6 %copy-start.19 = (bf16[2,2,2]{2,1,0:T(2,128)(2,1)S(1)}, bf16[2,2,2]{2,1,0:T(2,128)(2,1)}, u32[]{:S(2)}) copy-start(bf16[2,2,2]{2,1,0:T(2,128)(2,1)} %constant.267.clone) | copy-start | bytes 52
  324.6 15.1 %all-to-all-start = ((f32[32,1,16,128]{3,2,1,0:T(8,128)}), f32[32,1,16,128]{3,2,1,0:T(8,128)S(1)}, u32[]{:S(2)}, u32[]{:S(2)}) async-start(f32[32,1,16,128]{3,2,1,0:T(8,128)} %bitcast.24), calls=%async_computation | async-start | bytes 524288 | tf_op jit(solution)/shard_map/all_to_all | solution.py:440
  347.4 12.3 %all-to-all-start.1 = ((bf16[32,1,18,128]{3,2,1,0:T(8,128)(2,1)}), bf16[32,1,18,128]{3,2,1,0:T(8,128)(2,1)S(1)}, u32[]{:S(2)}, u32[]{:S(2)}) async-start(bf16[32,1,18,128]{3,2,1,0:T(8,128)(2,1)} %broadcast_in_dim.27), calls=%async_computation.1 | async-start | bytes 393216 | tf_op jit(solution)/shard_map/all_to_all | solution.py:457
  362.5 86.3 %collective-permute-start.27 = (bf16[3,4,128,256]{3,2,1,0:T(8,128)(2,1)S(1)}, bf16[3,4,128,256]{3,2,1,0:T(8,128)(2,1)S(1)}, u32[]{:S(2)}, u32[]{:S(2)}) collective-permute-start(bf16[3,4,128,256]{3,2,1,0:T(8,128)(2,1)S(1)} %mix.8.refs_3_), channel_id=1, source_target_pairs={{0,16},{4,20},{8,24},{12,28},{16,0},{20,4},{24,8},{28,12},{1,17},{... | collective-permute-start | bytes 2359304 | tf_op jit(solution)/shard_map/ppermute | solution.py:392
  366.6 99.1 %collective-permute-start.26 = (bf16[3,4,128,256]{3,2,1,0:T(8,128)(2,1)S(1)}, bf16[3,4,128,256]{3,2,1,0:T(8,128)(2,1)S(1)}, u32[]{:S(2)}, u32[]{:S(2)}) collective-permute-start(bf16[3,4,128,256]{3,2,1,0:T(8,128)(2,1)S(1)} %mix.9.refs_3_), channel_id=1, source_target_pairs={{0,20},{4,16},{8,28},{12,24},{16,4},{20,0},{24,12},{28,8},{1,21},{... | collective-permute-start | bytes 2359304 | tf_op jit(solution)/shard_map/ppermute | solution.py:392
  371.0 103.2 %collective-permute-start.25 = (bf16[3,4,128,256]{3,2,1,0:T(8,128)(2,1)}, bf16[3,4,128,256]{3,2,1,0:T(8,128)(2,1)}, u32[]{:S(2)}, u32[]{:S(2)}) collective-permute-start(bf16[3,4,128,256]{3,2,1,0:T(8,128)(2,1)} %mix.10.refs_3_), channel_id=1, source_target_pairs={{0,8},{4,12},{8,16},{12,20},{16,24},{20,28},{24,0},{28,4},{1,9},{5... | collective-permute-start | bytes 2359304 | tf_op jit(solution)/shard_map/ppermute | solution.py:392
  375.3 125.9 %collective-permute-start.24 = (bf16[3,4,128,256]{3,2,1,0:T(8,128)(2,1)}, bf16[3,4,128,256]{3,2,1,0:T(8,128)(2,1)}, u32[]{:S(2)}, u32[]{:S(2)}) collective-permute-start(bf16[3,4,128,256]{3,2,1,0:T(8,128)(2,1)} %mix.11.refs_3_), channel_id=1, source_target_pairs={{0,12},{4,8},{8,20},{12,16},{16,28},{20,24},{24,4},{28,0},{1,13},{... | collective-permute-start | bytes 2359304 | tf_op jit(solution)/shard_map/ppermute | solution.py:392
  380.4 123.0 %collective-permute-start.23 = (bf16[3,4,128,256]{3,2,1,0:T(8,128)(2,1)S(1)}, bf16[3,4,128,256]{3,2,1,0:T(8,128)(2,1)}, u32[]{:S(2)}, u32[]{:S(2)}) collective-permute-start(bf16[3,4,128,256]{3,2,1,0:T(8,128)(2,1)S(1)} %mix.12.refs_3_), channel_id=1, source_target_pairs={{0,24},{4,28},{8,0},{12,4},{16,8},{20,12},{24,16},{28,20},{1,25},{... | collective-permute-start | bytes 2359304 | tf_op jit(solution)/shard_map/ppermute | solution.py:392
  448.9 0.9 copy-start
  449.8 55.7 %collective-permute-start.22 = (bf16[3,4,128,256]{3,2,1,0:T(8,128)(2,1)S(1)}, bf16[3,4,128,256]{3,2,1,0:T(8,128)(2,1)}, u32[]{:S(2)}, u32[]{:S(2)}) collective-permute-start(bf16[3,4,128,256]{3,2,1,0:T(8,128)(2,1)S(1)} %mix.14.refs_3_), channel_id=1, source_target_pairs={{0,4},{4,0},{8,12},{12,8},{16,20},{20,16},{24,28},{28,24},{1,5},{5... | collective-permute-start | bytes 2359304 | tf_op jit(solution)/shard_map/ppermute | solution.py:392
  465.7 0.9 copy-start.2
  466.6 38.8 %collective-permute-start.21 = (bf16[3,4,128,256]{3,2,1,0:T(8,128)(2,1)S(1)}, bf16[3,4,128,256]{3,2,1,0:T(8,128)(2,1)}, u32[]{:S(2)}, u32[]{:S(2)}) collective-permute-start(bf16[3,4,128,256]{3,2,1,0:T(8,128)(2,1)S(1)} %mix.13.refs_3_), channel_id=1, source_target_pairs={{0,28},{4,24},{8,4},{12,0},{16,12},{20,8},{24,20},{28,16},{1,29},{... | collective-permute-start | bytes 2359304 | tf_op jit(solution)/shard_map/ppermute | solution.py:392
  470.7 1.1 copy-start.1
  471.8 1.4 copy-start.3
  (3 other events, 2.5 us)
